TPU v7x, 32 devices: a whole 2x2x4 slice. The times are simulated.
32 devices in a mesh: ta: 4 (over x, core), xyz: 8 (over z, y).
Axes of the slice: x: 2, y: 2, z: 4, core: 2. Of those that a mesh axis runs over, the one named last changes fastest.
Arguments:
- nulls: bfloat16 [16, 32, 32, 16, 128], P('ta', 'xyz'), may hold values from -1.1953125 to 1.1953125
- time_links: bfloat16 [8, 32, 32, 64, 128], P('ta', 'xyz'), may hold values from -0.5 to 0.5
- space_links: bfloat16 [16, 16, 32, 64, 128], P('ta', 'xyz'), may hold values from -0.5 to 0.5
- owner_lists: int32 [8, 64], replicated, may hold values from -1 to 255, as said below
Outputs:
- coarse_links: float32 [4, 512, 1024], P('ta', 'xyz')
Inputs may be any that keep to these rules, and one draw needn't show every extreme that they name: `owner_lists`: row d lists, in increasing order, the aggregates that shard d owns, followed by -1 in the remaining slots; each of the 256 aggregate ids appears exactly once. Exactly half of the shards own 64 aggregates each and the others none. The 32 aggregates with ids q * 32 to q * 32 + 31 belong to exactly 4 owners, 8 to each.
All inputs are finite; a program needn't handle non-finite values.
Results may differ from a plain program's by a relative error of at most 0.0029.
Values may be sent and summed in bfloat16 or wider, within the bound.
No kernel may reach another device: no remote copies, remote signals or barrier semaphores. Data moves between devices by JAX's collectives and lax.ppermute only.
A program may use at most 64 MiB of HBM per device.

v0:
```python
import jax
import jax.numpy as jnp
from jax import lax
from jax.sharding import PartitionSpec as P


def shifted(array, axis, by):
    count = lax.axis_size(axis)
    return lax.ppermute(array, axis, [(i, (i + by) % count) for i in range(count)])


def forward_image(link_mats, upper_nulls):
    half_width = link_mats.shape[-2]
    upper_real = upper_nulls[..., :half_width]
    upper_imag = upper_nulls[..., half_width:]
    paired = jnp.stack(
        [
            jnp.concatenate([upper_real, -upper_imag], axis=-1),
            jnp.concatenate([upper_imag, upper_real], axis=-1),
        ],
        axis=-3,
    )
    image_pair = jnp.einsum(
        "...ik,...pnk->...pni", link_mats, paired, preferred_element_type=jnp.float32
    )
    joined = jnp.concatenate([image_pair[..., 0, :, :], image_pair[..., 1, :, :]], axis=-1)
    return joined.astype(jnp.bfloat16)


def conjugate_pair(lower_nulls):
    half_width = lower_nulls.shape[-1] // 2
    turned = jnp.concatenate(
        [-lower_nulls[..., half_width:], lower_nulls[..., :half_width]], axis=-1
    )
    return jnp.stack([lower_nulls, turned], axis=-3)


def on_device(nulls, time_links, space_links, owner_lists):
    time_rows, space_rows, side_rows, vectors, doubled = nulls.shape
    time_aggs = time_rows // 2
    space_aggs = space_rows // 2
    side_aggs = side_rows // 4
    local_count = time_aggs * space_aggs * side_aggs
    edge_time = shifted(nulls[0:1], "ta", -1)
    upper_time = jnp.concatenate([nulls[2::2], edge_time], axis=0)
    edge_space = shifted(nulls[:, 0:1], "xyz", -1)
    upper_space = jnp.concatenate([nulls[:, 2::2], edge_space], axis=1)
    image_time = forward_image(time_links, upper_time).reshape(
        time_aggs, space_aggs, 2, side_aggs, 4, vectors, doubled
    )
    pair_time = conjugate_pair(nulls[1::2]).reshape(
        time_aggs, space_aggs, 2, side_aggs, 4, 2, vectors, doubled
    )
    block_time = jnp.einsum(
        "txcaypnk,txcaymk->txapnm", pair_time, image_time, preferred_element_type=jnp.float32
    )
    image_space = forward_image(space_links, upper_space).reshape(
        time_aggs, 2, space_aggs, side_aggs, 4, vectors, doubled
    )
    pair_space = conjugate_pair(nulls[:, 1::2]).reshape(
        time_aggs, 2, space_aggs, side_aggs, 4, 2, vectors, doubled
    )
    block_space = jnp.einsum(
        "tcxaypnk,tcxaymk->txapnm", pair_space, image_space, preferred_element_type=jnp.float32
    )
    block_width = 2 * vectors * vectors
    link_rows = jnp.concatenate(
        [
            block_time.reshape(local_count, block_width),
            block_space.reshape(local_count, block_width),
        ],
        axis=1,
    )
    shard_index = lax.axis_index("xyz")
    my_list = lax.dynamic_index_in_dim(owner_lists, shard_index, 0, keepdims=False)
    present = my_list >= 0
    everything = lax.all_gather(link_rows, "xyz", axis=0, tiled=True)
    picked = everything[jnp.maximum(my_list, 0)]
    result = jnp.where(present[:, None], picked, 0.0)
    return result[None]


def solution(mesh):
    return jax.shard_map(
        on_device,
        mesh=mesh,
        in_specs=(
            P("ta", "xyz", None, None, None),
            P("ta", "xyz", None, None, None),
            P("ta", "xyz", None, None, None),
            P(),
        ),
        out_specs=P("ta", "xyz", None),
        check_vma=False,
    )
```

profile of v0, /device:TPU:0, one launch (start us, length us, event | category | flops | bytes accessed | tf_op | source)
XLA Modules:
  0.0 88.3 jit_solution(16451599250257205842)
XLA Ops:
  6.5 0.0 copy-start
  6.5 0.0 all-gather.2.cloned.1.call-start
  6.5 1.5 %fusion.37 = (bf16[1,4,32,16,128]{4,3,2,1,0:T(8,128)(2,1)S(1)}, bf16[1,4,32,16,128]{4,3,2,1,0:T(8,128)(2,1)S(1)}) fusion(bf16[4,4,32,16,128]{4,3,2,1,0:T(8,128)(2,1)} %param.4), kind=kLoop, calls=%fused_computation.48 | loop fusion | bytes 2097152 | tf_op jit(solution)/shard_map/slice | solution.py:45
  8.1 2.4 %collective-permute-start = (bf16[1,4,32,16,128]{4,3,2,1,0:T(8,128)(2,1)S(1)}, bf16[1,4,32,16,128]{4,3,2,1,0:T(8,128)(2,1)S(1)}, u32[]{:S(2)}, u32[]{:S(2)}) collective-permute-start(bf16[1,4,32,16,128]{4,3,2,1,0:T(8,128)(2,1)S(1)} %get-tuple-element.8), channel_id=1, source_target_pairs={{0,24},{8,0},{16,8},{24,16},{1,25},{9,1},{17,9},{25,17},{2,26},{10... | collective-permute-start | bytes 1572872 | tf_op jit(solution)/shard_map/ppermute | solution.py:9
  10.5 0.0 copy-done
  10.5 1.2 %fusion.39 = (bf16[4,1,32,16,128]{4,3,2,1,0:T(8,128)(2,1)}, bf16[4,1,32,16,128]{4,3,2,1,0:T(8,128)(2,1)}) fusion(bf16[4,4,32,16,128]{4,3,2,1,0:T(8,128)(2,1)S(1)} %copy-done), kind=kLoop, calls=%fused_computation.50 | loop fusion | bytes 2097152 | tf_op jit(solution)/shard_map/slice | solution.py:47
  11.7 4.6 %collective-permute-start.1 = (bf16[4,1,32,16,128]{4,3,2,1,0:T(8,128)(2,1)}, bf16[4,1,32,16,128]{4,3,2,1,0:T(8,128)(2,1)}, u32[]{:S(2)}, u32[]{:S(2)}) collective-permute-start(bf16[4,1,32,16,128]{4,3,2,1,0:T(8,128)(2,1)} %get-tuple-element.12), channel_id=1, source_target_pairs={{0,7},{1,0},{2,1},{3,2},{4,3},{5,4},{6,5},{7,6},{8,15},{9,8},{10,9... | collective-permute-start | bytes 1572872 | tf_op jit(solution)/shard_map/ppermute | solution.py:9
  16.2 0.2 slice.60
  16.4 0.2 slice.69
  16.6 0.4 slice_negate_fusion.1
  17.0 0.6 pad_maximum_fusion.4
  17.6 0.4 slice_negate_fusion
  18.1 0.6 pad_maximum_fusion.5
  18.7 0.0 collective-permute-done
  18.7 0.7 fusion.34
  19.4 0.0 copy-start.1
  19.4 1.2 %maximum_bitcast_fusion = (bf16[2,4,32,1,16,128]{5,4,3,2,1,0:T(8,128)(2,1)S(1)}, bf16[2,4,32,1,16,128]{5,4,3,2,1,0:T(8,128)(2,1)S(1)}) fusion(bf16[2,4,32,16,64]{4,3,2,1,0:T(8,128)(2,1)S(1)} %get-tuple-element.15, bf16[2,4,32,16,64]{4,3,2,1,0:T(8,128)(2,1)S(1)} %get-tuple-element.17, bf16[2,4,32,16,64]{4,3,2,1,0:T(8,128)(2,1)S(1)} %get-tuple-element.16), kind=kLoop, calls=%fused_computation.28 | loop fusion | flops 4194304 | bytes 3670016 | tf_op jit(solution)/shard_map/stack | solution.py:16
  20.6 1.0 %copy-done.1 = bf16[2,4,32,64,128]{4,3,2,1,0:T(8,128)(2,1)S(1)} copy-done((bf16[2,4,32,64,128]{4,3,2,1,0:T(8,128)(2,1)S(1)}, bf16[2,4,32,64,128]{4,3,2,1,0:T(8,128)(2,1)}, u32[]{:S(2)}) %copy-start.1) | copy-done | bytes 4194328
  21.6 2.3 %fusion.14 = bf16[2,4,32,2,16,64]{5,4,3,2,1,0:T(8,128)(2,1)S(1)} fusion(bf16[2,4,32,64,128]{4,3,2,1,0:T(8,128)(2,1)S(1)} %copy-done.1, bf16[2,4,32,1,16,128]{5,4,3,2,1,0:T(8,128)(2,1)S(1)} %get-tuple-element.14, bf16[2,4,32,1,16,128]{5,4,3,2,1,0:T(8,128)(2,1)S(1)} %get-tuple-element.13), kind=kOutput, calls=%fused_computation.17 | convolution fusion | flops 135790592 | bytes 7340032 | tf_op jit(solution)/shard_map/...ik,...pnk->...pni/dot_general | solution.py:23
  23.8 0.6 fusion.36
  24.4 0.0 copy-start.3
  24.4 1.0 %fusion.24 = f32[2,2,8,2,16,16]{5,4,3,2,1,0:T(8,128)S(1)} fusion(bf16[2,2,2,8,4,1,16,128]{7,6,4,3,2,1,0,5:T(8,128)(2,1)S(1)} %bitcast.63, bf16[2,2,2,8,4,1,16,128]{7,6,4,3,2,1,0,5:T(8,128)(2,1)S(1)} %bitcast.61, bf16[2,2,2,8,4,16,64]{6,5,4,3,2,1,0:T(8,128)(2,1)S(1)} %bitcast.65, bf16[2,2,2,8,4,16,64]{6,5,4,3,2,1,0:T(8,128)(2,1)S(1)} %bitcast.64), kind=kOutput, calls=%fused_computation.19 | convolution fusion | flops 36700160 | bytes 3211264 | tf_op jit(solution)/shard_map/txcaypnk,txcaymk->txapnm/dot_general | solution.py:54
  25.4 0.3 reshape.75
  25.7 1.8 %collective-permute-done.1 = bf16[4,1,32,16,128]{4,3,2,1,0:T(8,128)(2,1)} collective-permute-done((bf16[4,1,32,16,128]{4,3,2,1,0:T(8,128)(2,1)}, bf16[4,1,32,16,128]{4,3,2,1,0:T(8,128)(2,1)}, u32[]{:S(2)}, u32[]{:S(2)}) %collective-permute-start.1) | collective-permute-done | bytes 524320 | tf_op jit(solution)/shard_map/ppermute | solution.py:9
  27.5 0.0 copy-done.3
  27.5 1.9 %fusion.35 = (bf16[4,2,32,16,64]{4,3,2,1,0:T(8,128)(2,1)S(1)}, bf16[4,2,32,16,64]{4,3,2,1,0:T(8,128)(2,1)S(1)}, bf16[4,2,32,16,64]{4,3,2,1,0:T(8,128)(2,1)S(1)}) fusion(bf16[4,1,32,16,128]{4,3,2,1,0:T(8,128)(2,1)} %collective-permute-done.1, bf16[4,1,32,16,128]{4,3,2,1,0:T(8,128)(2,1)S(1)} %copy-done.3), kind=kLoop, calls=%fused_computation.46 | loop fusion | flops 2621440 | bytes 2621440 | tf_op jit(solution)/shard_map/neg | solution.py:18
  29.4 0.0 copy-start.2
  29.4 1.2 %maximum_bitcast_fusion.3 = (bf16[4,2,32,1,16,128]{5,4,3,2,1,0:T(8,128)(2,1)S(1)}, bf16[4,2,32,1,16,128]{5,4,3,2,1,0:T(8,128)(2,1)S(1)}) fusion(bf16[4,2,32,16,64]{4,3,2,1,0:T(8,128)(2,1)S(1)} %get-tuple-element.22, bf16[4,2,32,16,64]{4,3,2,1,0:T(8,128)(2,1)S(1)} %get-tuple-element.24, bf16[4,2,32,16,64]{4,3,2,1,0:T(8,128)(2,1)S(1)} %get-tuple-element.23), kind=kLoop, calls=%fused_computation.32 | loop fusion | flops 4194304 | bytes 3670016 | tf_op jit(solution)/shard_map/stack | solution.py:16
  30.6 1.0 %copy-done.2 = bf16[4,2,32,64,128]{4,3,2,1,0:T(8,128)(2,1)S(1)} copy-done((bf16[4,2,32,64,128]{4,3,2,1,0:T(8,128)(2,1)S(1)}, bf16[4,2,32,64,128]{4,3,2,1,0:T(8,128)(2,1)}, u32[]{:S(2)}) %copy-start.2) | copy-done | bytes 4194328
  31.6 2.3 %fusion.19 = bf16[4,2,32,2,16,64]{5,4,3,2,1,0:T(8,128)(2,1)S(1)} fusion(bf16[4,2,32,64,128]{4,3,2,1,0:T(8,128)(2,1)S(1)} %copy-done.2, bf16[4,2,32,1,16,128]{5,4,3,2,1,0:T(8,128)(2,1)S(1)} %get-tuple-element.21, bf16[4,2,32,1,16,128]{5,4,3,2,1,0:T(8,128)(2,1)S(1)} %get-tuple-element.20), kind=kOutput, calls=%fused_computation.18 | convolution fusion | flops 135790592 | bytes 7340032 | tf_op jit(solution)/shard_map/...ik,...pnk->...pni/dot_general | solution.py:23
  33.9 0.6 fusion.38
  34.4 1.0 %fusion.27 = f32[2,2,8,2,16,16]{5,4,3,2,1,0:T(8,128)S(1)} fusion(bf16[2,2,2,8,4,1,16,128]{7,6,4,3,2,1,0,5:T(8,128)(2,1)S(1)} %bitcast.62, bf16[2,2,2,8,4,1,16,128]{7,6,4,3,2,1,0,5:T(8,128)(2,1)S(1)} %bitcast.60, bf16[2,2,2,8,4,16,64]{6,5,4,3,2,1,0:T(8,128)(2,1)S(1)} %bitcast.67, bf16[2,2,2,8,4,16,64]{6,5,4,3,2,1,0:T(8,128)(2,1)S(1)} %bitcast.66), kind=kOutput, calls=%fused_computation.20 | convolution fusion | flops 36700160 | bytes 3211264 | tf_op jit(solution)/shard_map/tcxaypnk,tcxaymk->txapnm/dot_general | solution.py:63
  35.5 0.3 reshape.76
  35.7 0.7 pad_maximum_fusion.6
  36.4 0.0 all-gather.2.cloned.1.call-update
  36.4 0.7 maximum_bitcast_fusion.6
  37.1 0.7 compare_bitcast_fusion
  37.8 40.8 %all-gather.2.cloned.1.call-done = f32[256,1024]{1,0:T(8,128)} async-done(((f32[32,1024]{1,0:T(8,128)}), f32[256,1024]{1,0:T(8,128)}) %all-gather.2.cloned.1.call-update) | async-done | bytes 1048592 | tf_op jit(solution)/shard_map/all_gather | solution.py:77
  78.6 2.0 %gather_fusion = f32[64,1024]{1,0:T(8,128)S(1)} fusion(f32[256,1024]{1,0:T(8,128)} %all-gather.2.cloned.1.call-done, s32[1024]{0:T(1024)S(1)} %pad_clamp_fusion), kind=kCustom, calls=%fused_computation | custom fusion | bytes 524544 | tf_op jit(solution)/shard_map/gather | solution.py:78
  80.6 0.8 bitcast_select_fusion
  (1 shorter events, 0.0 us)
Async XLA Ops:
  6.5 4.0 %copy-start = (bf16[4,4,32,16,128]{4,3,2,1,0:T(8,128)(2,1)S(1)}, bf16[4,4,32,16,128]{4,3,2,1,0:T(8,128)(2,1)}, u32[]{:S(2)}) copy-start(bf16[4,4,32,16,128]{4,3,2,1,0:T(8,128)(2,1)} %param.4) | copy-start | bytes 6291460
  6.5 72.1 %all-gather.2.cloned.1.call-start = ((), (), s32[]{:S(2)}) async-start(), calls=%async_computation | async-start | bytes 1179648 | tf_op jit(solution)/shard_map/all_gather | solution.py:77
  8.1 10.6 %collective-permute-start = (bf16[1,4,32,16,128]{4,3,2,1,0:T(8,128)(2,1)S(1)}, bf16[1,4,32,16,128]{4,3,2,1,0:T(8,128)(2,1)S(1)}, u32[]{:S(2)}, u32[]{:S(2)}) collective-permute-start(bf16[1,4,32,16,128]{4,3,2,1,0:T(8,128)(2,1)S(1)} %get-tuple-element.8), channel_id=1, source_target_pairs={{0,24},{8,0},{16,8},{24,16},{1,25},{9,1},{17,9},{25,17},{2,26},{10... | collective-permute-start | bytes 1572872 | tf_op jit(solution)/shard_map/ppermute | solution.py:9
  11.7 15.8 %collective-permute-start.1 = (bf16[4,1,32,16,128]{4,3,2,1,0:T(8,128)(2,1)}, bf16[4,1,32,16,128]{4,3,2,1,0:T(8,128)(2,1)}, u32[]{:S(2)}, u32[]{:S(2)}) collective-permute-start(bf16[4,1,32,16,128]{4,3,2,1,0:T(8,128)(2,1)} %get-tuple-element.12), channel_id=1, source_target_pairs={{0,7},{1,0},{2,1},{3,2},{4,3},{5,4},{6,5},{7,6},{8,15},{9,8},{10,9... | collective-permute-start | bytes 1572872 | tf_op jit(solution)/shard_map/ppermute | solution.py:9
  19.4 2.2 %copy-start.1 = (bf16[2,4,32,64,128]{4,3,2,1,0:T(8,128)(2,1)S(1)}, bf16[2,4,32,64,128]{4,3,2,1,0:T(8,128)(2,1)}, u32[]{:S(2)}) copy-start(bf16[2,4,32,64,128]{4,3,2,1,0:T(8,128)(2,1)} %param.5) | copy-start | bytes 12582916
  24.4 3.1 %copy-start.3 = (bf16[4,1,32,16,128]{4,3,2,1,0:T(8,128)(2,1)S(1)}, bf16[4,1,32,16,128]{4,3,2,1,0:T(8,128)(2,1)}, u32[]{:S(2)}) copy-start(bf16[4,1,32,16,128]{4,3,2,1,0:T(8,128)(2,1)} %get-tuple-element.11) | copy-start | bytes 1572868
  29.4 2.2 %copy-start.2 = (bf16[4,2,32,64,128]{4,3,2,1,0:T(8,128)(2,1)S(1)}, bf16[4,2,32,64,128]{4,3,2,1,0:T(8,128)(2,1)}, u32[]{:S(2)}) copy-start(bf16[4,2,32,64,128]{4,3,2,1,0:T(8,128)(2,1)} %param.6) | copy-start | bytes 12582916
Sparse Core Ops, SparseCore 0:
  36.6 42.0 all-gather.1
where the time goes:
time: 88.6 us; the launch traced here: 88.3 us
  waiting for transfers between devices  42.5 us (48%)
  between operations  13.5 us (15%)
  other arithmetic  9.83 us (11%)
  local copies, waits for them, and re-layouts  8.77 us (10%)
  starting transfers between devices  6.99 us (8%)
  matrix products  6.58 us (7%)
    all_gather x1, waiting for transfers between devices, on_device(): everything = lax.all_gather(link_rows, 'xyz', axis=0, tiled=True)  40.8 us
    ppermute x2, starting transfers between devices, shifted(): lax.ppermute(array, axis, [(i, (i + by) % count) for i in range(count)])  6.99 us
    dot_general x2, matrix products, forward_image(): jnp.einsum('...ik,...pnk->...pni', link_mats, paired, preferred_element_t...  4.55 us
    neg x2, other arithmetic, forward_image(): -upper_imag  2.63 us
    another operation x2, other arithmetic, forward_image(): jnp.stack([jnp.concatenate([upper_real, -upper_imag], axis=-1), jnp.conca...  2.32 us
    unnamed x8, local copies, waits for them, and re-layouts  2.05 us
    gather x1, local copies, waits for them, and re-layouts, on_device(): picked = everything[jnp.maximum(my_list, 0)]  2.02 us
  transfers between devices with their start and end apart: 3, of which 2 were waited for; matrix products, arithmetic and copies ran while one was open for 12% of the time, Pallas kernels for 0%

commit v1 on v0

v1 whole, which is shorter than its diff:
```python
import jax
import jax.numpy as jnp
from jax import lax
from jax.experimental import pallas as pl
from jax.experimental.pallas import tpu as pltpu
from jax.sharding import PartitionSpec as P

ROW_DIMS = (((1,), (1,)), ((), ()))
MAT_DIMS = (((1,), (0,)), ((), ()))
SIDE = 4
MOST = 8


def shifted(array, axis, by):
    count = lax.axis_size(axis)
    return lax.ppermute(array, axis, [(i, (i + by) % count) for i in range(count)])


def dot(left, right, dims):
    return lax.dot_general(left, right, dims, preferred_element_type=jnp.float32)


def swapped(array):
    return pltpu.roll(array, array.shape[-1] // 2, axis=array.ndim - 1)


def lower_half(shape):
    return lax.broadcasted_iota(jnp.int32, shape, len(shape) - 1) < shape[-1] // 2


def signs(shape, dtype):
    return jnp.where(lower_half(shape), 1.0, -1.0).astype(dtype)


def image_item(links, lower, upper, slot, left_ref, right_ref):
    sites, vectors, width = lower.shape
    half = width // 2
    low = lower_half((vectors, width))
    sign = signs((vectors, width), jnp.bfloat16)
    for pair in range(sites // 2):
        agg, part = divmod(pair, SIDE // 2)
        at = 2 * pair
        up_a, up_b = upper[at], upper[at + 1]
        rows = jnp.concatenate([up_a * sign, swapped(up_a), up_b * sign, swapped(up_b)], axis=0)
        mats = links[pl.ds(at, 2)].reshape(2 * half, width)
        images = dot(rows, mats, ROW_DIMS)
        real = jnp.where(low, images[:vectors], images[2 * vectors : 3 * vectors])
        imag = jnp.where(low, images[vectors : 2 * vectors], images[3 * vectors :])
        cols = pl.ds((slot * 2 + part) * 2 * width, 2 * width)
        right_ref[pl.ds(agg * vectors, vectors), cols] = jnp.concatenate([real, imag], axis=1).astype(jnp.bfloat16)
        lo_a, lo_b = lower[at], lower[at + 1]
        lo_real = jnp.where(low, lo_a, swapped(lo_b))
        lo_imag = jnp.where(low, swapped(lo_a), lo_b)
        left_ref[pl.ds(agg * 2 * vectors, 2 * vectors), cols] = jnp.concatenate(
            [
                jnp.concatenate([lo_real, lo_imag], axis=1),
                jnp.concatenate([-lo_imag, lo_real], axis=1),
            ],
            axis=0,
        )


def adjoint_item(links, lower, slot, left_ref):
    sites, vectors, width = lower.shape
    half = width // 2
    low = lower_half((vectors, width))
    sign = signs((vectors, width), jnp.float32)
    for pair in range(sites // 2):
        agg, part = divmod(pair, SIDE // 2)
        at = 2 * pair
        lo_a, lo_b = lower[at], lower[at + 1]
        zero = jnp.zeros_like(lo_a)
        rows = jnp.concatenate(
            [
                jnp.where(low, lo_a, zero),
                jnp.where(low, swapped(lo_a), zero),
                jnp.where(low, zero, swapped(lo_b)),
                jnp.where(low, zero, lo_b),
            ],
            axis=0,
        )
        mats = links[pl.ds(at, 2)].reshape(2 * half, width)
        prod = dot(rows, mats, MAT_DIMS)
        adj_a = sign * prod[:vectors] + swapped(prod[vectors : 2 * vectors])
        adj_b = sign * prod[2 * vectors : 3 * vectors] + swapped(prod[3 * vectors :])
        turn_a = -sign * swapped(adj_a)
        turn_b = -sign * swapped(adj_b)
        cols = pl.ds((slot * 2 + part) * 2 * width, 2 * width)
        left_ref[pl.ds(agg * 2 * vectors, 2 * vectors), cols] = jnp.concatenate(
            [
                jnp.concatenate([adj_a, adj_b], axis=1),
                jnp.concatenate([turn_a, turn_b], axis=1),
            ],
            axis=0,
        ).astype(jnp.bfloat16)


def group_rows(left, right, vectors):
    full = dot(left, right, ROW_DIMS)
    aggs = full.shape[1] // vectors
    lanes = lax.broadcasted_iota(jnp.int32, (2 * vectors, full.shape[1]), 1) // vectors
    own = jnp.zeros((2 * vectors, full.shape[1]), jnp.float32)
    for agg in range(aggs):
        own = jnp.where(lanes == agg, full[agg * 2 * vectors : (agg + 1) * 2 * vectors], own)
    pieces = []
    lane_group = lax.broadcasted_iota(jnp.int32, (aggs, full.shape[1]), 1) // vectors
    sub = lax.broadcasted_iota(jnp.int32, (aggs, full.shape[1]), 0)
    total = full.shape[1]
    for piece in range(2 * vectors // aggs):
        value = own[piece * aggs : (piece + 1) * aggs]
        step = 1
        while step < aggs:
            sub_bit = (sub // step) % 2
            lane_bit = (lane_group // step) % 2
            up = pltpu.roll(pltpu.roll(value, aggs - step, axis=0), step * vectors, axis=1)
            down = pltpu.roll(pltpu.roll(value, step, axis=0), total - step * vectors, axis=1)
            value = jnp.where(sub_bit == lane_bit, value, jnp.where(sub_bit == 0, up, down))
            step *= 2
        pieces.append(value)
    return jnp.concatenate(pieces, axis=1)


def inner_kernel(place, lists, nulls, time_links, space_links, time_rows, space_rows, adjoint, picks, links, left, right, sems):
    time_count, space_count, sites, vectors, width = nulls.shape
    copies = []

    def fetch(source):
        slot = len(copies)
        copy = pltpu.make_async_copy(source, links.at[slot], sems.at[slot])
        copy.start()
        copies.append(copy)

    for x in range(4):
        fetch(time_links.at[0, x])
    for t in range(4):
        fetch(space_links.at[t, 0])
    for t in range(4):
        fetch(space_links.at[t, 1])
    me = place[0]
    shards, cap = lists.shape
    count = picks.shape[2]
    lane = lax.broadcasted_iota(jnp.int32, (MOST, cap), 1)
    want = lax.broadcasted_iota(jnp.int32, (MOST, cap), 0)
    column = lax.broadcasted_iota(jnp.int32, (MOST, count), 1)
    quarter = count // 4
    turned = (column // quarter % 2) * 2 * quarter + (column // (2 * quarter)) * quarter + column % quarter
    for shard in range(shards):
        mine = jnp.broadcast_to(lists[pl.ds(shard, 1), :], (MOST, cap))
        before = jnp.where((mine >= 0) & (mine < me * count), 1, 0)
        start = jnp.sum(before.astype(jnp.float32), axis=1, keepdims=True).astype(jnp.int32)
        inside = (mine >= me * count) & (mine < (me + 1) * count)
        match = inside & (lane - start == want)
        chosen = jnp.sum(jnp.where(match, mine - me * count + 1, 0).astype(jnp.float32), axis=1, keepdims=True)
        chosen = chosen.astype(jnp.int32) - 1
        picks[0, pl.ds(shard * MOST, MOST), :] = jnp.where(column == chosen, 1.0, 0.0)
        picks[1, pl.ds(shard * MOST, MOST), :] = jnp.where(turned == chosen, 1.0, 0.0)
    for a_x in range(2):
        for c in range(2):
            x = 2 * a_x + c
            copies[x].wait()
            image_item(links.at[x], nulls.at[1, x], nulls.at[2, x], c, left, right)
        time_rows[pl.ds(a_x * 8, 8), :] = group_rows(left[...], right[...], vectors)
    for a_t in range(2):
        for c in range(2):
            t = 2 * a_t + c
            copies[4 + t].wait()
            image_item(links.at[4 + t], nulls.at[t, 1], nulls.at[t, 2], c, left, right)
        space_rows[pl.ds(a_t * 8, 8), :] = group_rows(left[...], right[...], vectors)
    for t in range(4):
        copies[8 + t].wait()
        adjoint_item(links.at[8 + t], nulls.at[t, 3], t % 2, adjoint.at[t // 2])


def time_edge_kernel(nulls, edge, time_links, time_rows, links, left, right, sems):
    vectors = nulls.shape[-2]
    copies = []
    for x in range(4):
        copy = pltpu.make_async_copy(time_links.at[1, x], links.at[x], sems.at[x])
        copy.start()
        copies.append(copy)
    for a_x in range(2):
        for c in range(2):
            x = 2 * a_x + c
            copies[x].wait()
            image_item(links.at[x], nulls.at[0, x], edge.at[0, x], c, left, right)
        time_rows[pl.ds(a_x * 8, 8), :] = group_rows(left[...], right[...], vectors)


def final_kernel(edge, adjoint, picks, time_low, time_high, space_low, packed):
    sites, vectors, width = edge.shape[2:]
    aggs = sites // SIDE
    found = []
    for a_t in range(2):
        parts = []
        for c in range(2):
            for site in range(SIDE):
                rows = [edge[2 * a_t + c, 0, agg * SIDE + site] for agg in range(aggs)]
                parts.append(jnp.concatenate(rows, axis=0))
        found.append(group_rows(adjoint[a_t], jnp.concatenate(parts, axis=1), vectors))
    time_rows = jnp.concatenate([time_low[...], time_high[...]], axis=0).astype(jnp.bfloat16)
    space_rows = jnp.concatenate([space_low[...]] + found, axis=0).astype(jnp.bfloat16)
    wide = time_rows.shape[1]
    packed[:, pl.ds(0, wide)] = dot(picks[0].astype(jnp.bfloat16), time_rows, MAT_DIMS).astype(jnp.bfloat16)
    packed[:, pl.ds(wide, wide)] = dot(picks[1].astype(jnp.bfloat16), space_rows, MAT_DIMS).astype(jnp.bfloat16)


def on_device(nulls, time_links, space_links, owner_lists):
    time_count, space_count, sites, vectors, width = nulls.shape
    shards, cap = owner_lists.shape
    aggs = sites // SIDE
    local_count = (time_count // 2) * (space_count // 2) * aggs
    wide = 2 * vectors * vectors
    edge_space = shifted(nulls[:, 0:1], "xyz", -1)
    edge_time = shifted(nulls[0:1], "ta", -1)
    place = lax.axis_index("xyz").astype(jnp.int32).reshape(1)
    vmem = pl.BlockSpec(memory_space=pltpu.VMEM)
    smem = pl.BlockSpec(memory_space=pltpu.SMEM)
    anywhere = pl.BlockSpec(memory_space=pl.ANY)
    half = width // 2
    grouped = [
        pltpu.VMEM((2 * vectors * aggs, 8 * width), jnp.bfloat16),
        pltpu.VMEM((vectors * aggs, 8 * width), jnp.bfloat16),
    ]
    params = pltpu.CompilerParams(vmem_limit_bytes=40 * 1024 * 1024)
    time_low, space_low, adjoint, picks = pl.pallas_call(
        inner_kernel,
        in_specs=[smem, vmem, vmem, anywhere, anywhere],
        out_specs=[vmem] * 4,
        out_shape=[
            jax.ShapeDtypeStruct((2 * aggs, wide), jnp.float32),
            jax.ShapeDtypeStruct((2 * aggs, wide), jnp.float32),
            jax.ShapeDtypeStruct((2, 2 * vectors * aggs, 8 * width), jnp.bfloat16),
            jax.ShapeDtypeStruct((2, shards * MOST, local_count), jnp.float32),
        ],
        scratch_shapes=[pltpu.VMEM((12, sites, half, width), jnp.bfloat16)] + grouped + [pltpu.SemaphoreType.DMA((12,))],
        compiler_params=params,
        cost_estimate=pl.CostEstimate(flops=400 * 10**6, bytes_accessed=10 * 2**20, transcendentals=0),
        name="inner",
    )(place, owner_lists, nulls, time_links, space_links)
    time_high = pl.pallas_call(
        time_edge_kernel,
        in_specs=[vmem, vmem, anywhere],
        out_specs=vmem,
        out_shape=jax.ShapeDtypeStruct((2 * aggs, wide), jnp.float32),
        scratch_shapes=[pltpu.VMEM((4, sites, half, width), jnp.bfloat16)] + grouped + [pltpu.SemaphoreType.DMA((4,))],
        compiler_params=params,
        cost_estimate=pl.CostEstimate(flops=130 * 10**6, bytes_accessed=3 * 2**20, transcendentals=0),
        name="time_edge",
    )(nulls[3:4], edge_time, time_links)
    packed = pl.pallas_call(
        final_kernel,
        in_specs=[vmem] * 6,
        out_specs=vmem,
        out_shape=jax.ShapeDtypeStruct((shards * MOST, 2 * wide), jnp.bfloat16),
        compiler_params=params,
        cost_estimate=pl.CostEstimate(flops=130 * 10**6, bytes_accessed=2 * 2**20, transcendentals=0),
        name="final",
    )(edge_space, adjoint, picks, time_low, time_high, space_low)
    arrived = lax.all_to_all(packed, "xyz", 0, 0, tiled=True)
    if shards * MOST == cap:
        result = arrived.astype(jnp.float32)
    else:
        my_list = lax.dynamic_index_in_dim(owner_lists, lax.axis_index("xyz"), 0, keepdims=False)
        source = jnp.maximum(my_list, 0) // local_count
        order = jnp.arange(cap, dtype=jnp.int32)
        same = (source[:, None] == source[None, :]) & (order[None, :] < order[:, None])
        offset = jnp.sum(same.astype(jnp.int32), axis=1)
        picked = arrived[source * MOST + offset].astype(jnp.float32)
        result = jnp.where((my_list >= 0)[:, None], picked, 0.0)
    return result[None]


def solution(mesh):
    return jax.shard_map(
        on_device,
        mesh=mesh,
        in_specs=(
            P("ta", "xyz", None, None, None),
            P("ta", "xyz", None, None, None),
            P("ta", "xyz", None, None, None),
            P(),
        ),
        out_specs=P("ta", "xyz", None),
        check_vma=False,
    )
```

time: 88.6 us -> 41 us (0.46)
  waiting for transfers between devices: 42.5 us -> 0.01 us
  Pallas kernels: 0 us -> 13.9 us
  between operations: 13.5 us -> 0.06 us
  blocking collectives: 0 us -> 9.74 us
  other arithmetic: 9.83 us -> 0.72 us
  matrix products: 6.58 us -> 0 us
    all_gather x1 -> x0, waiting for transfers between devices: 40.8 us -> none  [on_device(): everything = lax.all_gather(link_rows, 'xyz', axis=0, tiled=True)]
    pallas_call x0 -> x3, Pallas kernels: none -> 13.9 us  [the longest x1 8.9 us: on_device(): pl.pallas_call(inner_kernel, in_specs=[smem, vmem, vmem, anywhere, anywhe...]
    all_to_all x0 -> x1, blocking collectives: none -> 9.74 us  [on_device(): arrived = lax.all_to_all(packed, 'xyz', 0, 0, tiled=True)]
    dot_general x4 -> x0, matrix products: 6.58 us -> none  [the longest x2 4.55 us: forward_image(): jnp.einsum('...ik,...pnk->...pni', link_mats, paired, preferred_element_t...]
    neg x4 -> x0, other arithmetic: 3.5 us -> none  [the longest x2 2.63 us: forward_image(): -upper_imag]
    unnamed x8 -> x10, local copies, waits for them, and re-layouts: 2.05 us -> 5.07 us
    another operation x2 -> x0, other arithmetic: 2.32 us -> none  [forward_image(): jnp.stack([jnp.concatenate([upper_real, -upper_imag], axis=-1), jnp.conca...]
    gather x1 -> x0, local copies, waits for them, and re-layouts: 2.02 us -> none  [on_device(): picked = everything[jnp.maximum(my_list, 0)]]
  transfers between devices with their start and end apart: 3 -> 2, of which waited for: 2 -> 0; matrix products, arithmetic and copies ran while one was open for 12% -> 5% of each run, Pallas kernels for 0% -> 32%
where the time goes in v1:
time: 41 us; the launch traced here: 40.6 us
  Pallas kernels  13.9 us (34%)
  blocking collectives  9.74 us (24%)
  local copies, waits for them, and re-layouts  9.28 us (23%)
  starting transfers between devices  6.94 us (17%)
  other arithmetic  0.72 us (2%)
    all_to_all x1, blocking collectives, on_device(): arrived = lax.all_to_all(packed, 'xyz', 0, 0, tiled=True)  9.74 us
    pallas_call x1, Pallas kernels, on_device(): pl.pallas_call(inner_kernel, in_specs=[smem, vmem, vmem, anywhere, anywhe...  8.9 us
    ppermute x2, starting transfers between devices, shifted(): lax.ppermute(array, axis, [(i, (i + by) % count) for i in range(count)])  6.94 us
    unnamed x10, local copies, waits for them, and re-layouts  5.07 us
    pallas_call x1, Pallas kernels, on_device(): pl.pallas_call(time_edge_kernel, in_specs=[vmem, vmem, anywhere], out_spe...  4.22 us
    slice x1, local copies, waits for them, and re-layouts, on_device(): edge_time = shifted(nulls[0:1], 'ta', -1)  2.33 us
    slice x1, local copies, waits for them, and re-layouts, on_device(): edge_space = shifted(nulls[:, 0:1], 'xyz', -1)  1.88 us
  transfers between devices with their start and end apart: 2, of which 0 were waited for; matrix products, arithmetic and copies ran while one was open for 5% of the time, Pallas kernels for 32%

profile of v1, /device:TPU:0, one launch (start us, length us, event | category | flops | bytes accessed | tf_op | source)
XLA Modules:
  0.0 40.6 jit_solution(8528802346465056768)
XLA Ops:
  0.0 0.0 copy-start.2
  0.0 2.3 %fusion = (bf16[1,4,32,16,128]{4,3,2,1,0:T(8,128)(2,1)}, bf16[1,4,32,16,128]{4,3,2,1,0:T(8,128)(2,1)S(1)}) fusion(bf16[4,4,32,16,128]{4,3,2,1,0:T(8,128)(2,1)} %nulls.1), kind=kLoop, calls=%fused_computation.1 | loop fusion | bytes 2097152 | tf_op jit(solution)/shard_map/slice | solution.py:214
  2.3 2.4 %collective-permute-start.1 = (bf16[1,4,32,16,128]{4,3,2,1,0:T(8,128)(2,1)}, bf16[1,4,32,16,128]{4,3,2,1,0:T(8,128)(2,1)}, u32[]{:S(2)}, u32[]{:S(2)}) collective-permute-start(bf16[1,4,32,16,128]{4,3,2,1,0:T(8,128)(2,1)} %get-tuple-element.13), channel_id=1, source_target_pairs={{0,24},{8,0},{16,8},{24,16},{1,25},{9,1},{17,9},{25,17},{2,26},{10... | collective-permute-start | bytes 1572872 | tf_op jit(solution)/shard_map/ppermute | solution.py:16
  4.7 1.9 %slice.9 = bf16[4,1,32,16,128]{4,3,2,1,0:T(8,128)(2,1)} slice(bf16[4,4,32,16,128]{4,3,2,1,0:T(8,128)(2,1)} %nulls.1), slice={[0:4], [0:1], [0:32], [0:16], [0:128]} | slice | bytes 1048576 | tf_op jit(solution)/shard_map/slice | solution.py:213
  6.6 4.6 %collective-permute-start = (bf16[4,1,32,16,128]{4,3,2,1,0:T(8,128)(2,1)}, bf16[4,1,32,16,128]{4,3,2,1,0:T(8,128)(2,1)S(1)}, u32[]{:S(2)}, u32[]{:S(2)}) collective-permute-start(bf16[4,1,32,16,128]{4,3,2,1,0:T(8,128)(2,1)} %slice.9), channel_id=1, source_target_pairs={{0,7},{1,0},{2,1},{3,2},{4,3},{5,4},{6,5},{7,6},{8,15},{9,8},{10,9... | collective-permute-start | bytes 1572872 | tf_op jit(solution)/shard_map/ppermute | solution.py:16
  11.1 0.0 copy-done.2
  11.1 0.0 copy-start
  11.2 2.2 %copy-done = bf16[2,4,32,64,128]{4,3,2,1,0:T(8,128)(2,1)S(1)} copy-done((bf16[2,4,32,64,128]{4,3,2,1,0:T(8,128)(2,1)S(1)}, bf16[2,4,32,64,128]{4,3,2,1,0:T(8,128)(2,1)}, u32[]{:S(2)}) %copy-start) | copy-done | bytes 4194328
  13.3 0.0 copy-start.3
  13.3 2.2 %copy-done.3 = bf16[4,2,32,64,128]{4,3,2,1,0:T(8,128)(2,1)S(1)} copy-done((bf16[4,2,32,64,128]{4,3,2,1,0:T(8,128)(2,1)S(1)}, bf16[4,2,32,64,128]{4,3,2,1,0:T(8,128)(2,1)}, u32[]{:S(2)}) %copy-start.3) | copy-done | bytes 4194328
  15.5 0.0 copy-start.4
  15.5 0.7 %copy-done.4 = s32[8,64]{1,0:T(8,128)S(1)} copy-done((s32[8,64]{1,0:T(8,128)S(1)}, s32[8,64]{1,0:T(8,128)}, u32[]{:S(2)}) %copy-start.4) | copy-done | bytes 2072
  16.2 0.0 copy-start.1
  16.2 8.9 %inner.1 = (f32[16,512]{1,0:T(8,128)S(1)}, f32[16,512]{1,0:T(8,128)S(1)}, bf16[2,256,1024]{2,1,0:T(8,128)(2,1)S(1)}, f32[2,64,32]{2,1,0:T(8,128)S(1)}) custom-call(s32[1]{0:T(128)} %bitcast.place, s32[8,64]{1,0:T(8,128)S(1)} %copy-done.4, bf16[4,4,32,16,128]{4,3,2,1,0:T(8,128)(2,1)S(1)} %copy-done.2, bf16[2,4,32,64,128]{4,3,2,1,0:T(8,128)(2,1)S(1)} %copy-done, ...), custom_call_target="tpu_custom_call" | custom-call | flops 400000000 | bytes 10485760 | tf_op jit(solution)/shard_map/inner/pallas_call | solution.py:225
  25.1 0.0 collective-permute-done.1.edge
  25.1 0.0 copy-done.1
  25.1 4.2 %time_edge.1.time_high = f32[16,512]{1,0:T(8,128)S(1)} custom-call(bf16[1,4,32,16,128]{4,3,2,1,0:T(8,128)(2,1)S(1)} %get-tuple-element.14.nulls, bf16[1,4,32,16,128]{4,3,2,1,0:T(8,128)(2,1)} %collective-permute-done.1.edge, bf16[2,4,32,64,128]{4,3,2,1,0:T(8,128)(2,1)S(1)} %copy-done.1), custom_call_target="tpu_custom_call" | custom-call | flops 130000000 | bytes 3145728 | tf_op jit(solution)/shard_map/time_edge/pallas_call | solution.py:240
  29.4 0.0 collective-permute-done.edge
  29.4 0.8 %final.1 = bf16[64,1024]{1,0:T(8,128)(2,1)S(1)} custom-call(bf16[4,1,32,16,128]{4,3,2,1,0:T(8,128)(2,1)S(1)} %collective-permute-done.edge, bf16[2,256,1024]{2,1,0:T(8,128)(2,1)S(1)} %get-tuple-element.9.adjoint, f32[2,64,32]{2,1,0:T(8,128)S(1)} %get-tuple-element.10.picks, f32[16,512]{1,0:T(8,128)S(1)} %get-tuple-element.11.time_low, ...), custom_call_target="tpu_custom_call" | custom-call | flops 130000000 | bytes 2097152 | tf_op jit(solution)/shard_map/final/pallas_call | solution.py:250
  30.2 9.7 %all_to_all.9 = bf16[8,8,1024]{2,1,0:T(8,128)(2,1)S(1)} all-to-all(bf16[8,8,1024]{2,1,0:T(8,128)(2,1)S(1)} %bitcast.5), channel_id=1, replica_groups=mesh['ta'=4,'xyz'=8] {'xyz'}, dimensions={0} | all-to-all | bytes 262144 | tf_op jit(solution)/shard_map/all_to_all | solution.py:259
  39.9 0.7 %bitcast_convert_fusion = f32[1,64,1024]{2,1,0:T(8,128)} fusion(bf16[8,8,1024]{2,1,0:T(8,128)(2,1)S(1)} %all_to_all.9), kind=kLoop, calls=%fused_computation | loop fusion | flops 65536 | bytes 393216 | tf_op jit(solution)/shard_map/convert_element_type | solution.py:261
Async XLA Ops:
  0.0 11.1 %copy-start.2 = (bf16[4,4,32,16,128]{4,3,2,1,0:T(8,128)(2,1)S(1)}, bf16[4,4,32,16,128]{4,3,2,1,0:T(8,128)(2,1)}, u32[]{:S(2)}) copy-start(bf16[4,4,32,16,128]{4,3,2,1,0:T(8,128)(2,1)} %nulls.1) | copy-start | bytes 6291460
  2.3 22.8 %collective-permute-start.1 = (bf16[1,4,32,16,128]{4,3,2,1,0:T(8,128)(2,1)}, bf16[1,4,32,16,128]{4,3,2,1,0:T(8,128)(2,1)}, u32[]{:S(2)}, u32[]{:S(2)}) collective-permute-start(bf16[1,4,32,16,128]{4,3,2,1,0:T(8,128)(2,1)} %get-tuple-element.13), channel_id=1, source_target_pairs={{0,24},{8,0},{16,8},{24,16},{1,25},{9,1},{17,9},{25,17},{2,26},{10... | collective-permute-start | bytes 1572872 | tf_op jit(solution)/shard_map/ppermute | solution.py:16
  6.6 22.8 %collective-permute-start = (bf16[4,1,32,16,128]{4,3,2,1,0:T(8,128)(2,1)}, bf16[4,1,32,16,128]{4,3,2,1,0:T(8,128)(2,1)S(1)}, u32[]{:S(2)}, u32[]{:S(2)}) collective-permute-start(bf16[4,1,32,16,128]{4,3,2,1,0:T(8,128)(2,1)} %slice.9), channel_id=1, source_target_pairs={{0,7},{1,0},{2,1},{3,2},{4,3},{5,4},{6,5},{7,6},{8,15},{9,8},{10,9... | collective-permute-start | bytes 1572872 | tf_op jit(solution)/shard_map/ppermute | solution.py:16
  11.1 2.2 %copy-start = (bf16[2,4,32,64,128]{4,3,2,1,0:T(8,128)(2,1)S(1)}, bf16[2,4,32,64,128]{4,3,2,1,0:T(8,128)(2,1)}, u32[]{:S(2)}) copy-start(bf16[2,4,32,64,128]{4,3,2,1,0:T(8,128)(2,1)} %time_links.3) | copy-start | bytes 12582916
  13.3 2.2 %copy-start.3 = (bf16[4,2,32,64,128]{4,3,2,1,0:T(8,128)(2,1)S(1)}, bf16[4,2,32,64,128]{4,3,2,1,0:T(8,128)(2,1)}, u32[]{:S(2)}) copy-start(bf16[4,2,32,64,128]{4,3,2,1,0:T(8,128)(2,1)} %space_links.1) | copy-start | bytes 12582916
  15.5 0.7 %copy-start.4 = (s32[8,64]{1,0:T(8,128)S(1)}, s32[8,64]{1,0:T(8,128)}, u32[]{:S(2)}) copy-start(s32[8,64]{1,0:T(8,128)} %lists.1) | copy-start | bytes 6148
  16.2 8.9 %copy-start.1 = (bf16[2,4,32,64,128]{4,3,2,1,0:T(8,128)(2,1)S(1)}, bf16[2,4,32,64,128]{4,3,2,1,0:T(8,128)(2,1)}, u32[]{:S(2)}) copy-start(bf16[2,4,32,64,128]{4,3,2,1,0:T(8,128)(2,1)} %time_links.3) | copy-start | bytes 12582916

commit v2 on v1

--- a/solution.py
+++ b/solution.py
@@ -35,29 +35,33 @@
 def image_item(links, lower, upper, slot, left_ref, right_ref):
     sites, vectors, width = lower.shape
     half = width // 2
-    low = lower_half((vectors, width))
+    aggs = sites // SIDE
     sign = signs((vectors, width), jnp.bfloat16)
-    for pair in range(sites // 2):
-        agg, part = divmod(pair, SIDE // 2)
-        at = 2 * pair
-        up_a, up_b = upper[at], upper[at + 1]
-        rows = jnp.concatenate([up_a * sign, swapped(up_a), up_b * sign, swapped(up_b)], axis=0)
-        mats = links[pl.ds(at, 2)].reshape(2 * half, width)
-        images = dot(rows, mats, ROW_DIMS)
-        real = jnp.where(low, images[:vectors], images[2 * vectors : 3 * vectors])
-        imag = jnp.where(low, images[vectors : 2 * vectors], images[3 * vectors :])
-        cols = pl.ds((slot * 2 + part) * 2 * width, 2 * width)
-        right_ref[pl.ds(agg * vectors, vectors), cols] = jnp.concatenate([real, imag], axis=1).astype(jnp.bfloat16)
-        lo_a, lo_b = lower[at], lower[at + 1]
-        lo_real = jnp.where(low, lo_a, swapped(lo_b))
-        lo_imag = jnp.where(low, swapped(lo_a), lo_b)
-        left_ref[pl.ds(agg * 2 * vectors, 2 * vectors), cols] = jnp.concatenate(
-            [
-                jnp.concatenate([lo_real, lo_imag], axis=1),
-                jnp.concatenate([-lo_imag, lo_real], axis=1),
-            ],
-            axis=0,
-        )
+    zero = jnp.zeros((vectors, width), jnp.bfloat16)
+    owner = lax.broadcasted_iota(jnp.int32, (half, 2 * aggs * vectors), 1) // (2 * vectors) % (aggs // 2)
+    for part in range(SIDE):
+        at = (slot * SIDE + part) * width
+        mats = []
+        plain, crossed = [], []
+        for agg in range(aggs):
+            site = agg * SIDE + part
+            up = upper[site]
+            pair = (up * sign, swapped(up))
+            for rows, value in zip((plain, crossed), pair):
+                rows.append(jnp.concatenate([value, zero] if agg % 2 == 0 else [zero, value], axis=1))
+            if agg % 2 == 0:
+                mats.append(jnp.concatenate([links[site], links[site + SIDE]], axis=1))
+            low = lower[site]
+            left_ref[pl.ds(agg * 2 * vectors, 2 * vectors), pl.ds(at, width)] = jnp.concatenate(
+                [low, -sign * swapped(low)], axis=0
+            )
+        images = dot(jnp.concatenate(mats, axis=0), jnp.concatenate(plain + crossed, axis=0), ROW_DIMS)
+        own = images[:half]
+        for pair in range(1, aggs // 2):
+            own = jnp.where(owner == pair, images[pair * half : (pair + 1) * half], own)
+        own = own.astype(jnp.bfloat16)
+        right_ref[pl.ds(at, half), :] = own[:, : aggs * vectors]
+        right_ref[pl.ds(at + half, half), :] = own[:, aggs * vectors :]
 
 
 def adjoint_item(links, lower, slot, left_ref):
@@ -65,38 +69,31 @@
     half = width // 2
     low = lower_half((vectors, width))
     sign = signs((vectors, width), jnp.float32)
-    for pair in range(sites // 2):
-        agg, part = divmod(pair, SIDE // 2)
-        at = 2 * pair
-        lo_a, lo_b = lower[at], lower[at + 1]
-        zero = jnp.zeros_like(lo_a)
-        rows = jnp.concatenate(
-            [
+    zero = jnp.zeros((vectors, width), jnp.bfloat16)
+    for agg in range(sites // SIDE):
+        rows = []
+        mats = []
+        for pair in range(SIDE // 2):
+            at = agg * SIDE + 2 * pair
+            lo_a, lo_b = lower[at], lower[at + 1]
+            rows += [
                 jnp.where(low, lo_a, zero),
                 jnp.where(low, swapped(lo_a), zero),
                 jnp.where(low, zero, swapped(lo_b)),
                 jnp.where(low, zero, lo_b),
-            ],
-            axis=0,
-        )
-        mats = links[pl.ds(at, 2)].reshape(2 * half, width)
-        prod = dot(rows, mats, MAT_DIMS)
-        adj_a = sign * prod[:vectors] + swapped(prod[vectors : 2 * vectors])
-        adj_b = sign * prod[2 * vectors : 3 * vectors] + swapped(prod[3 * vectors :])
-        turn_a = -sign * swapped(adj_a)
-        turn_b = -sign * swapped(adj_b)
-        cols = pl.ds((slot * 2 + part) * 2 * width, 2 * width)
-        left_ref[pl.ds(agg * 2 * vectors, 2 * vectors), cols] = jnp.concatenate(
-            [
-                jnp.concatenate([adj_a, adj_b], axis=1),
-                jnp.concatenate([turn_a, turn_b], axis=1),
-            ],
-            axis=0,
-        ).astype(jnp.bfloat16)
-
-
-def group_rows(left, right, vectors):
-    full = dot(left, right, ROW_DIMS)
+            ]
+            mats.append(jnp.concatenate([links[at], links[at + 1]], axis=0))
+        prod = dot(jnp.concatenate(rows, axis=0), jnp.concatenate(mats, axis=1), MAT_DIMS)
+        for part in range(SIDE):
+            top = part * 2 * vectors
+            mine = prod[top : top + 2 * vectors, part // 2 * width : (part // 2 + 1) * width]
+            adj = sign * mine[:vectors] + swapped(mine[vectors:])
+            both = jnp.concatenate([adj, -sign * swapped(adj)], axis=0).astype(jnp.bfloat16)
+            left_ref[pl.ds(agg * 2 * vectors, 2 * vectors), pl.ds((slot * SIDE + part) * width, width)] = both
+
+
+def group_rows(left, right, dims, vectors):
+    full = dot(left, right, dims)
     aggs = full.shape[1] // vectors
     lanes = lax.broadcasted_iota(jnp.int32, (2 * vectors, full.shape[1]), 1) // vectors
     own = jnp.zeros((2 * vectors, full.shape[1]), jnp.float32)
@@ -120,9 +117,20 @@
     return jnp.concatenate(pieces, axis=1)
 
 
-def inner_kernel(place, lists, nulls, time_links, space_links, time_rows, space_rows, adjoint, picks, links, left, right, sems):
+def edges_kernel(nulls, space_edge, time_edge, sems):
+    copies = [pltpu.make_async_copy(nulls.at[:, pl.ds(0, 1)], space_edge, sems.at[0])]
+    copies.append(pltpu.make_async_copy(nulls.at[pl.ds(0, 1)], time_edge, sems.at[1]))
+    for copy in copies:
+        copy.start()
+    for copy in copies:
+        copy.wait()
+
+
+def inner_kernel(place, lists, nulls, time_links, space_links, time_rows, space_rows, adjoint, picks, links, vecs, left, right, sems):
     time_count, space_count, sites, vectors, width = nulls.shape
     copies = []
+    base = pltpu.make_async_copy(nulls, vecs, sems.at[12])
+    base.start()
 
     def fetch(source):
         slot = len(copies)
@@ -154,21 +162,25 @@
         chosen = chosen.astype(jnp.int32) - 1
         picks[0, pl.ds(shard * MOST, MOST), :] = jnp.where(column == chosen, 1.0, 0.0)
         picks[1, pl.ds(shard * MOST, MOST), :] = jnp.where(turned == chosen, 1.0, 0.0)
+    base.wait()
     for a_x in range(2):
+        copies[2 * a_x].wait()
+        copies[2 * a_x + 1].wait()
         for c in range(2):
             x = 2 * a_x + c
-            copies[x].wait()
-            image_item(links.at[x], nulls.at[1, x], nulls.at[2, x], c, left, right)
-        time_rows[pl.ds(a_x * 8, 8), :] = group_rows(left[...], right[...], vectors)
+            image_item(links.at[x], vecs.at[1, x], vecs.at[2, x], c, left, right)
+        time_rows[pl.ds(a_x * 8, 8), :] = group_rows(left[...], right[...], MAT_DIMS, vectors)
     for a_t in range(2):
+        copies[4 + 2 * a_t].wait()
+        copies[5 + 2 * a_t].wait()
         for c in range(2):
             t = 2 * a_t + c
-            copies[4 + t].wait()
-            image_item(links.at[4 + t], nulls.at[t, 1], nulls.at[t, 2], c, left, right)
-        space_rows[pl.ds(a_t * 8, 8), :] = group_rows(left[...], right[...], vectors)
+            image_item(links.at[4 + t], vecs.at[t, 1], vecs.at[t, 2], c, left, right)
+        space_rows[pl.ds(a_t * 8, 8), :] = group_rows(left[...], right[...], MAT_DIMS, vectors)
     for t in range(4):
         copies[8 + t].wait()
-        adjoint_item(links.at[8 + t], nulls.at[t, 3], t % 2, adjoint.at[t // 2])
+    for t in range(4):
+        adjoint_item(links.at[8 + t], vecs.at[t, 3], t % 2, adjoint.at[t // 2])
 
 
 def time_edge_kernel(nulls, edge, time_links, time_rows, links, left, right, sems):
@@ -179,11 +191,12 @@
         copy.start()
         copies.append(copy)
     for a_x in range(2):
+        copies[2 * a_x].wait()
+        copies[2 * a_x + 1].wait()
         for c in range(2):
             x = 2 * a_x + c
-            copies[x].wait()
             image_item(links.at[x], nulls.at[0, x], edge.at[0, x], c, left, right)
-        time_rows[pl.ds(a_x * 8, 8), :] = group_rows(left[...], right[...], vectors)
+        time_rows[pl.ds(a_x * 8, 8), :] = group_rows(left[...], right[...], MAT_DIMS, vectors)
 
 
 def final_kernel(edge, adjoint, picks, time_low, time_high, space_low, packed):
@@ -196,7 +209,7 @@
             for site in range(SIDE):
                 rows = [edge[2 * a_t + c, 0, agg * SIDE + site] for agg in range(aggs)]
                 parts.append(jnp.concatenate(rows, axis=0))
-        found.append(group_rows(adjoint[a_t], jnp.concatenate(parts, axis=1), vectors))
+        found.append(group_rows(adjoint[a_t], jnp.concatenate(parts, axis=1), ROW_DIMS, vectors))
     time_rows = jnp.concatenate([time_low[...], time_high[...]], axis=0).astype(jnp.bfloat16)
     space_rows = jnp.concatenate([space_low[...]] + found, axis=0).astype(jnp.bfloat16)
     wide = time_rows.shape[1]
@@ -210,21 +223,36 @@
     aggs = sites // SIDE
     local_count = (time_count // 2) * (space_count // 2) * aggs
     wide = 2 * vectors * vectors
-    edge_space = shifted(nulls[:, 0:1], "xyz", -1)
-    edge_time = shifted(nulls[0:1], "ta", -1)
     place = lax.axis_index("xyz").astype(jnp.int32).reshape(1)
     vmem = pl.BlockSpec(memory_space=pltpu.VMEM)
     smem = pl.BlockSpec(memory_space=pltpu.SMEM)
     anywhere = pl.BlockSpec(memory_space=pl.ANY)
+    outside = pl.BlockSpec(memory_space=pltpu.HBM)
     half = width // 2
+    roomy = pltpu.CompilerParams(vmem_limit_bytes=58 * 1024 * 1024)
+    modest = pltpu.CompilerParams(vmem_limit_bytes=24 * 1024 * 1024)
     grouped = [
         pltpu.VMEM((2 * vectors * aggs, 8 * width), jnp.bfloat16),
-        pltpu.VMEM((vectors * aggs, 8 * width), jnp.bfloat16),
+        pltpu.VMEM((8 * width, vectors * aggs), jnp.bfloat16),
     ]
-    params = pltpu.CompilerParams(vmem_limit_bytes=40 * 1024 * 1024)
+    space_edge, time_edge = pl.pallas_call(
+        edges_kernel,
+        in_specs=[outside],
+        out_specs=[anywhere] * 2,
+        out_shape=[
+            jax.ShapeDtypeStruct((time_count, 1, sites, vectors, width), nulls.dtype),
+            jax.ShapeDtypeStruct((1, space_count, sites, vectors, width), nulls.dtype),
+        ],
+        scratch_shapes=[pltpu.SemaphoreType.DMA((2,))],
+        compiler_params=pltpu.CompilerParams(vmem_limit_bytes=62 * 1024 * 1024),
+        cost_estimate=pl.CostEstimate(flops=0, bytes_accessed=2**21, transcendentals=0),
+        name="edges",
+    )(nulls)
+    edge_space = shifted(space_edge, "xyz", -1)
+    edge_time = shifted(time_edge, "ta", -1)
     time_low, space_low, adjoint, picks = pl.pallas_call(
         inner_kernel,
-        in_specs=[smem, vmem, vmem, anywhere, anywhere],
+        in_specs=[smem, vmem, outside, outside, outside],
         out_specs=[vmem] * 4,
         out_shape=[
             jax.ShapeDtypeStruct((2 * aggs, wide), jnp.float32),
@@ -232,18 +260,23 @@
             jax.ShapeDtypeStruct((2, 2 * vectors * aggs, 8 * width), jnp.bfloat16),
             jax.ShapeDtypeStruct((2, shards * MOST, local_count), jnp.float32),
         ],
-        scratch_shapes=[pltpu.VMEM((12, sites, half, width), jnp.bfloat16)] + grouped + [pltpu.SemaphoreType.DMA((12,))],
-        compiler_params=params,
+        scratch_shapes=[
+            pltpu.VMEM((12, sites, half, width), jnp.bfloat16),
+            pltpu.VMEM(nulls.shape, nulls.dtype),
+        ]
+        + grouped
+        + [pltpu.SemaphoreType.DMA((13,))],
+        compiler_params=roomy,
         cost_estimate=pl.CostEstimate(flops=400 * 10**6, bytes_accessed=10 * 2**20, transcendentals=0),
         name="inner",
     )(place, owner_lists, nulls, time_links, space_links)
     time_high = pl.pallas_call(
         time_edge_kernel,
-        in_specs=[vmem, vmem, anywhere],
+        in_specs=[vmem, vmem, outside],
         out_specs=vmem,
         out_shape=jax.ShapeDtypeStruct((2 * aggs, wide), jnp.float32),
         scratch_shapes=[pltpu.VMEM((4, sites, half, width), jnp.bfloat16)] + grouped + [pltpu.SemaphoreType.DMA((4,))],
-        compiler_params=params,
+        compiler_params=modest,
         cost_estimate=pl.CostEstimate(flops=130 * 10**6, bytes_accessed=3 * 2**20, transcendentals=0),
         name="time_edge",
     )(nulls[3:4], edge_time, time_links)
@@ -252,7 +285,7 @@
         in_specs=[vmem] * 6,
         out_specs=vmem,
         out_shape=jax.ShapeDtypeStruct((shards * MOST, 2 * wide), jnp.bfloat16),
-        compiler_params=params,
+        compiler_params=modest,
         cost_estimate=pl.CostEstimate(flops=130 * 10**6, bytes_accessed=2 * 2**20, transcendentals=0),
         name="final",
     )(edge_space, adjoint, picks, time_low, time_high, space_low)

time: 41 us -> 66.4 us (1.62)
  Pallas kernels: 13.9 us -> 44.5 us
  local copies, waits for them, and re-layouts: 9.28 us -> 1.1 us
  blocking collectives: 9.74 us -> 12.7 us
    pallas_call x2 -> x3, Pallas kernels: 13.1 us -> 43.7 us  [the longest x1 32.9 us: on_device(): pl.pallas_call(edges_kernel, in_specs=[outside], out_specs=[anywhere] * 2...]
    unnamed x10, local copies, waits for them, and re-layouts: 5.07 us -> 0.03 us
    slice x2 -> x1, local copies, waits for them, and re-layouts: 4.21 us -> 1.08 us  [on_device(): nulls[3:4]]
    all_to_all x1, blocking collectives: 9.74 us -> 12.7 us  [on_device(): arrived = lax.all_to_all(packed, 'xyz', 0, 0, tiled=True)]
  transfers between devices with their start and end apart: 2 -> 2, of which waited for: 0 -> 0; matrix products, arithmetic and copies ran while one was open for 5% -> 2% of each run, Pallas kernels for 32% -> 16%
where the time goes in v2:
time: 66.4 us; the launch traced here: 66.1 us
  Pallas kernels  44.5 us (67%)
  blocking collectives  12.7 us (19%)
  starting transfers between devices  6.99 us (11%)
  local copies, waits for them, and re-layouts  1.1 us (2%)
  other arithmetic  0.72 us (1%)
    pallas_call x1, Pallas kernels, on_device(): pl.pallas_call(edges_kernel, in_specs=[outside], out_specs=[anywhere] * 2...  32.9 us
    all_to_all x1, blocking collectives, on_device(): arrived = lax.all_to_all(packed, 'xyz', 0, 0, tiled=True)  12.7 us
    pallas_call x1, Pallas kernels, on_device(): pl.pallas_call(inner_kernel, in_specs=[smem, vmem, outside, outside, outs...  8.79 us
    ppermute x2, starting transfers between devices, shifted(): lax.ppermute(array, axis, [(i, (i + by) % count) for i in range(count)])  6.99 us
    pallas_call x1, Pallas kernels, on_device(): pl.pallas_call(time_edge_kernel, in_specs=[vmem, vmem, outside], out_spec...  2.07 us
  transfers between devices with their start and end apart: 2, of which 0 were waited for; matrix products, arithmetic and copies ran while one was open for 2% of the time, Pallas kernels for 16%

profile of v2, /device:TPU:0, one launch (start us, length us, event | category | flops | bytes accessed | tf_op | source)
XLA Modules:
  0.0 66.1 jit_solution(10349399253897865297)
XLA Ops:
  0.0 32.9 %edges.1 = (bf16[4,1,32,16,128]{4,3,2,1,0:T(8,128)(2,1)}, bf16[1,4,32,16,128]{4,3,2,1,0:T(8,128)(2,1)}) custom-call(bf16[4,4,32,16,128]{4,3,2,1,0:T(8,128)(2,1)} %nulls.3), custom_call_target="tpu_custom_call" | custom-call | bytes 2097152 | tf_op jit(solution)/shard_map/edges/pallas_call | solution.py:238
  32.9 2.4 %collective-permute-start.1 = (bf16[1,4,32,16,128]{4,3,2,1,0:T(8,128)(2,1)}, bf16[1,4,32,16,128]{4,3,2,1,0:T(8,128)(2,1)S(1)}, u32[]{:S(2)}, u32[]{:S(2)}) collective-permute-start(bf16[1,4,32,16,128]{4,3,2,1,0:T(8,128)(2,1)} %get-tuple-element.15), channel_id=1, source_target_pairs={{0,24},{8,0},{16,8},{24,16},{1,25},{9,1},{17,9},{25,17},{2,26},{10... | collective-permute-start | bytes 1572872 | tf_op jit(solution)/shard_map/ppermute | solution.py:16
  35.3 4.6 %collective-permute-start = (bf16[4,1,32,16,128]{4,3,2,1,0:T(8,128)(2,1)}, bf16[4,1,32,16,128]{4,3,2,1,0:T(8,128)(2,1)S(1)}, u32[]{:S(2)}, u32[]{:S(2)}) collective-permute-start(bf16[4,1,32,16,128]{4,3,2,1,0:T(8,128)(2,1)} %get-tuple-element.11), channel_id=1, source_target_pairs={{0,7},{1,0},{2,1},{3,2},{4,3},{5,4},{6,5},{7,6},{8,15},{9,8},{10,9... | collective-permute-start | bytes 1572872 | tf_op jit(solution)/shard_map/ppermute | solution.py:16
  39.9 1.1 %slice.3.nulls = bf16[1,4,32,16,128]{4,3,2,1,0:T(8,128)(2,1)S(1)} slice(bf16[4,4,32,16,128]{4,3,2,1,0:T(8,128)(2,1)} %nulls.3), slice={[3:4], [0:4], [0:32], [0:16], [0:128]} | slice | bytes 1048576 | tf_op jit(solution)/shard_map/slice | solution.py:282
  41.0 0.0 copy-start
  41.0 8.8 %inner.1 = (f32[16,512]{1,0:T(8,128)}, f32[16,512]{1,0:T(8,128)}, bf16[2,256,1024]{2,1,0:T(8,128)(2,1)}, f32[2,64,32]{2,1,0:T(8,128)}) custom-call(s32[1]{0:T(128)} %bitcast.place, s32[8,64]{1,0:T(8,128)} %lists.1, bf16[4,4,32,16,128]{4,3,2,1,0:T(8,128)(2,1)} %nulls.3, bf16[2,4,32,64,128]{4,3,2,1,0:T(8,128)(2,1)} %time_links.3, ...), custom_call_target="tpu_custom_call" | custom-call | flops 400000000 | bytes 10485760 | tf_op jit(solution)/shard_map/inner/pallas_call | solution.py:253
  49.8 0.0 copy-start.1
  49.8 0.0 copy-start.2
  49.8 0.0 copy-start.3
  49.8 0.0 copy-start.4
  49.8 0.0 collective-permute-done.1.edge
  49.8 0.0 copy-done
  49.8 2.1 %time_edge.1.time_high = f32[16,512]{1,0:T(8,128)S(1)} custom-call(bf16[1,4,32,16,128]{4,3,2,1,0:T(8,128)(2,1)S(1)} %slice.3.nulls, bf16[1,4,32,16,128]{4,3,2,1,0:T(8,128)(2,1)S(1)} %collective-permute-done.1.edge, bf16[2,4,32,64,128]{4,3,2,1,0:T(8,128)(2,1)S(1)} %copy-done), custom_call_target="tpu_custom_call" | custom-call | flops 130000000 | bytes 3145728 | tf_op jit(solution)/shard_map/time_edge/pallas_call | solution.py:273
  51.9 0.0 collective-permute-done.edge
  51.9 0.0 copy-done.1
  51.9 0.0 copy-done.2
  51.9 0.0 copy-done.3
  51.9 0.0 copy-done.4
  52.0 0.8 %final.1 = bf16[64,1024]{1,0:T(8,128)(2,1)S(1)} custom-call(bf16[4,1,32,16,128]{4,3,2,1,0:T(8,128)(2,1)S(1)} %collective-permute-done.edge, bf16[2,256,1024]{2,1,0:T(8,128)(2,1)S(1)} %copy-done.1, f32[2,64,32]{2,1,0:T(8,128)S(1)} %copy-done.2, f32[16,512]{1,0:T(8,128)S(1)} %copy-done.3, f32[16,512]{1,0:T(8,128)S(1)} %time_edge.1.time_high, ...), custom_call_target="tpu_custom_call" | custom-call | flops 130000000 | bytes 2097152 | tf_op jit(solution)/shard_map/final/pallas_call | solution.py:283
  52.7 12.7 %all_to_all.9 = bf16[8,8,1024]{2,1,0:T(8,128)(2,1)S(1)} all-to-all(bf16[8,8,1024]{2,1,0:T(8,128)(2,1)S(1)} %bitcast.5), channel_id=1, replica_groups=mesh['ta'=4,'xyz'=8] {'xyz'}, dimensions={0} | all-to-all | bytes 262144 | tf_op jit(solution)/shard_map/all_to_all | solution.py:292
  65.4 0.7 %bitcast_convert_fusion = f32[1,64,1024]{2,1,0:T(8,128)} fusion(bf16[8,8,1024]{2,1,0:T(8,128)(2,1)S(1)} %all_to_all.9), kind=kLoop, calls=%fused_computation | loop fusion | flops 65536 | bytes 393216 | tf_op jit(solution)/shard_map/convert_element_type | solution.py:294
Async XLA Ops:
  32.9 16.9 %collective-permute-start.1 = (bf16[1,4,32,16,128]{4,3,2,1,0:T(8,128)(2,1)}, bf16[1,4,32,16,128]{4,3,2,1,0:T(8,128)(2,1)S(1)}, u32[]{:S(2)}, u32[]{:S(2)}) collective-permute-start(bf16[1,4,32,16,128]{4,3,2,1,0:T(8,128)(2,1)} %get-tuple-element.15), channel_id=1, source_target_pairs={{0,24},{8,0},{16,8},{24,16},{1,25},{9,1},{17,9},{25,17},{2,26},{10... | collective-permute-start | bytes 1572872 | tf_op jit(solution)/shard_map/ppermute | solution.py:16
  35.3 16.6 %collective-permute-start = (bf16[4,1,32,16,128]{4,3,2,1,0:T(8,128)(2,1)}, bf16[4,1,32,16,128]{4,3,2,1,0:T(8,128)(2,1)S(1)}, u32[]{:S(2)}, u32[]{:S(2)}) collective-permute-start(bf16[4,1,32,16,128]{4,3,2,1,0:T(8,128)(2,1)} %get-tuple-element.11), channel_id=1, source_target_pairs={{0,7},{1,0},{2,1},{3,2},{4,3},{5,4},{6,5},{7,6},{8,15},{9,8},{10,9... | collective-permute-start | bytes 1572872 | tf_op jit(solution)/shard_map/ppermute | solution.py:16
  41.0 8.9 %copy-start = (bf16[2,4,32,64,128]{4,3,2,1,0:T(8,128)(2,1)S(1)}, bf16[2,4,32,64,128]{4,3,2,1,0:T(8,128)(2,1)}, u32[]{:S(2)}) copy-start(bf16[2,4,32,64,128]{4,3,2,1,0:T(8,128)(2,1)} %time_links.3) | copy-start | bytes 12582916
  49.8 2.1 %copy-start.1 = (bf16[2,256,1024]{2,1,0:T(8,128)(2,1)S(1)}, bf16[2,256,1024]{2,1,0:T(8,128)(2,1)}, u32[]{:S(2)}) copy-start(bf16[2,256,1024]{2,1,0:T(8,128)(2,1)} %get-tuple-element.12.adjoint) | copy-start | bytes 3145732
  49.8 2.1 %copy-start.2 = (f32[2,64,32]{2,1,0:T(8,128)S(1)}, f32[2,64,32]{2,1,0:T(8,128)}, u32[]{:S(2)}) copy-start(f32[2,64,32]{2,1,0:T(8,128)} %get-tuple-element.13.picks) | copy-start | bytes 49156
  49.8 2.1 %copy-start.3 = (f32[16,512]{1,0:T(8,128)S(1)}, f32[16,512]{1,0:T(8,128)}, u32[]{:S(2)}) copy-start(f32[16,512]{1,0:T(8,128)} %get-tuple-element.14.time_low) | copy-start | bytes 98308
  49.8 2.1 %copy-start.4 = (f32[16,512]{1,0:T(8,128)S(1)}, f32[16,512]{1,0:T(8,128)}, u32[]{:S(2)}) copy-start(f32[16,512]{1,0:T(8,128)} %get-tuple-element.16.space_low) | copy-start | bytes 98308

commit v3 on v2

--- a/solution.py
+++ b/solution.py
@@ -117,9 +117,11 @@
     return jnp.concatenate(pieces, axis=1)
 
 
-def edges_kernel(nulls, space_edge, time_edge, sems):
-    copies = [pltpu.make_async_copy(nulls.at[:, pl.ds(0, 1)], space_edge, sems.at[0])]
-    copies.append(pltpu.make_async_copy(nulls.at[pl.ds(0, 1)], time_edge, sems.at[1]))
+def slice_kernel(nulls, space_edge, time_edge, sems):
+    copies = [
+        pltpu.make_async_copy(nulls.at[:, pl.ds(0, 1)], space_edge, sems.at[0]),
+        pltpu.make_async_copy(nulls.at[pl.ds(0, 1)], time_edge, sems.at[1]),
+    ]
     for copy in copies:
         copy.start()
     for copy in copies:
@@ -183,19 +185,22 @@
         adjoint_item(links.at[8 + t], vecs.at[t, 3], t % 2, adjoint.at[t // 2])
 
 
-def time_edge_kernel(nulls, edge, time_links, time_rows, links, left, right, sems):
+def time_edge_kernel(nulls, edge, time_links, time_rows, links, vecs, left, right, sems):
     vectors = nulls.shape[-2]
     copies = []
+    base = pltpu.make_async_copy(nulls.at[3], vecs, sems.at[4])
+    base.start()
     for x in range(4):
         copy = pltpu.make_async_copy(time_links.at[1, x], links.at[x], sems.at[x])
         copy.start()
         copies.append(copy)
+    base.wait()
     for a_x in range(2):
         copies[2 * a_x].wait()
         copies[2 * a_x + 1].wait()
         for c in range(2):
             x = 2 * a_x + c
-            image_item(links.at[x], nulls.at[0, x], edge.at[0, x], c, left, right)
+            image_item(links.at[x], vecs.at[x], edge.at[0, x], c, left, right)
         time_rows[pl.ds(a_x * 8, 8), :] = group_rows(left[...], right[...], MAT_DIMS, vectors)
 
 
@@ -235,21 +240,22 @@
         pltpu.VMEM((2 * vectors * aggs, 8 * width), jnp.bfloat16),
         pltpu.VMEM((8 * width, vectors * aggs), jnp.bfloat16),
     ]
+    first = pltpu.CompilerParams(vmem_limit_bytes=60 * 1024 * 1024)
     space_edge, time_edge = pl.pallas_call(
-        edges_kernel,
+        slice_kernel,
         in_specs=[outside],
-        out_specs=[anywhere] * 2,
+        out_specs=[vmem] * 2,
         out_shape=[
             jax.ShapeDtypeStruct((time_count, 1, sites, vectors, width), nulls.dtype),
             jax.ShapeDtypeStruct((1, space_count, sites, vectors, width), nulls.dtype),
         ],
         scratch_shapes=[pltpu.SemaphoreType.DMA((2,))],
-        compiler_params=pltpu.CompilerParams(vmem_limit_bytes=62 * 1024 * 1024),
-        cost_estimate=pl.CostEstimate(flops=0, bytes_accessed=2**21, transcendentals=0),
-        name="edges",
+        compiler_params=first,
+        cost_estimate=pl.CostEstimate(flops=1000, bytes_accessed=1000, transcendentals=0),
+        name="slices",
     )(nulls)
+    edge_time = shifted(time_edge, "ta", -1)
     edge_space = shifted(space_edge, "xyz", -1)
-    edge_time = shifted(time_edge, "ta", -1)
     time_low, space_low, adjoint, picks = pl.pallas_call(
         inner_kernel,
         in_specs=[smem, vmem, outside, outside, outside],
@@ -267,26 +273,31 @@
         + grouped
         + [pltpu.SemaphoreType.DMA((13,))],
         compiler_params=roomy,
-        cost_estimate=pl.CostEstimate(flops=400 * 10**6, bytes_accessed=10 * 2**20, transcendentals=0),
+        cost_estimate=pl.CostEstimate(flops=1000, bytes_accessed=1000, transcendentals=0),
         name="inner",
     )(place, owner_lists, nulls, time_links, space_links)
     time_high = pl.pallas_call(
         time_edge_kernel,
-        in_specs=[vmem, vmem, outside],
+        in_specs=[outside, vmem, outside],
         out_specs=vmem,
         out_shape=jax.ShapeDtypeStruct((2 * aggs, wide), jnp.float32),
-        scratch_shapes=[pltpu.VMEM((4, sites, half, width), jnp.bfloat16)] + grouped + [pltpu.SemaphoreType.DMA((4,))],
+        scratch_shapes=[
+            pltpu.VMEM((4, sites, half, width), jnp.bfloat16),
+            pltpu.VMEM(nulls.shape[1:], nulls.dtype),
+        ]
+        + grouped
+        + [pltpu.SemaphoreType.DMA((5,))],
         compiler_params=modest,
-        cost_estimate=pl.CostEstimate(flops=130 * 10**6, bytes_accessed=3 * 2**20, transcendentals=0),
+        cost_estimate=pl.CostEstimate(flops=1000, bytes_accessed=1000, transcendentals=0),
         name="time_edge",
-    )(nulls[3:4], edge_time, time_links)
+    )(nulls, edge_time, time_links)
     packed = pl.pallas_call(
         final_kernel,
         in_specs=[vmem] * 6,
         out_specs=vmem,
         out_shape=jax.ShapeDtypeStruct((shards * MOST, 2 * wide), jnp.bfloat16),
         compiler_params=modest,
-        cost_estimate=pl.CostEstimate(flops=130 * 10**6, bytes_accessed=2 * 2**20, transcendentals=0),
+        cost_estimate=pl.CostEstimate(flops=1000, bytes_accessed=1000, transcendentals=0),
         name="final",
     )(edge_space, adjoint, picks, time_low, time_high, space_low)
     arrived = lax.all_to_all(packed, "xyz", 0, 0, tiled=True)

time: 66.4 us -> 35.7 us (0.54)
  Pallas kernels: 44.5 us -> 13.6 us
  local copies, waits for them, and re-layouts: 1.1 us -> 2.2 us
  blocking collectives: 12.7 us -> 11.9 us
    pallas_call x2, Pallas kernels: 34.9 us -> 4.35 us  [the longest x1 2.24 us: on_device(): pl.pallas_call(slice_kernel, in_specs=[outside], out_specs=[vmem] * 2, ou...]
    unnamed x10 -> x12, local copies, waits for them, and re-layouts: 0.03 us -> 2.2 us
    slice x1 -> x0, local copies, waits for them, and re-layouts: 1.08 us -> none  [on_device(): nulls[3:4]]
    all_to_all x1, blocking collectives: 12.7 us -> 11.9 us  [on_device(): arrived = lax.all_to_all(packed, 'xyz', 0, 0, tiled=True)]
  transfers between devices with their start and end apart: 2 -> 2, of which waited for: 0 -> 0; matrix products, arithmetic and copies ran while one was open for 2% -> 0% of each run, Pallas kernels for 16% -> 30%
where the time goes in v3:
time: 35.7 us; the launch traced here: 35.5 us
  Pallas kernels  13.6 us (38%)
  blocking collectives  11.9 us (33%)
  starting transfers between devices  6.99 us (20%)
  local copies, waits for them, and re-layouts  2.2 us (6%)
  other arithmetic  0.72 us (2%)
    all_to_all x1, blocking collectives, on_device(): arrived = lax.all_to_all(packed, 'xyz', 0, 0, tiled=True)  11.9 us
    pallas_call x1, Pallas kernels, on_device(): pl.pallas_call(inner_kernel, in_specs=[smem, vmem, outside, outside, outs...  8.43 us
    ppermute x2, starting transfers between devices, shifted(): lax.ppermute(array, axis, [(i, (i + by) % count) for i in range(count)])  6.99 us
    pallas_call x1, Pallas kernels, on_device(): pl.pallas_call(slice_kernel, in_specs=[outside], out_specs=[vmem] * 2, ou...  2.24 us
    unnamed x12, local copies, waits for them, and re-layouts  2.2 us
    pallas_call x1, Pallas kernels, on_device(): pl.pallas_call(time_edge_kernel, in_specs=[outside, vmem, outside], out_s...  2.11 us
    pallas_call x1, Pallas kernels, on_device(): pl.pallas_call(final_kernel, in_specs=[vmem] * 6, out_specs=vmem, out_sha...  0.79 us
    convert_element_type x1, other arithmetic, on_device(): result = arrived.astype(jnp.float32)  0.72 us
  transfers between devices with their start and end apart: 2, of which 0 were waited for; matrix products, arithmetic and copies ran while one was open for 0% of the time, Pallas kernels for 30%

profile of v3, /device:TPU:0, one launch (start us, length us, event | category | flops | bytes accessed | tf_op | source)
XLA Modules:
  0.0 35.5 jit_solution(6410107775361947839)
XLA Ops:
  0.0 2.2 %slices.1 = (bf16[4,1,32,16,128]{4,3,2,1,0:T(8,128)(2,1)}, bf16[1,4,32,16,128]{4,3,2,1,0:T(8,128)(2,1)}) custom-call(bf16[4,4,32,16,128]{4,3,2,1,0:T(8,128)(2,1)} %nulls.5), custom_call_target="tpu_custom_call" | custom-call | flops 1000 | bytes 1000 | tf_op jit(solution)/shard_map/slices/pallas_call | solution.py:244
  2.2 2.4 %collective-permute-start.1 = (bf16[1,4,32,16,128]{4,3,2,1,0:T(8,128)(2,1)}, bf16[1,4,32,16,128]{4,3,2,1,0:T(8,128)(2,1)S(1)}, u32[]{:S(2)}, u32[]{:S(2)}) collective-permute-start(bf16[1,4,32,16,128]{4,3,2,1,0:T(8,128)(2,1)} %get-tuple-element.15), channel_id=1, source_target_pairs={{0,24},{8,0},{16,8},{24,16},{1,25},{9,1},{17,9},{25,17},{2,26},{10... | collective-permute-start | bytes 1572872 | tf_op jit(solution)/shard_map/ppermute | solution.py:16
  4.7 4.6 %collective-permute-start = (bf16[4,1,32,16,128]{4,3,2,1,0:T(8,128)(2,1)}, bf16[4,1,32,16,128]{4,3,2,1,0:T(8,128)(2,1)S(1)}, u32[]{:S(2)}, u32[]{:S(2)}) collective-permute-start(bf16[4,1,32,16,128]{4,3,2,1,0:T(8,128)(2,1)} %get-tuple-element.11), channel_id=1, source_target_pairs={{0,7},{1,0},{2,1},{3,2},{4,3},{5,4},{6,5},{7,6},{8,15},{9,8},{10,9... | collective-permute-start | bytes 1572872 | tf_op jit(solution)/shard_map/ppermute | solution.py:16
  9.2 0.0 copy-start
  9.2 8.4 %inner.1 = (f32[16,512]{1,0:T(8,128)}, f32[16,512]{1,0:T(8,128)}, bf16[2,256,1024]{2,1,0:T(8,128)(2,1)}, f32[2,64,32]{2,1,0:T(8,128)}) custom-call(s32[1]{0:T(128)} %bitcast.place, s32[8,64]{1,0:T(8,128)} %lists.1, bf16[4,4,32,16,128]{4,3,2,1,0:T(8,128)(2,1)} %nulls.5, bf16[2,4,32,64,128]{4,3,2,1,0:T(8,128)(2,1)} %time_links.3, ...), custom_call_target="tpu_custom_call" | custom-call | flops 1000 | bytes 1000 | tf_op jit(solution)/shard_map/inner/pallas_call | solution.py:259
  17.7 0.0 collective-permute-done.1.edge
  17.7 0.0 copy-done
  17.7 0.0 copy-start.1
  17.7 2.2 %copy-done.1 = bf16[2,4,32,64,128]{4,3,2,1,0:T(8,128)(2,1)S(1)} copy-done((bf16[2,4,32,64,128]{4,3,2,1,0:T(8,128)(2,1)S(1)}, bf16[2,4,32,64,128]{4,3,2,1,0:T(8,128)(2,1)}, u32[]{:S(2)}) %copy-start.1) | copy-done | bytes 4194328
  19.9 0.0 copy-start.2
  19.9 0.0 copy-start.3
  19.9 0.0 copy-start.4
  19.9 0.0 copy-start.5
  19.9 2.1 %time_edge.1.time_high = f32[16,512]{1,0:T(8,128)S(1)} custom-call(bf16[4,4,32,16,128]{4,3,2,1,0:T(8,128)(2,1)S(1)} %copy-done, bf16[1,4,32,16,128]{4,3,2,1,0:T(8,128)(2,1)S(1)} %collective-permute-done.1.edge, bf16[2,4,32,64,128]{4,3,2,1,0:T(8,128)(2,1)S(1)} %copy-done.1), custom_call_target="tpu_custom_call" | custom-call | flops 1000 | bytes 1000 | tf_op jit(solution)/shard_map/time_edge/pallas_call | solution.py:279
  22.0 0.0 collective-permute-done.edge
  22.0 0.0 copy-done.2
  22.0 0.0 copy-done.3
  22.0 0.0 copy-done.4
  22.1 0.0 copy-done.5
  22.1 0.8 %final.1 = bf16[64,1024]{1,0:T(8,128)(2,1)S(1)} custom-call(bf16[4,1,32,16,128]{4,3,2,1,0:T(8,128)(2,1)S(1)} %collective-permute-done.edge, bf16[2,256,1024]{2,1,0:T(8,128)(2,1)S(1)} %copy-done.2, f32[2,64,32]{2,1,0:T(8,128)S(1)} %copy-done.3, f32[16,512]{1,0:T(8,128)S(1)} %copy-done.4, f32[16,512]{1,0:T(8,128)S(1)} %time_edge.1.time_high, ...), custom_call_target="tpu_custom_call" | custom-call | flops 1000 | bytes 1000 | tf_op jit(solution)/shard_map/final/pallas_call | solution.py:294
  22.9 11.9 %all_to_all.9 = bf16[8,8,1024]{2,1,0:T(8,128)(2,1)S(1)} all-to-all(bf16[8,8,1024]{2,1,0:T(8,128)(2,1)S(1)} %bitcast.5), channel_id=1, replica_groups=mesh['ta'=4,'xyz'=8] {'xyz'}, dimensions={0} | all-to-all | bytes 262144 | tf_op jit(solution)/shard_map/all_to_all | solution.py:303
  34.8 0.7 %bitcast_convert_fusion = f32[1,64,1024]{2,1,0:T(8,128)} fusion(bf16[8,8,1024]{2,1,0:T(8,128)(2,1)S(1)} %all_to_all.9), kind=kLoop, calls=%fused_computation | loop fusion | flops 65536 | bytes 393216 | tf_op jit(solution)/shard_map/convert_element_type | solution.py:305
Async XLA Ops:
  2.2 15.4 %collective-permute-start.1 = (bf16[1,4,32,16,128]{4,3,2,1,0:T(8,128)(2,1)}, bf16[1,4,32,16,128]{4,3,2,1,0:T(8,128)(2,1)S(1)}, u32[]{:S(2)}, u32[]{:S(2)}) collective-permute-start(bf16[1,4,32,16,128]{4,3,2,1,0:T(8,128)(2,1)} %get-tuple-element.15), channel_id=1, source_target_pairs={{0,24},{8,0},{16,8},{24,16},{1,25},{9,1},{17,9},{25,17},{2,26},{10... | collective-permute-start | bytes 1572872 | tf_op jit(solution)/shard_map/ppermute | solution.py:16
  4.7 17.3 %collective-permute-start = (bf16[4,1,32,16,128]{4,3,2,1,0:T(8,128)(2,1)}, bf16[4,1,32,16,128]{4,3,2,1,0:T(8,128)(2,1)S(1)}, u32[]{:S(2)}, u32[]{:S(2)}) collective-permute-start(bf16[4,1,32,16,128]{4,3,2,1,0:T(8,128)(2,1)} %get-tuple-element.11), channel_id=1, source_target_pairs={{0,7},{1,0},{2,1},{3,2},{4,3},{5,4},{6,5},{7,6},{8,15},{9,8},{10,9... | collective-permute-start | bytes 1572872 | tf_op jit(solution)/shard_map/ppermute | solution.py:16
  9.2 8.4 %copy-start = (bf16[4,4,32,16,128]{4,3,2,1,0:T(8,128)(2,1)S(1)}, bf16[4,4,32,16,128]{4,3,2,1,0:T(8,128)(2,1)}, u32[]{:S(2)}) copy-start(bf16[4,4,32,16,128]{4,3,2,1,0:T(8,128)(2,1)} %nulls.5) | copy-start | bytes 6291460
  17.7 2.2 %copy-start.1 = (bf16[2,4,32,64,128]{4,3,2,1,0:T(8,128)(2,1)S(1)}, bf16[2,4,32,64,128]{4,3,2,1,0:T(8,128)(2,1)}, u32[]{:S(2)}) copy-start(bf16[2,4,32,64,128]{4,3,2,1,0:T(8,128)(2,1)} %time_links.3) | copy-start | bytes 12582916
  19.9 2.1 %copy-start.2 = (bf16[2,256,1024]{2,1,0:T(8,128)(2,1)S(1)}, bf16[2,256,1024]{2,1,0:T(8,128)(2,1)}, u32[]{:S(2)}) copy-start(bf16[2,256,1024]{2,1,0:T(8,128)(2,1)} %get-tuple-element.12.adjoint) | copy-start | bytes 3145732
  19.9 2.2 %copy-start.3 = (f32[2,64,32]{2,1,0:T(8,128)S(1)}, f32[2,64,32]{2,1,0:T(8,128)}, u32[]{:S(2)}) copy-start(f32[2,64,32]{2,1,0:T(8,128)} %get-tuple-element.13.picks) | copy-start | bytes 49156
  19.9 2.2 %copy-start.4 = (f32[16,512]{1,0:T(8,128)S(1)}, f32[16,512]{1,0:T(8,128)}, u32[]{:S(2)}) copy-start(f32[16,512]{1,0:T(8,128)} %get-tuple-element.14.time_low) | copy-start | bytes 98308
  19.9 2.2 %copy-start.5 = (f32[16,512]{1,0:T(8,128)S(1)}, f32[16,512]{1,0:T(8,128)}, u32[]{:S(2)}) copy-start(f32[16,512]{1,0:T(8,128)} %get-tuple-element.16.space_low) | copy-start | bytes 98308

commit v4 on v3

--- a/solution.py
+++ b/solution.py
@@ -234,13 +234,14 @@
     anywhere = pl.BlockSpec(memory_space=pl.ANY)
     outside = pl.BlockSpec(memory_space=pltpu.HBM)
     half = width // 2
-    roomy = pltpu.CompilerParams(vmem_limit_bytes=58 * 1024 * 1024)
+    roomy = pltpu.CompilerParams(vmem_limit_bytes=54 * 1024 * 1024)
+    middle = pltpu.CompilerParams(vmem_limit_bytes=52 * 1024 * 1024)
     modest = pltpu.CompilerParams(vmem_limit_bytes=24 * 1024 * 1024)
     grouped = [
         pltpu.VMEM((2 * vectors * aggs, 8 * width), jnp.bfloat16),
         pltpu.VMEM((8 * width, vectors * aggs), jnp.bfloat16),
     ]
-    first = pltpu.CompilerParams(vmem_limit_bytes=60 * 1024 * 1024)
+    first = pltpu.CompilerParams(vmem_limit_bytes=52 * 1024 * 1024)
     space_edge, time_edge = pl.pallas_call(
         slice_kernel,
         in_specs=[outside],
@@ -287,7 +288,7 @@
         ]
         + grouped
         + [pltpu.SemaphoreType.DMA((5,))],
-        compiler_params=modest,
+        compiler_params=middle,
         cost_estimate=pl.CostEstimate(flops=1000, bytes_accessed=1000, transcendentals=0),
         name="time_edge",
     )(nulls, edge_time, time_links)

time: 35.7 us -> 34.5 us (0.966)
  local copies, waits for them, and re-layouts: 2.2 us -> 0.02 us
  blocking collectives: 11.9 us -> 12.8 us
    unnamed x12 -> x8, local copies, waits for them, and re-layouts: 2.2 us -> 0.02 us
    pallas_call x1, Pallas kernels: 2.11 us -> 3.37 us  [on_device(): pl.pallas_call(time_edge_kernel, in_specs=[outside, vmem, outside], out_s...]
    pallas_call x1, Pallas kernels: 2.24 us -> 1.22 us  [on_device(): pl.pallas_call(slice_kernel, in_specs=[outside], out_specs=[vmem] * 2, ou...]
    all_to_all x1, blocking collectives: 11.9 us -> 12.8 us  [on_device(): arrived = lax.all_to_all(packed, 'xyz', 0, 0, tiled=True)]
  transfers between devices with their start and end apart: 2 -> 2, of which waited for: 0 -> 0; matrix products, arithmetic and copies ran while one was open for 0% -> 0% of each run, Pallas kernels for 30% -> 34%
where the time goes in v4:
time: 34.5 us; the launch traced here: 34.3 us
  Pallas kernels  13.7 us (40%)
  blocking collectives  12.8 us (37%)
  starting transfers between devices  6.99 us (20%)
  other arithmetic  0.72 us (2%)
    all_to_all x1, blocking collectives, on_device(): arrived = lax.all_to_all(packed, 'xyz', 0, 0, tiled=True)  12.8 us
    pallas_call x1, Pallas kernels, on_device(): pl.pallas_call(inner_kernel, in_specs=[smem, vmem, outside, outside, outs...  8.28 us
    ppermute x2, starting transfers between devices, shifted(): lax.ppermute(array, axis, [(i, (i + by) % count) for i in range(count)])  6.99 us
    pallas_call x1, Pallas kernels, on_device(): pl.pallas_call(time_edge_kernel, in_specs=[outside, vmem, outside], out_s...  3.37 us
    pallas_call x1, Pallas kernels, on_device(): pl.pallas_call(slice_kernel, in_specs=[outside], out_specs=[vmem] * 2, ou...  1.22 us
    pallas_call x1, Pallas kernels, on_device(): pl.pallas_call(final_kernel, in_specs=[vmem] * 6, out_specs=vmem, out_sha...  0.79 us
    convert_element_type x1, other arithmetic, on_device(): result = arrived.astype(jnp.float32)  0.72 us
  transfers between devices with their start and end apart: 2, of which 0 were waited for; matrix products, arithmetic and copies ran while one was open for 0% of the time, Pallas kernels for 34%

profile of v4, /device:TPU:0, one launch (start us, length us, event | category | flops | bytes accessed | tf_op | source)
XLA Modules:
  0.0 34.3 jit_solution(1918303556736816932)
XLA Ops:
  0.0 1.2 %slices.1 = (bf16[4,1,32,16,128]{4,3,2,1,0:T(8,128)(2,1)S(1)}, bf16[1,4,32,16,128]{4,3,2,1,0:T(8,128)(2,1)S(1)}) custom-call(bf16[4,4,32,16,128]{4,3,2,1,0:T(8,128)(2,1)} %nulls.5), custom_call_target="tpu_custom_call" | custom-call | flops 1000 | bytes 1000 | tf_op jit(solution)/shard_map/slices/pallas_call | solution.py:245
  1.2 2.4 %collective-permute-start.1 = (bf16[1,4,32,16,128]{4,3,2,1,0:T(8,128)(2,1)S(1)}, bf16[1,4,32,16,128]{4,3,2,1,0:T(8,128)(2,1)S(1)}, u32[]{:S(2)}, u32[]{:S(2)}) collective-permute-start(bf16[1,4,32,16,128]{4,3,2,1,0:T(8,128)(2,1)S(1)} %get-tuple-element.15), channel_id=1, source_target_pairs={{0,24},{8,0},{16,8},{24,16},{1,25},{9,1},{17,9},{25,17},{2,26},{10... | collective-permute-start | bytes 1572872 | tf_op jit(solution)/shard_map/ppermute | solution.py:16
  3.7 4.6 %collective-permute-start = (bf16[4,1,32,16,128]{4,3,2,1,0:T(8,128)(2,1)S(1)}, bf16[4,1,32,16,128]{4,3,2,1,0:T(8,128)(2,1)S(1)}, u32[]{:S(2)}, u32[]{:S(2)}) collective-permute-start(bf16[4,1,32,16,128]{4,3,2,1,0:T(8,128)(2,1)S(1)} %get-tuple-element.11), channel_id=1, source_target_pairs={{0,7},{1,0},{2,1},{3,2},{4,3},{5,4},{6,5},{7,6},{8,15},{9,8},{10,9... | collective-permute-start | bytes 1572872 | tf_op jit(solution)/shard_map/ppermute | solution.py:16
  8.2 8.3 %inner.1 = (f32[16,512]{1,0:T(8,128)}, f32[16,512]{1,0:T(8,128)}, bf16[2,256,1024]{2,1,0:T(8,128)(2,1)}, f32[2,64,32]{2,1,0:T(8,128)}) custom-call(s32[1]{0:T(128)} %bitcast.place, s32[8,64]{1,0:T(8,128)} %lists.1, bf16[4,4,32,16,128]{4,3,2,1,0:T(8,128)(2,1)} %nulls.5, bf16[2,4,32,64,128]{4,3,2,1,0:T(8,128)(2,1)} %time_links.3, ...), custom_call_target="tpu_custom_call" | custom-call | flops 1000 | bytes 1000 | tf_op jit(solution)/shard_map/inner/pallas_call | solution.py:260
  16.5 0.0 copy-start
  16.5 0.0 copy-start.1
  16.5 0.0 copy-start.2
  16.5 0.0 copy-start.3
  16.5 0.0 collective-permute-done.1.edge
  16.6 3.4 %time_edge.1.time_high = f32[16,512]{1,0:T(8,128)S(1)} custom-call(bf16[4,4,32,16,128]{4,3,2,1,0:T(8,128)(2,1)} %nulls.5, bf16[1,4,32,16,128]{4,3,2,1,0:T(8,128)(2,1)S(1)} %collective-permute-done.1.edge, bf16[2,4,32,64,128]{4,3,2,1,0:T(8,128)(2,1)} %time_links.3), custom_call_target="tpu_custom_call" | custom-call | flops 1000 | bytes 1000 | tf_op jit(solution)/shard_map/time_edge/pallas_call | solution.py:280
  19.9 0.0 collective-permute-done.edge
  19.9 0.0 copy-done
  20.0 0.0 copy-done.1
  20.0 0.0 copy-done.2
  20.0 0.0 copy-done.3
  20.0 0.8 %final.1 = bf16[64,1024]{1,0:T(8,128)(2,1)S(1)} custom-call(bf16[4,1,32,16,128]{4,3,2,1,0:T(8,128)(2,1)S(1)} %collective-permute-done.edge, bf16[2,256,1024]{2,1,0:T(8,128)(2,1)S(1)} %copy-done, f32[2,64,32]{2,1,0:T(8,128)S(1)} %copy-done.1, f32[16,512]{1,0:T(8,128)S(1)} %copy-done.2, f32[16,512]{1,0:T(8,128)S(1)} %time_edge.1.time_high, f32[16,512]{1,0:T(8,128)S(1)} %copy-done.3), custom_call_target="tpu_custom_call" | custom-call | flops 1000 | bytes 1000 | tf_op jit(solution)/shard_map/final/pallas_call | solution.py:295
  20.8 12.8 %all_to_all.9 = bf16[8,8,1024]{2,1,0:T(8,128)(2,1)S(1)} all-to-all(bf16[8,8,1024]{2,1,0:T(8,128)(2,1)S(1)} %bitcast.5), channel_id=1, replica_groups=mesh['ta'=4,'xyz'=8] {'xyz'}, dimensions={0} | all-to-all | bytes 262144 | tf_op jit(solution)/shard_map/all_to_all | solution.py:304
  33.6 0.7 %bitcast_convert_fusion = f32[1,64,1024]{2,1,0:T(8,128)} fusion(bf16[8,8,1024]{2,1,0:T(8,128)(2,1)S(1)} %all_to_all.9), kind=kLoop, calls=%fused_computation | loop fusion | flops 65536 | bytes 393216 | tf_op jit(solution)/shard_map/convert_element_type | solution.py:306
Async XLA Ops:
  1.2 15.3 %collective-permute-start.1 = (bf16[1,4,32,16,128]{4,3,2,1,0:T(8,128)(2,1)S(1)}, bf16[1,4,32,16,128]{4,3,2,1,0:T(8,128)(2,1)S(1)}, u32[]{:S(2)}, u32[]{:S(2)}) collective-permute-start(bf16[1,4,32,16,128]{4,3,2,1,0:T(8,128)(2,1)S(1)} %get-tuple-element.15), channel_id=1, source_target_pairs={{0,24},{8,0},{16,8},{24,16},{1,25},{9,1},{17,9},{25,17},{2,26},{10... | collective-permute-start | bytes 1572872 | tf_op jit(solution)/shard_map/ppermute | solution.py:16
  3.7 16.3 %collective-permute-start = (bf16[4,1,32,16,128]{4,3,2,1,0:T(8,128)(2,1)S(1)}, bf16[4,1,32,16,128]{4,3,2,1,0:T(8,128)(2,1)S(1)}, u32[]{:S(2)}, u32[]{:S(2)}) collective-permute-start(bf16[4,1,32,16,128]{4,3,2,1,0:T(8,128)(2,1)S(1)} %get-tuple-element.11), channel_id=1, source_target_pairs={{0,7},{1,0},{2,1},{3,2},{4,3},{5,4},{6,5},{7,6},{8,15},{9,8},{10,9... | collective-permute-start | bytes 1572872 | tf_op jit(solution)/shard_map/ppermute | solution.py:16
  16.5 3.4 %copy-start = (bf16[2,256,1024]{2,1,0:T(8,128)(2,1)S(1)}, bf16[2,256,1024]{2,1,0:T(8,128)(2,1)}, u32[]{:S(2)}) copy-start(bf16[2,256,1024]{2,1,0:T(8,128)(2,1)} %get-tuple-element.12.adjoint) | copy-start | bytes 3145732
  16.5 3.4 %copy-start.1 = (f32[2,64,32]{2,1,0:T(8,128)S(1)}, f32[2,64,32]{2,1,0:T(8,128)}, u32[]{:S(2)}) copy-start(f32[2,64,32]{2,1,0:T(8,128)} %get-tuple-element.13.picks) | copy-start | bytes 49156
  16.5 3.4 %copy-start.2 = (f32[16,512]{1,0:T(8,128)S(1)}, f32[16,512]{1,0:T(8,128)}, u32[]{:S(2)}) copy-start(f32[16,512]{1,0:T(8,128)} %get-tuple-element.14.time_low) | copy-start | bytes 98308
  16.5 3.4 %copy-start.3 = (f32[16,512]{1,0:T(8,128)S(1)}, f32[16,512]{1,0:T(8,128)}, u32[]{:S(2)}) copy-start(f32[16,512]{1,0:T(8,128)} %get-tuple-element.16.space_low) | copy-start | bytes 98308

commit v5 on v4

--- a/solution.py
+++ b/solution.py
@@ -155,7 +155,7 @@
     quarter = count // 4
     turned = (column // quarter % 2) * 2 * quarter + (column // (2 * quarter)) * quarter + column % quarter
     for shard in range(shards):
-        mine = jnp.broadcast_to(lists[pl.ds(shard, 1), :], (MOST, cap))
+        mine = jnp.broadcast_to(lists[pl.ds(jnp.bitwise_xor(me, shard), 1), :], (MOST, cap))
         before = jnp.where((mine >= 0) & (mine < me * count), 1, 0)
         start = jnp.sum(before.astype(jnp.float32), axis=1, keepdims=True).astype(jnp.int32)
         inside = (mine >= me * count) & (mine < (me + 1) * count)
@@ -204,7 +204,7 @@
         time_rows[pl.ds(a_x * 8, 8), :] = group_rows(left[...], right[...], MAT_DIMS, vectors)
 
 
-def final_kernel(edge, adjoint, picks, time_low, time_high, space_low, packed):
+def final_kernel(edge, adjoint, picks, time_low, time_high, space_low, *packed):
     sites, vectors, width = edge.shape[2:]
     aggs = sites // SIDE
     found = []
@@ -217,9 +217,19 @@
         found.append(group_rows(adjoint[a_t], jnp.concatenate(parts, axis=1), ROW_DIMS, vectors))
     time_rows = jnp.concatenate([time_low[...], time_high[...]], axis=0).astype(jnp.bfloat16)
     space_rows = jnp.concatenate([space_low[...]] + found, axis=0).astype(jnp.bfloat16)
-    wide = time_rows.shape[1]
-    packed[:, pl.ds(0, wide)] = dot(picks[0].astype(jnp.bfloat16), time_rows, MAT_DIMS).astype(jnp.bfloat16)
-    packed[:, pl.ds(wide, wide)] = dot(picks[1].astype(jnp.bfloat16), space_rows, MAT_DIMS).astype(jnp.bfloat16)
+    time_sent = dot(picks[0].astype(jnp.bfloat16), time_rows, MAT_DIMS)
+    space_sent = dot(picks[1].astype(jnp.bfloat16), space_rows, MAT_DIMS)
+    for turn, out in enumerate(packed):
+        mine = slice(turn * MOST, (turn + 1) * MOST)
+        out[...] = jnp.concatenate([time_sent[mine], space_sent[mine]], axis=1).astype(jnp.bfloat16)
+
+
+def unpack_kernel(place, *refs):
+    me = place[0]
+    result = refs[-1]
+    for turn, arrived in enumerate(refs[-2::-1]):
+        source = jnp.bitwise_xor(me, turn)
+        result[pl.ds(pl.multiple_of(source * MOST, MOST), MOST), :] = arrived[...].astype(jnp.float32)
 
 
 def on_device(nulls, time_links, space_links, owner_lists):
@@ -295,22 +305,33 @@
     packed = pl.pallas_call(
         final_kernel,
         in_specs=[vmem] * 6,
-        out_specs=vmem,
-        out_shape=jax.ShapeDtypeStruct((shards * MOST, 2 * wide), jnp.bfloat16),
+        out_specs=[vmem] * shards,
+        out_shape=[jax.ShapeDtypeStruct((MOST, 2 * wide), jnp.bfloat16)] * shards,
         compiler_params=modest,
         cost_estimate=pl.CostEstimate(flops=1000, bytes_accessed=1000, transcendentals=0),
         name="final",
     )(edge_space, adjoint, picks, time_low, time_high, space_low)
-    arrived = lax.all_to_all(packed, "xyz", 0, 0, tiled=True)
+    turns = range(shards - 1, 0, -1)
+    arrived = [lax.ppermute(packed[turn], "xyz", [(i, i ^ turn) for i in range(shards)]) for turn in turns]
+    arrived.append(packed[0])
+    arrived = pl.pallas_call(
+        unpack_kernel,
+        in_specs=[smem] + [vmem] * shards,
+        out_specs=vmem,
+        out_shape=jax.ShapeDtypeStruct((shards * MOST, 2 * wide), jnp.float32),
+        compiler_params=modest,
+        cost_estimate=pl.CostEstimate(flops=1000, bytes_accessed=1000, transcendentals=0),
+        name="unpack",
+    )(place, *arrived)
     if shards * MOST == cap:
-        result = arrived.astype(jnp.float32)
+        result = arrived
     else:
         my_list = lax.dynamic_index_in_dim(owner_lists, lax.axis_index("xyz"), 0, keepdims=False)
         source = jnp.maximum(my_list, 0) // local_count
         order = jnp.arange(cap, dtype=jnp.int32)
         same = (source[:, None] == source[None, :]) & (order[None, :] < order[:, None])
         offset = jnp.sum(same.astype(jnp.int32), axis=1)
-        picked = arrived[source * MOST + offset].astype(jnp.float32)
+        picked = arrived[source * MOST + offset]
         result = jnp.where((my_list >= 0)[:, None], picked, 0.0)
     return result[None]
 

time: 34.5 us -> 35.7 us (1.035)
  blocking collectives: 12.8 us -> 0 us
  starting transfers between devices: 6.99 us -> 18.2 us
  waiting for transfers between devices: 0.01 us -> 2.8 us
  other arithmetic: 0.72 us -> 0 us
  Pallas kernels: 13.7 us -> 14.4 us
    all_to_all x1 -> x0, blocking collectives: 12.8 us -> none  [on_device(): arrived = lax.all_to_all(packed, 'xyz', 0, 0, tiled=True)]
    ppermute x0 -> x7, starting transfers between devices: none -> 11.2 us  [on_device(): lax.ppermute(packed[turn], 'xyz', [(i, i ^ turn) for i in range(shards)])]
    ppermute x0 -> x7, waiting for transfers between devices: none -> 2.8 us  [on_device(): lax.ppermute(packed[turn], 'xyz', [(i, i ^ turn) for i in range(shards)])]
    convert_element_type x1 -> x0, other arithmetic: 0.72 us -> none  [on_device(): result = arrived.astype(jnp.float32)]
    pallas_call x1 -> x2, Pallas kernels: 0.79 us -> 1.51 us  [the longest x1 0.78 us: on_device(): pl.pallas_call(final_kernel, in_specs=[vmem] * 6, out_specs=[vmem] * shar...]
  transfers between devices with their start and end apart: 2 -> 9, of which waited for: 0 -> 3; matrix products, arithmetic and copies ran while one was open for 0% -> 0% of each run, Pallas kernels for 34% -> 33%
where the time goes in v5:
time: 35.7 us; the launch traced here: 35.5 us
  starting transfers between devices  18.2 us (51%)
  Pallas kernels  14.4 us (40%)
  waiting for transfers between devices  2.8 us (8%)
    ppermute x7, starting transfers between devices, on_device(): lax.ppermute(packed[turn], 'xyz', [(i, i ^ turn) for i in range(shards)])  11.2 us
    pallas_call x1, Pallas kernels, on_device(): pl.pallas_call(inner_kernel, in_specs=[smem, vmem, outside, outside, outs...  8.3 us
    ppermute x2, starting transfers between devices, shifted(): lax.ppermute(array, axis, [(i, (i + by) % count) for i in range(count)])  6.99 us
    pallas_call x1, Pallas kernels, on_device(): pl.pallas_call(time_edge_kernel, in_specs=[outside, vmem, outside], out_s...  3.37 us
    ppermute x7, waiting for transfers between devices, on_device(): lax.ppermute(packed[turn], 'xyz', [(i, i ^ turn) for i in range(shards)])  2.8 us
    pallas_call x1, Pallas kernels, on_device(): pl.pallas_call(slice_kernel, in_specs=[outside], out_specs=[vmem] * 2, ou...  1.22 us
    pallas_call x1, Pallas kernels, on_device(): pl.pallas_call(final_kernel, in_specs=[vmem] * 6, out_specs=[vmem] * shar...  0.78 us
    pallas_call x1, Pallas kernels, on_device(): pl.pallas_call(unpack_kernel, in_specs=[smem] + [vmem] * shards, out_spec...  0.72 us
  transfers between devices with their start and end apart: 9, of which 3 were waited for; matrix products, arithmetic and copies ran while one was open for 0% of the time, Pallas kernels for 33%

profile of v5, /device:TPU:0, one launch (start us, length us, event | category | flops | bytes accessed | tf_op | source)
XLA Modules:
  0.0 35.5 jit_solution(17841775815252754971)
XLA Ops:
  0.0 1.2 %slices.1 = (bf16[4,1,32,16,128]{4,3,2,1,0:T(8,128)(2,1)S(1)}, bf16[1,4,32,16,128]{4,3,2,1,0:T(8,128)(2,1)S(1)}) custom-call(bf16[4,4,32,16,128]{4,3,2,1,0:T(8,128)(2,1)} %nulls.5), custom_call_target="tpu_custom_call" | custom-call | flops 1000 | bytes 1000 | tf_op jit(solution)/shard_map/slices/pallas_call | solution.py:255
  1.2 2.4 %collective-permute-start.1 = (bf16[1,4,32,16,128]{4,3,2,1,0:T(8,128)(2,1)S(1)}, bf16[1,4,32,16,128]{4,3,2,1,0:T(8,128)(2,1)S(1)}, u32[]{:S(2)}, u32[]{:S(2)}) collective-permute-start(bf16[1,4,32,16,128]{4,3,2,1,0:T(8,128)(2,1)S(1)} %get-tuple-element.23), channel_id=1, source_target_pairs={{0,24},{8,0},{16,8},{24,16},{1,25},{9,1},{17,9},{25,17},{2,26},{10... | collective-permute-start | bytes 1572872 | tf_op jit(solution)/shard_map/ppermute | solution.py:16
  3.7 4.6 %collective-permute-start = (bf16[4,1,32,16,128]{4,3,2,1,0:T(8,128)(2,1)S(1)}, bf16[4,1,32,16,128]{4,3,2,1,0:T(8,128)(2,1)S(1)}, u32[]{:S(2)}, u32[]{:S(2)}) collective-permute-start(bf16[4,1,32,16,128]{4,3,2,1,0:T(8,128)(2,1)S(1)} %get-tuple-element.19), channel_id=1, source_target_pairs={{0,7},{1,0},{2,1},{3,2},{4,3},{5,4},{6,5},{7,6},{8,15},{9,8},{10,9... | collective-permute-start | bytes 1572872 | tf_op jit(solution)/shard_map/ppermute | solution.py:16
  8.2 8.3 %inner.1 = (f32[16,512]{1,0:T(8,128)}, f32[16,512]{1,0:T(8,128)}, bf16[2,256,1024]{2,1,0:T(8,128)(2,1)}, f32[2,64,32]{2,1,0:T(8,128)}) custom-call(s32[1]{0:T(128)} %bitcast.place, s32[8,64]{1,0:T(8,128)} %lists.1, bf16[4,4,32,16,128]{4,3,2,1,0:T(8,128)(2,1)} %nulls.5, bf16[2,4,32,64,128]{4,3,2,1,0:T(8,128)(2,1)} %time_links.3, ...), custom_call_target="tpu_custom_call" | custom-call | flops 1000 | bytes 1000 | tf_op jit(solution)/shard_map/inner/pallas_call | solution.py:270
  16.5 0.0 copy-start
  16.5 0.0 copy-start.1
  16.5 0.0 copy-start.2
  16.6 0.0 copy-start.3
  16.6 0.0 collective-permute-done.1.edge
  16.6 3.4 %time_edge.1.time_high = f32[16,512]{1,0:T(8,128)S(1)} custom-call(bf16[4,4,32,16,128]{4,3,2,1,0:T(8,128)(2,1)} %nulls.5, bf16[1,4,32,16,128]{4,3,2,1,0:T(8,128)(2,1)S(1)} %collective-permute-done.1.edge, bf16[2,4,32,64,128]{4,3,2,1,0:T(8,128)(2,1)} %time_links.3), custom_call_target="tpu_custom_call" | custom-call | flops 1000 | bytes 1000 | tf_op jit(solution)/shard_map/time_edge/pallas_call | solution.py:290
  20.0 0.0 collective-permute-done.edge
  20.0 0.0 copy-done
  20.0 0.0 copy-done.1
  20.0 0.0 copy-done.2
  20.0 0.0 copy-done.3
  20.0 0.8 %final.1 = (bf16[8,1024]{1,0:T(8,128)(2,1)S(1)}, bf16[8,1024]{1,0:T(8,128)(2,1)S(1)}, bf16[8,1024]{1,0:T(8,128)(2,1)S(1)}, bf16[8,1024]{1,0:T(8,128)(2,1)S(1)}, ...) custom-call(bf16[4,1,32,16,128]{4,3,2,1,0:T(8,128)(2,1)S(1)} %collec, ...), custom_call_target="tpu_custom_call" | custom-call | flops 1000 | bytes 1000 | tf_op jit(solution)/shard_map/final/pallas_call | solution.py:305
  20.8 4.4 %collective-permute-start.2 = (bf16[8,1024]{1,0:T(8,128)(2,1)S(1)}, bf16[8,1024]{1,0:T(8,128)(2,1)S(1)}, u32[]{:S(2)}, u32[]{:S(2)}) collective-permute-start(bf16[8,1024]{1,0:T(8,128)(2,1)S(1)} %get-tuple-element.25), channel_id=1, source_target_pairs={{0,7},{1,6},{2,5},{3,4},{4,3},{5,2},{6,1},{7,0},{8,15},{9,14},{10,... | collective-permute-start | bytes 49160 | tf_op jit(solution)/shard_map/ppermute | solution.py:315
  25.2 0.0 collective-permute-start.3
  25.2 0.0 collective-permute-start.4
  25.2 3.3 %collective-permute-start.5 = (bf16[8,1024]{1,0:T(8,128)(2,1)S(1)}, bf16[8,1024]{1,0:T(8,128)(2,1)S(1)}, u32[]{:S(2)}, u32[]{:S(2)}) collective-permute-start(bf16[8,1024]{1,0:T(8,128)(2,1)S(1)} %get-tuple-element.28), channel_id=1, source_target_pairs={{0,4},{1,5},{2,6},{3,7},{4,0},{5,1},{6,2},{7,3},{8,12},{9,13},{10,... | collective-permute-start | bytes 49160 | tf_op jit(solution)/shard_map/ppermute | solution.py:315
  28.5 2.0 %collective-permute-start.6 = (bf16[8,1024]{1,0:T(8,128)(2,1)S(1)}, bf16[8,1024]{1,0:T(8,128)(2,1)S(1)}, u32[]{:S(2)}, u32[]{:S(2)}) collective-permute-start(bf16[8,1024]{1,0:T(8,128)(2,1)S(1)} %get-tuple-element.29), channel_id=1, source_target_pairs={{0,3},{1,2},{2,1},{3,0},{4,7},{5,6},{6,5},{7,4},{8,11},{9,10},{10,... | collective-permute-start | bytes 49160 | tf_op jit(solution)/shard_map/ppermute | solution.py:315
  30.5 0.0 collective-permute-done.2.refs_0_
  30.5 0.6 %collective-permute-start.7 = (bf16[8,1024]{1,0:T(8,128)(2,1)S(1)}, bf16[8,1024]{1,0:T(8,128)(2,1)S(1)}, u32[]{:S(2)}, u32[]{:S(2)}) collective-permute-start(bf16[8,1024]{1,0:T(8,128)(2,1)S(1)} %get-tuple-element.30), channel_id=1, source_target_pairs={{0,2},{1,3},{2,0},{3,1},{4,6},{5,7},{6,4},{7,5},{8,10},{9,11},{10,... | collective-permute-start | bytes 49160 | tf_op jit(solution)/shard_map/ppermute | solution.py:315
  31.1 0.0 collective-permute-done.3.refs_1_
  31.1 0.9 %collective-permute-start.8 = (bf16[8,1024]{1,0:T(8,128)(2,1)S(1)}, bf16[8,1024]{1,0:T(8,128)(2,1)S(1)}, u32[]{:S(2)}, u32[]{:S(2)}) collective-permute-start(bf16[8,1024]{1,0:T(8,128)(2,1)S(1)} %get-tuple-element.31), channel_id=1, source_target_pairs={{0,1},{1,0},{2,3},{3,2},{4,5},{5,4},{6,7},{7,6},{8,9},{9,8},{10,11... | collective-permute-start | bytes 49160 | tf_op jit(solution)/shard_map/ppermute | solution.py:315
  32.0 0.0 collective-permute-done.4.refs_2_
  32.0 0.0 collective-permute-done.5.refs_3_
  32.0 1.1 %collective-permute-done.6.refs_4_ = bf16[8,1024]{1,0:T(8,128)(2,1)S(1)} collective-permute-done((bf16[8,1024]{1,0:T(8,128)(2,1)S(1)}, bf16[8,1024]{1,0:T(8,128)(2,1)S(1)}, u32[]{:S(2)}, u32[]{:S(2)}) %collective-permute-start.6) | collective-permute-done | bytes 16416 | tf_op jit(solution)/shard_map/ppermute | solution.py:315
  33.1 1.1 %collective-permute-done.7.refs_5_ = bf16[8,1024]{1,0:T(8,128)(2,1)S(1)} collective-permute-done((bf16[8,1024]{1,0:T(8,128)(2,1)S(1)}, bf16[8,1024]{1,0:T(8,128)(2,1)S(1)}, u32[]{:S(2)}, u32[]{:S(2)}) %collective-permute-start.7) | collective-permute-done | bytes 16416 | tf_op jit(solution)/shard_map/ppermute | solution.py:315
  34.2 0.6 %collective-permute-done.8.refs_6_ = bf16[8,1024]{1,0:T(8,128)(2,1)S(1)} collective-permute-done((bf16[8,1024]{1,0:T(8,128)(2,1)S(1)}, bf16[8,1024]{1,0:T(8,128)(2,1)S(1)}, u32[]{:S(2)}, u32[]{:S(2)}) %collective-permute-start.8) | collective-permute-done | bytes 16416 | tf_op jit(solution)/shard_map/ppermute | solution.py:315
  34.8 0.7 %unpack.1 = f32[64,1024]{1,0:T(8,128)} custom-call(s32[1]{0:T(128)} %bitcast.place, bf16[8,1024]{1,0:T(8,128)(2,1)S(1)} %collective-permute-done.2.refs_0_, bf16[8,1024]{1,0:T(8,128)(2,1)S(1)} %collective-permute-done.3.refs_1_, bf16[8,1024]{1,0:T(8,128)(2,1)S(1)} %collective-permute-done.4.refs_2_, bf16[8,1024]{1,0:T(8,128)(2,1)S(1)} %collective-permute-done.5.refs_3_, ...), custom_call_target="tpu_custom_call" | custom-call | flops 1000 | bytes 1000 | tf_op jit(solution)/shard_map/unpack/pallas_call | solution.py:317
Async XLA Ops:
  1.2 15.3 %collective-permute-start.1 = (bf16[1,4,32,16,128]{4,3,2,1,0:T(8,128)(2,1)S(1)}, bf16[1,4,32,16,128]{4,3,2,1,0:T(8,128)(2,1)S(1)}, u32[]{:S(2)}, u32[]{:S(2)}) collective-permute-start(bf16[1,4,32,16,128]{4,3,2,1,0:T(8,128)(2,1)S(1)} %get-tuple-element.23), channel_id=1, source_target_pairs={{0,24},{8,0},{16,8},{24,16},{1,25},{9,1},{17,9},{25,17},{2,26},{10... | collective-permute-start | bytes 1572872 | tf_op jit(solution)/shard_map/ppermute | solution.py:16
  3.7 16.3 %collective-permute-start = (bf16[4,1,32,16,128]{4,3,2,1,0:T(8,128)(2,1)S(1)}, bf16[4,1,32,16,128]{4,3,2,1,0:T(8,128)(2,1)S(1)}, u32[]{:S(2)}, u32[]{:S(2)}) collective-permute-start(bf16[4,1,32,16,128]{4,3,2,1,0:T(8,128)(2,1)S(1)} %get-tuple-element.19), channel_id=1, source_target_pairs={{0,7},{1,0},{2,1},{3,2},{4,3},{5,4},{6,5},{7,6},{8,15},{9,8},{10,9... | collective-permute-start | bytes 1572872 | tf_op jit(solution)/shard_map/ppermute | solution.py:16
  16.5 3.4 %copy-start = (bf16[2,256,1024]{2,1,0:T(8,128)(2,1)S(1)}, bf16[2,256,1024]{2,1,0:T(8,128)(2,1)}, u32[]{:S(2)}) copy-start(bf16[2,256,1024]{2,1,0:T(8,128)(2,1)} %get-tuple-element.20.adjoint) | copy-start | bytes 3145732
  16.5 3.4 %copy-start.1 = (f32[2,64,32]{2,1,0:T(8,128)S(1)}, f32[2,64,32]{2,1,0:T(8,128)}, u32[]{:S(2)}) copy-start(f32[2,64,32]{2,1,0:T(8,128)} %get-tuple-element.21.picks) | copy-start | bytes 49156
  16.5 3.4 %copy-start.2 = (f32[16,512]{1,0:T(8,128)S(1)}, f32[16,512]{1,0:T(8,128)}, u32[]{:S(2)}) copy-start(f32[16,512]{1,0:T(8,128)} %get-tuple-element.22.time_low) | copy-start | bytes 98308
  16.6 3.4 %copy-start.3 = (f32[16,512]{1,0:T(8,128)S(1)}, f32[16,512]{1,0:T(8,128)}, u32[]{:S(2)}) copy-start(f32[16,512]{1,0:T(8,128)} %get-tuple-element.24.space_low) | copy-start | bytes 98308
  20.8 9.7 %collective-permute-start.2 = (bf16[8,1024]{1,0:T(8,128)(2,1)S(1)}, bf16[8,1024]{1,0:T(8,128)(2,1)S(1)}, u32[]{:S(2)}, u32[]{:S(2)}) collective-permute-start(bf16[8,1024]{1,0:T(8,128)(2,1)S(1)} %get-tuple-element.25), channel_id=1, source_target_pairs={{0,7},{1,6},{2,5},{3,4},{4,3},{5,2},{6,1},{7,0},{8,15},{9,14},{10,... | collective-permute-start | bytes 49160 | tf_op jit(solution)/shard_map/ppermute | solution.py:315
  25.2 5.9 %collective-permute-start.3 = (bf16[8,1024]{1,0:T(8,128)(2,1)S(1)}, bf16[8,1024]{1,0:T(8,128)(2,1)S(1)}, u32[]{:S(2)}, u32[]{:S(2)}) collective-permute-start(bf16[8,1024]{1,0:T(8,128)(2,1)S(1)} %get-tuple-element.26), channel_id=1, source_target_pairs={{0,6},{1,7},{2,4},{3,5},{4,2},{5,3},{6,0},{7,1},{8,14},{9,15},{10,... | collective-permute-start | bytes 49160 | tf_op jit(solution)/shard_map/ppermute | solution.py:315
  25.2 6.8 %collective-permute-start.4 = (bf16[8,1024]{1,0:T(8,128)(2,1)S(1)}, bf16[8,1024]{1,0:T(8,128)(2,1)S(1)}, u32[]{:S(2)}, u32[]{:S(2)}) collective-permute-start(bf16[8,1024]{1,0:T(8,128)(2,1)S(1)} %get-tuple-element.27), channel_id=1, source_target_pairs={{0,5},{1,4},{2,7},{3,6},{4,1},{5,0},{6,3},{7,2},{8,13},{9,12},{10,... | collective-permute-start | bytes 49160 | tf_op jit(solution)/shard_map/ppermute | solution.py:315
  25.2 6.8 %collective-permute-start.5 = (bf16[8,1024]{1,0:T(8,128)(2,1)S(1)}, bf16[8,1024]{1,0:T(8,128)(2,1)S(1)}, u32[]{:S(2)}, u32[]{:S(2)}) collective-permute-start(bf16[8,1024]{1,0:T(8,128)(2,1)S(1)} %get-tuple-element.28), channel_id=1, source_target_pairs={{0,4},{1,5},{2,6},{3,7},{4,0},{5,1},{6,2},{7,3},{8,12},{9,13},{10,... | collective-permute-start | bytes 49160 | tf_op jit(solution)/shard_map/ppermute | solution.py:315
  28.5 4.6 %collective-permute-start.6 = (bf16[8,1024]{1,0:T(8,128)(2,1)S(1)}, bf16[8,1024]{1,0:T(8,128)(2,1)S(1)}, u32[]{:S(2)}, u32[]{:S(2)}) collective-permute-start(bf16[8,1024]{1,0:T(8,128)(2,1)S(1)} %get-tuple-element.29), channel_id=1, source_target_pairs={{0,3},{1,2},{2,1},{3,0},{4,7},{5,6},{6,5},{7,4},{8,11},{9,10},{10,... | collective-permute-start | bytes 49160 | tf_op jit(solution)/shard_map/ppermute | solution.py:315
  30.5 3.7 %collective-permute-start.7 = (bf16[8,1024]{1,0:T(8,128)(2,1)S(1)}, bf16[8,1024]{1,0:T(8,128)(2,1)S(1)}, u32[]{:S(2)}, u32[]{:S(2)}) collective-permute-start(bf16[8,1024]{1,0:T(8,128)(2,1)S(1)} %get-tuple-element.30), channel_id=1, source_target_pairs={{0,2},{1,3},{2,0},{3,1},{4,6},{5,7},{6,4},{7,5},{8,10},{9,11},{10,... | collective-permute-start | bytes 49160 | tf_op jit(solution)/shard_map/ppermute | solution.py:315
  31.1 3.7 %collective-permute-start.8 = (bf16[8,1024]{1,0:T(8,128)(2,1)S(1)}, bf16[8,1024]{1,0:T(8,128)(2,1)S(1)}, u32[]{:S(2)}, u32[]{:S(2)}) collective-permute-start(bf16[8,1024]{1,0:T(8,128)(2,1)S(1)} %get-tuple-element.31), channel_id=1, source_target_pairs={{0,1},{1,0},{2,3},{3,2},{4,5},{5,4},{6,7},{7,6},{8,9},{9,8},{10,11... | collective-permute-start | bytes 49160 | tf_op jit(solution)/shard_map/ppermute | solution.py:315

commit v6 on v5

--- a/solution.py
+++ b/solution.py
@@ -14,6 +14,10 @@
 def shifted(array, axis, by):
     count = lax.axis_size(axis)
     return lax.ppermute(array, axis, [(i, (i + by) % count) for i in range(count)])
+
+
+def crossed(array, axis, bits):
+    return lax.ppermute(array, axis, [(i, i ^ bits) for i in range(lax.axis_size(axis))])
 
 
 def dot(left, right, dims):
@@ -148,22 +152,29 @@
         fetch(space_links.at[t, 1])
     me = place[0]
     shards, cap = lists.shape
-    count = picks.shape[2]
+    count = picks.shape[2] // 2
     lane = lax.broadcasted_iota(jnp.int32, (MOST, cap), 1)
     want = lax.broadcasted_iota(jnp.int32, (MOST, cap), 0)
-    column = lax.broadcasted_iota(jnp.int32, (MOST, count), 1)
+    column = lax.broadcasted_iota(jnp.int32, (MOST, 2 * count), 1)
     quarter = count // 4
-    turned = (column // quarter % 2) * 2 * quarter + (column // (2 * quarter)) * quarter + column % quarter
-    for shard in range(shards):
-        mine = jnp.broadcast_to(lists[pl.ds(jnp.bitwise_xor(me, shard), 1), :], (MOST, cap))
-        before = jnp.where((mine >= 0) & (mine < me * count), 1, 0)
-        start = jnp.sum(before.astype(jnp.float32), axis=1, keepdims=True).astype(jnp.int32)
-        inside = (mine >= me * count) & (mine < (me + 1) * count)
-        match = inside & (lane - start == want)
-        chosen = jnp.sum(jnp.where(match, mine - me * count + 1, 0).astype(jnp.float32), axis=1, keepdims=True)
-        chosen = chosen.astype(jnp.int32) - 1
-        picks[0, pl.ds(shard * MOST, MOST), :] = jnp.where(column == chosen, 1.0, 0.0)
-        picks[1, pl.ds(shard * MOST, MOST), :] = jnp.where(turned == chosen, 1.0, 0.0)
+    inside = column % count
+    turned = (inside // quarter % 2) * 2 * quarter + (inside // (2 * quarter)) * quarter + inside % quarter
+    own_column = column < count
+    side = lax.rem(me, 2)
+    for turn in range(shards // 2):
+        owner = 2 * jnp.bitwise_xor(me // 2, turn) + side
+        mine = jnp.broadcast_to(lists[pl.ds(owner, 1), :], (MOST, cap))
+        for parity in range(2):
+            source = me - side + parity
+            before = jnp.where((mine >= 0) & (mine < source * count), 1, 0)
+            start = jnp.sum(before.astype(jnp.float32), axis=1, keepdims=True).astype(jnp.int32)
+            match = (mine >= source * count) & (mine < (source + 1) * count) & (lane - start == want)
+            chosen = jnp.sum(jnp.where(match, mine - source * count + 1, 0).astype(jnp.float32), axis=1, keepdims=True)
+            chosen = chosen.astype(jnp.int32) - 1
+            here = own_column == (side == parity)
+            rows = pl.ds((2 * turn + parity) * MOST, MOST)
+            picks[0, rows, :] = jnp.where(here & (inside == chosen), 1.0, 0.0)
+            picks[1, rows, :] = jnp.where(here & (turned == chosen), 1.0, 0.0)
     base.wait()
     for a_x in range(2):
         copies[2 * a_x].wait()
@@ -185,7 +196,7 @@
         adjoint_item(links.at[8 + t], vecs.at[t, 3], t % 2, adjoint.at[t // 2])
 
 
-def time_edge_kernel(nulls, edge, time_links, time_rows, links, vecs, left, right, sems):
+def time_edge_kernel(nulls, edge, time_links, time_low, space_low, early, links, vecs, left, right, sems):
     vectors = nulls.shape[-2]
     copies = []
     base = pltpu.make_async_copy(nulls.at[3], vecs, sems.at[4])
@@ -195,16 +206,18 @@
         copy.start()
         copies.append(copy)
     base.wait()
+    found = []
     for a_x in range(2):
         copies[2 * a_x].wait()
         copies[2 * a_x + 1].wait()
         for c in range(2):
             x = 2 * a_x + c
             image_item(links.at[x], vecs.at[x], edge.at[0, x], c, left, right)
-        time_rows[pl.ds(a_x * 8, 8), :] = group_rows(left[...], right[...], MAT_DIMS, vectors)
-
-
-def final_kernel(edge, adjoint, picks, time_low, time_high, space_low, *packed):
+        found.append(group_rows(left[...], right[...], MAT_DIMS, vectors))
+    early[...] = jnp.concatenate([time_low[...]] + found + [space_low[...]], axis=0).astype(jnp.bfloat16)
+
+
+def final_kernel(edge, adjoint, late):
     sites, vectors, width = edge.shape[2:]
     aggs = sites // SIDE
     found = []
@@ -215,21 +228,30 @@
                 rows = [edge[2 * a_t + c, 0, agg * SIDE + site] for agg in range(aggs)]
                 parts.append(jnp.concatenate(rows, axis=0))
         found.append(group_rows(adjoint[a_t], jnp.concatenate(parts, axis=1), ROW_DIMS, vectors))
-    time_rows = jnp.concatenate([time_low[...], time_high[...]], axis=0).astype(jnp.bfloat16)
-    space_rows = jnp.concatenate([space_low[...]] + found, axis=0).astype(jnp.bfloat16)
+    late[...] = jnp.concatenate(found, axis=0).astype(jnp.bfloat16)
+
+
+def pack_kernel(picks, early, early_other, late, late_other, *packed):
+    half_count = late.shape[0]
+    count = 2 * half_count
+    time_rows = jnp.concatenate([early[pl.ds(0, count), :], early_other[pl.ds(0, count), :]], axis=0)
+    space_rows = jnp.concatenate(
+        [early[pl.ds(count, half_count), :], late[...], early_other[pl.ds(count, half_count), :], late_other[...]],
+        axis=0,
+    )
     time_sent = dot(picks[0].astype(jnp.bfloat16), time_rows, MAT_DIMS)
     space_sent = dot(picks[1].astype(jnp.bfloat16), space_rows, MAT_DIMS)
     for turn, out in enumerate(packed):
-        mine = slice(turn * MOST, (turn + 1) * MOST)
+        mine = slice(turn * 2 * MOST, (turn + 1) * 2 * MOST)
         out[...] = jnp.concatenate([time_sent[mine], space_sent[mine]], axis=1).astype(jnp.bfloat16)
 
 
 def unpack_kernel(place, *refs):
-    me = place[0]
+    pair = place[0] // 2
     result = refs[-1]
     for turn, arrived in enumerate(refs[-2::-1]):
-        source = jnp.bitwise_xor(me, turn)
-        result[pl.ds(pl.multiple_of(source * MOST, MOST), MOST), :] = arrived[...].astype(jnp.float32)
+        source = jnp.bitwise_xor(pair, turn)
+        result[pl.ds(pl.multiple_of(source * 2 * MOST, 2 * MOST), 2 * MOST), :] = arrived[...].astype(jnp.float32)
 
 
 def on_device(nulls, time_links, space_links, owner_lists):
@@ -275,7 +297,7 @@
             jax.ShapeDtypeStruct((2 * aggs, wide), jnp.float32),
             jax.ShapeDtypeStruct((2 * aggs, wide), jnp.float32),
             jax.ShapeDtypeStruct((2, 2 * vectors * aggs, 8 * width), jnp.bfloat16),
-            jax.ShapeDtypeStruct((2, shards * MOST, local_count), jnp.float32),
+            jax.ShapeDtypeStruct((2, shards * MOST, 2 * local_count), jnp.float32),
         ],
         scratch_shapes=[
             pltpu.VMEM((12, sites, half, width), jnp.bfloat16),
@@ -287,11 +309,11 @@
         cost_estimate=pl.CostEstimate(flops=1000, bytes_accessed=1000, transcendentals=0),
         name="inner",
     )(place, owner_lists, nulls, time_links, space_links)
-    time_high = pl.pallas_call(
+    early = pl.pallas_call(
         time_edge_kernel,
-        in_specs=[outside, vmem, outside],
+        in_specs=[outside, vmem, outside, vmem, vmem],
         out_specs=vmem,
-        out_shape=jax.ShapeDtypeStruct((2 * aggs, wide), jnp.float32),
+        out_shape=jax.ShapeDtypeStruct((6 * aggs, wide), jnp.bfloat16),
         scratch_shapes=[
             pltpu.VMEM((4, sites, half, width), jnp.bfloat16),
             pltpu.VMEM(nulls.shape[1:], nulls.dtype),
@@ -301,22 +323,33 @@
         compiler_params=middle,
         cost_estimate=pl.CostEstimate(flops=1000, bytes_accessed=1000, transcendentals=0),
         name="time_edge",
-    )(nulls, edge_time, time_links)
+    )(nulls, edge_time, time_links, time_low, space_low)
+    late = pl.pallas_call(
+        final_kernel,
+        in_specs=[vmem] * 2,
+        out_specs=vmem,
+        out_shape=jax.ShapeDtypeStruct((2 * aggs, wide), jnp.bfloat16),
+        compiler_params=modest,
+        cost_estimate=pl.CostEstimate(flops=1000, bytes_accessed=1000, transcendentals=0),
+        name="final",
+    )(edge_space, adjoint)
+    early_other = crossed(early, "xyz", 1)
+    late_other = crossed(late, "xyz", 1)
+    pairs = shards // 2
     packed = pl.pallas_call(
-        final_kernel,
-        in_specs=[vmem] * 6,
-        out_specs=[vmem] * shards,
-        out_shape=[jax.ShapeDtypeStruct((MOST, 2 * wide), jnp.bfloat16)] * shards,
+        pack_kernel,
+        in_specs=[vmem] * 5,
+        out_specs=[vmem] * pairs,
+        out_shape=[jax.ShapeDtypeStruct((2 * MOST, 2 * wide), jnp.bfloat16)] * pairs,
         compiler_params=modest,
         cost_estimate=pl.CostEstimate(flops=1000, bytes_accessed=1000, transcendentals=0),
-        name="final",
-    )(edge_space, adjoint, picks, time_low, time_high, space_low)
-    turns = range(shards - 1, 0, -1)
-    arrived = [lax.ppermute(packed[turn], "xyz", [(i, i ^ turn) for i in range(shards)]) for turn in turns]
+        name="pack",
+    )(picks, early, early_other, late, late_other)
+    arrived = [crossed(packed[turn], "xyz", 2 * turn) for turn in range(pairs - 1, 0, -1)]
     arrived.append(packed[0])
     arrived = pl.pallas_call(
         unpack_kernel,
-        in_specs=[smem] + [vmem] * shards,
+        in_specs=[smem] + [vmem] * pairs,
         out_specs=vmem,
         out_shape=jax.ShapeDtypeStruct((shards * MOST, 2 * wide), jnp.float32),
         compiler_params=modest,

time: 35.7 us -> 33.8 us (0.947)
  starting transfers between devices: 18.2 us -> 13.6 us
  local copies, waits for them, and re-layouts: 0.02 us -> 1.6 us
  waiting for transfers between devices: 2.8 us -> 3.98 us
    ppermute x7 -> x5, starting transfers between devices: 11.2 us -> 6.57 us  [crossed(): lax.ppermute(array, axis, [(i, i ^ bits) for i in range(lax.axis_size(axi...]
    unnamed x8, local copies, waits for them, and re-layouts: 0.02 us -> 1.6 us
    ppermute x7 -> x5, waiting for transfers between devices: 2.8 us -> 3.98 us  [crossed(): lax.ppermute(array, axis, [(i, i ^ bits) for i in range(lax.axis_size(axi...]
    pallas_call x3 -> x4, Pallas kernels: 4.88 us -> 4.86 us  [the longest x1 3.32 us: on_device(): pl.pallas_call(time_edge_kernel, in_specs=[outside, vmem, outside, vmem,...]
  transfers between devices with their start and end apart: 9 -> 7, of which waited for: 3 -> 4; matrix products, arithmetic and copies ran while one was open for 0% -> 0% of each run, Pallas kernels for 33% -> 36%
where the time goes in v6:
time: 33.8 us; the launch traced here: 33.6 us
  Pallas kernels  14.4 us (43%)
  starting transfers between devices  13.6 us (40%)
  waiting for transfers between devices  3.98 us (12%)
  local copies, waits for them, and re-layouts  1.6 us (5%)
    pallas_call x1, Pallas kernels, on_device(): pl.pallas_call(inner_kernel, in_specs=[smem, vmem, outside, outside, outs...  8.28 us
    ppermute x2, starting transfers between devices, shifted(): lax.ppermute(array, axis, [(i, (i + by) % count) for i in range(count)])  6.99 us
    ppermute x5, starting transfers between devices, crossed(): lax.ppermute(array, axis, [(i, i ^ bits) for i in range(lax.axis_size(axi...  6.57 us
    ppermute x5, waiting for transfers between devices, crossed(): lax.ppermute(array, axis, [(i, i ^ bits) for i in range(lax.axis_size(axi...  3.98 us
    pallas_call x1, Pallas kernels, on_device(): pl.pallas_call(time_edge_kernel, in_specs=[outside, vmem, outside, vmem,...  3.32 us
    unnamed x8, local copies, waits for them, and re-layouts  1.6 us
    pallas_call x1, Pallas kernels, on_device(): pl.pallas_call(slice_kernel, in_specs=[outside], out_specs=[vmem] * 2, ou...  1.22 us
    pallas_call x1, Pallas kernels, on_device(): pl.pallas_call(unpack_kernel, in_specs=[smem] + [vmem] * pairs, out_specs...  0.72 us
  transfers between devices with their start and end apart: 7, of which 4 were waited for; matrix products, arithmetic and copies ran while one was open for 0% of the time, Pallas kernels for 36%

profile of v6, /device:TPU:0, one launch (start us, length us, event | category | flops | bytes accessed | tf_op | source)
XLA Modules:
  0.0 33.6 jit_solution(4254554761204735216)
XLA Ops:
  0.0 1.2 %slices.1 = (bf16[4,1,32,16,128]{4,3,2,1,0:T(8,128)(2,1)S(1)}, bf16[1,4,32,16,128]{4,3,2,1,0:T(8,128)(2,1)S(1)}) custom-call(bf16[4,4,32,16,128]{4,3,2,1,0:T(8,128)(2,1)} %nulls.5), custom_call_target="tpu_custom_call" | custom-call | flops 1000 | bytes 1000 | tf_op jit(solution)/shard_map/slices/pallas_call | solution.py:277
  1.2 2.4 %collective-permute-start = (bf16[1,4,32,16,128]{4,3,2,1,0:T(8,128)(2,1)S(1)}, bf16[1,4,32,16,128]{4,3,2,1,0:T(8,128)(2,1)S(1)}, u32[]{:S(2)}, u32[]{:S(2)}) collective-permute-start(bf16[1,4,32,16,128]{4,3,2,1,0:T(8,128)(2,1)S(1)} %get-tuple-element.16), channel_id=1, source_target_pairs={{0,24},{8,0},{16,8},{24,16},{1,25},{9,1},{17,9},{25,17},{2,26},{10... | collective-permute-start | bytes 1572872 | tf_op jit(solution)/shard_map/ppermute | solution.py:16
  3.7 4.6 %collective-permute-start.2 = (bf16[4,1,32,16,128]{4,3,2,1,0:T(8,128)(2,1)S(1)}, bf16[4,1,32,16,128]{4,3,2,1,0:T(8,128)(2,1)S(1)}, u32[]{:S(2)}, u32[]{:S(2)}) collective-permute-start(bf16[4,1,32,16,128]{4,3,2,1,0:T(8,128)(2,1)S(1)} %get-tuple-element.19), channel_id=1, source_target_pairs={{0,7},{1,0},{2,1},{3,2},{4,3},{5,4},{6,5},{7,6},{8,15},{9,8},{10,9... | collective-permute-start | bytes 1572872 | tf_op jit(solution)/shard_map/ppermute | solution.py:16
  8.2 8.3 %inner.1 = (f32[16,512]{1,0:T(8,128)}, f32[16,512]{1,0:T(8,128)}, bf16[2,256,1024]{2,1,0:T(8,128)(2,1)}, f32[2,64,64]{2,1,0:T(8,128)}) custom-call(s32[1]{0:T(128)} %bitcast.place, s32[8,64]{1,0:T(8,128)} %lists.1, bf16[4,4,32,16,128]{4,3,2,1,0:T(8,128)(2,1)} %nulls.5, bf16[2,4,32,64,128]{4,3,2,1,0:T(8,128)(2,1)} %time_links.3, ...), custom_call_target="tpu_custom_call" | custom-call | flops 1000 | bytes 1000 | tf_op jit(solution)/shard_map/inner/pallas_call | solution.py:292
  16.5 0.0 copy-start
  16.5 0.0 collective-permute-done.edge
  16.5 0.0 copy-start.2
  16.5 0.8 %copy-done.2 = f32[16,512]{1,0:T(8,128)S(1)} copy-done((f32[16,512]{1,0:T(8,128)S(1)}, f32[16,512]{1,0:T(8,128)}, u32[]{:S(2)}) %copy-start.2) | copy-done | bytes 32792
  17.4 0.0 copy-start.3
  17.4 0.8 %copy-done.3 = f32[16,512]{1,0:T(8,128)S(1)} copy-done((f32[16,512]{1,0:T(8,128)S(1)}, f32[16,512]{1,0:T(8,128)}, u32[]{:S(2)}) %copy-start.3) | copy-done | bytes 32792
  18.1 0.0 copy-start.1
  18.1 3.3 %time_edge.1.early = bf16[48,512]{1,0:T(8,128)(2,1)S(1)} custom-call(bf16[4,4,32,16,128]{4,3,2,1,0:T(8,128)(2,1)} %nulls.5, bf16[1,4,32,16,128]{4,3,2,1,0:T(8,128)(2,1)S(1)} %collective-permute-done.edge, bf16[2,4,32,64,128]{4,3,2,1,0:T(8,128)(2,1)} %time_links.3, f32[16,512]{1,0:T(8,128)S(1)} %copy-done.2, f32[16,512]{1,0:T(8,128)S(1)} %copy-done.3), custom_call_target="tpu_custom_call" | custom-call | flops 1000 | bytes 1000 | tf_op jit(solution)/shard_map/time_edge/pallas_call | solution.py:312
  21.5 0.1 collective-permute-start.1
  21.5 0.0 collective-permute-done.2.edge
  21.5 0.0 copy-done
  21.6 0.7 %final.1.late = bf16[16,512]{1,0:T(8,128)(2,1)S(1)} custom-call(bf16[4,1,32,16,128]{4,3,2,1,0:T(8,128)(2,1)S(1)} %collective-permute-done.2.edge, bf16[2,256,1024]{2,1,0:T(8,128)(2,1)S(1)} %copy-done), custom_call_target="tpu_custom_call" | custom-call | flops 1000 | bytes 1000 | tf_op jit(solution)/shard_map/final/pallas_call | solution.py:327
  22.2 2.0 %collective-permute-start.3 = (bf16[16,512]{1,0:T(8,128)(2,1)S(1)}, bf16[16,512]{1,0:T(8,128)(2,1)S(1)}, u32[]{:S(2)}, u32[]{:S(2)}) collective-permute-start(bf16[16,512]{1,0:T(8,128)(2,1)S(1)} %final.1.late), channel_id=1, source_target_pairs={{0,1},{1,0},{2,3},{3,2},{4,5},{5,4},{6,7},{7,6},{8,9},{9,8},{10,11... | collective-permute-start | bytes 49160 | tf_op jit(solution)/shard_map/ppermute | solution.py:20
  24.3 1.7 %collective-permute-done.3.late_other = bf16[16,512]{1,0:T(8,128)(2,1)S(1)} collective-permute-done((bf16[16,512]{1,0:T(8,128)(2,1)S(1)}, bf16[16,512]{1,0:T(8,128)(2,1)S(1)}, u32[]{:S(2)}, u32[]{:S(2)}) %collective-permute-start.3) | collective-permute-done | bytes 16416 | tf_op jit(solution)/shard_map/ppermute | solution.py:20
  26.0 0.0 collective-permute-done.1.early_other
  26.0 0.0 copy-done.1
  26.0 0.2 pack.1
  26.2 1.4 %collective-permute-start.4 = (bf16[16,1024]{1,0:T(8,128)(2,1)S(1)}, bf16[16,1024]{1,0:T(8,128)(2,1)S(1)}, u32[]{:S(2)}, u32[]{:S(2)}) collective-permute-start(bf16[16,1024]{1,0:T(8,128)(2,1)S(1)} %get-tuple-element.21), channel_id=1, source_target_pairs={{0,6},{1,7},{2,4},{3,5},{4,2},{5,3},{6,0},{7,1},{8,14},{9,15},{10,... | collective-permute-start | bytes 98312 | tf_op jit(solution)/shard_map/ppermute | solution.py:20
  27.6 0.0 collective-permute-start.5
  27.6 3.0 %collective-permute-start.6 = (bf16[16,1024]{1,0:T(8,128)(2,1)S(1)}, bf16[16,1024]{1,0:T(8,128)(2,1)S(1)}, u32[]{:S(2)}, u32[]{:S(2)}) collective-permute-start(bf16[16,1024]{1,0:T(8,128)(2,1)S(1)} %get-tuple-element.23), channel_id=1, source_target_pairs={{0,2},{1,3},{2,0},{3,1},{4,6},{5,7},{6,4},{7,5},{8,10},{9,11},{10,... | collective-permute-start | bytes 98312 | tf_op jit(solution)/shard_map/ppermute | solution.py:20
  30.6 1.3 %collective-permute-done.4.refs_0_ = bf16[16,1024]{1,0:T(8,128)(2,1)S(1)} collective-permute-done((bf16[16,1024]{1,0:T(8,128)(2,1)S(1)}, bf16[16,1024]{1,0:T(8,128)(2,1)S(1)}, u32[]{:S(2)}, u32[]{:S(2)}) %collective-permute-start.4) | collective-permute-done | bytes 32800 | tf_op jit(solution)/shard_map/ppermute | solution.py:20
  32.0 0.8 %collective-permute-done.5.refs_1_ = bf16[16,1024]{1,0:T(8,128)(2,1)S(1)} collective-permute-done((bf16[16,1024]{1,0:T(8,128)(2,1)S(1)}, bf16[16,1024]{1,0:T(8,128)(2,1)S(1)}, u32[]{:S(2)}, u32[]{:S(2)}) %collective-permute-start.5) | collective-permute-done | bytes 32800 | tf_op jit(solution)/shard_map/ppermute | solution.py:20
  32.8 0.1 collective-permute-done.6.refs_2_
  32.9 0.7 %unpack.1 = f32[64,1024]{1,0:T(8,128)} custom-call(s32[1]{0:T(128)} %bitcast.place, bf16[16,1024]{1,0:T(8,128)(2,1)S(1)} %collective-permute-done.4.refs_0_, bf16[16,1024]{1,0:T(8,128)(2,1)S(1)} %collective-permute-done.5.refs_1_, bf16[16,1024]{1,0:T(8,128)(2,1)S(1)} %collective-permute-done.6.refs_2_, bf16[16,1024]{1,0:T(8,128)(2,1)S(1)} %get-tuple-element.24.refs_3_), custom_call_target="tpu_custom_call" | custom-call | flops 1000 | bytes 1000 | tf_op jit(solution)/shard_map/unpack/pallas_call | solution.py:350
Async XLA Ops:
  1.2 15.3 %collective-permute-start = (bf16[1,4,32,16,128]{4,3,2,1,0:T(8,128)(2,1)S(1)}, bf16[1,4,32,16,128]{4,3,2,1,0:T(8,128)(2,1)S(1)}, u32[]{:S(2)}, u32[]{:S(2)}) collective-permute-start(bf16[1,4,32,16,128]{4,3,2,1,0:T(8,128)(2,1)S(1)} %get-tuple-element.16), channel_id=1, source_target_pairs={{0,24},{8,0},{16,8},{24,16},{1,25},{9,1},{17,9},{25,17},{2,26},{10... | collective-permute-start | bytes 1572872 | tf_op jit(solution)/shard_map/ppermute | solution.py:16
  3.7 17.9 %collective-permute-start.2 = (bf16[4,1,32,16,128]{4,3,2,1,0:T(8,128)(2,1)S(1)}, bf16[4,1,32,16,128]{4,3,2,1,0:T(8,128)(2,1)S(1)}, u32[]{:S(2)}, u32[]{:S(2)}) collective-permute-start(bf16[4,1,32,16,128]{4,3,2,1,0:T(8,128)(2,1)S(1)} %get-tuple-element.19), channel_id=1, source_target_pairs={{0,7},{1,0},{2,1},{3,2},{4,3},{5,4},{6,5},{7,6},{8,15},{9,8},{10,9... | collective-permute-start | bytes 1572872 | tf_op jit(solution)/shard_map/ppermute | solution.py:16
  16.5 5.0 %copy-start = (bf16[2,256,1024]{2,1,0:T(8,128)(2,1)S(1)}, bf16[2,256,1024]{2,1,0:T(8,128)(2,1)}, u32[]{:S(2)}) copy-start(bf16[2,256,1024]{2,1,0:T(8,128)(2,1)} %get-tuple-element.20.adjoint) | copy-start | bytes 3145732
  16.5 0.8 %copy-start.2 = (f32[16,512]{1,0:T(8,128)S(1)}, f32[16,512]{1,0:T(8,128)}, u32[]{:S(2)}) copy-start(f32[16,512]{1,0:T(8,128)} %get-tuple-element.17.time_low) | copy-start | bytes 98308
  17.4 0.8 %copy-start.3 = (f32[16,512]{1,0:T(8,128)S(1)}, f32[16,512]{1,0:T(8,128)}, u32[]{:S(2)}) copy-start(f32[16,512]{1,0:T(8,128)} %get-tuple-element.18.space_low) | copy-start | bytes 98308
  18.1 7.9 %copy-start.1 = (f32[2,64,64]{2,1,0:T(8,128)S(1)}, f32[2,64,64]{2,1,0:T(8,128)}, u32[]{:S(2)}) copy-start(f32[2,64,64]{2,1,0:T(8,128)} %get-tuple-element.15.picks) | copy-start | bytes 98308
  21.5 4.5 %collective-permute-start.1 = (bf16[48,512]{1,0:T(8,128)(2,1)S(1)}, bf16[48,512]{1,0:T(8,128)(2,1)S(1)}, u32[]{:S(2)}, u32[]{:S(2)}) collective-permute-start(bf16[48,512]{1,0:T(8,128)(2,1)S(1)} %time_edge.1.early), channel_id=1, source_target_pairs={{0,1},{1,0},{2,3},{3,2},{4,5},{5,4},{6,7},{7,6},{8,9},{9,8},{10,11... | collective-permute-start | bytes 147464 | tf_op jit(solution)/shard_map/ppermute | solution.py:20
  22.2 3.8 %collective-permute-start.3 = (bf16[16,512]{1,0:T(8,128)(2,1)S(1)}, bf16[16,512]{1,0:T(8,128)(2,1)S(1)}, u32[]{:S(2)}, u32[]{:S(2)}) collective-permute-start(bf16[16,512]{1,0:T(8,128)(2,1)S(1)} %final.1.late), channel_id=1, source_target_pairs={{0,1},{1,0},{2,3},{3,2},{4,5},{5,4},{6,7},{7,6},{8,9},{9,8},{10,11... | collective-permute-start | bytes 49160 | tf_op jit(solution)/shard_map/ppermute | solution.py:20
  26.2 5.8 %collective-permute-start.4 = (bf16[16,1024]{1,0:T(8,128)(2,1)S(1)}, bf16[16,1024]{1,0:T(8,128)(2,1)S(1)}, u32[]{:S(2)}, u32[]{:S(2)}) collective-permute-start(bf16[16,1024]{1,0:T(8,128)(2,1)S(1)} %get-tuple-element.21), channel_id=1, source_target_pairs={{0,6},{1,7},{2,4},{3,5},{4,2},{5,3},{6,0},{7,1},{8,14},{9,15},{10,... | collective-permute-start | bytes 98312 | tf_op jit(solution)/shard_map/ppermute | solution.py:20
  27.6 5.2 %collective-permute-start.5 = (bf16[16,1024]{1,0:T(8,128)(2,1)S(1)}, bf16[16,1024]{1,0:T(8,128)(2,1)S(1)}, u32[]{:S(2)}, u32[]{:S(2)}) collective-permute-start(bf16[16,1024]{1,0:T(8,128)(2,1)S(1)} %get-tuple-element.22), channel_id=1, source_target_pairs={{0,4},{1,5},{2,6},{3,7},{4,0},{5,1},{6,2},{7,3},{8,12},{9,13},{10,... | collective-permute-start | bytes 98312 | tf_op jit(solution)/shard_map/ppermute | solution.py:20
  27.6 5.3 %collective-permute-start.6 = (bf16[16,1024]{1,0:T(8,128)(2,1)S(1)}, bf16[16,1024]{1,0:T(8,128)(2,1)S(1)}, u32[]{:S(2)}, u32[]{:S(2)}) collective-permute-start(bf16[16,1024]{1,0:T(8,128)(2,1)S(1)} %get-tuple-element.23), channel_id=1, source_target_pairs={{0,2},{1,3},{2,0},{3,1},{4,6},{5,7},{6,4},{7,5},{8,10},{9,11},{10,... | collective-permute-start | bytes 98312 | tf_op jit(solution)/shard_map/ppermute | solution.py:20

commit v7 on v6

--- a/solution.py
+++ b/solution.py
@@ -132,10 +132,10 @@
         copy.wait()
 
 
-def inner_kernel(place, lists, nulls, time_links, space_links, time_rows, space_rows, adjoint, picks, links, vecs, left, right, sems):
+def inner_kernel(place, lists, nulls, time_links, space_links, early, adjoint, picks, links, vecs, left, right, sems):
     time_count, space_count, sites, vectors, width = nulls.shape
     copies = []
-    base = pltpu.make_async_copy(nulls, vecs, sems.at[12])
+    base = pltpu.make_async_copy(nulls, vecs, sems.at[16])
     base.start()
 
     def fetch(source):
@@ -148,6 +148,8 @@
         fetch(time_links.at[0, x])
     for t in range(4):
         fetch(space_links.at[t, 0])
+    for x in range(4):
+        fetch(time_links.at[1, x])
     for t in range(4):
         fetch(space_links.at[t, 1])
     me = place[0]
@@ -176,74 +178,63 @@
             picks[0, rows, :] = jnp.where(here & (inside == chosen), 1.0, 0.0)
             picks[1, rows, :] = jnp.where(here & (turned == chosen), 1.0, 0.0)
     base.wait()
+    found = []
     for a_x in range(2):
         copies[2 * a_x].wait()
         copies[2 * a_x + 1].wait()
         for c in range(2):
             x = 2 * a_x + c
             image_item(links.at[x], vecs.at[1, x], vecs.at[2, x], c, left, right)
-        time_rows[pl.ds(a_x * 8, 8), :] = group_rows(left[...], right[...], MAT_DIMS, vectors)
+        found.append(group_rows(left[...], right[...], MAT_DIMS, vectors))
     for a_t in range(2):
         copies[4 + 2 * a_t].wait()
         copies[5 + 2 * a_t].wait()
         for c in range(2):
             t = 2 * a_t + c
             image_item(links.at[4 + t], vecs.at[t, 1], vecs.at[t, 2], c, left, right)
-        space_rows[pl.ds(a_t * 8, 8), :] = group_rows(left[...], right[...], MAT_DIMS, vectors)
+        found.append(group_rows(left[...], right[...], MAT_DIMS, vectors))
+    early[...] = jnp.concatenate(found, axis=0).astype(jnp.bfloat16)
+    for x in range(4):
+        copies[8 + x].wait()
+    for x in range(4):
+        adjoint_item(links.at[8 + x], vecs.at[3, x], x % 2, adjoint.at[x // 2])
     for t in range(4):
-        copies[8 + t].wait()
+        copies[12 + t].wait()
     for t in range(4):
-        adjoint_item(links.at[8 + t], vecs.at[t, 3], t % 2, adjoint.at[t // 2])
-
-
-def time_edge_kernel(nulls, edge, time_links, time_low, space_low, early, links, vecs, left, right, sems):
-    vectors = nulls.shape[-2]
-    copies = []
-    base = pltpu.make_async_copy(nulls.at[3], vecs, sems.at[4])
-    base.start()
-    for x in range(4):
-        copy = pltpu.make_async_copy(time_links.at[1, x], links.at[x], sems.at[x])
-        copy.start()
-        copies.append(copy)
-    base.wait()
+        adjoint_item(links.at[12 + t], vecs.at[t, 3], t % 2, adjoint.at[2 + t // 2])
+
+
+def edge_rows(uppers, adjoint, vectors):
+    parts = []
+    for upper in uppers:
+        sites = upper.shape[0]
+        for site in range(SIDE):
+            rows = [upper[agg * SIDE + site] for agg in range(sites // SIDE)]
+            parts.append(jnp.concatenate(rows, axis=0))
+    return group_rows(adjoint, jnp.concatenate(parts, axis=1), ROW_DIMS, vectors)
+
+
+def final_kernel(time_edge, space_edge, adjoint, late):
+    vectors = space_edge.shape[3]
     found = []
     for a_x in range(2):
-        copies[2 * a_x].wait()
-        copies[2 * a_x + 1].wait()
-        for c in range(2):
-            x = 2 * a_x + c
-            image_item(links.at[x], vecs.at[x], edge.at[0, x], c, left, right)
-        found.append(group_rows(left[...], right[...], MAT_DIMS, vectors))
-    early[...] = jnp.concatenate([time_low[...]] + found + [space_low[...]], axis=0).astype(jnp.bfloat16)
-
-
-def final_kernel(edge, adjoint, late):
-    sites, vectors, width = edge.shape[2:]
-    aggs = sites // SIDE
-    found = []
+        uppers = [time_edge.at[0, 2 * a_x + c] for c in range(2)]
+        found.append(edge_rows(uppers, adjoint[a_x], vectors))
     for a_t in range(2):
-        parts = []
-        for c in range(2):
-            for site in range(SIDE):
-                rows = [edge[2 * a_t + c, 0, agg * SIDE + site] for agg in range(aggs)]
-                parts.append(jnp.concatenate(rows, axis=0))
-        found.append(group_rows(adjoint[a_t], jnp.concatenate(parts, axis=1), ROW_DIMS, vectors))
+        uppers = [space_edge.at[2 * a_t + c, 0] for c in range(2)]
+        found.append(edge_rows(uppers, adjoint[2 + a_t], vectors))
     late[...] = jnp.concatenate(found, axis=0).astype(jnp.bfloat16)
 
 
 def pack_kernel(picks, early, early_other, late, late_other, *packed):
-    half_count = late.shape[0]
-    count = 2 * half_count
-    time_rows = jnp.concatenate([early[pl.ds(0, count), :], early_other[pl.ds(0, count), :]], axis=0)
-    space_rows = jnp.concatenate(
-        [early[pl.ds(count, half_count), :], late[...], early_other[pl.ds(count, half_count), :], late_other[...]],
-        axis=0,
-    )
-    time_sent = dot(picks[0].astype(jnp.bfloat16), time_rows, MAT_DIMS)
-    space_sent = dot(picks[1].astype(jnp.bfloat16), space_rows, MAT_DIMS)
-    for turn, out in enumerate(packed):
-        mine = slice(turn * 2 * MOST, (turn + 1) * 2 * MOST)
-        out[...] = jnp.concatenate([time_sent[mine], space_sent[mine]], axis=1).astype(jnp.bfloat16)
+    half_count = late.shape[0] // 2
+    pieces = (early, late, early_other, late_other)
+    for half, width in enumerate((late.shape[1],) * 2):
+        rows = jnp.concatenate([piece[pl.ds(half * half_count, half_count), :] for piece in pieces], axis=0)
+        sent = dot(picks[half].astype(jnp.bfloat16), rows, MAT_DIMS)
+        for turn, out in enumerate(packed):
+            mine = sent[turn * 2 * MOST : (turn + 1) * 2 * MOST]
+            out[:, pl.ds(half * width, width)] = mine.astype(jnp.bfloat16)
 
 
 def unpack_kernel(place, *refs):
@@ -266,13 +257,8 @@
     anywhere = pl.BlockSpec(memory_space=pl.ANY)
     outside = pl.BlockSpec(memory_space=pltpu.HBM)
     half = width // 2
-    roomy = pltpu.CompilerParams(vmem_limit_bytes=54 * 1024 * 1024)
-    middle = pltpu.CompilerParams(vmem_limit_bytes=52 * 1024 * 1024)
+    roomy = pltpu.CompilerParams(vmem_limit_bytes=51 * 1024 * 1024)
     modest = pltpu.CompilerParams(vmem_limit_bytes=24 * 1024 * 1024)
-    grouped = [
-        pltpu.VMEM((2 * vectors * aggs, 8 * width), jnp.bfloat16),
-        pltpu.VMEM((8 * width, vectors * aggs), jnp.bfloat16),
-    ]
     first = pltpu.CompilerParams(vmem_limit_bytes=52 * 1024 * 1024)
     space_edge, time_edge = pl.pallas_call(
         slice_kernel,
@@ -289,50 +275,35 @@
     )(nulls)
     edge_time = shifted(time_edge, "ta", -1)
     edge_space = shifted(space_edge, "xyz", -1)
-    time_low, space_low, adjoint, picks = pl.pallas_call(
+    early, adjoint, picks = pl.pallas_call(
         inner_kernel,
         in_specs=[smem, vmem, outside, outside, outside],
-        out_specs=[vmem] * 4,
+        out_specs=[vmem] * 3,
         out_shape=[
-            jax.ShapeDtypeStruct((2 * aggs, wide), jnp.float32),
-            jax.ShapeDtypeStruct((2 * aggs, wide), jnp.float32),
-            jax.ShapeDtypeStruct((2, 2 * vectors * aggs, 8 * width), jnp.bfloat16),
+            jax.ShapeDtypeStruct((4 * aggs, wide), jnp.bfloat16),
+            jax.ShapeDtypeStruct((4, 2 * vectors * aggs, 8 * width), jnp.bfloat16),
             jax.ShapeDtypeStruct((2, shards * MOST, 2 * local_count), jnp.float32),
         ],
         scratch_shapes=[
-            pltpu.VMEM((12, sites, half, width), jnp.bfloat16),
+            pltpu.VMEM((16, sites, half, width), jnp.bfloat16),
             pltpu.VMEM(nulls.shape, nulls.dtype),
-        ]
-        + grouped
-        + [pltpu.SemaphoreType.DMA((13,))],
+            pltpu.VMEM((2 * vectors * aggs, 8 * width), jnp.bfloat16),
+            pltpu.VMEM((8 * width, vectors * aggs), jnp.bfloat16),
+            pltpu.SemaphoreType.DMA((17,)),
+        ],
         compiler_params=roomy,
         cost_estimate=pl.CostEstimate(flops=1000, bytes_accessed=1000, transcendentals=0),
         name="inner",
     )(place, owner_lists, nulls, time_links, space_links)
-    early = pl.pallas_call(
-        time_edge_kernel,
-        in_specs=[outside, vmem, outside, vmem, vmem],
-        out_specs=vmem,
-        out_shape=jax.ShapeDtypeStruct((6 * aggs, wide), jnp.bfloat16),
-        scratch_shapes=[
-            pltpu.VMEM((4, sites, half, width), jnp.bfloat16),
-            pltpu.VMEM(nulls.shape[1:], nulls.dtype),
-        ]
-        + grouped
-        + [pltpu.SemaphoreType.DMA((5,))],
-        compiler_params=middle,
-        cost_estimate=pl.CostEstimate(flops=1000, bytes_accessed=1000, transcendentals=0),
-        name="time_edge",
-    )(nulls, edge_time, time_links, time_low, space_low)
     late = pl.pallas_call(
         final_kernel,
-        in_specs=[vmem] * 2,
+        in_specs=[vmem] * 3,
         out_specs=vmem,
-        out_shape=jax.ShapeDtypeStruct((2 * aggs, wide), jnp.bfloat16),
+        out_shape=jax.ShapeDtypeStruct((4 * aggs, wide), jnp.bfloat16),
         compiler_params=modest,
         cost_estimate=pl.CostEstimate(flops=1000, bytes_accessed=1000, transcendentals=0),
         name="final",
-    )(edge_space, adjoint)
+    )(edge_time, edge_space, adjoint)
     early_other = crossed(early, "xyz", 1)
     late_other = crossed(late, "xyz", 1)
     pairs = shards // 2

time: 33.8 us -> 33.8 us (level)
  waiting for transfers between devices: 3.98 us -> 10.2 us
  Pallas kernels: 14.4 us -> 10.6 us
  starting transfers between devices: 13.6 us -> 12.1 us
  local copies, waits for them, and re-layouts: 1.6 us -> 0.69 us
    ppermute x5, waiting for transfers between devices: 3.98 us -> 7.67 us  [crossed(): lax.ppermute(array, axis, [(i, i ^ bits) for i in range(lax.axis_size(axi...]
    pallas_call x2 -> x1, Pallas kernels: 3.98 us -> 0.93 us  [on_device(): pl.pallas_call(final_kernel, in_specs=[vmem] * 3, out_specs=vmem, out_sha...]
    ppermute x2, waiting for transfers between devices: 0.01 us -> 2.56 us  [shifted(): lax.ppermute(array, axis, [(i, (i + by) % count) for i in range(count)])]
    ppermute x5, starting transfers between devices: 6.57 us -> 5.07 us  [crossed(): lax.ppermute(array, axis, [(i, i ^ bits) for i in range(lax.axis_size(axi...]
    unnamed x8 -> x2, local copies, waits for them, and re-layouts: 1.6 us -> 0.69 us
    pallas_call x1, Pallas kernels: 8.28 us -> 7.58 us  [on_device(): pl.pallas_call(inner_kernel, in_specs=[smem, vmem, outside, outside, outs...]
  transfers between devices with their start and end apart: 7 -> 7, of which waited for: 4 -> 4; matrix products, arithmetic and copies ran while one was open for 0% -> 0% of each run, Pallas kernels for 36% -> 25%
where the time goes in v7:
time: 33.8 us; the launch traced here: 33.6 us
  starting transfers between devices  12.1 us (36%)
  Pallas kernels  10.6 us (31%)
  waiting for transfers between devices  10.2 us (30%)
  local copies, waits for them, and re-layouts  0.69 us (2%)
    ppermute x5, waiting for transfers between devices, crossed(): lax.ppermute(array, axis, [(i, i ^ bits) for i in range(lax.axis_size(axi...  7.67 us
    pallas_call x1, Pallas kernels, on_device(): pl.pallas_call(inner_kernel, in_specs=[smem, vmem, outside, outside, outs...  7.58 us
    ppermute x2, starting transfers between devices, shifted(): lax.ppermute(array, axis, [(i, (i + by) % count) for i in range(count)])  6.99 us
    ppermute x5, starting transfers between devices, crossed(): lax.ppermute(array, axis, [(i, i ^ bits) for i in range(lax.axis_size(axi...  5.07 us
    ppermute x2, waiting for transfers between devices, shifted(): lax.ppermute(array, axis, [(i, (i + by) % count) for i in range(count)])  2.56 us
    pallas_call x1, Pallas kernels, on_device(): pl.pallas_call(slice_kernel, in_specs=[outside], out_specs=[vmem] * 2, ou...  1.22 us
    pallas_call x1, Pallas kernels, on_device(): pl.pallas_call(final_kernel, in_specs=[vmem] * 3, out_specs=vmem, out_sha...  0.93 us
    pallas_call x1, Pallas kernels, on_device(): pl.pallas_call(unpack_kernel, in_specs=[smem] + [vmem] * pairs, out_specs...  0.73 us
  transfers between devices with their start and end apart: 7, of which 4 were waited for; matrix products, arithmetic and copies ran while one was open for 0% of the time, Pallas kernels for 25%

profile of v7, /device:TPU:0, one launch (start us, length us, event | category | flops | bytes accessed | tf_op | source)
XLA Modules:
  0.0 33.6 jit_solution(2364100546830524485)
XLA Ops:
  0.0 1.2 %slices.1 = (bf16[4,1,32,16,128]{4,3,2,1,0:T(8,128)(2,1)S(1)}, bf16[1,4,32,16,128]{4,3,2,1,0:T(8,128)(2,1)S(1)}) custom-call(bf16[4,4,32,16,128]{4,3,2,1,0:T(8,128)(2,1)} %nulls.3), custom_call_target="tpu_custom_call" | custom-call | flops 1000 | bytes 1000 | tf_op jit(solution)/shard_map/slices/pallas_call | solution.py:263
  1.2 2.4 %collective-permute-start.1 = (bf16[1,4,32,16,128]{4,3,2,1,0:T(8,128)(2,1)S(1)}, bf16[1,4,32,16,128]{4,3,2,1,0:T(8,128)(2,1)S(1)}, u32[]{:S(2)}, u32[]{:S(2)}) collective-permute-start(bf16[1,4,32,16,128]{4,3,2,1,0:T(8,128)(2,1)S(1)} %get-tuple-element.16), channel_id=1, source_target_pairs={{0,24},{8,0},{16,8},{24,16},{1,25},{9,1},{17,9},{25,17},{2,26},{10... | collective-permute-start | bytes 1572872 | tf_op jit(solution)/shard_map/ppermute | solution.py:16
  3.7 4.6 %collective-permute-start.2 = (bf16[4,1,32,16,128]{4,3,2,1,0:T(8,128)(2,1)S(1)}, bf16[4,1,32,16,128]{4,3,2,1,0:T(8,128)(2,1)S(1)}, u32[]{:S(2)}, u32[]{:S(2)}) collective-permute-start(bf16[4,1,32,16,128]{4,3,2,1,0:T(8,128)(2,1)S(1)} %get-tuple-element.17), channel_id=1, source_target_pairs={{0,7},{1,0},{2,1},{3,2},{4,3},{5,4},{6,5},{7,6},{8,15},{9,8},{10,9... | collective-permute-start | bytes 1572872 | tf_op jit(solution)/shard_map/ppermute | solution.py:16
  8.2 0.0 copy-start
  8.2 0.7 %copy-done = s32[8,64]{1,0:T(8,128)S(1)} copy-done((s32[8,64]{1,0:T(8,128)S(1)}, s32[8,64]{1,0:T(8,128)}, u32[]{:S(2)}) %copy-start) | copy-done | bytes 2072
  8.9 7.6 %inner.1 = (bf16[32,512]{1,0:T(8,128)(2,1)S(1)}, bf16[4,256,1024]{2,1,0:T(8,128)(2,1)S(1)}, f32[2,64,64]{2,1,0:T(8,128)S(1)}) custom-call(s32[1]{0:T(128)} %bitcast.place, s32[8,64]{1,0:T(8,128)S(1)} %copy-done, bf16[4,4,32,16,128]{4,3,2,1,0:T(8,128)(2,1)} %nulls.3, bf16[2,4,32,64,128]{4,3,2,1,0:T(8,128)(2,1)} %time_links.1, ...), custom_call_target="tpu_custom_call" | custom-call | flops 1000 | bytes 1000 | tf_op jit(solution)/shard_map/inner/pallas_call | solution.py:278
  16.5 0.1 collective-permute-start
  16.6 0.0 collective-permute-done.1.time_edge
  16.6 2.6 %collective-permute-done.2.space_edge = bf16[4,1,32,16,128]{4,3,2,1,0:T(8,128)(2,1)S(1)} collective-permute-done((bf16[4,1,32,16,128]{4,3,2,1,0:T(8,128)(2,1)S(1)}, bf16[4,1,32,16,128]{4,3,2,1,0:T(8,128)(2,1)S(1)}, u32[]{:S(2)}, u32[]{:S(2)}) %collective-permute-start.2) | collective-permute-done | bytes 524320 | tf_op jit(solution)/shard_map/ppermute | solution.py:16
  19.1 0.9 %final.1.late = bf16[32,512]{1,0:T(8,128)(2,1)S(1)} custom-call(bf16[1,4,32,16,128]{4,3,2,1,0:T(8,128)(2,1)S(1)} %collective-permute-done.1.time_edge, bf16[4,1,32,16,128]{4,3,2,1,0:T(8,128)(2,1)S(1)} %collective-permute-done.2.space_edge, bf16[4,256,1024]{2,1,0:T(8,128)(2,1)S(1)} %get-tuple-element.18.adjoint), custom_call_target="tpu_custom_call" | custom-call | flops 1000 | bytes 1000 | tf_op jit(solution)/shard_map/final/pallas_call | solution.py:298
  20.1 0.5 %collective-permute-start.3 = (bf16[32,512]{1,0:T(8,128)(2,1)S(1)}, bf16[32,512]{1,0:T(8,128)(2,1)S(1)}, u32[]{:S(2)}, u32[]{:S(2)}) collective-permute-start(bf16[32,512]{1,0:T(8,128)(2,1)S(1)} %final.1.late), channel_id=1, source_target_pairs={{0,1},{1,0},{2,3},{3,2},{4,5},{5,4},{6,7},{7,6},{8,9},{9,8},{10,11... | collective-permute-start | bytes 98312 | tf_op jit(solution)/shard_map/ppermute | solution.py:20
  20.5 0.0 collective-permute-done.early_other
  20.5 3.5 %collective-permute-done.3.late_other = bf16[32,512]{1,0:T(8,128)(2,1)S(1)} collective-permute-done((bf16[32,512]{1,0:T(8,128)(2,1)S(1)}, bf16[32,512]{1,0:T(8,128)(2,1)S(1)}, u32[]{:S(2)}, u32[]{:S(2)}) %collective-permute-start.3) | collective-permute-done | bytes 32800 | tf_op jit(solution)/shard_map/ppermute | solution.py:20
  24.0 0.2 pack.1
  24.2 3.9 %collective-permute-start.4 = (bf16[16,1024]{1,0:T(8,128)(2,1)S(1)}, bf16[16,1024]{1,0:T(8,128)(2,1)S(1)}, u32[]{:S(2)}, u32[]{:S(2)}) collective-permute-start(bf16[16,1024]{1,0:T(8,128)(2,1)S(1)} %get-tuple-element.19), channel_id=1, source_target_pairs={{0,6},{1,7},{2,4},{3,5},{4,2},{5,3},{6,0},{7,1},{8,14},{9,15},{10,... | collective-permute-start | bytes 98312 | tf_op jit(solution)/shard_map/ppermute | solution.py:20
  28.1 0.0 collective-permute-start.5
  28.1 0.6 %collective-permute-start.6 = (bf16[16,1024]{1,0:T(8,128)(2,1)S(1)}, bf16[16,1024]{1,0:T(8,128)(2,1)S(1)}, u32[]{:S(2)}, u32[]{:S(2)}) collective-permute-start(bf16[16,1024]{1,0:T(8,128)(2,1)S(1)} %get-tuple-element.21), channel_id=1, source_target_pairs={{0,2},{1,3},{2,0},{3,1},{4,6},{5,7},{6,4},{7,5},{8,10},{9,11},{10,... | collective-permute-start | bytes 98312 | tf_op jit(solution)/shard_map/ppermute | solution.py:20
  28.7 1.3 %collective-permute-done.4.refs_0_ = bf16[16,1024]{1,0:T(8,128)(2,1)S(1)} collective-permute-done((bf16[16,1024]{1,0:T(8,128)(2,1)S(1)}, bf16[16,1024]{1,0:T(8,128)(2,1)S(1)}, u32[]{:S(2)}, u32[]{:S(2)}) %collective-permute-start.4) | collective-permute-done | bytes 32800 | tf_op jit(solution)/shard_map/ppermute | solution.py:20
  30.0 2.9 %collective-permute-done.5.refs_1_ = bf16[16,1024]{1,0:T(8,128)(2,1)S(1)} collective-permute-done((bf16[16,1024]{1,0:T(8,128)(2,1)S(1)}, bf16[16,1024]{1,0:T(8,128)(2,1)S(1)}, u32[]{:S(2)}, u32[]{:S(2)}) %collective-permute-start.5) | collective-permute-done | bytes 32800 | tf_op jit(solution)/shard_map/ppermute | solution.py:20
  32.9 0.0 collective-permute-done.6.refs_2_
  32.9 0.7 %unpack.1 = f32[64,1024]{1,0:T(8,128)} custom-call(s32[1]{0:T(128)} %bitcast.place, bf16[16,1024]{1,0:T(8,128)(2,1)S(1)} %collective-permute-done.4.refs_0_, bf16[16,1024]{1,0:T(8,128)(2,1)S(1)} %collective-permute-done.5.refs_1_, bf16[16,1024]{1,0:T(8,128)(2,1)S(1)} %collective-permute-done.6.refs_2_, bf16[16,1024]{1,0:T(8,128)(2,1)S(1)} %get-tuple-element.22.refs_3_), custom_call_target="tpu_custom_call" | custom-call | flops 1000 | bytes 1000 | tf_op jit(solution)/shard_map/unpack/pallas_call | solution.py:321
Async XLA Ops:
  1.2 15.3 %collective-permute-start.1 = (bf16[1,4,32,16,128]{4,3,2,1,0:T(8,128)(2,1)S(1)}, bf16[1,4,32,16,128]{4,3,2,1,0:T(8,128)(2,1)S(1)}, u32[]{:S(2)}, u32[]{:S(2)}) collective-permute-start(bf16[1,4,32,16,128]{4,3,2,1,0:T(8,128)(2,1)S(1)} %get-tuple-element.16), channel_id=1, source_target_pairs={{0,24},{8,0},{16,8},{24,16},{1,25},{9,1},{17,9},{25,17},{2,26},{10... | collective-permute-start | bytes 1572872 | tf_op jit(solution)/shard_map/ppermute | solution.py:16
  3.7 15.5 %collective-permute-start.2 = (bf16[4,1,32,16,128]{4,3,2,1,0:T(8,128)(2,1)S(1)}, bf16[4,1,32,16,128]{4,3,2,1,0:T(8,128)(2,1)S(1)}, u32[]{:S(2)}, u32[]{:S(2)}) collective-permute-start(bf16[4,1,32,16,128]{4,3,2,1,0:T(8,128)(2,1)S(1)} %get-tuple-element.17), channel_id=1, source_target_pairs={{0,7},{1,0},{2,1},{3,2},{4,3},{5,4},{6,5},{7,6},{8,15},{9,8},{10,9... | collective-permute-start | bytes 1572872 | tf_op jit(solution)/shard_map/ppermute | solution.py:16
  8.2 0.7 %copy-start = (s32[8,64]{1,0:T(8,128)S(1)}, s32[8,64]{1,0:T(8,128)}, u32[]{:S(2)}) copy-start(s32[8,64]{1,0:T(8,128)} %lists.1) | copy-start | bytes 6148
  16.5 4.1 %collective-permute-start = (bf16[32,512]{1,0:T(8,128)(2,1)S(1)}, bf16[32,512]{1,0:T(8,128)(2,1)S(1)}, u32[]{:S(2)}, u32[]{:S(2)}) collective-permute-start(bf16[32,512]{1,0:T(8,128)(2,1)S(1)} %get-tuple-element.15.early), channel_id=1, source_target_pairs={{0,1},{1,0},{2,3},{3,2},{4,5},{5,4},{6,7},{7,6},{8,9},{9,8},{10,11... | collective-permute-start | bytes 98312 | tf_op jit(solution)/shard_map/ppermute | solution.py:20
  20.1 4.0 %collective-permute-start.3 = (bf16[32,512]{1,0:T(8,128)(2,1)S(1)}, bf16[32,512]{1,0:T(8,128)(2,1)S(1)}, u32[]{:S(2)}, u32[]{:S(2)}) collective-permute-start(bf16[32,512]{1,0:T(8,128)(2,1)S(1)} %final.1.late), channel_id=1, source_target_pairs={{0,1},{1,0},{2,3},{3,2},{4,5},{5,4},{6,7},{7,6},{8,9},{9,8},{10,11... | collective-permute-start | bytes 98312 | tf_op jit(solution)/shard_map/ppermute | solution.py:20
  24.2 5.8 %collective-permute-start.4 = (bf16[16,1024]{1,0:T(8,128)(2,1)S(1)}, bf16[16,1024]{1,0:T(8,128)(2,1)S(1)}, u32[]{:S(2)}, u32[]{:S(2)}) collective-permute-start(bf16[16,1024]{1,0:T(8,128)(2,1)S(1)} %get-tuple-element.19), channel_id=1, source_target_pairs={{0,6},{1,7},{2,4},{3,5},{4,2},{5,3},{6,0},{7,1},{8,14},{9,15},{10,... | collective-permute-start | bytes 98312 | tf_op jit(solution)/shard_map/ppermute | solution.py:20
  28.1 4.8 %collective-permute-start.5 = (bf16[16,1024]{1,0:T(8,128)(2,1)S(1)}, bf16[16,1024]{1,0:T(8,128)(2,1)S(1)}, u32[]{:S(2)}, u32[]{:S(2)}) collective-permute-start(bf16[16,1024]{1,0:T(8,128)(2,1)S(1)} %get-tuple-element.20), channel_id=1, source_target_pairs={{0,4},{1,5},{2,6},{3,7},{4,0},{5,1},{6,2},{7,3},{8,12},{9,13},{10,... | collective-permute-start | bytes 98312 | tf_op jit(solution)/shard_map/ppermute | solution.py:20
  28.1 4.8 %collective-permute-start.6 = (bf16[16,1024]{1,0:T(8,128)(2,1)S(1)}, bf16[16,1024]{1,0:T(8,128)(2,1)S(1)}, u32[]{:S(2)}, u32[]{:S(2)}) collective-permute-start(bf16[16,1024]{1,0:T(8,128)(2,1)S(1)} %get-tuple-element.21), channel_id=1, source_target_pairs={{0,2},{1,3},{2,0},{3,1},{4,6},{5,7},{6,4},{7,5},{8,10},{9,11},{10,... | collective-permute-start | bytes 98312 | tf_op jit(solution)/shard_map/ppermute | solution.py:20

commit v8 on v7

--- a/solution.py
+++ b/solution.py
@@ -121,15 +121,16 @@
     return jnp.concatenate(pieces, axis=1)
 
 
-def slice_kernel(nulls, space_edge, time_edge, sems):
-    copies = [
-        pltpu.make_async_copy(nulls.at[:, pl.ds(0, 1)], space_edge, sems.at[0]),
-        pltpu.make_async_copy(nulls.at[pl.ds(0, 1)], time_edge, sems.at[1]),
-    ]
-    for copy in copies:
-        copy.start()
-    for copy in copies:
-        copy.wait()
+def space_slice_kernel(nulls, edge, sem):
+    copy = pltpu.make_async_copy(nulls.at[:, pl.ds(0, 1)], edge, sem)
+    copy.start()
+    copy.wait()
+
+
+def time_slice_kernel(nulls, edge, sem):
+    copy = pltpu.make_async_copy(nulls.at[pl.ds(0, 1)], edge, sem)
+    copy.start()
+    copy.wait()
 
 
 def inner_kernel(place, lists, nulls, time_links, space_links, early, adjoint, picks, links, vecs, left, right, sems):
@@ -214,7 +215,7 @@
     return group_rows(adjoint, jnp.concatenate(parts, axis=1), ROW_DIMS, vectors)
 
 
-def final_kernel(time_edge, space_edge, adjoint, late):
+def final_kernel(space_edge, time_edge, adjoint, late):
     vectors = space_edge.shape[3]
     found = []
     for a_x in range(2):
@@ -260,18 +261,25 @@
     roomy = pltpu.CompilerParams(vmem_limit_bytes=51 * 1024 * 1024)
     modest = pltpu.CompilerParams(vmem_limit_bytes=24 * 1024 * 1024)
     first = pltpu.CompilerParams(vmem_limit_bytes=52 * 1024 * 1024)
-    space_edge, time_edge = pl.pallas_call(
-        slice_kernel,
+    space_edge = pl.pallas_call(
+        space_slice_kernel,
         in_specs=[outside],
-        out_specs=[vmem] * 2,
-        out_shape=[
-            jax.ShapeDtypeStruct((time_count, 1, sites, vectors, width), nulls.dtype),
-            jax.ShapeDtypeStruct((1, space_count, sites, vectors, width), nulls.dtype),
-        ],
-        scratch_shapes=[pltpu.SemaphoreType.DMA((2,))],
+        out_specs=vmem,
+        out_shape=jax.ShapeDtypeStruct((time_count, 1, sites, vectors, width), nulls.dtype),
+        scratch_shapes=[pltpu.SemaphoreType.DMA],
         compiler_params=first,
         cost_estimate=pl.CostEstimate(flops=1000, bytes_accessed=1000, transcendentals=0),
-        name="slices",
+        name="space_slice",
+    )(nulls)
+    time_edge = pl.pallas_call(
+        time_slice_kernel,
+        in_specs=[outside],
+        out_specs=vmem,
+        out_shape=jax.ShapeDtypeStruct((1, space_count, sites, vectors, width), nulls.dtype),
+        scratch_shapes=[pltpu.SemaphoreType.DMA],
+        compiler_params=first,
+        cost_estimate=pl.CostEstimate(flops=1000, bytes_accessed=1000, transcendentals=0),
+        name="time_slice",
     )(nulls)
     edge_time = shifted(time_edge, "ta", -1)
     edge_space = shifted(space_edge, "xyz", -1)
@@ -303,7 +311,7 @@
         compiler_params=modest,
         cost_estimate=pl.CostEstimate(flops=1000, bytes_accessed=1000, transcendentals=0),
         name="final",
-    )(edge_time, edge_space, adjoint)
+    )(edge_space, edge_time, adjoint)
     early_other = crossed(early, "xyz", 1)
     late_other = crossed(late, "xyz", 1)
     pairs = shards // 2

time: 33.8 us -> 33 us (0.976)
  Pallas kernels: 10.6 us -> 11.5 us
  waiting for transfers between devices: 10.2 us -> 9.49 us
  local copies, waits for them, and re-layouts: 0.69 us -> 0.01 us
    pallas_call x1 -> x2, Pallas kernels: 1.22 us -> 2.11 us  [the longest x1 1.06 us: on_device(): pl.pallas_call(space_slice_kernel, in_specs=[outside], out_specs=vmem, ou...]
    ppermute x2, waiting for transfers between devices: 2.56 us -> 1.75 us  [shifted(): lax.ppermute(array, axis, [(i, (i + by) % count) for i in range(count)])]
    unnamed x2, local copies, waits for them, and re-layouts: 0.69 us -> 0.01 us
  transfers between devices with their start and end apart: 7 -> 7, of which waited for: 4 -> 5; matrix products, arithmetic and copies ran while one was open for 0% -> 0% of each run, Pallas kernels for 25% -> 29%
where the time goes in v8:
time: 33 us; the launch traced here: 32.8 us
  starting transfers between devices  11.8 us (36%)
  Pallas kernels  11.5 us (35%)
  waiting for transfers between devices  9.49 us (29%)
    ppermute x5, waiting for transfers between devices, crossed(): lax.ppermute(array, axis, [(i, i ^ bits) for i in range(lax.axis_size(axi...  7.74 us
    pallas_call x1, Pallas kernels, on_device(): pl.pallas_call(inner_kernel, in_specs=[smem, vmem, outside, outside, outs...  7.59 us
    ppermute x2, starting transfers between devices, shifted(): lax.ppermute(array, axis, [(i, (i + by) % count) for i in range(count)])  6.76 us
    ppermute x5, starting transfers between devices, crossed(): lax.ppermute(array, axis, [(i, i ^ bits) for i in range(lax.axis_size(axi...  5 us
    ppermute x2, waiting for transfers between devices, shifted(): lax.ppermute(array, axis, [(i, (i + by) % count) for i in range(count)])  1.75 us
    pallas_call x1, Pallas kernels, on_device(): pl.pallas_call(space_slice_kernel, in_specs=[outside], out_specs=vmem, ou...  1.06 us
    pallas_call x1, Pallas kernels, on_device(): pl.pallas_call(time_slice_kernel, in_specs=[outside], out_specs=vmem, out...  1.05 us
    pallas_call x1, Pallas kernels, on_device(): pl.pallas_call(final_kernel, in_specs=[vmem] * 3, out_specs=vmem, out_sha...  0.93 us
  transfers between devices with their start and end apart: 7, of which 5 were waited for; matrix products, arithmetic and copies ran while one was open for 0% of the time, Pallas kernels for 29%

profile of v8, /device:TPU:0, one launch (start us, length us, event | category | flops | bytes accessed | tf_op | source)
XLA Modules:
  0.0 32.8 jit_solution(6216956136752313037)
XLA Ops:
  0.0 0.0 copy-start
  0.0 1.1 %space_slice.1 = bf16[4,1,32,16,128]{4,3,2,1,0:T(8,128)(2,1)S(1)} custom-call(bf16[4,4,32,16,128]{4,3,2,1,0:T(8,128)(2,1)} %nulls.5), custom_call_target="tpu_custom_call" | custom-call | flops 1000 | bytes 1000 | tf_op jit(solution)/shard_map/space_slice/pallas_call | solution.py:264
  1.1 6.1 %collective-permute-start.1 = (bf16[4,1,32,16,128]{4,3,2,1,0:T(8,128)(2,1)S(1)}, bf16[4,1,32,16,128]{4,3,2,1,0:T(8,128)(2,1)S(1)}, u32[]{:S(2)}, u32[]{:S(2)}) collective-permute-start(bf16[4,1,32,16,128]{4,3,2,1,0:T(8,128)(2,1)S(1)} %space_slice.1), channel_id=1, source_target_pairs={{0,7},{1,0},{2,1},{3,2},{4,3},{5,4},{6,5},{7,6},{8,15},{9,8},{10,9... | collective-permute-start | bytes 1572872 | tf_op jit(solution)/shard_map/ppermute | solution.py:16
  7.1 1.0 %time_slice.1 = bf16[1,4,32,16,128]{4,3,2,1,0:T(8,128)(2,1)S(1)} custom-call(bf16[4,4,32,16,128]{4,3,2,1,0:T(8,128)(2,1)} %nulls.5), custom_call_target="tpu_custom_call" | custom-call | flops 1000 | bytes 1000 | tf_op jit(solution)/shard_map/time_slice/pallas_call | solution.py:274
  8.2 0.7 %collective-permute-start.2 = (bf16[1,4,32,16,128]{4,3,2,1,0:T(8,128)(2,1)S(1)}, bf16[1,4,32,16,128]{4,3,2,1,0:T(8,128)(2,1)S(1)}, u32[]{:S(2)}, u32[]{:S(2)}) collective-permute-start(bf16[1,4,32,16,128]{4,3,2,1,0:T(8,128)(2,1)S(1)} %time_slice.1), channel_id=1, source_target_pairs={{0,24},{8,0},{16,8},{24,16},{1,25},{9,1},{17,9},{25,17},{2,26},{10... | collective-permute-start | bytes 1572872 | tf_op jit(solution)/shard_map/ppermute | solution.py:16
  8.9 0.0 copy-done
  8.9 7.6 %inner.1 = (bf16[32,512]{1,0:T(8,128)(2,1)S(1)}, bf16[4,256,1024]{2,1,0:T(8,128)(2,1)S(1)}, f32[2,64,64]{2,1,0:T(8,128)S(1)}) custom-call(s32[1]{0:T(128)} %bitcast.place, s32[8,64]{1,0:T(8,128)S(1)} %copy-done, bf16[4,4,32,16,128]{4,3,2,1,0:T(8,128)(2,1)} %nulls.5, bf16[2,4,32,64,128]{4,3,2,1,0:T(8,128)(2,1)} %time_links.1, ...), custom_call_target="tpu_custom_call" | custom-call | flops 1000 | bytes 1000 | tf_op jit(solution)/shard_map/inner/pallas_call | solution.py:286
  16.5 0.1 collective-permute-start
  16.6 1.7 %collective-permute-done.1.space_edge = bf16[4,1,32,16,128]{4,3,2,1,0:T(8,128)(2,1)S(1)} collective-permute-done((bf16[4,1,32,16,128]{4,3,2,1,0:T(8,128)(2,1)S(1)}, bf16[4,1,32,16,128]{4,3,2,1,0:T(8,128)(2,1)S(1)}, u32[]{:S(2)}, u32[]{:S(2)}) %collective-permute-start.1) | collective-permute-done | bytes 524320 | tf_op jit(solution)/shard_map/ppermute | solution.py:16
  18.3 0.0 collective-permute-done.2.time_edge
  18.3 0.9 %final.1.late = bf16[32,512]{1,0:T(8,128)(2,1)S(1)} custom-call(bf16[4,1,32,16,128]{4,3,2,1,0:T(8,128)(2,1)S(1)} %collective-permute-done.1.space_edge, bf16[1,4,32,16,128]{4,3,2,1,0:T(8,128)(2,1)S(1)} %collective-permute-done.2.time_edge, bf16[4,256,1024]{2,1,0:T(8,128)(2,1)S(1)} %get-tuple-element.14.adjoint), custom_call_target="tpu_custom_call" | custom-call | flops 1000 | bytes 1000 | tf_op jit(solution)/shard_map/final/pallas_call | solution.py:306
  19.3 0.4 %collective-permute-start.3 = (bf16[32,512]{1,0:T(8,128)(2,1)S(1)}, bf16[32,512]{1,0:T(8,128)(2,1)S(1)}, u32[]{:S(2)}, u32[]{:S(2)}) collective-permute-start(bf16[32,512]{1,0:T(8,128)(2,1)S(1)} %final.1.late), channel_id=1, source_target_pairs={{0,1},{1,0},{2,3},{3,2},{4,5},{5,4},{6,7},{7,6},{8,9},{9,8},{10,11... | collective-permute-start | bytes 98312 | tf_op jit(solution)/shard_map/ppermute | solution.py:20
  19.6 0.8 %collective-permute-done.early_other = bf16[32,512]{1,0:T(8,128)(2,1)S(1)} collective-permute-done((bf16[32,512]{1,0:T(8,128)(2,1)S(1)}, bf16[32,512]{1,0:T(8,128)(2,1)S(1)}, u32[]{:S(2)}, u32[]{:S(2)}) %collective-permute-start) | collective-permute-done | bytes 32800 | tf_op jit(solution)/shard_map/ppermute | solution.py:20
  20.5 2.7 %collective-permute-done.3.late_other = bf16[32,512]{1,0:T(8,128)(2,1)S(1)} collective-permute-done((bf16[32,512]{1,0:T(8,128)(2,1)S(1)}, bf16[32,512]{1,0:T(8,128)(2,1)S(1)}, u32[]{:S(2)}, u32[]{:S(2)}) %collective-permute-start.3) | collective-permute-done | bytes 32800 | tf_op jit(solution)/shard_map/ppermute | solution.py:20
  23.2 0.2 pack.1
  23.4 3.9 %collective-permute-start.4 = (bf16[16,1024]{1,0:T(8,128)(2,1)S(1)}, bf16[16,1024]{1,0:T(8,128)(2,1)S(1)}, u32[]{:S(2)}, u32[]{:S(2)}) collective-permute-start(bf16[16,1024]{1,0:T(8,128)(2,1)S(1)} %get-tuple-element.15), channel_id=1, source_target_pairs={{0,6},{1,7},{2,4},{3,5},{4,2},{5,3},{6,0},{7,1},{8,14},{9,15},{10,... | collective-permute-start | bytes 98312 | tf_op jit(solution)/shard_map/ppermute | solution.py:20
  27.3 0.0 collective-permute-start.5
  27.3 0.6 %collective-permute-start.6 = (bf16[16,1024]{1,0:T(8,128)(2,1)S(1)}, bf16[16,1024]{1,0:T(8,128)(2,1)S(1)}, u32[]{:S(2)}, u32[]{:S(2)}) collective-permute-start(bf16[16,1024]{1,0:T(8,128)(2,1)S(1)} %get-tuple-element.17), channel_id=1, source_target_pairs={{0,2},{1,3},{2,0},{3,1},{4,6},{5,7},{6,4},{7,5},{8,10},{9,11},{10,... | collective-permute-start | bytes 98312 | tf_op jit(solution)/shard_map/ppermute | solution.py:20
  27.9 1.3 %collective-permute-done.4.refs_0_ = bf16[16,1024]{1,0:T(8,128)(2,1)S(1)} collective-permute-done((bf16[16,1024]{1,0:T(8,128)(2,1)S(1)}, bf16[16,1024]{1,0:T(8,128)(2,1)S(1)}, u32[]{:S(2)}, u32[]{:S(2)}) %collective-permute-start.4) | collective-permute-done | bytes 32800 | tf_op jit(solution)/shard_map/ppermute | solution.py:20
  29.2 2.9 %collective-permute-done.5.refs_1_ = bf16[16,1024]{1,0:T(8,128)(2,1)S(1)} collective-permute-done((bf16[16,1024]{1,0:T(8,128)(2,1)S(1)}, bf16[16,1024]{1,0:T(8,128)(2,1)S(1)}, u32[]{:S(2)}, u32[]{:S(2)}) %collective-permute-start.5) | collective-permute-done | bytes 32800 | tf_op jit(solution)/shard_map/ppermute | solution.py:20
  32.1 0.0 collective-permute-done.6.refs_2_
  32.1 0.7 %unpack.1 = f32[64,1024]{1,0:T(8,128)} custom-call(s32[1]{0:T(128)} %bitcast.place, bf16[16,1024]{1,0:T(8,128)(2,1)S(1)} %collective-permute-done.4.refs_0_, bf16[16,1024]{1,0:T(8,128)(2,1)S(1)} %collective-permute-done.5.refs_1_, bf16[16,1024]{1,0:T(8,128)(2,1)S(1)} %collective-permute-done.6.refs_2_, bf16[16,1024]{1,0:T(8,128)(2,1)S(1)} %get-tuple-element.18.refs_3_), custom_call_target="tpu_custom_call" | custom-call | flops 1000 | bytes 1000 | tf_op jit(solution)/shard_map/unpack/pallas_call | solution.py:329
Async XLA Ops:
  0.0 8.9 %copy-start = (s32[8,64]{1,0:T(8,128)S(1)}, s32[8,64]{1,0:T(8,128)}, u32[]{:S(2)}) copy-start(s32[8,64]{1,0:T(8,128)} %lists.1) | copy-start | bytes 6148
  1.1 17.2 %collective-permute-start.1 = (bf16[4,1,32,16,128]{4,3,2,1,0:T(8,128)(2,1)S(1)}, bf16[4,1,32,16,128]{4,3,2,1,0:T(8,128)(2,1)S(1)}, u32[]{:S(2)}, u32[]{:S(2)}) collective-permute-start(bf16[4,1,32,16,128]{4,3,2,1,0:T(8,128)(2,1)S(1)} %space_slice.1), channel_id=1, source_target_pairs={{0,7},{1,0},{2,1},{3,2},{4,3},{5,4},{6,5},{7,6},{8,15},{9,8},{10,9... | collective-permute-start | bytes 1572872 | tf_op jit(solution)/shard_map/ppermute | solution.py:16
  8.2 10.1 %collective-permute-start.2 = (bf16[1,4,32,16,128]{4,3,2,1,0:T(8,128)(2,1)S(1)}, bf16[1,4,32,16,128]{4,3,2,1,0:T(8,128)(2,1)S(1)}, u32[]{:S(2)}, u32[]{:S(2)}) collective-permute-start(bf16[1,4,32,16,128]{4,3,2,1,0:T(8,128)(2,1)S(1)} %time_slice.1), channel_id=1, source_target_pairs={{0,24},{8,0},{16,8},{24,16},{1,25},{9,1},{17,9},{25,17},{2,26},{10... | collective-permute-start | bytes 1572872 | tf_op jit(solution)/shard_map/ppermute | solution.py:16
  16.5 4.0 %collective-permute-start = (bf16[32,512]{1,0:T(8,128)(2,1)S(1)}, bf16[32,512]{1,0:T(8,128)(2,1)S(1)}, u32[]{:S(2)}, u32[]{:S(2)}) collective-permute-start(bf16[32,512]{1,0:T(8,128)(2,1)S(1)} %get-tuple-element.13.early), channel_id=1, source_target_pairs={{0,1},{1,0},{2,3},{3,2},{4,5},{5,4},{6,7},{7,6},{8,9},{9,8},{10,11... | collective-permute-start | bytes 98312 | tf_op jit(solution)/shard_map/ppermute | solution.py:20
  19.3 4.0 %collective-permute-start.3 = (bf16[32,512]{1,0:T(8,128)(2,1)S(1)}, bf16[32,512]{1,0:T(8,128)(2,1)S(1)}, u32[]{:S(2)}, u32[]{:S(2)}) collective-permute-start(bf16[32,512]{1,0:T(8,128)(2,1)S(1)} %final.1.late), channel_id=1, source_target_pairs={{0,1},{1,0},{2,3},{3,2},{4,5},{5,4},{6,7},{7,6},{8,9},{9,8},{10,11... | collective-permute-start | bytes 98312 | tf_op jit(solution)/shard_map/ppermute | solution.py:20
  23.4 5.8 %collective-permute-start.4 = (bf16[16,1024]{1,0:T(8,128)(2,1)S(1)}, bf16[16,1024]{1,0:T(8,128)(2,1)S(1)}, u32[]{:S(2)}, u32[]{:S(2)}) collective-permute-start(bf16[16,1024]{1,0:T(8,128)(2,1)S(1)} %get-tuple-element.15), channel_id=1, source_target_pairs={{0,6},{1,7},{2,4},{3,5},{4,2},{5,3},{6,0},{7,1},{8,14},{9,15},{10,... | collective-permute-start | bytes 98312 | tf_op jit(solution)/shard_map/ppermute | solution.py:20
  27.3 4.8 %collective-permute-start.5 = (bf16[16,1024]{1,0:T(8,128)(2,1)S(1)}, bf16[16,1024]{1,0:T(8,128)(2,1)S(1)}, u32[]{:S(2)}, u32[]{:S(2)}) collective-permute-start(bf16[16,1024]{1,0:T(8,128)(2,1)S(1)} %get-tuple-element.16), channel_id=1, source_target_pairs={{0,4},{1,5},{2,6},{3,7},{4,0},{5,1},{6,2},{7,3},{8,12},{9,13},{10,... | collective-permute-start | bytes 98312 | tf_op jit(solution)/shard_map/ppermute | solution.py:20
  27.3 4.8 %collective-permute-start.6 = (bf16[16,1024]{1,0:T(8,128)(2,1)S(1)}, bf16[16,1024]{1,0:T(8,128)(2,1)S(1)}, u32[]{:S(2)}, u32[]{:S(2)}) collective-permute-start(bf16[16,1024]{1,0:T(8,128)(2,1)S(1)} %get-tuple-element.17), channel_id=1, source_target_pairs={{0,2},{1,3},{2,0},{3,1},{4,6},{5,7},{6,4},{7,5},{8,10},{9,11},{10,... | collective-permute-start | bytes 98312 | tf_op jit(solution)/shard_map/ppermute | solution.py:20

commit v9 on v8

--- a/solution.py
+++ b/solution.py
@@ -18,6 +18,36 @@
 
 def crossed(array, axis, bits):
     return lax.ppermute(array, axis, [(i, i ^ bits) for i in range(lax.axis_size(axis))])
+
+
+def pair_turns(pair, pairs):
+    last = pairs - 1
+    turns = [(pair, pair)]
+    for step in range(1, last):
+        inside = pair < last
+        turns.append(
+            (
+                jnp.where(inside, lax.rem(pair + step, last), pair),
+                jnp.where(inside, lax.rem(pair + last - step, last), pair),
+            )
+        )
+    for other in range(last):
+        partner = jnp.where(pair == last, other, jnp.where(pair == other, last, pair))
+        turns.append((partner, partner))
+    return turns
+
+
+def delivered(packed, axis):
+    shards = lax.axis_size(axis)
+    last = shards // 2 - 1
+    arrived = []
+    for step in range(1, last):
+        moves = [(2 * i + side, 2 * ((i + step) % last) + side) for i in range(last) for side in range(2)]
+        arrived.append(lax.ppermute(packed[step], axis, moves))
+    for other in range(last):
+        moves = [(2 * i + side, 2 * j + side) for i, j in ((other, last), (last, other)) for side in range(2)]
+        arrived.append(lax.ppermute(packed[last + other], axis, moves))
+    return arrived + [packed[0]]
 
 
 def dot(left, right, dims):
@@ -164,8 +194,8 @@
     turned = (inside // quarter % 2) * 2 * quarter + (inside // (2 * quarter)) * quarter + inside % quarter
     own_column = column < count
     side = lax.rem(me, 2)
-    for turn in range(shards // 2):
-        owner = 2 * jnp.bitwise_xor(me // 2, turn) + side
+    for turn, (target, _) in enumerate(pair_turns(me // 2, shards // 2)):
+        owner = 2 * target + side
         mine = jnp.broadcast_to(lists[pl.ds(owner, 1), :], (MOST, cap))
         for parity in range(2):
             source = me - side + parity
@@ -239,11 +269,12 @@
 
 
 def unpack_kernel(place, *refs):
-    pair = place[0] // 2
     result = refs[-1]
-    for turn, arrived in enumerate(refs[-2::-1]):
-        source = jnp.bitwise_xor(pair, turn)
-        result[pl.ds(pl.multiple_of(source * 2 * MOST, 2 * MOST), 2 * MOST), :] = arrived[...].astype(jnp.float32)
+    pairs = result.shape[0] // (2 * MOST)
+    turns = pair_turns(place[0] // 2, pairs)
+    for arrived, (_, source) in zip(refs[:-1], turns[1:] + turns[:1]):
+        rows = pl.ds(pl.multiple_of(source * 2 * MOST, 2 * MOST), 2 * MOST)
+        result[rows, :] = arrived[...].astype(jnp.float32)
 
 
 def on_device(nulls, time_links, space_links, owner_lists):
@@ -252,6 +283,7 @@
     aggs = sites // SIDE
     local_count = (time_count // 2) * (space_count // 2) * aggs
     wide = 2 * vectors * vectors
+    turns = shards - 2
     place = lax.axis_index("xyz").astype(jnp.int32).reshape(1)
     vmem = pl.BlockSpec(memory_space=pltpu.VMEM)
     smem = pl.BlockSpec(memory_space=pltpu.SMEM)
@@ -290,7 +322,7 @@
         out_shape=[
             jax.ShapeDtypeStruct((4 * aggs, wide), jnp.bfloat16),
             jax.ShapeDtypeStruct((4, 2 * vectors * aggs, 8 * width), jnp.bfloat16),
-            jax.ShapeDtypeStruct((2, shards * MOST, 2 * local_count), jnp.float32),
+            jax.ShapeDtypeStruct((2, turns * 2 * MOST, 2 * local_count), jnp.float32),
         ],
         scratch_shapes=[
             pltpu.VMEM((16, sites, half, width), jnp.bfloat16),
@@ -314,21 +346,19 @@
     )(edge_space, edge_time, adjoint)
     early_other = crossed(early, "xyz", 1)
     late_other = crossed(late, "xyz", 1)
-    pairs = shards // 2
     packed = pl.pallas_call(
         pack_kernel,
         in_specs=[vmem] * 5,
-        out_specs=[vmem] * pairs,
-        out_shape=[jax.ShapeDtypeStruct((2 * MOST, 2 * wide), jnp.bfloat16)] * pairs,
+        out_specs=[vmem] * turns,
+        out_shape=[jax.ShapeDtypeStruct((2 * MOST, 2 * wide), jnp.bfloat16)] * turns,
         compiler_params=modest,
         cost_estimate=pl.CostEstimate(flops=1000, bytes_accessed=1000, transcendentals=0),
         name="pack",
     )(picks, early, early_other, late, late_other)
-    arrived = [crossed(packed[turn], "xyz", 2 * turn) for turn in range(pairs - 1, 0, -1)]
-    arrived.append(packed[0])
+    arrived = delivered(packed, "xyz")
     arrived = pl.pallas_call(
         unpack_kernel,
-        in_specs=[smem] + [vmem] * pairs,
+        in_specs=[smem] + [vmem] * turns,
         out_specs=vmem,
         out_shape=jax.ShapeDtypeStruct((shards * MOST, 2 * wide), jnp.float32),
         compiler_params=modest,

time: 33 us -> 39.6 us (1.20)
  the two profiles are of different devices: /device:TPU:0 before, /device:TPU:26 now
where the time goes in v9:
time: 39.6 us; the launch traced here: 39.3 us
  starting transfers between devices  18.8 us (47%)
  Pallas kernels  11.6 us (29%)
  waiting for transfers between devices  8.88 us (22%)
    ppermute x3, starting transfers between devices, delivered(): arrived.append(lax.ppermute(packed[last + other], axis, moves))  11.2 us
    pallas_call x1, Pallas kernels, on_device(): pl.pallas_call(inner_kernel, in_specs=[smem, vmem, outside, outside, outs...  7.61 us
    ppermute x2, starting transfers between devices, crossed(): lax.ppermute(array, axis, [(i, i ^ bits) for i in range(lax.axis_size(axi...  4.75 us
    ppermute x3, waiting for transfers between devices, delivered(): arrived.append(lax.ppermute(packed[last + other], axis, moves))  3.85 us
    ppermute x2, waiting for transfers between devices, shifted(): lax.ppermute(array, axis, [(i, (i + by) % count) for i in range(count)])  3.13 us
    ppermute x2, waiting for transfers between devices, crossed(): lax.ppermute(array, axis, [(i, i ^ bits) for i in range(lax.axis_size(axi...  1.89 us
    ppermute x2, starting transfers between devices, shifted(): lax.ppermute(array, axis, [(i, (i + by) % count) for i in range(count)])  1.52 us
    ppermute x2, starting transfers between devices, delivered(): arrived.append(lax.ppermute(packed[step], axis, moves))  1.33 us
  transfers between devices with their start and end apart: 9, of which 4 were waited for; matrix products, arithmetic and copies ran while one was open for 0% of the time, Pallas kernels for 24%

profile of v9, /device:TPU:26, one launch (start us, length us, event | category | flops | bytes accessed | tf_op | source)
XLA Modules:
  0.0 39.3 jit_solution(1246152530780141249)
XLA Ops:
  0.0 0.0 copy-start
  0.0 1.1 %space_slice.1 = bf16[4,1,32,16,128]{4,3,2,1,0:T(8,128)(2,1)S(1)} custom-call(bf16[4,4,32,16,128]{4,3,2,1,0:T(8,128)(2,1)} %nulls.5), custom_call_target="tpu_custom_call" | custom-call | flops 1000 | bytes 1000 | tf_op jit(solution)/shard_map/space_slice/pallas_call | solution.py:296
  1.1 1.5 %collective-permute-start.1 = (bf16[4,1,32,16,128]{4,3,2,1,0:T(8,128)(2,1)S(1)}, bf16[4,1,32,16,128]{4,3,2,1,0:T(8,128)(2,1)S(1)}, u32[]{:S(2)}, u32[]{:S(2)}) collective-permute-start(bf16[4,1,32,16,128]{4,3,2,1,0:T(8,128)(2,1)S(1)} %space_slice.1), channel_id=1, source_target_pairs={{0,7},{1,0},{2,1},{3,2},{4,3},{5,4},{6,5},{7,6},{8,15},{9,8},{10,9... | collective-permute-start | bytes 1572872 | tf_op jit(solution)/shard_map/ppermute | solution.py:16
  2.5 1.0 %time_slice.1 = bf16[1,4,32,16,128]{4,3,2,1,0:T(8,128)(2,1)S(1)} custom-call(bf16[4,4,32,16,128]{4,3,2,1,0:T(8,128)(2,1)} %nulls.5), custom_call_target="tpu_custom_call" | custom-call | flops 1000 | bytes 1000 | tf_op jit(solution)/shard_map/time_slice/pallas_call | solution.py:306
  3.6 0.1 collective-permute-start.2
  3.7 0.0 copy-done
  3.7 7.6 %inner.1 = (bf16[32,512]{1,0:T(8,128)(2,1)S(1)}, bf16[4,256,1024]{2,1,0:T(8,128)(2,1)S(1)}, f32[2,96,64]{2,1,0:T(8,128)S(1)}) custom-call(s32[1]{0:T(128)} %bitcast.place, s32[8,64]{1,0:T(8,128)S(1)} %copy-done, bf16[4,4,32,16,128]{4,3,2,1,0:T(8,128)(2,1)} %nulls.5, bf16[2,4,32,64,128]{4,3,2,1,0:T(8,128)(2,1)} %time_links.1, ...), custom_call_target="tpu_custom_call" | custom-call | flops 1000 | bytes 1000 | tf_op jit(solution)/shard_map/inner/pallas_call | solution.py:318
  11.3 0.7 %collective-permute-start = (bf16[32,512]{1,0:T(8,128)(2,1)S(1)}, bf16[32,512]{1,0:T(8,128)(2,1)S(1)}, u32[]{:S(2)}, u32[]{:S(2)}) collective-permute-start(bf16[32,512]{1,0:T(8,128)(2,1)S(1)} %get-tuple-element.15.early), channel_id=1, source_target_pairs={{0,1},{1,0},{2,3},{3,2},{4,5},{5,4},{6,7},{7,6},{8,9},{9,8},{10,11... | collective-permute-start | bytes 98312 | tf_op jit(solution)/shard_map/ppermute | solution.py:20
  12.0 3.1 %collective-permute-done.1.space_edge = bf16[4,1,32,16,128]{4,3,2,1,0:T(8,128)(2,1)S(1)} collective-permute-done((bf16[4,1,32,16,128]{4,3,2,1,0:T(8,128)(2,1)S(1)}, bf16[4,1,32,16,128]{4,3,2,1,0:T(8,128)(2,1)S(1)}, u32[]{:S(2)}, u32[]{:S(2)}) %collective-permute-start.1) | collective-permute-done | bytes 524320 | tf_op jit(solution)/shard_map/ppermute | solution.py:16
  15.1 0.0 collective-permute-done.2.time_edge
  15.1 0.9 %final.1.late = bf16[32,512]{1,0:T(8,128)(2,1)S(1)} custom-call(bf16[4,1,32,16,128]{4,3,2,1,0:T(8,128)(2,1)S(1)} %collective-permute-done.1.space_edge, bf16[1,4,32,16,128]{4,3,2,1,0:T(8,128)(2,1)S(1)} %collective-permute-done.2.time_edge, bf16[4,256,1024]{2,1,0:T(8,128)(2,1)S(1)} %get-tuple-element.16.adjoint), custom_call_target="tpu_custom_call" | custom-call | flops 1000 | bytes 1000 | tf_op jit(solution)/shard_map/final/pallas_call | solution.py:338
  16.0 4.1 %collective-permute-start.3 = (bf16[32,512]{1,0:T(8,128)(2,1)S(1)}, bf16[32,512]{1,0:T(8,128)(2,1)S(1)}, u32[]{:S(2)}, u32[]{:S(2)}) collective-permute-start(bf16[32,512]{1,0:T(8,128)(2,1)S(1)} %final.1.late), channel_id=1, source_target_pairs={{0,1},{1,0},{2,3},{3,2},{4,5},{5,4},{6,7},{7,6},{8,9},{9,8},{10,11... | collective-permute-start | bytes 98312 | tf_op jit(solution)/shard_map/ppermute | solution.py:20
  20.1 0.0 collective-permute-done.early_other
  20.1 1.9 %collective-permute-done.3.late_other = bf16[32,512]{1,0:T(8,128)(2,1)S(1)} collective-permute-done((bf16[32,512]{1,0:T(8,128)(2,1)S(1)}, bf16[32,512]{1,0:T(8,128)(2,1)S(1)}, u32[]{:S(2)}, u32[]{:S(2)}) %collective-permute-start.3) | collective-permute-done | bytes 32800 | tf_op jit(solution)/shard_map/ppermute | solution.py:20
  22.0 0.2 pack.1
  22.2 0.7 %collective-permute-start.4 = (bf16[16,1024]{1,0:T(8,128)(2,1)S(1)}, bf16[16,1024]{1,0:T(8,128)(2,1)S(1)}, u32[]{:S(2)}, u32[]{:S(2)}) collective-permute-start(bf16[16,1024]{1,0:T(8,128)(2,1)S(1)} %get-tuple-element.17), channel_id=1, source_target_pairs={{0,2},{1,3},{2,4},{3,5},{4,0},{5,1},{8,10},{9,11},{10,12},{11,13},... | collective-permute-start | bytes 98312 | tf_op jit(solution)/shard_map/ppermute | solution.py:46
  22.8 0.7 %collective-permute-start.5 = (bf16[16,1024]{1,0:T(8,128)(2,1)S(1)}, bf16[16,1024]{1,0:T(8,128)(2,1)S(1)}, u32[]{:S(2)}, u32[]{:S(2)}) collective-permute-start(bf16[16,1024]{1,0:T(8,128)(2,1)S(1)} %get-tuple-element.18), channel_id=1, source_target_pairs={{0,4},{1,5},{2,0},{3,1},{4,2},{5,3},{8,12},{9,13},{10,8},{11,9},{1... | collective-permute-start | bytes 98312 | tf_op jit(solution)/shard_map/ppermute | solution.py:46
  23.5 7.3 %collective-permute-start.6 = (bf16[16,1024]{1,0:T(8,128)(2,1)S(1)}, bf16[16,1024]{1,0:T(8,128)(2,1)S(1)}, u32[]{:S(2)}, u32[]{:S(2)}) collective-permute-start(bf16[16,1024]{1,0:T(8,128)(2,1)S(1)} %get-tuple-element.19), channel_id=1, source_target_pairs={{0,6},{1,7},{6,0},{7,1},{8,14},{9,15},{14,8},{15,9},{16,22},{17,23... | collective-permute-start | bytes 98312 | tf_op jit(solution)/shard_map/ppermute | solution.py:49
  30.9 1.9 %collective-permute-start.7 = (bf16[16,1024]{1,0:T(8,128)(2,1)S(1)}, bf16[16,1024]{1,0:T(8,128)(2,1)S(1)}, u32[]{:S(2)}, u32[]{:S(2)}) collective-permute-start(bf16[16,1024]{1,0:T(8,128)(2,1)S(1)} %get-tuple-element.20), channel_id=1, source_target_pairs={{2,6},{3,7},{6,2},{7,3},{10,14},{11,15},{14,10},{15,11},{18,22},{1... | collective-permute-start | bytes 98312 | tf_op jit(solution)/shard_map/ppermute | solution.py:49
  32.8 1.9 %collective-permute-start.8 = (bf16[16,1024]{1,0:T(8,128)(2,1)S(1)}, bf16[16,1024]{1,0:T(8,128)(2,1)S(1)}, u32[]{:S(2)}, u32[]{:S(2)}) collective-permute-start(bf16[16,1024]{1,0:T(8,128)(2,1)S(1)} %get-tuple-element.21), channel_id=1, source_target_pairs={{4,6},{5,7},{6,4},{7,5},{12,14},{13,15},{14,12},{15,13},{20,22},{2... | collective-permute-start | bytes 98312 | tf_op jit(solution)/shard_map/ppermute | solution.py:49
  34.7 0.0 collective-permute-done.4.refs_0_
  34.7 0.0 collective-permute-done.5.refs_1_
  34.7 0.0 collective-permute-done.6.refs_2_
  34.7 2.8 %collective-permute-done.7.refs_3_ = bf16[16,1024]{1,0:T(8,128)(2,1)S(1)} collective-permute-done((bf16[16,1024]{1,0:T(8,128)(2,1)S(1)}, bf16[16,1024]{1,0:T(8,128)(2,1)S(1)}, u32[]{:S(2)}, u32[]{:S(2)}) %collective-permute-start.7) | collective-permute-done | bytes 32800 | tf_op jit(solution)/shard_map/ppermute | solution.py:49
  37.6 1.0 %collective-permute-done.8.refs_4_ = bf16[16,1024]{1,0:T(8,128)(2,1)S(1)} collective-permute-done((bf16[16,1024]{1,0:T(8,128)(2,1)S(1)}, bf16[16,1024]{1,0:T(8,128)(2,1)S(1)}, u32[]{:S(2)}, u32[]{:S(2)}) %collective-permute-start.8) | collective-permute-done | bytes 32800 | tf_op jit(solution)/shard_map/ppermute | solution.py:49
  38.6 0.7 %unpack.1 = f32[64,1024]{1,0:T(8,128)} custom-call(s32[1]{0:T(128)} %bitcast.place, bf16[16,1024]{1,0:T(8,128)(2,1)S(1)} %collective-permute-done.4.refs_0_, bf16[16,1024]{1,0:T(8,128)(2,1)S(1)} %collective-permute-done.5.refs_1_, bf16[16,1024]{1,0:T(8,128)(2,1)S(1)} %collective-permute-done.6.refs_2_, bf16[16,1024]{1,0:T(8,128)(2,1)S(1)} %collective-permute-done.7.refs_3_, ...), custom_call_target="tpu_custom_call" | custom-call | flops 1000 | bytes 1000 | tf_op jit(solution)/shard_map/unpack/pallas_call | solution.py:359
Async XLA Ops:
  0.0 3.7 %copy-start = (s32[8,64]{1,0:T(8,128)S(1)}, s32[8,64]{1,0:T(8,128)}, u32[]{:S(2)}) copy-start(s32[8,64]{1,0:T(8,128)} %lists.1) | copy-start | bytes 6148
  1.1 14.0 %collective-permute-start.1 = (bf16[4,1,32,16,128]{4,3,2,1,0:T(8,128)(2,1)S(1)}, bf16[4,1,32,16,128]{4,3,2,1,0:T(8,128)(2,1)S(1)}, u32[]{:S(2)}, u32[]{:S(2)}) collective-permute-start(bf16[4,1,32,16,128]{4,3,2,1,0:T(8,128)(2,1)S(1)} %space_slice.1), channel_id=1, source_target_pairs={{0,7},{1,0},{2,1},{3,2},{4,3},{5,4},{6,5},{7,6},{8,15},{9,8},{10,9... | collective-permute-start | bytes 1572872 | tf_op jit(solution)/shard_map/ppermute | solution.py:16
  3.6 11.5 %collective-permute-start.2 = (bf16[1,4,32,16,128]{4,3,2,1,0:T(8,128)(2,1)S(1)}, bf16[1,4,32,16,128]{4,3,2,1,0:T(8,128)(2,1)S(1)}, u32[]{:S(2)}, u32[]{:S(2)}) collective-permute-start(bf16[1,4,32,16,128]{4,3,2,1,0:T(8,128)(2,1)S(1)} %time_slice.1), channel_id=1, source_target_pairs={{0,24},{8,0},{16,8},{24,16},{1,25},{9,1},{17,9},{25,17},{2,26},{10... | collective-permute-start | bytes 1572872 | tf_op jit(solution)/shard_map/ppermute | solution.py:16
  11.3 8.8 %collective-permute-start = (bf16[32,512]{1,0:T(8,128)(2,1)S(1)}, bf16[32,512]{1,0:T(8,128)(2,1)S(1)}, u32[]{:S(2)}, u32[]{:S(2)}) collective-permute-start(bf16[32,512]{1,0:T(8,128)(2,1)S(1)} %get-tuple-element.15.early), channel_id=1, source_target_pairs={{0,1},{1,0},{2,3},{3,2},{4,5},{5,4},{6,7},{7,6},{8,9},{9,8},{10,11... | collective-permute-start | bytes 98312 | tf_op jit(solution)/shard_map/ppermute | solution.py:20
  16.0 6.0 %collective-permute-start.3 = (bf16[32,512]{1,0:T(8,128)(2,1)S(1)}, bf16[32,512]{1,0:T(8,128)(2,1)S(1)}, u32[]{:S(2)}, u32[]{:S(2)}) collective-permute-start(bf16[32,512]{1,0:T(8,128)(2,1)S(1)} %final.1.late), channel_id=1, source_target_pairs={{0,1},{1,0},{2,3},{3,2},{4,5},{5,4},{6,7},{7,6},{8,9},{9,8},{10,11... | collective-permute-start | bytes 98312 | tf_op jit(solution)/shard_map/ppermute | solution.py:20
  22.2 12.5 %collective-permute-start.4 = (bf16[16,1024]{1,0:T(8,128)(2,1)S(1)}, bf16[16,1024]{1,0:T(8,128)(2,1)S(1)}, u32[]{:S(2)}, u32[]{:S(2)}) collective-permute-start(bf16[16,1024]{1,0:T(8,128)(2,1)S(1)} %get-tuple-element.17), channel_id=1, source_target_pairs={{0,2},{1,3},{2,4},{3,5},{4,0},{5,1},{8,10},{9,11},{10,12},{11,13},... | collective-permute-start | bytes 98312 | tf_op jit(solution)/shard_map/ppermute | solution.py:46
  22.8 11.9 %collective-permute-start.5 = (bf16[16,1024]{1,0:T(8,128)(2,1)S(1)}, bf16[16,1024]{1,0:T(8,128)(2,1)S(1)}, u32[]{:S(2)}, u32[]{:S(2)}) collective-permute-start(bf16[16,1024]{1,0:T(8,128)(2,1)S(1)} %get-tuple-element.18), channel_id=1, source_target_pairs={{0,4},{1,5},{2,0},{3,1},{4,2},{5,3},{8,12},{9,13},{10,8},{11,9},{1... | collective-permute-start | bytes 98312 | tf_op jit(solution)/shard_map/ppermute | solution.py:46
  23.5 11.2 %collective-permute-start.6 = (bf16[16,1024]{1,0:T(8,128)(2,1)S(1)}, bf16[16,1024]{1,0:T(8,128)(2,1)S(1)}, u32[]{:S(2)}, u32[]{:S(2)}) collective-permute-start(bf16[16,1024]{1,0:T(8,128)(2,1)S(1)} %get-tuple-element.19), channel_id=1, source_target_pairs={{0,6},{1,7},{6,0},{7,1},{8,14},{9,15},{14,8},{15,9},{16,22},{17,23... | collective-permute-start | bytes 98312 | tf_op jit(solution)/shard_map/ppermute | solution.py:49
  30.9 6.7 %collective-permute-start.7 = (bf16[16,1024]{1,0:T(8,128)(2,1)S(1)}, bf16[16,1024]{1,0:T(8,128)(2,1)S(1)}, u32[]{:S(2)}, u32[]{:S(2)}) collective-permute-start(bf16[16,1024]{1,0:T(8,128)(2,1)S(1)} %get-tuple-element.20), channel_id=1, source_target_pairs={{2,6},{3,7},{6,2},{7,3},{10,14},{11,15},{14,10},{15,11},{18,22},{1... | collective-permute-start | bytes 98312 | tf_op jit(solution)/shard_map/ppermute | solution.py:49
  32.8 5.8 %collective-permute-start.8 = (bf16[16,1024]{1,0:T(8,128)(2,1)S(1)}, bf16[16,1024]{1,0:T(8,128)(2,1)S(1)}, u32[]{:S(2)}, u32[]{:S(2)}) collective-permute-start(bf16[16,1024]{1,0:T(8,128)(2,1)S(1)} %get-tuple-element.21), channel_id=1, source_target_pairs={{4,6},{5,7},{6,4},{7,5},{12,14},{13,15},{14,12},{15,13},{20,22},{2... | collective-permute-start | bytes 98312 | tf_op jit(solution)/shard_map/ppermute | solution.py:49

commit v10 on v9

--- a/solution.py
+++ b/solution.py
@@ -42,10 +42,12 @@
     last = shards // 2 - 1
     arrived = []
     for step in range(1, last):
-        moves = [(2 * i + side, 2 * ((i + step) % last) + side) for i in range(last) for side in range(2)]
+        targets = [(i + step) % last for i in range(last)] + [last]
+        moves = [(2 * i + side, 2 * j + side) for i, j in enumerate(targets) for side in range(2)]
         arrived.append(lax.ppermute(packed[step], axis, moves))
     for other in range(last):
-        moves = [(2 * i + side, 2 * j + side) for i, j in ((other, last), (last, other)) for side in range(2)]
+        targets = [last if i == other else other if i == last else i for i in range(last + 1)]
+        moves = [(2 * i + side, 2 * j + side) for i, j in enumerate(targets) for side in range(2)]
         arrived.append(lax.ppermute(packed[last + other], axis, moves))
     return arrived + [packed[0]]
 

time: 39.6 us -> 39.6 us (level)
  no operation moved by 1% of the time
where the time goes in v10:
time: 39.6 us; the launch traced here: 39.3 us
  starting transfers between devices  18.8 us (47%)
  Pallas kernels  11.6 us (29%)
  waiting for transfers between devices  8.88 us (22%)
    ppermute x3, starting transfers between devices, delivered(): arrived.append(lax.ppermute(packed[last + other], axis, moves))  11.2 us
    pallas_call x1, Pallas kernels, on_device(): pl.pallas_call(inner_kernel, in_specs=[smem, vmem, outside, outside, outs...  7.61 us
    ppermute x2, starting transfers between devices, crossed(): lax.ppermute(array, axis, [(i, i ^ bits) for i in range(lax.axis_size(axi...  4.75 us
    ppermute x3, waiting for transfers between devices, delivered(): arrived.append(lax.ppermute(packed[last + other], axis, moves))  3.85 us
    ppermute x2, waiting for transfers between devices, shifted(): lax.ppermute(array, axis, [(i, (i + by) % count) for i in range(count)])  3.13 us
    ppermute x2, waiting for transfers between devices, crossed(): lax.ppermute(array, axis, [(i, i ^ bits) for i in range(lax.axis_size(axi...  1.89 us
    ppermute x2, starting transfers between devices, shifted(): lax.ppermute(array, axis, [(i, (i + by) % count) for i in range(count)])  1.52 us
    ppermute x2, starting transfers between devices, delivered(): arrived.append(lax.ppermute(packed[step], axis, moves))  1.33 us
  transfers between devices with their start and end apart: 9, of which 4 were waited for; matrix products, arithmetic and copies ran while one was open for 0% of the time, Pallas kernels for 24%

profile of v10, /device:TPU:26, one launch (start us, length us, event | category | flops | bytes accessed | tf_op | source)
XLA Modules:
  0.0 39.3 jit_solution(12217895278012236237)
XLA Ops:
  0.0 0.0 copy-start
  0.0 1.1 %space_slice.1 = bf16[4,1,32,16,128]{4,3,2,1,0:T(8,128)(2,1)S(1)} custom-call(bf16[4,4,32,16,128]{4,3,2,1,0:T(8,128)(2,1)} %nulls.5), custom_call_target="tpu_custom_call" | custom-call | flops 1000 | bytes 1000 | tf_op jit(solution)/shard_map/space_slice/pallas_call | solution.py:298
  1.1 1.5 %collective-permute-start.1 = (bf16[4,1,32,16,128]{4,3,2,1,0:T(8,128)(2,1)S(1)}, bf16[4,1,32,16,128]{4,3,2,1,0:T(8,128)(2,1)S(1)}, u32[]{:S(2)}, u32[]{:S(2)}) collective-permute-start(bf16[4,1,32,16,128]{4,3,2,1,0:T(8,128)(2,1)S(1)} %space_slice.1), channel_id=1, source_target_pairs={{0,7},{1,0},{2,1},{3,2},{4,3},{5,4},{6,5},{7,6},{8,15},{9,8},{10,9... | collective-permute-start | bytes 1572872 | tf_op jit(solution)/shard_map/ppermute | solution.py:16
  2.5 1.0 %time_slice.1 = bf16[1,4,32,16,128]{4,3,2,1,0:T(8,128)(2,1)S(1)} custom-call(bf16[4,4,32,16,128]{4,3,2,1,0:T(8,128)(2,1)} %nulls.5), custom_call_target="tpu_custom_call" | custom-call | flops 1000 | bytes 1000 | tf_op jit(solution)/shard_map/time_slice/pallas_call | solution.py:308
  3.6 0.1 collective-permute-start.2
  3.7 0.0 copy-done
  3.7 7.6 %inner.1 = (bf16[32,512]{1,0:T(8,128)(2,1)S(1)}, bf16[4,256,1024]{2,1,0:T(8,128)(2,1)S(1)}, f32[2,96,64]{2,1,0:T(8,128)S(1)}) custom-call(s32[1]{0:T(128)} %bitcast.place, s32[8,64]{1,0:T(8,128)S(1)} %copy-done, bf16[4,4,32,16,128]{4,3,2,1,0:T(8,128)(2,1)} %nulls.5, bf16[2,4,32,64,128]{4,3,2,1,0:T(8,128)(2,1)} %time_links.1, ...), custom_call_target="tpu_custom_call" | custom-call | flops 1000 | bytes 1000 | tf_op jit(solution)/shard_map/inner/pallas_call | solution.py:320
  11.3 0.7 %collective-permute-start = (bf16[32,512]{1,0:T(8,128)(2,1)S(1)}, bf16[32,512]{1,0:T(8,128)(2,1)S(1)}, u32[]{:S(2)}, u32[]{:S(2)}) collective-permute-start(bf16[32,512]{1,0:T(8,128)(2,1)S(1)} %get-tuple-element.15.early), channel_id=1, source_target_pairs={{0,1},{1,0},{2,3},{3,2},{4,5},{5,4},{6,7},{7,6},{8,9},{9,8},{10,11... | collective-permute-start | bytes 98312 | tf_op jit(solution)/shard_map/ppermute | solution.py:20
  12.0 3.1 %collective-permute-done.1.space_edge = bf16[4,1,32,16,128]{4,3,2,1,0:T(8,128)(2,1)S(1)} collective-permute-done((bf16[4,1,32,16,128]{4,3,2,1,0:T(8,128)(2,1)S(1)}, bf16[4,1,32,16,128]{4,3,2,1,0:T(8,128)(2,1)S(1)}, u32[]{:S(2)}, u32[]{:S(2)}) %collective-permute-start.1) | collective-permute-done | bytes 524320 | tf_op jit(solution)/shard_map/ppermute | solution.py:16
  15.1 0.0 collective-permute-done.2.time_edge
  15.1 0.9 %final.1.late = bf16[32,512]{1,0:T(8,128)(2,1)S(1)} custom-call(bf16[4,1,32,16,128]{4,3,2,1,0:T(8,128)(2,1)S(1)} %collective-permute-done.1.space_edge, bf16[1,4,32,16,128]{4,3,2,1,0:T(8,128)(2,1)S(1)} %collective-permute-done.2.time_edge, bf16[4,256,1024]{2,1,0:T(8,128)(2,1)S(1)} %get-tuple-element.16.adjoint), custom_call_target="tpu_custom_call" | custom-call | flops 1000 | bytes 1000 | tf_op jit(solution)/shard_map/final/pallas_call | solution.py:340
  16.0 4.1 %collective-permute-start.3 = (bf16[32,512]{1,0:T(8,128)(2,1)S(1)}, bf16[32,512]{1,0:T(8,128)(2,1)S(1)}, u32[]{:S(2)}, u32[]{:S(2)}) collective-permute-start(bf16[32,512]{1,0:T(8,128)(2,1)S(1)} %final.1.late), channel_id=1, source_target_pairs={{0,1},{1,0},{2,3},{3,2},{4,5},{5,4},{6,7},{7,6},{8,9},{9,8},{10,11... | collective-permute-start | bytes 98312 | tf_op jit(solution)/shard_map/ppermute | solution.py:20
  20.1 0.0 collective-permute-done.early_other
  20.1 1.9 %collective-permute-done.3.late_other = bf16[32,512]{1,0:T(8,128)(2,1)S(1)} collective-permute-done((bf16[32,512]{1,0:T(8,128)(2,1)S(1)}, bf16[32,512]{1,0:T(8,128)(2,1)S(1)}, u32[]{:S(2)}, u32[]{:S(2)}) %collective-permute-start.3) | collective-permute-done | bytes 32800 | tf_op jit(solution)/shard_map/ppermute | solution.py:20
  22.0 0.2 pack.1
  22.2 0.7 %collective-permute-start.4 = (bf16[16,1024]{1,0:T(8,128)(2,1)S(1)}, bf16[16,1024]{1,0:T(8,128)(2,1)S(1)}, u32[]{:S(2)}, u32[]{:S(2)}) collective-permute-start(bf16[16,1024]{1,0:T(8,128)(2,1)S(1)} %get-tuple-element.17), channel_id=1, source_target_pairs={{0,2},{1,3},{2,4},{3,5},{4,0},{5,1},{6,6},{7,7},{8,10},{9,11},{10,... | collective-permute-start | bytes 98312 | tf_op jit(solution)/shard_map/ppermute | solution.py:47
  22.8 0.7 %collective-permute-start.5 = (bf16[16,1024]{1,0:T(8,128)(2,1)S(1)}, bf16[16,1024]{1,0:T(8,128)(2,1)S(1)}, u32[]{:S(2)}, u32[]{:S(2)}) collective-permute-start(bf16[16,1024]{1,0:T(8,128)(2,1)S(1)} %get-tuple-element.18), channel_id=1, source_target_pairs={{0,4},{1,5},{2,0},{3,1},{4,2},{5,3},{6,6},{7,7},{8,12},{9,13},{10,... | collective-permute-start | bytes 98312 | tf_op jit(solution)/shard_map/ppermute | solution.py:47
  23.5 7.3 %collective-permute-start.6 = (bf16[16,1024]{1,0:T(8,128)(2,1)S(1)}, bf16[16,1024]{1,0:T(8,128)(2,1)S(1)}, u32[]{:S(2)}, u32[]{:S(2)}) collective-permute-start(bf16[16,1024]{1,0:T(8,128)(2,1)S(1)} %get-tuple-element.19), channel_id=1, source_target_pairs={{0,6},{1,7},{2,2},{3,3},{4,4},{5,5},{6,0},{7,1},{8,14},{9,15},{10,... | collective-permute-start | bytes 98312 | tf_op jit(solution)/shard_map/ppermute | solution.py:51
  30.9 1.9 %collective-permute-start.7 = (bf16[16,1024]{1,0:T(8,128)(2,1)S(1)}, bf16[16,1024]{1,0:T(8,128)(2,1)S(1)}, u32[]{:S(2)}, u32[]{:S(2)}) collective-permute-start(bf16[16,1024]{1,0:T(8,128)(2,1)S(1)} %get-tuple-element.20), channel_id=1, source_target_pairs={{0,0},{1,1},{2,6},{3,7},{4,4},{5,5},{6,2},{7,3},{8,8},{9,9},{10,14... | collective-permute-start | bytes 98312 | tf_op jit(solution)/shard_map/ppermute | solution.py:51
  32.8 1.9 %collective-permute-start.8 = (bf16[16,1024]{1,0:T(8,128)(2,1)S(1)}, bf16[16,1024]{1,0:T(8,128)(2,1)S(1)}, u32[]{:S(2)}, u32[]{:S(2)}) collective-permute-start(bf16[16,1024]{1,0:T(8,128)(2,1)S(1)} %get-tuple-element.21), channel_id=1, source_target_pairs={{0,0},{1,1},{2,2},{3,3},{4,6},{5,7},{6,4},{7,5},{8,8},{9,9},{10,10... | collective-permute-start | bytes 98312 | tf_op jit(solution)/shard_map/ppermute | solution.py:51
  34.7 0.0 collective-permute-done.4.refs_0_
  34.7 0.0 collective-permute-done.5.refs_1_
  34.7 0.0 collective-permute-done.6.refs_2_
  34.7 2.8 %collective-permute-done.7.refs_3_ = bf16[16,1024]{1,0:T(8,128)(2,1)S(1)} collective-permute-done((bf16[16,1024]{1,0:T(8,128)(2,1)S(1)}, bf16[16,1024]{1,0:T(8,128)(2,1)S(1)}, u32[]{:S(2)}, u32[]{:S(2)}) %collective-permute-start.7) | collective-permute-done | bytes 32800 | tf_op jit(solution)/shard_map/ppermute | solution.py:51
  37.6 1.0 %collective-permute-done.8.refs_4_ = bf16[16,1024]{1,0:T(8,128)(2,1)S(1)} collective-permute-done((bf16[16,1024]{1,0:T(8,128)(2,1)S(1)}, bf16[16,1024]{1,0:T(8,128)(2,1)S(1)}, u32[]{:S(2)}, u32[]{:S(2)}) %collective-permute-start.8) | collective-permute-done | bytes 32800 | tf_op jit(solution)/shard_map/ppermute | solution.py:51
  38.6 0.7 %unpack.1 = f32[64,1024]{1,0:T(8,128)} custom-call(s32[1]{0:T(128)} %bitcast.place, bf16[16,1024]{1,0:T(8,128)(2,1)S(1)} %collective-permute-done.4.refs_0_, bf16[16,1024]{1,0:T(8,128)(2,1)S(1)} %collective-permute-done.5.refs_1_, bf16[16,1024]{1,0:T(8,128)(2,1)S(1)} %collective-permute-done.6.refs_2_, bf16[16,1024]{1,0:T(8,128)(2,1)S(1)} %collective-permute-done.7.refs_3_, ...), custom_call_target="tpu_custom_call" | custom-call | flops 1000 | bytes 1000 | tf_op jit(solution)/shard_map/unpack/pallas_call | solution.py:361
Async XLA Ops:
  0.0 3.7 %copy-start = (s32[8,64]{1,0:T(8,128)S(1)}, s32[8,64]{1,0:T(8,128)}, u32[]{:S(2)}) copy-start(s32[8,64]{1,0:T(8,128)} %lists.1) | copy-start | bytes 6148
  1.1 14.0 %collective-permute-start.1 = (bf16[4,1,32,16,128]{4,3,2,1,0:T(8,128)(2,1)S(1)}, bf16[4,1,32,16,128]{4,3,2,1,0:T(8,128)(2,1)S(1)}, u32[]{:S(2)}, u32[]{:S(2)}) collective-permute-start(bf16[4,1,32,16,128]{4,3,2,1,0:T(8,128)(2,1)S(1)} %space_slice.1), channel_id=1, source_target_pairs={{0,7},{1,0},{2,1},{3,2},{4,3},{5,4},{6,5},{7,6},{8,15},{9,8},{10,9... | collective-permute-start | bytes 1572872 | tf_op jit(solution)/shard_map/ppermute | solution.py:16
  3.6 11.5 %collective-permute-start.2 = (bf16[1,4,32,16,128]{4,3,2,1,0:T(8,128)(2,1)S(1)}, bf16[1,4,32,16,128]{4,3,2,1,0:T(8,128)(2,1)S(1)}, u32[]{:S(2)}, u32[]{:S(2)}) collective-permute-start(bf16[1,4,32,16,128]{4,3,2,1,0:T(8,128)(2,1)S(1)} %time_slice.1), channel_id=1, source_target_pairs={{0,24},{8,0},{16,8},{24,16},{1,25},{9,1},{17,9},{25,17},{2,26},{10... | collective-permute-start | bytes 1572872 | tf_op jit(solution)/shard_map/ppermute | solution.py:16
  11.3 8.8 %collective-permute-start = (bf16[32,512]{1,0:T(8,128)(2,1)S(1)}, bf16[32,512]{1,0:T(8,128)(2,1)S(1)}, u32[]{:S(2)}, u32[]{:S(2)}) collective-permute-start(bf16[32,512]{1,0:T(8,128)(2,1)S(1)} %get-tuple-element.15.early), channel_id=1, source_target_pairs={{0,1},{1,0},{2,3},{3,2},{4,5},{5,4},{6,7},{7,6},{8,9},{9,8},{10,11... | collective-permute-start | bytes 98312 | tf_op jit(solution)/shard_map/ppermute | solution.py:20
  16.0 6.0 %collective-permute-start.3 = (bf16[32,512]{1,0:T(8,128)(2,1)S(1)}, bf16[32,512]{1,0:T(8,128)(2,1)S(1)}, u32[]{:S(2)}, u32[]{:S(2)}) collective-permute-start(bf16[32,512]{1,0:T(8,128)(2,1)S(1)} %final.1.late), channel_id=1, source_target_pairs={{0,1},{1,0},{2,3},{3,2},{4,5},{5,4},{6,7},{7,6},{8,9},{9,8},{10,11... | collective-permute-start | bytes 98312 | tf_op jit(solution)/shard_map/ppermute | solution.py:20
  22.2 12.5 %collective-permute-start.4 = (bf16[16,1024]{1,0:T(8,128)(2,1)S(1)}, bf16[16,1024]{1,0:T(8,128)(2,1)S(1)}, u32[]{:S(2)}, u32[]{:S(2)}) collective-permute-start(bf16[16,1024]{1,0:T(8,128)(2,1)S(1)} %get-tuple-element.17), channel_id=1, source_target_pairs={{0,2},{1,3},{2,4},{3,5},{4,0},{5,1},{6,6},{7,7},{8,10},{9,11},{10,... | collective-permute-start | bytes 98312 | tf_op jit(solution)/shard_map/ppermute | solution.py:47
  22.8 11.9 %collective-permute-start.5 = (bf16[16,1024]{1,0:T(8,128)(2,1)S(1)}, bf16[16,1024]{1,0:T(8,128)(2,1)S(1)}, u32[]{:S(2)}, u32[]{:S(2)}) collective-permute-start(bf16[16,1024]{1,0:T(8,128)(2,1)S(1)} %get-tuple-element.18), channel_id=1, source_target_pairs={{0,4},{1,5},{2,0},{3,1},{4,2},{5,3},{6,6},{7,7},{8,12},{9,13},{10,... | collective-permute-start | bytes 98312 | tf_op jit(solution)/shard_map/ppermute | solution.py:47
  23.5 11.2 %collective-permute-start.6 = (bf16[16,1024]{1,0:T(8,128)(2,1)S(1)}, bf16[16,1024]{1,0:T(8,128)(2,1)S(1)}, u32[]{:S(2)}, u32[]{:S(2)}) collective-permute-start(bf16[16,1024]{1,0:T(8,128)(2,1)S(1)} %get-tuple-element.19), channel_id=1, source_target_pairs={{0,6},{1,7},{2,2},{3,3},{4,4},{5,5},{6,0},{7,1},{8,14},{9,15},{10,... | collective-permute-start | bytes 98312 | tf_op jit(solution)/shard_map/ppermute | solution.py:51
  30.9 6.7 %collective-permute-start.7 = (bf16[16,1024]{1,0:T(8,128)(2,1)S(1)}, bf16[16,1024]{1,0:T(8,128)(2,1)S(1)}, u32[]{:S(2)}, u32[]{:S(2)}) collective-permute-start(bf16[16,1024]{1,0:T(8,128)(2,1)S(1)} %get-tuple-element.20), channel_id=1, source_target_pairs={{0,0},{1,1},{2,6},{3,7},{4,4},{5,5},{6,2},{7,3},{8,8},{9,9},{10,14... | collective-permute-start | bytes 98312 | tf_op jit(solution)/shard_map/ppermute | solution.py:51
  32.8 5.8 %collective-permute-start.8 = (bf16[16,1024]{1,0:T(8,128)(2,1)S(1)}, bf16[16,1024]{1,0:T(8,128)(2,1)S(1)}, u32[]{:S(2)}, u32[]{:S(2)}) collective-permute-start(bf16[16,1024]{1,0:T(8,128)(2,1)S(1)} %get-tuple-element.21), channel_id=1, source_target_pairs={{0,0},{1,1},{2,2},{3,3},{4,6},{5,7},{6,4},{7,5},{8,8},{9,9},{10,10... | collective-permute-start | bytes 98312 | tf_op jit(solution)/shard_map/ppermute | solution.py:51

commit v11 on v8

--- a/solution.py
+++ b/solution.py
@@ -165,7 +165,7 @@
     own_column = column < count
     side = lax.rem(me, 2)
     for turn in range(shards // 2):
-        owner = 2 * jnp.bitwise_xor(me // 2, turn) + side
+        owner = 2 * turn + side
         mine = jnp.broadcast_to(lists[pl.ds(owner, 1), :], (MOST, cap))
         for parity in range(2):
             source = me - side + parity
@@ -227,23 +227,13 @@
     late[...] = jnp.concatenate(found, axis=0).astype(jnp.bfloat16)
 
 
-def pack_kernel(picks, early, early_other, late, late_other, *packed):
+def pack_kernel(picks, early, early_other, late, late_other, packed):
     half_count = late.shape[0] // 2
     pieces = (early, late, early_other, late_other)
     for half, width in enumerate((late.shape[1],) * 2):
         rows = jnp.concatenate([piece[pl.ds(half * half_count, half_count), :] for piece in pieces], axis=0)
         sent = dot(picks[half].astype(jnp.bfloat16), rows, MAT_DIMS)
-        for turn, out in enumerate(packed):
-            mine = sent[turn * 2 * MOST : (turn + 1) * 2 * MOST]
-            out[:, pl.ds(half * width, width)] = mine.astype(jnp.bfloat16)
-
-
-def unpack_kernel(place, *refs):
-    pair = place[0] // 2
-    result = refs[-1]
-    for turn, arrived in enumerate(refs[-2::-1]):
-        source = jnp.bitwise_xor(pair, turn)
-        result[pl.ds(pl.multiple_of(source * 2 * MOST, 2 * MOST), 2 * MOST), :] = arrived[...].astype(jnp.float32)
+        packed[:, pl.ds(half * width, width)] = sent.astype(jnp.bfloat16)
 
 
 def on_device(nulls, time_links, space_links, owner_lists):
@@ -314,27 +304,17 @@
     )(edge_space, edge_time, adjoint)
     early_other = crossed(early, "xyz", 1)
     late_other = crossed(late, "xyz", 1)
-    pairs = shards // 2
     packed = pl.pallas_call(
         pack_kernel,
         in_specs=[vmem] * 5,
-        out_specs=[vmem] * pairs,
-        out_shape=[jax.ShapeDtypeStruct((2 * MOST, 2 * wide), jnp.bfloat16)] * pairs,
+        out_specs=vmem,
+        out_shape=jax.ShapeDtypeStruct((shards * MOST, 2 * wide), jnp.bfloat16),
         compiler_params=modest,
         cost_estimate=pl.CostEstimate(flops=1000, bytes_accessed=1000, transcendentals=0),
         name="pack",
     )(picks, early, early_other, late, late_other)
-    arrived = [crossed(packed[turn], "xyz", 2 * turn) for turn in range(pairs - 1, 0, -1)]
-    arrived.append(packed[0])
-    arrived = pl.pallas_call(
-        unpack_kernel,
-        in_specs=[smem] + [vmem] * pairs,
-        out_specs=vmem,
-        out_shape=jax.ShapeDtypeStruct((shards * MOST, 2 * wide), jnp.float32),
-        compiler_params=modest,
-        cost_estimate=pl.CostEstimate(flops=1000, bytes_accessed=1000, transcendentals=0),
-        name="unpack",
-    )(place, *arrived)
+    groups = [list(range(side, shards, 2)) for side in range(2)]
+    arrived = lax.all_to_all(packed, "xyz", 0, 0, axis_index_groups=groups, tiled=True).astype(jnp.float32)
     if shards * MOST == cap:
         result = arrived
     else:

time: 33 us -> 35.1 us (1.064)
  blocking collectives: 0 us -> 10.8 us
  starting transfers between devices: 11.8 us -> 7.22 us
  waiting for transfers between devices: 9.49 us -> 5.32 us
  other arithmetic: 0 us -> 0.72 us
  Pallas kernels: 11.5 us -> 10.8 us
    all_to_all x0 -> x1, blocking collectives: none -> 10.8 us  [on_device(): lax.all_to_all(packed, 'xyz', 0, 0, axis_index_groups=groups, tiled=True)]
    ppermute x5 -> x2, starting transfers between devices: 5 us -> 0.46 us  [crossed(): lax.ppermute(array, axis, [(i, i ^ bits) for i in range(lax.axis_size(axi...]
    ppermute x5 -> x2, waiting for transfers between devices: 7.74 us -> 3.57 us  [crossed(): lax.ppermute(array, axis, [(i, i ^ bits) for i in range(lax.axis_size(axi...]
    pallas_call x2 -> x1, Pallas kernels: 0.88 us -> 0.16 us  [on_device(): pl.pallas_call(pack_kernel, in_specs=[vmem] * 5, out_specs=vmem, out_shap...]
    convert_element_type x0 -> x1, other arithmetic: none -> 0.72 us  [on_device(): lax.all_to_all(packed, 'xyz', 0, 0, axis_index_groups=groups, tiled=True)]
  transfers between devices with their start and end apart: 7 -> 4, of which waited for: 5 -> 3; matrix products, arithmetic and copies ran while one was open for 0% -> 0% of each run, Pallas kernels for 29% -> 27%
where the time goes in v11:
time: 35.1 us; the launch traced here: 34.9 us
  Pallas kernels  10.8 us (31%)
  blocking collectives  10.8 us (31%)
  starting transfers between devices  7.22 us (21%)
  waiting for transfers between devices  5.32 us (15%)
  other arithmetic  0.72 us (2%)
    all_to_all x1, blocking collectives, on_device(): lax.all_to_all(packed, 'xyz', 0, 0, axis_index_groups=groups, tiled=True)  10.8 us
    pallas_call x1, Pallas kernels, on_device(): pl.pallas_call(inner_kernel, in_specs=[smem, vmem, outside, outside, outs...  7.58 us
    ppermute x2, starting transfers between devices, shifted(): lax.ppermute(array, axis, [(i, (i + by) % count) for i in range(count)])  6.76 us
    ppermute x2, waiting for transfers between devices, crossed(): lax.ppermute(array, axis, [(i, i ^ bits) for i in range(lax.axis_size(axi...  3.57 us
    ppermute x2, waiting for transfers between devices, shifted(): lax.ppermute(array, axis, [(i, (i + by) % count) for i in range(count)])  1.75 us
    pallas_call x1, Pallas kernels, on_device(): pl.pallas_call(space_slice_kernel, in_specs=[outside], out_specs=vmem, ou...  1.06 us
    pallas_call x1, Pallas kernels, on_device(): pl.pallas_call(time_slice_kernel, in_specs=[outside], out_specs=vmem, out...  1.05 us
    pallas_call x1, Pallas kernels, on_device(): pl.pallas_call(final_kernel, in_specs=[vmem] * 3, out_specs=vmem, out_sha...  0.93 us
  transfers between devices with their start and end apart: 4, of which 3 were waited for; matrix products, arithmetic and copies ran while one was open for 0% of the time, Pallas kernels for 27%

profile of v11, /device:TPU:0, one launch (start us, length us, event | category | flops | bytes accessed | tf_op | source)
XLA Modules:
  0.0 34.9 jit_solution(398425230829832509)
XLA Ops:
  0.0 0.0 copy-start
  0.0 1.1 %space_slice.1 = bf16[4,1,32,16,128]{4,3,2,1,0:T(8,128)(2,1)S(1)} custom-call(bf16[4,4,32,16,128]{4,3,2,1,0:T(8,128)(2,1)} %nulls.5), custom_call_target="tpu_custom_call" | custom-call | flops 1000 | bytes 1000 | tf_op jit(solution)/shard_map/space_slice/pallas_call | solution.py:254
  1.1 6.1 %collective-permute-start.1 = (bf16[4,1,32,16,128]{4,3,2,1,0:T(8,128)(2,1)S(1)}, bf16[4,1,32,16,128]{4,3,2,1,0:T(8,128)(2,1)S(1)}, u32[]{:S(2)}, u32[]{:S(2)}) collective-permute-start(bf16[4,1,32,16,128]{4,3,2,1,0:T(8,128)(2,1)S(1)} %space_slice.1), channel_id=1, source_target_pairs={{0,7},{1,0},{2,1},{3,2},{4,3},{5,4},{6,5},{7,6},{8,15},{9,8},{10,9... | collective-permute-start | bytes 1572872 | tf_op jit(solution)/shard_map/ppermute | solution.py:16
  7.1 1.0 %time_slice.1 = bf16[1,4,32,16,128]{4,3,2,1,0:T(8,128)(2,1)S(1)} custom-call(bf16[4,4,32,16,128]{4,3,2,1,0:T(8,128)(2,1)} %nulls.5), custom_call_target="tpu_custom_call" | custom-call | flops 1000 | bytes 1000 | tf_op jit(solution)/shard_map/time_slice/pallas_call | solution.py:264
  8.2 0.7 %collective-permute-start.2 = (bf16[1,4,32,16,128]{4,3,2,1,0:T(8,128)(2,1)S(1)}, bf16[1,4,32,16,128]{4,3,2,1,0:T(8,128)(2,1)S(1)}, u32[]{:S(2)}, u32[]{:S(2)}) collective-permute-start(bf16[1,4,32,16,128]{4,3,2,1,0:T(8,128)(2,1)S(1)} %time_slice.1), channel_id=1, source_target_pairs={{0,24},{8,0},{16,8},{24,16},{1,25},{9,1},{17,9},{25,17},{2,26},{10... | collective-permute-start | bytes 1572872 | tf_op jit(solution)/shard_map/ppermute | solution.py:16
  8.9 0.0 copy-done
  8.9 7.6 %inner.1 = (bf16[32,512]{1,0:T(8,128)(2,1)S(1)}, bf16[4,256,1024]{2,1,0:T(8,128)(2,1)S(1)}, f32[2,64,64]{2,1,0:T(8,128)S(1)}) custom-call(s32[1]{0:T(128)} %bitcast.place, s32[8,64]{1,0:T(8,128)S(1)} %copy-done, bf16[4,4,32,16,128]{4,3,2,1,0:T(8,128)(2,1)} %nulls.5, bf16[2,4,32,64,128]{4,3,2,1,0:T(8,128)(2,1)} %time_links.1, ...), custom_call_target="tpu_custom_call" | custom-call | flops 1000 | bytes 1000 | tf_op jit(solution)/shard_map/inner/pallas_call | solution.py:276
  16.5 0.1 collective-permute-start
  16.6 1.8 %collective-permute-done.1.space_edge = bf16[4,1,32,16,128]{4,3,2,1,0:T(8,128)(2,1)S(1)} collective-permute-done((bf16[4,1,32,16,128]{4,3,2,1,0:T(8,128)(2,1)S(1)}, bf16[4,1,32,16,128]{4,3,2,1,0:T(8,128)(2,1)S(1)}, u32[]{:S(2)}, u32[]{:S(2)}) %collective-permute-start.1) | collective-permute-done | bytes 524320 | tf_op jit(solution)/shard_map/ppermute | solution.py:16
  18.3 0.0 collective-permute-done.2.time_edge
  18.3 0.9 %final.1.late = bf16[32,512]{1,0:T(8,128)(2,1)S(1)} custom-call(bf16[4,1,32,16,128]{4,3,2,1,0:T(8,128)(2,1)S(1)} %collective-permute-done.1.space_edge, bf16[1,4,32,16,128]{4,3,2,1,0:T(8,128)(2,1)S(1)} %collective-permute-done.2.time_edge, bf16[4,256,1024]{2,1,0:T(8,128)(2,1)S(1)} %get-tuple-element.10.adjoint), custom_call_target="tpu_custom_call" | custom-call | flops 1000 | bytes 1000 | tf_op jit(solution)/shard_map/final/pallas_call | solution.py:296
  19.3 0.4 %collective-permute-start.3 = (bf16[32,512]{1,0:T(8,128)(2,1)S(1)}, bf16[32,512]{1,0:T(8,128)(2,1)S(1)}, u32[]{:S(2)}, u32[]{:S(2)}) collective-permute-start(bf16[32,512]{1,0:T(8,128)(2,1)S(1)} %final.1.late), channel_id=1, source_target_pairs={{0,1},{1,0},{2,3},{3,2},{4,5},{5,4},{6,7},{7,6},{8,9},{9,8},{10,11... | collective-permute-start | bytes 98312 | tf_op jit(solution)/shard_map/ppermute | solution.py:20
  19.6 0.8 %collective-permute-done.early_other = bf16[32,512]{1,0:T(8,128)(2,1)S(1)} collective-permute-done((bf16[32,512]{1,0:T(8,128)(2,1)S(1)}, bf16[32,512]{1,0:T(8,128)(2,1)S(1)}, u32[]{:S(2)}, u32[]{:S(2)}) %collective-permute-start) | collective-permute-done | bytes 32800 | tf_op jit(solution)/shard_map/ppermute | solution.py:20
  20.5 2.8 %collective-permute-done.3.late_other = bf16[32,512]{1,0:T(8,128)(2,1)S(1)} collective-permute-done((bf16[32,512]{1,0:T(8,128)(2,1)S(1)}, bf16[32,512]{1,0:T(8,128)(2,1)S(1)}, u32[]{:S(2)}, u32[]{:S(2)}) %collective-permute-start.3) | collective-permute-done | bytes 32800 | tf_op jit(solution)/shard_map/ppermute | solution.py:20
  23.2 0.2 pack.1
  23.4 10.8 %all_to_all.9 = bf16[4,16,1024]{2,1,0:T(8,128)(2,1)S(1)} all-to-all(bf16[4,16,1024]{2,1,0:T(8,128)(2,1)S(1)} %bitcast.6), channel_id=1, replica_groups={{0,2,4,6},{1,3,5,7},{8,10,12,14},{9,11,13,15},{16,18,20,22},{17,19,21,2..., dimensions={0} | all-to-all | bytes 262144 | tf_op jit(solution)/shard_map/all_to_all | solution.py:317
  34.2 0.7 %bitcast_convert_fusion = f32[1,64,1024]{2,1,0:T(8,128)} fusion(bf16[1,64,1024]{2,1,0:T(8,128)(2,1)S(1)} %bitcast.7), kind=kLoop, calls=%fused_computation | loop fusion | flops 65536 | bytes 393216 | tf_op jit(solution)/shard_map/convert_element_type | solution.py:317
Async XLA Ops:
  0.0 8.9 %copy-start = (s32[8,64]{1,0:T(8,128)S(1)}, s32[8,64]{1,0:T(8,128)}, u32[]{:S(2)}) copy-start(s32[8,64]{1,0:T(8,128)} %lists.1) | copy-start | bytes 6148
  1.1 17.2 %collective-permute-start.1 = (bf16[4,1,32,16,128]{4,3,2,1,0:T(8,128)(2,1)S(1)}, bf16[4,1,32,16,128]{4,3,2,1,0:T(8,128)(2,1)S(1)}, u32[]{:S(2)}, u32[]{:S(2)}) collective-permute-start(bf16[4,1,32,16,128]{4,3,2,1,0:T(8,128)(2,1)S(1)} %space_slice.1), channel_id=1, source_target_pairs={{0,7},{1,0},{2,1},{3,2},{4,3},{5,4},{6,5},{7,6},{8,15},{9,8},{10,9... | collective-permute-start | bytes 1572872 | tf_op jit(solution)/shard_map/ppermute | solution.py:16
  8.2 10.1 %collective-permute-start.2 = (bf16[1,4,32,16,128]{4,3,2,1,0:T(8,128)(2,1)S(1)}, bf16[1,4,32,16,128]{4,3,2,1,0:T(8,128)(2,1)S(1)}, u32[]{:S(2)}, u32[]{:S(2)}) collective-permute-start(bf16[1,4,32,16,128]{4,3,2,1,0:T(8,128)(2,1)S(1)} %time_slice.1), channel_id=1, source_target_pairs={{0,24},{8,0},{16,8},{24,16},{1,25},{9,1},{17,9},{25,17},{2,26},{10... | collective-permute-start | bytes 1572872 | tf_op jit(solution)/shard_map/ppermute | solution.py:16
  16.5 4.0 %collective-permute-start = (bf16[32,512]{1,0:T(8,128)(2,1)S(1)}, bf16[32,512]{1,0:T(8,128)(2,1)S(1)}, u32[]{:S(2)}, u32[]{:S(2)}) collective-permute-start(bf16[32,512]{1,0:T(8,128)(2,1)S(1)} %get-tuple-element.9.early), channel_id=1, source_target_pairs={{0,1},{1,0},{2,3},{3,2},{4,5},{5,4},{6,7},{7,6},{8,9},{9,8},{10,11... | collective-permute-start | bytes 98312 | tf_op jit(solution)/shard_map/ppermute | solution.py:20
  19.3 4.0 %collective-permute-start.3 = (bf16[32,512]{1,0:T(8,128)(2,1)S(1)}, bf16[32,512]{1,0:T(8,128)(2,1)S(1)}, u32[]{:S(2)}, u32[]{:S(2)}) collective-permute-start(bf16[32,512]{1,0:T(8,128)(2,1)S(1)} %final.1.late), channel_id=1, source_target_pairs={{0,1},{1,0},{2,3},{3,2},{4,5},{5,4},{6,7},{7,6},{8,9},{9,8},{10,11... | collective-permute-start | bytes 98312 | tf_op jit(solution)/shard_map/ppermute | solution.py:20

commit v12 on v7

--- a/solution.py
+++ b/solution.py
@@ -1,3 +1,5 @@
+import functools
+
 import jax
 import jax.numpy as jnp
 from jax import lax
@@ -121,11 +123,13 @@
     return jnp.concatenate(pieces, axis=1)
 
 
-def slice_kernel(nulls, space_edge, time_edge, sems):
-    copies = [
-        pltpu.make_async_copy(nulls.at[:, pl.ds(0, 1)], space_edge, sems.at[0]),
-        pltpu.make_async_copy(nulls.at[pl.ds(0, 1)], time_edge, sems.at[1]),
-    ]
+def slice_kernel(nulls, *refs, sources):
+    edges, sems = refs[:-1], refs[-1]
+    copies = []
+    for edge, (start, count, at, space) in zip(edges, sources):
+        for row in range(count):
+            source = nulls.at[pl.ds(start + row, 1), pl.ds(at, space)]
+            copies.append(pltpu.make_async_copy(source, edge.at[pl.ds(row, 1)], sems.at[len(copies)]))
     for copy in copies:
         copy.start()
     for copy in copies:
@@ -214,16 +218,20 @@
     return group_rows(adjoint, jnp.concatenate(parts, axis=1), ROW_DIMS, vectors)
 
 
-def final_kernel(time_edge, space_edge, adjoint, late):
+def middle_kernel(space_edge, time_first, time_second, adjoint, found):
     vectors = space_edge.shape[3]
-    found = []
-    for a_x in range(2):
-        uppers = [time_edge.at[0, 2 * a_x + c] for c in range(2)]
-        found.append(edge_rows(uppers, adjoint[a_x], vectors))
-    for a_t in range(2):
-        uppers = [space_edge.at[2 * a_t + c, 0] for c in range(2)]
-        found.append(edge_rows(uppers, adjoint[2 + a_t], vectors))
-    late[...] = jnp.concatenate(found, axis=0).astype(jnp.bfloat16)
+    rows = []
+    for a_x, time_edge in enumerate((time_first, time_second)):
+        uppers = [time_edge.at[0, c] for c in range(2)]
+        rows.append(edge_rows(uppers, adjoint[a_x], vectors))
+    rows.append(edge_rows([space_edge.at[c, 0] for c in range(2)], adjoint[2], vectors))
+    found[...] = jnp.concatenate(rows, axis=0)
+
+
+def final_kernel(space_edge, adjoint, found, late):
+    vectors = space_edge.shape[3]
+    rows = edge_rows([space_edge.at[c, 0] for c in range(2)], adjoint[3], vectors)
+    late[...] = jnp.concatenate([found[...], rows], axis=0).astype(jnp.bfloat16)
 
 
 def pack_kernel(picks, early, early_other, late, late_other, *packed):
@@ -237,12 +245,22 @@
             out[:, pl.ds(half * width, width)] = mine.astype(jnp.bfloat16)
 
 
-def unpack_kernel(place, *refs):
+def unpack_kernel(place, *refs, turns):
     pair = place[0] // 2
     result = refs[-1]
-    for turn, arrived in enumerate(refs[-2::-1]):
+    for turn, arrived in zip(turns, refs[:-1]):
         source = jnp.bitwise_xor(pair, turn)
         result[pl.ds(pl.multiple_of(source * 2 * MOST, 2 * MOST), 2 * MOST), :] = arrived[...].astype(jnp.float32)
+
+
+def finish_kernel(place, arrived, unfinished, result, rows, sem, turn):
+    source = jnp.bitwise_xor(place[0] // 2, turn)
+    rows[...] = arrived[...].astype(jnp.float32)
+    copy = pltpu.make_async_copy(
+        rows, result.at[pl.ds(pl.multiple_of(source * 2 * MOST, 2 * MOST), 2 * MOST)], sem
+    )
+    copy.start()
+    copy.wait()
 
 
 def on_device(nulls, time_links, space_links, owner_lists):
@@ -260,21 +278,30 @@
     roomy = pltpu.CompilerParams(vmem_limit_bytes=51 * 1024 * 1024)
     modest = pltpu.CompilerParams(vmem_limit_bytes=24 * 1024 * 1024)
     first = pltpu.CompilerParams(vmem_limit_bytes=52 * 1024 * 1024)
-    space_edge, time_edge = pl.pallas_call(
-        slice_kernel,
-        in_specs=[outside],
-        out_specs=[vmem] * 2,
-        out_shape=[
-            jax.ShapeDtypeStruct((time_count, 1, sites, vectors, width), nulls.dtype),
-            jax.ShapeDtypeStruct((1, space_count, sites, vectors, width), nulls.dtype),
-        ],
-        scratch_shapes=[pltpu.SemaphoreType.DMA((2,))],
-        compiler_params=first,
-        cost_estimate=pl.CostEstimate(flops=1000, bytes_accessed=1000, transcendentals=0),
-        name="slices",
-    )(nulls)
-    edge_time = shifted(time_edge, "ta", -1)
-    edge_space = shifted(space_edge, "xyz", -1)
+    tiny = pl.CostEstimate(flops=1000, bytes_accessed=1000, transcendentals=0)
+    half_time = time_count // 2
+
+    def sliced(name, *sources):
+        shapes = [(count, space, sites, vectors, width) for _, count, _, space in sources]
+        return pl.pallas_call(
+            functools.partial(slice_kernel, sources=sources),
+            in_specs=[outside],
+            out_specs=[vmem] * len(sources),
+            out_shape=[jax.ShapeDtypeStruct(shape, nulls.dtype) for shape in shapes],
+            scratch_shapes=[pltpu.SemaphoreType.DMA((sum(source[1] for source in sources),))],
+            compiler_params=first,
+            cost_estimate=tiny,
+            name=name,
+        )(nulls)
+
+    half_space = space_count // 2
+    (space_first,) = sliced("slice_first", (0, half_time, 0, 1))
+    space_second, time_first, time_second = sliced(
+        "slice_rest", (half_time, half_time, 0, 1), (0, 1, 0, half_space), (0, 1, half_space, half_space)
+    )
+    edge_first = shifted(space_first, "xyz", -1)
+    edge_times = [shifted(time_first, "ta", -1), shifted(time_second, "ta", -1)]
+    edge_second = shifted(space_second, "xyz", -1)
     early, adjoint, picks = pl.pallas_call(
         inner_kernel,
         in_specs=[smem, vmem, outside, outside, outside],
@@ -292,18 +319,27 @@
             pltpu.SemaphoreType.DMA((17,)),
         ],
         compiler_params=roomy,
-        cost_estimate=pl.CostEstimate(flops=1000, bytes_accessed=1000, transcendentals=0),
+        cost_estimate=tiny,
         name="inner",
     )(place, owner_lists, nulls, time_links, space_links)
+    found = pl.pallas_call(
+        middle_kernel,
+        in_specs=[vmem] * 4,
+        out_specs=vmem,
+        out_shape=jax.ShapeDtypeStruct((3 * aggs, wide), jnp.float32),
+        compiler_params=modest,
+        cost_estimate=tiny,
+        name="middle",
+    )(edge_first, *edge_times, adjoint)
     late = pl.pallas_call(
         final_kernel,
         in_specs=[vmem] * 3,
         out_specs=vmem,
         out_shape=jax.ShapeDtypeStruct((4 * aggs, wide), jnp.bfloat16),
         compiler_params=modest,
-        cost_estimate=pl.CostEstimate(flops=1000, bytes_accessed=1000, transcendentals=0),
+        cost_estimate=tiny,
         name="final",
-    )(edge_time, edge_space, adjoint)
+    )(edge_second, adjoint, found)
     early_other = crossed(early, "xyz", 1)
     late_other = crossed(late, "xyz", 1)
     pairs = shards // 2
@@ -313,20 +349,32 @@
         out_specs=[vmem] * pairs,
         out_shape=[jax.ShapeDtypeStruct((2 * MOST, 2 * wide), jnp.bfloat16)] * pairs,
         compiler_params=modest,
-        cost_estimate=pl.CostEstimate(flops=1000, bytes_accessed=1000, transcendentals=0),
+        cost_estimate=tiny,
         name="pack",
     )(picks, early, early_other, late, late_other)
-    arrived = [crossed(packed[turn], "xyz", 2 * turn) for turn in range(pairs - 1, 0, -1)]
-    arrived.append(packed[0])
+    turns = list(range(2, pairs)) + [1]
+    arrived = [crossed(packed[turn], "xyz", 2 * turn) for turn in turns]
+    whole = jax.ShapeDtypeStruct((shards * MOST, 2 * wide), jnp.float32)
+    unfinished = pl.pallas_call(
+        functools.partial(unpack_kernel, turns=[0] + turns[:-1]),
+        in_specs=[smem] + [vmem] * (pairs - 1),
+        out_specs=vmem,
+        out_shape=whole,
+        compiler_params=modest,
+        cost_estimate=tiny,
+        name="unpack",
+    )(place, packed[0], *arrived[:-1])
     arrived = pl.pallas_call(
-        unpack_kernel,
-        in_specs=[smem] + [vmem] * pairs,
-        out_specs=vmem,
-        out_shape=jax.ShapeDtypeStruct((shards * MOST, 2 * wide), jnp.float32),
+        functools.partial(finish_kernel, turn=turns[-1]),
+        in_specs=[smem, vmem, outside],
+        out_specs=outside,
+        out_shape=whole,
+        scratch_shapes=[pltpu.VMEM((2 * MOST, 2 * wide), jnp.float32), pltpu.SemaphoreType.DMA],
+        input_output_aliases={2: 0},
         compiler_params=modest,
-        cost_estimate=pl.CostEstimate(flops=1000, bytes_accessed=1000, transcendentals=0),
-        name="unpack",
-    )(place, *arrived)
+        cost_estimate=tiny,
+        name="finish",
+    )(place, arrived[-1], unfinished)
     if shards * MOST == cap:
         result = arrived
     else:

time: 33.8 us -> 32.6 us (0.964)
  waiting for transfers between devices: 10.2 us -> 5.86 us
  Pallas kernels: 10.6 us -> 12.6 us
  starting transfers between devices: 12.1 us -> 13.9 us
  local copies, waits for them, and re-layouts: 0.69 us -> 0.01 us
    ppermute x2 -> x4, waiting for transfers between devices: 2.56 us -> 0.01 us  [shifted(): lax.ppermute(array, axis, [(i, (i + by) % count) for i in range(count)])]
    pallas_call x2 -> x5, Pallas kernels: 1.94 us -> 4.34 us  [the longest x2 2.19 us: sliced(): pl.pallas_call(functools.partial(slice_kernel, sources=sources), in_specs...]
    ppermute x5, waiting for transfers between devices: 7.67 us -> 5.85 us  [crossed(): lax.ppermute(array, axis, [(i, i ^ bits) for i in range(lax.axis_size(axi...]
    ppermute x2 -> x4, starting transfers between devices: 6.99 us -> 8.22 us  [shifted(): lax.ppermute(array, axis, [(i, (i + by) % count) for i in range(count)])]
    unnamed x2, local copies, waits for them, and re-layouts: 0.69 us -> 0.01 us
    ppermute x5, starting transfers between devices: 5.07 us -> 5.65 us  [crossed(): lax.ppermute(array, axis, [(i, i ^ bits) for i in range(lax.axis_size(axi...]
    pallas_call x1, Pallas kernels: 0.93 us -> 0.52 us  [on_device(): pl.pallas_call(final_kernel, in_specs=[vmem] * 3, out_specs=vmem, out_sha...]
  transfers between devices with their start and end apart: 7 -> 9, of which waited for: 4 -> 4; matrix products, arithmetic and copies ran while one was open for 0% -> 0% of each run, Pallas kernels for 25% -> 33%
where the time goes in v12:
time: 32.6 us; the launch traced here: 32.4 us
  starting transfers between devices  13.9 us (43%)
  Pallas kernels  12.6 us (39%)
  waiting for transfers between devices  5.86 us (18%)
    ppermute x4, starting transfers between devices, shifted(): lax.ppermute(array, axis, [(i, (i + by) % count) for i in range(count)])  8.22 us
    pallas_call x1, Pallas kernels, on_device(): pl.pallas_call(inner_kernel, in_specs=[smem, vmem, outside, outside, outs...  7.58 us
    ppermute x5, waiting for transfers between devices, crossed(): lax.ppermute(array, axis, [(i, i ^ bits) for i in range(lax.axis_size(axi...  5.85 us
    ppermute x5, starting transfers between devices, crossed(): lax.ppermute(array, axis, [(i, i ^ bits) for i in range(lax.axis_size(axi...  5.65 us
    pallas_call x2, Pallas kernels, sliced(): pl.pallas_call(functools.partial(slice_kernel, sources=sources), in_specs...  2.19 us
    pallas_call x1, Pallas kernels, on_device(): pl.pallas_call(middle_kernel, in_specs=[vmem] * 4, out_specs=vmem, out_sh...  0.79 us
    pallas_call x1, Pallas kernels, on_device(): pl.pallas_call(functools.partial(unpack_kernel, turns=[0] + turns[:-1]),...  0.72 us
  transfers between devices with their start and end apart: 9, of which 4 were waited for; matrix products, arithmetic and copies ran while one was open for 0% of the time, Pallas kernels for 33%

profile of v12, /device:TPU:0, one launch (start us, length us, event | category | flops | bytes accessed | tf_op | source)
XLA Modules:
  0.0 32.4 jit_solution(13571587440791227248)
XLA Ops:
  0.0 0.0 copy-start
  0.0 1.0 %slice_first.1 = bf16[2,1,32,16,128]{4,3,2,1,0:T(8,128)(2,1)S(1)} custom-call(bf16[4,4,32,16,128]{4,3,2,1,0:T(8,128)(2,1)} %nulls.5), custom_call_target="tpu_custom_call" | custom-call | flops 1000 | bytes 1000 | tf_op jit(solution)/shard_map/slice_first/pallas_call | solution.py:286
  1.0 6.1 %collective-permute-start.2 = (bf16[2,1,32,16,128]{4,3,2,1,0:T(8,128)(2,1)S(1)}, bf16[2,1,32,16,128]{4,3,2,1,0:T(8,128)(2,1)S(1)}, u32[]{:S(2)}, u32[]{:S(2)}) collective-permute-start(bf16[2,1,32,16,128]{4,3,2,1,0:T(8,128)(2,1)S(1)} %slice_first.1), channel_id=1, source_target_pairs={{0,7},{1,0},{2,1},{3,2},{4,3},{5,4},{6,5},{7,6},{8,15},{9,8},{10,9... | collective-permute-start | bytes 786440 | tf_op jit(solution)/shard_map/ppermute | solution.py:18
  7.1 1.2 %slice_rest.1 = (bf16[2,1,32,16,128]{4,3,2,1,0:T(8,128)(2,1)S(1)}, bf16[1,2,32,16,128]{4,3,2,1,0:T(8,128)(2,1)S(1)}, bf16[1,2,32,16,128]{4,3,2,1,0:T(8,128)(2,1)S(1)}) custom-call(bf16[4,4,32,16,128]{4,3,2,1,0:T(8,128)(2,1)} %nulls.5), custom_call_target="tpu_custom_call" | custom-call | flops 1000 | bytes 1000 | tf_op jit(solution)/shard_map/slice_rest/pallas_call | solution.py:286
  8.3 0.7 %collective-permute-start.3 = (bf16[1,2,32,16,128]{4,3,2,1,0:T(8,128)(2,1)S(1)}, bf16[1,2,32,16,128]{4,3,2,1,0:T(8,128)(2,1)S(1)}, u32[]{:S(2)}, u32[]{:S(2)}) collective-permute-start(bf16[1,2,32,16,128]{4,3,2,1,0:T(8,128)(2,1)S(1)} %get-tuple-element.19), channel_id=1, source_target_pairs={{0,24},{8,0},{16,8},{24,16},{1,25},{9,1},{17,9},{25,17},{2,26},{10... | collective-permute-start | bytes 786440 | tf_op jit(solution)/shard_map/ppermute | solution.py:18
  9.0 1.0 %collective-permute-start.4 = (bf16[1,2,32,16,128]{4,3,2,1,0:T(8,128)(2,1)S(1)}, bf16[1,2,32,16,128]{4,3,2,1,0:T(8,128)(2,1)S(1)}, u32[]{:S(2)}, u32[]{:S(2)}) collective-permute-start(bf16[1,2,32,16,128]{4,3,2,1,0:T(8,128)(2,1)S(1)} %get-tuple-element.20), channel_id=1, source_target_pairs={{0,24},{8,0},{16,8},{24,16},{1,25},{9,1},{17,9},{25,17},{2,26},{10... | collective-permute-start | bytes 786440 | tf_op jit(solution)/shard_map/ppermute | solution.py:18
  9.9 0.5 %collective-permute-start.1 = (bf16[2,1,32,16,128]{4,3,2,1,0:T(8,128)(2,1)S(1)}, bf16[2,1,32,16,128]{4,3,2,1,0:T(8,128)(2,1)S(1)}, u32[]{:S(2)}, u32[]{:S(2)}) collective-permute-start(bf16[2,1,32,16,128]{4,3,2,1,0:T(8,128)(2,1)S(1)} %get-tuple-element.17), channel_id=1, source_target_pairs={{0,7},{1,0},{2,1},{3,2},{4,3},{5,4},{6,5},{7,6},{8,15},{9,8},{10,9... | collective-permute-start | bytes 786440 | tf_op jit(solution)/shard_map/ppermute | solution.py:18
  10.4 0.0 copy-done
  10.4 7.6 %inner.1 = (bf16[32,512]{1,0:T(8,128)(2,1)S(1)}, bf16[4,256,1024]{2,1,0:T(8,128)(2,1)S(1)}, f32[2,64,64]{2,1,0:T(8,128)S(1)}) custom-call(s32[1]{0:T(128)} %bitcast.place, s32[8,64]{1,0:T(8,128)S(1)} %copy-done, bf16[4,4,32,16,128]{4,3,2,1,0:T(8,128)(2,1)} %nulls.5, bf16[2,4,32,64,128]{4,3,2,1,0:T(8,128)(2,1)} %time_links.1, ...), custom_call_target="tpu_custom_call" | custom-call | flops 1000 | bytes 1000 | tf_op jit(solution)/shard_map/inner/pallas_call | solution.py:305
  18.0 1.6 %collective-permute-start = (bf16[32,512]{1,0:T(8,128)(2,1)S(1)}, bf16[32,512]{1,0:T(8,128)(2,1)S(1)}, u32[]{:S(2)}, u32[]{:S(2)}) collective-permute-start(bf16[32,512]{1,0:T(8,128)(2,1)S(1)} %get-tuple-element.16.early), channel_id=1, source_target_pairs={{0,1},{1,0},{2,3},{3,2},{4,5},{5,4},{6,7},{7,6},{8,9},{9,8},{10,11... | collective-permute-start | bytes 98312 | tf_op jit(solution)/shard_map/ppermute | solution.py:22
  19.6 0.0 collective-permute-done.2.space_edge
  19.6 0.0 collective-permute-done.3.time_first
  19.6 0.0 collective-permute-done.4.time_second
  19.6 0.8 %middle.1.found = f32[24,512]{1,0:T(8,128)S(1)} custom-call(bf16[2,1,32,16,128]{4,3,2,1,0:T(8,128)(2,1)S(1)} %collective-permute-done.2.space_edge, bf16[1,2,32,16,128]{4,3,2,1,0:T(8,128)(2,1)S(1)} %collective-permute-done.3.time_first, bf16[1,2,32,16,128]{4,3,2,1,0:T(8,128)(2,1)S(1)} %collective-permute-done.4.time_second, ...), custom_call_target="tpu_custom_call" | custom-call | flops 1000 | bytes 1000 | tf_op jit(solution)/shard_map/middle/pallas_call | solution.py:325
  20.4 0.0 collective-permute-done.1.space_edge
  20.4 0.5 %final.1.late = bf16[32,512]{1,0:T(8,128)(2,1)S(1)} custom-call(bf16[2,1,32,16,128]{4,3,2,1,0:T(8,128)(2,1)S(1)} %collective-permute-done.1.space_edge, bf16[4,256,1024]{2,1,0:T(8,128)(2,1)S(1)} %get-tuple-element.18.adjoint, f32[24,512]{1,0:T(8,128)S(1)} %middle.1.found), custom_call_target="tpu_custom_call" | custom-call | flops 1000 | bytes 1000 | tf_op jit(solution)/shard_map/final/pallas_call | solution.py:334
  21.0 0.5 %collective-permute-start.5 = (bf16[32,512]{1,0:T(8,128)(2,1)S(1)}, bf16[32,512]{1,0:T(8,128)(2,1)S(1)}, u32[]{:S(2)}, u32[]{:S(2)}) collective-permute-start(bf16[32,512]{1,0:T(8,128)(2,1)S(1)} %final.1.late), channel_id=1, source_target_pairs={{0,1},{1,0},{2,3},{3,2},{4,5},{5,4},{6,7},{7,6},{8,9},{9,8},{10,11... | collective-permute-start | bytes 98312 | tf_op jit(solution)/shard_map/ppermute | solution.py:22
  21.5 0.5 %collective-permute-done.early_other = bf16[32,512]{1,0:T(8,128)(2,1)S(1)} collective-permute-done((bf16[32,512]{1,0:T(8,128)(2,1)S(1)}, bf16[32,512]{1,0:T(8,128)(2,1)S(1)}, u32[]{:S(2)}, u32[]{:S(2)}) %collective-permute-start) | collective-permute-done | bytes 32800 | tf_op jit(solution)/shard_map/ppermute | solution.py:22
  22.0 2.9 %collective-permute-done.5.late_other = bf16[32,512]{1,0:T(8,128)(2,1)S(1)} collective-permute-done((bf16[32,512]{1,0:T(8,128)(2,1)S(1)}, bf16[32,512]{1,0:T(8,128)(2,1)S(1)}, u32[]{:S(2)}, u32[]{:S(2)}) %collective-permute-start.5) | collective-permute-done | bytes 32800 | tf_op jit(solution)/shard_map/ppermute | solution.py:22
  24.9 0.2 pack.1
  25.0 0.1 collective-permute-start.7
  25.1 1.7 %collective-permute-start.8 = (bf16[16,1024]{1,0:T(8,128)(2,1)S(1)}, bf16[16,1024]{1,0:T(8,128)(2,1)S(1)}, u32[]{:S(2)}, u32[]{:S(2)}) collective-permute-start(bf16[16,1024]{1,0:T(8,128)(2,1)S(1)} %get-tuple-element.24), channel_id=1, source_target_pairs={{0,6},{1,7},{2,4},{3,5},{4,2},{5,3},{6,0},{7,1},{8,14},{9,15},{10,... | collective-permute-start | bytes 98312 | tf_op jit(solution)/shard_map/ppermute | solution.py:22
  26.8 1.8 %collective-permute-start.6 = (bf16[16,1024]{1,0:T(8,128)(2,1)S(1)}, bf16[16,1024]{1,0:T(8,128)(2,1)S(1)}, u32[]{:S(2)}, u32[]{:S(2)}) collective-permute-start(bf16[16,1024]{1,0:T(8,128)(2,1)S(1)} %get-tuple-element.21), channel_id=1, source_target_pairs={{0,2},{1,3},{2,0},{3,1},{4,6},{5,7},{6,4},{7,5},{8,10},{9,11},{10,... | collective-permute-start | bytes 98312 | tf_op jit(solution)/shard_map/ppermute | solution.py:22
  28.6 1.3 %collective-permute-done.7.refs_1_ = bf16[16,1024]{1,0:T(8,128)(2,1)S(1)} collective-permute-done((bf16[16,1024]{1,0:T(8,128)(2,1)S(1)}, bf16[16,1024]{1,0:T(8,128)(2,1)S(1)}, u32[]{:S(2)}, u32[]{:S(2)}) %collective-permute-start.7) | collective-permute-done | bytes 32800 | tf_op jit(solution)/shard_map/ppermute | solution.py:22
  29.9 1.1 %collective-permute-done.8.refs_2_ = bf16[16,1024]{1,0:T(8,128)(2,1)S(1)} collective-permute-done((bf16[16,1024]{1,0:T(8,128)(2,1)S(1)}, bf16[16,1024]{1,0:T(8,128)(2,1)S(1)}, u32[]{:S(2)}, u32[]{:S(2)}) %collective-permute-start.8) | collective-permute-done | bytes 32800 | tf_op jit(solution)/shard_map/ppermute | solution.py:22
  31.0 0.7 %unpack.1.unfinished = f32[64,1024]{1,0:T(8,128)} custom-call(s32[1]{0:T(128)} %bitcast.place, bf16[16,1024]{1,0:T(8,128)(2,1)S(1)} %get-tuple-element.22.refs_0_, bf16[16,1024]{1,0:T(8,128)(2,1)S(1)} %collective-permute-done.7.refs_1_, bf16[16,1024]{1,0:T(8,128)(2,1)S(1)} %collective-permute-done.8.refs_2_), custom_call_target="tpu_custom_call" | custom-call | flops 1000 | bytes 1000 | tf_op jit(solution)/shard_map/unpack/pallas_call | solution.py:358
  31.8 0.0 collective-permute-done.6.arrived
  31.8 0.6 %finish.1 = f32[64,1024]{1,0:T(8,128)} custom-call(s32[1]{0:T(128)} %bitcast.place, bf16[16,1024]{1,0:T(8,128)(2,1)S(1)} %collective-permute-done.6.arrived, f32[64,1024]{1,0:T(8,128)} %unpack.1.unfinished), custom_call_target="tpu_custom_call", output_to_operand_aliasing={{}: (2, {})} | custom-call | flops 1000 | bytes 1000 | tf_op jit(solution)/shard_map/finish/pallas_call | solution.py:367
Async XLA Ops:
  0.0 10.4 %copy-start = (s32[8,64]{1,0:T(8,128)S(1)}, s32[8,64]{1,0:T(8,128)}, u32[]{:S(2)}) copy-start(s32[8,64]{1,0:T(8,128)} %lists.1) | copy-start | bytes 6148
  1.0 18.6 %collective-permute-start.2 = (bf16[2,1,32,16,128]{4,3,2,1,0:T(8,128)(2,1)S(1)}, bf16[2,1,32,16,128]{4,3,2,1,0:T(8,128)(2,1)S(1)}, u32[]{:S(2)}, u32[]{:S(2)}) collective-permute-start(bf16[2,1,32,16,128]{4,3,2,1,0:T(8,128)(2,1)S(1)} %slice_first.1), channel_id=1, source_target_pairs={{0,7},{1,0},{2,1},{3,2},{4,3},{5,4},{6,5},{7,6},{8,15},{9,8},{10,9... | collective-permute-start | bytes 786440 | tf_op jit(solution)/shard_map/ppermute | solution.py:18
  8.3 11.4 %collective-permute-start.3 = (bf16[1,2,32,16,128]{4,3,2,1,0:T(8,128)(2,1)S(1)}, bf16[1,2,32,16,128]{4,3,2,1,0:T(8,128)(2,1)S(1)}, u32[]{:S(2)}, u32[]{:S(2)}) collective-permute-start(bf16[1,2,32,16,128]{4,3,2,1,0:T(8,128)(2,1)S(1)} %get-tuple-element.19), channel_id=1, source_target_pairs={{0,24},{8,0},{16,8},{24,16},{1,25},{9,1},{17,9},{25,17},{2,26},{10... | collective-permute-start | bytes 786440 | tf_op jit(solution)/shard_map/ppermute | solution.py:18
  9.0 10.7 %collective-permute-start.4 = (bf16[1,2,32,16,128]{4,3,2,1,0:T(8,128)(2,1)S(1)}, bf16[1,2,32,16,128]{4,3,2,1,0:T(8,128)(2,1)S(1)}, u32[]{:S(2)}, u32[]{:S(2)}) collective-permute-start(bf16[1,2,32,16,128]{4,3,2,1,0:T(8,128)(2,1)S(1)} %get-tuple-element.20), channel_id=1, source_target_pairs={{0,24},{8,0},{16,8},{24,16},{1,25},{9,1},{17,9},{25,17},{2,26},{10... | collective-permute-start | bytes 786440 | tf_op jit(solution)/shard_map/ppermute | solution.py:18
  9.9 10.5 %collective-permute-start.1 = (bf16[2,1,32,16,128]{4,3,2,1,0:T(8,128)(2,1)S(1)}, bf16[2,1,32,16,128]{4,3,2,1,0:T(8,128)(2,1)S(1)}, u32[]{:S(2)}, u32[]{:S(2)}) collective-permute-start(bf16[2,1,32,16,128]{4,3,2,1,0:T(8,128)(2,1)S(1)} %get-tuple-element.17), channel_id=1, source_target_pairs={{0,7},{1,0},{2,1},{3,2},{4,3},{5,4},{6,5},{7,6},{8,15},{9,8},{10,9... | collective-permute-start | bytes 786440 | tf_op jit(solution)/shard_map/ppermute | solution.py:18
  18.0 4.0 %collective-permute-start = (bf16[32,512]{1,0:T(8,128)(2,1)S(1)}, bf16[32,512]{1,0:T(8,128)(2,1)S(1)}, u32[]{:S(2)}, u32[]{:S(2)}) collective-permute-start(bf16[32,512]{1,0:T(8,128)(2,1)S(1)} %get-tuple-element.16.early), channel_id=1, source_target_pairs={{0,1},{1,0},{2,3},{3,2},{4,5},{5,4},{6,7},{7,6},{8,9},{9,8},{10,11... | collective-permute-start | bytes 98312 | tf_op jit(solution)/shard_map/ppermute | solution.py:22
  21.0 3.9 %collective-permute-start.5 = (bf16[32,512]{1,0:T(8,128)(2,1)S(1)}, bf16[32,512]{1,0:T(8,128)(2,1)S(1)}, u32[]{:S(2)}, u32[]{:S(2)}) collective-permute-start(bf16[32,512]{1,0:T(8,128)(2,1)S(1)} %final.1.late), channel_id=1, source_target_pairs={{0,1},{1,0},{2,3},{3,2},{4,5},{5,4},{6,7},{7,6},{8,9},{9,8},{10,11... | collective-permute-start | bytes 98312 | tf_op jit(solution)/shard_map/ppermute | solution.py:22
  25.0 4.9 %collective-permute-start.7 = (bf16[16,1024]{1,0:T(8,128)(2,1)S(1)}, bf16[16,1024]{1,0:T(8,128)(2,1)S(1)}, u32[]{:S(2)}, u32[]{:S(2)}) collective-permute-start(bf16[16,1024]{1,0:T(8,128)(2,1)S(1)} %get-tuple-element.23), channel_id=1, source_target_pairs={{0,4},{1,5},{2,6},{3,7},{4,0},{5,1},{6,2},{7,3},{8,12},{9,13},{10,... | collective-permute-start | bytes 98312 | tf_op jit(solution)/shard_map/ppermute | solution.py:22
  25.1 5.9 %collective-permute-start.8 = (bf16[16,1024]{1,0:T(8,128)(2,1)S(1)}, bf16[16,1024]{1,0:T(8,128)(2,1)S(1)}, u32[]{:S(2)}, u32[]{:S(2)}) collective-permute-start(bf16[16,1024]{1,0:T(8,128)(2,1)S(1)} %get-tuple-element.24), channel_id=1, source_target_pairs={{0,6},{1,7},{2,4},{3,5},{4,2},{5,3},{6,0},{7,1},{8,14},{9,15},{10,... | collective-permute-start | bytes 98312 | tf_op jit(solution)/shard_map/ppermute | solution.py:22
  26.8 4.9 %collective-permute-start.6 = (bf16[16,1024]{1,0:T(8,128)(2,1)S(1)}, bf16[16,1024]{1,0:T(8,128)(2,1)S(1)}, u32[]{:S(2)}, u32[]{:S(2)}) collective-permute-start(bf16[16,1024]{1,0:T(8,128)(2,1)S(1)} %get-tuple-element.21), channel_id=1, source_target_pairs={{0,2},{1,3},{2,0},{3,1},{4,6},{5,7},{6,4},{7,5},{8,10},{9,11},{10,... | collective-permute-start | bytes 98312 | tf_op jit(solution)/shard_map/ppermute | solution.py:22

commit v13 on v12

--- a/solution.py
+++ b/solution.py
@@ -42,9 +42,10 @@
     sites, vectors, width = lower.shape
     half = width // 2
     aggs = sites // SIDE
+    lanes = aggs * vectors
     sign = signs((vectors, width), jnp.bfloat16)
     zero = jnp.zeros((vectors, width), jnp.bfloat16)
-    owner = lax.broadcasted_iota(jnp.int32, (half, 2 * aggs * vectors), 1) // (2 * vectors) % (aggs // 2)
+    owner = lax.broadcasted_iota(jnp.int32, (half, 2 * lanes), 1) // (2 * vectors) % (aggs // 2)
     for part in range(SIDE):
         at = (slot * SIDE + part) * width
         mats = []
@@ -57,17 +58,14 @@
                 rows.append(jnp.concatenate([value, zero] if agg % 2 == 0 else [zero, value], axis=1))
             if agg % 2 == 0:
                 mats.append(jnp.concatenate([links[site], links[site + SIDE]], axis=1))
-            low = lower[site]
-            left_ref[pl.ds(agg * 2 * vectors, 2 * vectors), pl.ds(at, width)] = jnp.concatenate(
-                [low, -sign * swapped(low)], axis=0
-            )
+            left_ref[pl.ds(agg * vectors, vectors), pl.ds(at, width)] = lower[site]
         images = dot(jnp.concatenate(mats, axis=0), jnp.concatenate(plain + crossed, axis=0), ROW_DIMS)
         own = images[:half]
         for pair in range(1, aggs // 2):
             own = jnp.where(owner == pair, images[pair * half : (pair + 1) * half], own)
         own = own.astype(jnp.bfloat16)
-        right_ref[pl.ds(at, half), :] = own[:, : aggs * vectors]
-        right_ref[pl.ds(at + half, half), :] = own[:, aggs * vectors :]
+        right_ref[pl.ds(at, half), :] = own
+        right_ref[pl.ds(at + half, half), :] = jnp.concatenate([own[:, lanes:], -own[:, :lanes]], axis=1)
 
 
 def adjoint_item(links, lower, slot, left_ref):
@@ -94,23 +92,23 @@
             top = part * 2 * vectors
             mine = prod[top : top + 2 * vectors, part // 2 * width : (part // 2 + 1) * width]
             adj = sign * mine[:vectors] + swapped(mine[vectors:])
-            both = jnp.concatenate([adj, -sign * swapped(adj)], axis=0).astype(jnp.bfloat16)
-            left_ref[pl.ds(agg * 2 * vectors, 2 * vectors), pl.ds((slot * SIDE + part) * width, width)] = both
+            left_ref[pl.ds(agg * vectors, vectors), pl.ds((slot * SIDE + part) * width, width)] = adj.astype(jnp.bfloat16)
 
 
 def group_rows(left, right, dims, vectors):
     full = dot(left, right, dims)
-    aggs = full.shape[1] // vectors
-    lanes = lax.broadcasted_iota(jnp.int32, (2 * vectors, full.shape[1]), 1) // vectors
-    own = jnp.zeros((2 * vectors, full.shape[1]), jnp.float32)
-    for agg in range(aggs):
-        own = jnp.where(lanes == agg, full[agg * 2 * vectors : (agg + 1) * 2 * vectors], own)
+    total = full.shape[1] // 2
+    aggs = total // vectors
+    lanes = lax.broadcasted_iota(jnp.int32, (vectors, 2 * total), 1) // vectors % aggs
+    own = full[:vectors]
+    for agg in range(1, aggs):
+        own = jnp.where(lanes == agg, full[agg * vectors : (agg + 1) * vectors], own)
     pieces = []
-    lane_group = lax.broadcasted_iota(jnp.int32, (aggs, full.shape[1]), 1) // vectors
-    sub = lax.broadcasted_iota(jnp.int32, (aggs, full.shape[1]), 0)
-    total = full.shape[1]
+    lane_group = lax.broadcasted_iota(jnp.int32, (aggs, total), 1) // vectors
+    sub = lax.broadcasted_iota(jnp.int32, (aggs, total), 0)
     for piece in range(2 * vectors // aggs):
-        value = own[piece * aggs : (piece + 1) * aggs]
+        part, row = divmod(piece * aggs, vectors)
+        value = own[row : row + aggs, part * total : (part + 1) * total]
         step = 1
         while step < aggs:
             sub_bit = (sub // step) % 2
@@ -136,26 +134,7 @@
         copy.wait()
 
 
-def inner_kernel(place, lists, nulls, time_links, space_links, early, adjoint, picks, links, vecs, left, right, sems):
-    time_count, space_count, sites, vectors, width = nulls.shape
-    copies = []
-    base = pltpu.make_async_copy(nulls, vecs, sems.at[16])
-    base.start()
-
-    def fetch(source):
-        slot = len(copies)
-        copy = pltpu.make_async_copy(source, links.at[slot], sems.at[slot])
-        copy.start()
-        copies.append(copy)
-
-    for x in range(4):
-        fetch(time_links.at[0, x])
-    for t in range(4):
-        fetch(space_links.at[t, 0])
-    for x in range(4):
-        fetch(time_links.at[1, x])
-    for t in range(4):
-        fetch(space_links.at[t, 1])
+def choose_rows(place, lists, picks):
     me = place[0]
     shards, cap = lists.shape
     count = picks.shape[2] // 2
@@ -181,7 +160,33 @@
             rows = pl.ds((2 * turn + parity) * MOST, MOST)
             picks[0, rows, :] = jnp.where(here & (inside == chosen), 1.0, 0.0)
             picks[1, rows, :] = jnp.where(here & (turned == chosen), 1.0, 0.0)
-    base.wait()
+
+
+def inner_kernel(nulls, time_links, space_links, early, adjoint, links, vecs, left, right, sems):
+    time_count, space_count, sites, vectors, width = nulls.shape
+    copies = []
+    bases = [pltpu.make_async_copy(nulls.at[t], vecs.at[t], sems.at[16 + t]) for t in range(4)]
+    bases[1].start()
+    bases[2].start()
+
+    def fetch(source):
+        slot = len(copies)
+        copy = pltpu.make_async_copy(source, links.at[slot], sems.at[slot])
+        copy.start()
+        copies.append(copy)
+
+    for x in range(4):
+        fetch(time_links.at[0, x])
+    bases[0].start()
+    bases[3].start()
+    for t in range(4):
+        fetch(space_links.at[t, 0])
+    for x in range(4):
+        fetch(time_links.at[1, x])
+    for t in range(4):
+        fetch(space_links.at[t, 1])
+    bases[1].wait()
+    bases[2].wait()
     found = []
     for a_x in range(2):
         copies[2 * a_x].wait()
@@ -190,6 +195,8 @@
             x = 2 * a_x + c
             image_item(links.at[x], vecs.at[1, x], vecs.at[2, x], c, left, right)
         found.append(group_rows(left[...], right[...], MAT_DIMS, vectors))
+    bases[0].wait()
+    bases[3].wait()
     for a_t in range(2):
         copies[4 + 2 * a_t].wait()
         copies[5 + 2 * a_t].wait()
@@ -209,16 +216,20 @@
 
 
 def edge_rows(uppers, adjoint, vectors):
+    width = uppers[0].shape[-1]
+    sign = signs((vectors, width), jnp.bfloat16)
     parts = []
     for upper in uppers:
         sites = upper.shape[0]
         for site in range(SIDE):
             rows = [upper[agg * SIDE + site] for agg in range(sites // SIDE)]
-            parts.append(jnp.concatenate(rows, axis=0))
+            turned = [sign * swapped(row) for row in rows]
+            parts.append(jnp.concatenate(rows + turned, axis=0))
     return group_rows(adjoint, jnp.concatenate(parts, axis=1), ROW_DIMS, vectors)
 
 
-def middle_kernel(space_edge, time_first, time_second, adjoint, found):
+def middle_kernel(place, lists, space_edge, time_first, time_second, adjoint, found, picks):
+    choose_rows(place, lists, picks)
     vectors = space_edge.shape[3]
     rows = []
     for a_x, time_edge in enumerate((time_first, time_second)):
@@ -251,16 +262,6 @@
     for turn, arrived in zip(turns, refs[:-1]):
         source = jnp.bitwise_xor(pair, turn)
         result[pl.ds(pl.multiple_of(source * 2 * MOST, 2 * MOST), 2 * MOST), :] = arrived[...].astype(jnp.float32)
-
-
-def finish_kernel(place, arrived, unfinished, result, rows, sem, turn):
-    source = jnp.bitwise_xor(place[0] // 2, turn)
-    rows[...] = arrived[...].astype(jnp.float32)
-    copy = pltpu.make_async_copy(
-        rows, result.at[pl.ds(pl.multiple_of(source * 2 * MOST, 2 * MOST), 2 * MOST)], sem
-    )
-    copy.start()
-    copy.wait()
 
 
 def on_device(nulls, time_links, space_links, owner_lists):
@@ -295,42 +296,47 @@
         )(nulls)
 
     half_space = space_count // 2
-    (space_first,) = sliced("slice_first", (0, half_time, 0, 1))
-    space_second, time_first, time_second = sliced(
-        "slice_rest", (half_time, half_time, 0, 1), (0, 1, 0, half_space), (0, 1, half_space, half_space)
+    space_first, space_second, time_first, time_second = sliced(
+        "slices",
+        (0, half_time, 0, 1),
+        (half_time, half_time, 0, 1),
+        (0, 1, 0, half_space),
+        (0, 1, half_space, half_space),
     )
     edge_first = shifted(space_first, "xyz", -1)
     edge_times = [shifted(time_first, "ta", -1), shifted(time_second, "ta", -1)]
     edge_second = shifted(space_second, "xyz", -1)
-    early, adjoint, picks = pl.pallas_call(
+    early, adjoint = pl.pallas_call(
         inner_kernel,
-        in_specs=[smem, vmem, outside, outside, outside],
-        out_specs=[vmem] * 3,
+        in_specs=[outside] * 3,
+        out_specs=[vmem] * 2,
         out_shape=[
             jax.ShapeDtypeStruct((4 * aggs, wide), jnp.bfloat16),
-            jax.ShapeDtypeStruct((4, 2 * vectors * aggs, 8 * width), jnp.bfloat16),
-            jax.ShapeDtypeStruct((2, shards * MOST, 2 * local_count), jnp.float32),
+            jax.ShapeDtypeStruct((4, vectors * aggs, 8 * width), jnp.bfloat16),
         ],
         scratch_shapes=[
             pltpu.VMEM((16, sites, half, width), jnp.bfloat16),
             pltpu.VMEM(nulls.shape, nulls.dtype),
-            pltpu.VMEM((2 * vectors * aggs, 8 * width), jnp.bfloat16),
-            pltpu.VMEM((8 * width, vectors * aggs), jnp.bfloat16),
-            pltpu.SemaphoreType.DMA((17,)),
+            pltpu.VMEM((vectors * aggs, 8 * width), jnp.bfloat16),
+            pltpu.VMEM((8 * width, 2 * vectors * aggs), jnp.bfloat16),
+            pltpu.SemaphoreType.DMA((20,)),
         ],
         compiler_params=roomy,
         cost_estimate=tiny,
         name="inner",
-    )(place, owner_lists, nulls, time_links, space_links)
-    found = pl.pallas_call(
+    )(nulls, time_links, space_links)
+    found, picks = pl.pallas_call(
         middle_kernel,
-        in_specs=[vmem] * 4,
-        out_specs=vmem,
-        out_shape=jax.ShapeDtypeStruct((3 * aggs, wide), jnp.float32),
+        in_specs=[smem] + [vmem] * 5,
+        out_specs=[vmem] * 2,
+        out_shape=[
+            jax.ShapeDtypeStruct((3 * aggs, wide), jnp.float32),
+            jax.ShapeDtypeStruct((2, shards * MOST, 2 * local_count), jnp.float32),
+        ],
         compiler_params=modest,
         cost_estimate=tiny,
         name="middle",
-    )(edge_first, *edge_times, adjoint)
+    )(place, owner_lists, edge_first, *edge_times, adjoint)
     late = pl.pallas_call(
         final_kernel,
         in_specs=[vmem] * 3,
@@ -354,27 +360,15 @@
     )(picks, early, early_other, late, late_other)
     turns = list(range(2, pairs)) + [1]
     arrived = [crossed(packed[turn], "xyz", 2 * turn) for turn in turns]
-    whole = jax.ShapeDtypeStruct((shards * MOST, 2 * wide), jnp.float32)
-    unfinished = pl.pallas_call(
-        functools.partial(unpack_kernel, turns=[0] + turns[:-1]),
-        in_specs=[smem] + [vmem] * (pairs - 1),
+    arrived = pl.pallas_call(
+        functools.partial(unpack_kernel, turns=turns + [0]),
+        in_specs=[smem] + [vmem] * pairs,
         out_specs=vmem,
-        out_shape=whole,
+        out_shape=jax.ShapeDtypeStruct((shards * MOST, 2 * wide), jnp.float32),
         compiler_params=modest,
         cost_estimate=tiny,
         name="unpack",
-    )(place, packed[0], *arrived[:-1])
-    arrived = pl.pallas_call(
-        functools.partial(finish_kernel, turn=turns[-1]),
-        in_specs=[smem, vmem, outside],
-        out_specs=outside,
-        out_shape=whole,
-        scratch_shapes=[pltpu.VMEM((2 * MOST, 2 * wide), jnp.float32), pltpu.SemaphoreType.DMA],
-        input_output_aliases={2: 0},
-        compiler_params=modest,
-        cost_estimate=tiny,
-        name="finish",
-    )(place, arrived[-1], unfinished)
+    )(place, *arrived, packed[0])
     if shards * MOST == cap:
         result = arrived
     else:

time: 32.6 us -> 32 us (0.982)
  Pallas kernels: 12.6 us -> 10.9 us
  waiting for transfers between devices: 5.86 us -> 6.85 us
    ppermute x5, waiting for transfers between devices: 5.85 us -> 6.84 us  [crossed(): lax.ppermute(array, axis, [(i, i ^ bits) for i in range(lax.axis_size(axi...]
    pallas_call x4 -> x3, Pallas kernels: 9.74 us -> 8.83 us  [the longest x1 7.19 us: on_device(): pl.pallas_call(inner_kernel, in_specs=[outside] * 3, out_specs=[vmem] * 2...]
    pallas_call x2 -> x1, Pallas kernels: 2.19 us -> 1.34 us  [sliced(): pl.pallas_call(functools.partial(slice_kernel, sources=sources), in_specs...]
  transfers between devices with their start and end apart: 9 -> 9, of which waited for: 4 -> 5; matrix products, arithmetic and copies ran while one was open for 0% -> 0% of each run, Pallas kernels for 33% -> 27%
where the time goes in v13:
time: 32 us; the launch traced here: 31.9 us
  starting transfers between devices  14.1 us (44%)
  Pallas kernels  10.9 us (34%)
  waiting for transfers between devices  6.85 us (21%)
    ppermute x4, starting transfers between devices, shifted(): lax.ppermute(array, axis, [(i, (i + by) % count) for i in range(count)])  8.17 us
    pallas_call x1, Pallas kernels, on_device(): pl.pallas_call(inner_kernel, in_specs=[outside] * 3, out_specs=[vmem] * 2...  7.19 us
    ppermute x5, waiting for transfers between devices, crossed(): lax.ppermute(array, axis, [(i, i ^ bits) for i in range(lax.axis_size(axi...  6.84 us
    ppermute x5, starting transfers between devices, crossed(): lax.ppermute(array, axis, [(i, i ^ bits) for i in range(lax.axis_size(axi...  5.88 us
    pallas_call x1, Pallas kernels, sliced(): pl.pallas_call(functools.partial(slice_kernel, sources=sources), in_specs...  1.34 us
    pallas_call x1, Pallas kernels, on_device(): pl.pallas_call(middle_kernel, in_specs=[smem] + [vmem] * 5, out_specs=[vm...  0.92 us
    pallas_call x1, Pallas kernels, on_device(): pl.pallas_call(functools.partial(unpack_kernel, turns=turns + [0]), in_sp...  0.73 us
  transfers between devices with their start and end apart: 9, of which 5 were waited for; matrix products, arithmetic and copies ran while one was open for 0% of the time, Pallas kernels for 27%

profile of v13, /device:TPU:0, one launch (start us, length us, event | category | flops | bytes accessed | tf_op | source)
XLA Modules:
  0.0 31.9 jit_solution(10773984274786306745)
XLA Ops:
  0.0 1.3 %slices.1 = (bf16[2,1,32,16,128]{4,3,2,1,0:T(8,128)(2,1)S(1)}, bf16[2,1,32,16,128]{4,3,2,1,0:T(8,128)(2,1)S(1)}, bf16[1,2,32,16,128]{4,3,2,1,0:T(8,128)(2,1)S(1)}, bf16[1,2,32,16,128]{4,3,2,1,0:T(8,128)(2,1)S(1)}) custom-call(bf16[4,4,32,16,128]{4,3,2,1,0:T(8,128)(2,1)} %nulls.3), custom_call_target="tpu_custom_call" | custom-call | flops 1000 | bytes 1000 | tf_op jit(solution)/shard_map/slices/pallas_call | solution.py:287
  1.3 6.1 %collective-permute-start = (bf16[2,1,32,16,128]{4,3,2,1,0:T(8,128)(2,1)S(1)}, bf16[2,1,32,16,128]{4,3,2,1,0:T(8,128)(2,1)S(1)}, u32[]{:S(2)}, u32[]{:S(2)}) collective-permute-start(bf16[2,1,32,16,128]{4,3,2,1,0:T(8,128)(2,1)S(1)} %get-tuple-element.17), channel_id=1, source_target_pairs={{0,7},{1,0},{2,1},{3,2},{4,3},{5,4},{6,5},{7,6},{8,15},{9,8},{10,9... | collective-permute-start | bytes 786440 | tf_op jit(solution)/shard_map/ppermute | solution.py:18
  7.4 0.7 %collective-permute-start.1 = (bf16[1,2,32,16,128]{4,3,2,1,0:T(8,128)(2,1)S(1)}, bf16[1,2,32,16,128]{4,3,2,1,0:T(8,128)(2,1)S(1)}, u32[]{:S(2)}, u32[]{:S(2)}) collective-permute-start(bf16[1,2,32,16,128]{4,3,2,1,0:T(8,128)(2,1)S(1)} %get-tuple-element.18), channel_id=1, source_target_pairs={{0,24},{8,0},{16,8},{24,16},{1,25},{9,1},{17,9},{25,17},{2,26},{10... | collective-permute-start | bytes 786440 | tf_op jit(solution)/shard_map/ppermute | solution.py:18
  8.1 1.0 %collective-permute-start.2 = (bf16[1,2,32,16,128]{4,3,2,1,0:T(8,128)(2,1)S(1)}, bf16[1,2,32,16,128]{4,3,2,1,0:T(8,128)(2,1)S(1)}, u32[]{:S(2)}, u32[]{:S(2)}) collective-permute-start(bf16[1,2,32,16,128]{4,3,2,1,0:T(8,128)(2,1)S(1)} %get-tuple-element.19), channel_id=1, source_target_pairs={{0,24},{8,0},{16,8},{24,16},{1,25},{9,1},{17,9},{25,17},{2,26},{10... | collective-permute-start | bytes 786440 | tf_op jit(solution)/shard_map/ppermute | solution.py:18
  9.0 0.0 copy-start
  9.0 0.5 %collective-permute-start.4 = (bf16[2,1,32,16,128]{4,3,2,1,0:T(8,128)(2,1)S(1)}, bf16[2,1,32,16,128]{4,3,2,1,0:T(8,128)(2,1)S(1)}, u32[]{:S(2)}, u32[]{:S(2)}) collective-permute-start(bf16[2,1,32,16,128]{4,3,2,1,0:T(8,128)(2,1)S(1)} %get-tuple-element.23), channel_id=1, source_target_pairs={{0,7},{1,0},{2,1},{3,2},{4,3},{5,4},{6,5},{7,6},{8,15},{9,8},{10,9... | collective-permute-start | bytes 786440 | tf_op jit(solution)/shard_map/ppermute | solution.py:18
  9.5 7.2 %inner.1 = (bf16[32,512]{1,0:T(8,128)(2,1)S(1)}, bf16[4,128,1024]{2,1,0:T(8,128)(2,1)S(1)}) custom-call(bf16[4,4,32,16,128]{4,3,2,1,0:T(8,128)(2,1)} %nulls.3, bf16[2,4,32,64,128]{4,3,2,1,0:T(8,128)(2,1)} %time_links.1, bf16[4,2,32,64,128]{4,3,2,1,0:T(8,128)(2,1)} %space_links.1), custom_call_target="tpu_custom_call" | custom-call | flops 1000 | bytes 1000 | tf_op jit(solution)/shard_map/inner/pallas_call | solution.py:309
  16.7 1.6 %collective-permute-start.3 = (bf16[32,512]{1,0:T(8,128)(2,1)S(1)}, bf16[32,512]{1,0:T(8,128)(2,1)S(1)}, u32[]{:S(2)}, u32[]{:S(2)}) collective-permute-start(bf16[32,512]{1,0:T(8,128)(2,1)S(1)} %get-tuple-element.22.early), channel_id=1, source_target_pairs={{0,1},{1,0},{2,3},{3,2},{4,5},{5,4},{6,7},{7,6},{8,9},{9,8},{10,11... | collective-permute-start | bytes 98312 | tf_op jit(solution)/shard_map/ppermute | solution.py:22
  18.3 0.0 collective-permute-done.space_edge
  18.3 0.0 collective-permute-done.1.time_first
  18.3 0.0 collective-permute-done.2.time_second
  18.3 0.0 copy-done
  18.3 0.9 %middle.1 = (f32[24,512]{1,0:T(8,128)S(1)}, f32[2,64,64]{2,1,0:T(8,128)S(1)}) custom-call(s32[1]{0:T(128)} %bitcast.place, s32[8,64]{1,0:T(8,128)S(1)} %copy-done, bf16[2,1,32,16,128]{4,3,2,1,0:T(8,128)(2,1)S(1)} %collective-permute-done.space_edge, bf16[1,2,32,16,128]{4,3,2,1,0:T(8,128)(2,1)S(1)} %collective-permute-done.1.time_first, ...), custom_call_target="tpu_custom_call" | custom-call | flops 1000 | bytes 1000 | tf_op jit(solution)/shard_map/middle/pallas_call | solution.py:328
  19.3 0.0 collective-permute-done.4.space_edge
  19.3 0.6 %final.1.late = bf16[32,512]{1,0:T(8,128)(2,1)S(1)} custom-call(bf16[2,1,32,16,128]{4,3,2,1,0:T(8,128)(2,1)S(1)} %collective-permute-done.4.space_edge, bf16[4,128,1024]{2,1,0:T(8,128)(2,1)S(1)} %get-tuple-element.20.adjoint, f32[24,512]{1,0:T(8,128)S(1)} %get-tuple-element.24.found), custom_call_target="tpu_custom_call" | custom-call | flops 1000 | bytes 1000 | tf_op jit(solution)/shard_map/final/pallas_call | solution.py:340
  19.8 0.5 %collective-permute-start.5 = (bf16[32,512]{1,0:T(8,128)(2,1)S(1)}, bf16[32,512]{1,0:T(8,128)(2,1)S(1)}, u32[]{:S(2)}, u32[]{:S(2)}) collective-permute-start(bf16[32,512]{1,0:T(8,128)(2,1)S(1)} %final.1.late), channel_id=1, source_target_pairs={{0,1},{1,0},{2,3},{3,2},{4,5},{5,4},{6,7},{7,6},{8,9},{9,8},{10,11... | collective-permute-start | bytes 98312 | tf_op jit(solution)/shard_map/ppermute | solution.py:22
  20.3 0.4 %collective-permute-done.3.early_other = bf16[32,512]{1,0:T(8,128)(2,1)S(1)} collective-permute-done((bf16[32,512]{1,0:T(8,128)(2,1)S(1)}, bf16[32,512]{1,0:T(8,128)(2,1)S(1)}, u32[]{:S(2)}, u32[]{:S(2)}) %collective-permute-start.3) | collective-permute-done | bytes 32800 | tf_op jit(solution)/shard_map/ppermute | solution.py:22
  20.7 3.1 %collective-permute-done.5.late_other = bf16[32,512]{1,0:T(8,128)(2,1)S(1)} collective-permute-done((bf16[32,512]{1,0:T(8,128)(2,1)S(1)}, bf16[32,512]{1,0:T(8,128)(2,1)S(1)}, u32[]{:S(2)}, u32[]{:S(2)}) %collective-permute-start.5) | collective-permute-done | bytes 32800 | tf_op jit(solution)/shard_map/ppermute | solution.py:22
  23.8 0.2 pack.1
  23.9 0.4 %collective-permute-start.6 = (bf16[16,1024]{1,0:T(8,128)(2,1)S(1)}, bf16[16,1024]{1,0:T(8,128)(2,1)S(1)}, u32[]{:S(2)}, u32[]{:S(2)}) collective-permute-start(bf16[16,1024]{1,0:T(8,128)(2,1)S(1)} %get-tuple-element.25), channel_id=1, source_target_pairs={{0,4},{1,5},{2,6},{3,7},{4,0},{5,1},{6,2},{7,3},{8,12},{9,13},{10,... | collective-permute-start | bytes 98312 | tf_op jit(solution)/shard_map/ppermute | solution.py:22
  24.3 2.9 %collective-permute-start.7 = (bf16[16,1024]{1,0:T(8,128)(2,1)S(1)}, bf16[16,1024]{1,0:T(8,128)(2,1)S(1)}, u32[]{:S(2)}, u32[]{:S(2)}) collective-permute-start(bf16[16,1024]{1,0:T(8,128)(2,1)S(1)} %get-tuple-element.26), channel_id=1, source_target_pairs={{0,6},{1,7},{2,4},{3,5},{4,2},{5,3},{6,0},{7,1},{8,14},{9,15},{10,... | collective-permute-start | bytes 98312 | tf_op jit(solution)/shard_map/ppermute | solution.py:22
  27.2 0.5 %collective-permute-start.8 = (bf16[16,1024]{1,0:T(8,128)(2,1)S(1)}, bf16[16,1024]{1,0:T(8,128)(2,1)S(1)}, u32[]{:S(2)}, u32[]{:S(2)}) collective-permute-start(bf16[16,1024]{1,0:T(8,128)(2,1)S(1)} %get-tuple-element.27), channel_id=1, source_target_pairs={{0,2},{1,3},{2,0},{3,1},{4,6},{5,7},{6,4},{7,5},{8,10},{9,11},{10,... | collective-permute-start | bytes 98312 | tf_op jit(solution)/shard_map/ppermute | solution.py:22
  27.7 1.2 %collective-permute-done.6.refs_0_ = bf16[16,1024]{1,0:T(8,128)(2,1)S(1)} collective-permute-done((bf16[16,1024]{1,0:T(8,128)(2,1)S(1)}, bf16[16,1024]{1,0:T(8,128)(2,1)S(1)}, u32[]{:S(2)}, u32[]{:S(2)}) %collective-permute-start.6) | collective-permute-done | bytes 32800 | tf_op jit(solution)/shard_map/ppermute | solution.py:22
  28.9 1.1 %collective-permute-done.7.refs_1_ = bf16[16,1024]{1,0:T(8,128)(2,1)S(1)} collective-permute-done((bf16[16,1024]{1,0:T(8,128)(2,1)S(1)}, bf16[16,1024]{1,0:T(8,128)(2,1)S(1)}, u32[]{:S(2)}, u32[]{:S(2)}) %collective-permute-start.7) | collective-permute-done | bytes 32800 | tf_op jit(solution)/shard_map/ppermute | solution.py:22
  30.0 1.1 %collective-permute-done.8.refs_2_ = bf16[16,1024]{1,0:T(8,128)(2,1)S(1)} collective-permute-done((bf16[16,1024]{1,0:T(8,128)(2,1)S(1)}, bf16[16,1024]{1,0:T(8,128)(2,1)S(1)}, u32[]{:S(2)}, u32[]{:S(2)}) %collective-permute-start.8) | collective-permute-done | bytes 32800 | tf_op jit(solution)/shard_map/ppermute | solution.py:22
  31.1 0.7 %unpack.1 = f32[64,1024]{1,0:T(8,128)} custom-call(s32[1]{0:T(128)} %bitcast.place, bf16[16,1024]{1,0:T(8,128)(2,1)S(1)} %collective-permute-done.6.refs_0_, bf16[16,1024]{1,0:T(8,128)(2,1)S(1)} %collective-permute-done.7.refs_1_, bf16[16,1024]{1,0:T(8,128)(2,1)S(1)} %collective-permute-done.8.refs_2_, bf16[16,1024]{1,0:T(8,128)(2,1)S(1)} %get-tuple-element.28.refs_3_), custom_call_target="tpu_custom_call" | custom-call | flops 1000 | bytes 1000 | tf_op jit(solution)/shard_map/unpack/pallas_call | solution.py:363
Async XLA Ops:
  1.3 17.0 %collective-permute-start = (bf16[2,1,32,16,128]{4,3,2,1,0:T(8,128)(2,1)S(1)}, bf16[2,1,32,16,128]{4,3,2,1,0:T(8,128)(2,1)S(1)}, u32[]{:S(2)}, u32[]{:S(2)}) collective-permute-start(bf16[2,1,32,16,128]{4,3,2,1,0:T(8,128)(2,1)S(1)} %get-tuple-element.17), channel_id=1, source_target_pairs={{0,7},{1,0},{2,1},{3,2},{4,3},{5,4},{6,5},{7,6},{8,15},{9,8},{10,9... | collective-permute-start | bytes 786440 | tf_op jit(solution)/shard_map/ppermute | solution.py:18
  7.4 10.9 %collective-permute-start.1 = (bf16[1,2,32,16,128]{4,3,2,1,0:T(8,128)(2,1)S(1)}, bf16[1,2,32,16,128]{4,3,2,1,0:T(8,128)(2,1)S(1)}, u32[]{:S(2)}, u32[]{:S(2)}) collective-permute-start(bf16[1,2,32,16,128]{4,3,2,1,0:T(8,128)(2,1)S(1)} %get-tuple-element.18), channel_id=1, source_target_pairs={{0,24},{8,0},{16,8},{24,16},{1,25},{9,1},{17,9},{25,17},{2,26},{10... | collective-permute-start | bytes 786440 | tf_op jit(solution)/shard_map/ppermute | solution.py:18
  8.1 10.3 %collective-permute-start.2 = (bf16[1,2,32,16,128]{4,3,2,1,0:T(8,128)(2,1)S(1)}, bf16[1,2,32,16,128]{4,3,2,1,0:T(8,128)(2,1)S(1)}, u32[]{:S(2)}, u32[]{:S(2)}) collective-permute-start(bf16[1,2,32,16,128]{4,3,2,1,0:T(8,128)(2,1)S(1)} %get-tuple-element.19), channel_id=1, source_target_pairs={{0,24},{8,0},{16,8},{24,16},{1,25},{9,1},{17,9},{25,17},{2,26},{10... | collective-permute-start | bytes 786440 | tf_op jit(solution)/shard_map/ppermute | solution.py:18
  9.0 9.3 %copy-start = (s32[8,64]{1,0:T(8,128)S(1)}, s32[8,64]{1,0:T(8,128)}, u32[]{:S(2)}) copy-start(s32[8,64]{1,0:T(8,128)} %lists.1) | copy-start | bytes 6148
  9.0 10.2 %collective-permute-start.4 = (bf16[2,1,32,16,128]{4,3,2,1,0:T(8,128)(2,1)S(1)}, bf16[2,1,32,16,128]{4,3,2,1,0:T(8,128)(2,1)S(1)}, u32[]{:S(2)}, u32[]{:S(2)}) collective-permute-start(bf16[2,1,32,16,128]{4,3,2,1,0:T(8,128)(2,1)S(1)} %get-tuple-element.23), channel_id=1, source_target_pairs={{0,7},{1,0},{2,1},{3,2},{4,3},{5,4},{6,5},{7,6},{8,15},{9,8},{10,9... | collective-permute-start | bytes 786440 | tf_op jit(solution)/shard_map/ppermute | solution.py:18
  16.7 4.0 %collective-permute-start.3 = (bf16[32,512]{1,0:T(8,128)(2,1)S(1)}, bf16[32,512]{1,0:T(8,128)(2,1)S(1)}, u32[]{:S(2)}, u32[]{:S(2)}) collective-permute-start(bf16[32,512]{1,0:T(8,128)(2,1)S(1)} %get-tuple-element.22.early), channel_id=1, source_target_pairs={{0,1},{1,0},{2,3},{3,2},{4,5},{5,4},{6,7},{7,6},{8,9},{9,8},{10,11... | collective-permute-start | bytes 98312 | tf_op jit(solution)/shard_map/ppermute | solution.py:22
  19.8 3.9 %collective-permute-start.5 = (bf16[32,512]{1,0:T(8,128)(2,1)S(1)}, bf16[32,512]{1,0:T(8,128)(2,1)S(1)}, u32[]{:S(2)}, u32[]{:S(2)}) collective-permute-start(bf16[32,512]{1,0:T(8,128)(2,1)S(1)} %final.1.late), channel_id=1, source_target_pairs={{0,1},{1,0},{2,3},{3,2},{4,5},{5,4},{6,7},{7,6},{8,9},{9,8},{10,11... | collective-permute-start | bytes 98312 | tf_op jit(solution)/shard_map/ppermute | solution.py:22
  23.9 5.0 %collective-permute-start.6 = (bf16[16,1024]{1,0:T(8,128)(2,1)S(1)}, bf16[16,1024]{1,0:T(8,128)(2,1)S(1)}, u32[]{:S(2)}, u32[]{:S(2)}) collective-permute-start(bf16[16,1024]{1,0:T(8,128)(2,1)S(1)} %get-tuple-element.25), channel_id=1, source_target_pairs={{0,4},{1,5},{2,6},{3,7},{4,0},{5,1},{6,2},{7,3},{8,12},{9,13},{10,... | collective-permute-start | bytes 98312 | tf_op jit(solution)/shard_map/ppermute | solution.py:22
  24.3 5.7 %collective-permute-start.7 = (bf16[16,1024]{1,0:T(8,128)(2,1)S(1)}, bf16[16,1024]{1,0:T(8,128)(2,1)S(1)}, u32[]{:S(2)}, u32[]{:S(2)}) collective-permute-start(bf16[16,1024]{1,0:T(8,128)(2,1)S(1)} %get-tuple-element.26), channel_id=1, source_target_pairs={{0,6},{1,7},{2,4},{3,5},{4,2},{5,3},{6,0},{7,1},{8,14},{9,15},{10,... | collective-permute-start | bytes 98312 | tf_op jit(solution)/shard_map/ppermute | solution.py:22
  27.2 3.9 %collective-permute-start.8 = (bf16[16,1024]{1,0:T(8,128)(2,1)S(1)}, bf16[16,1024]{1,0:T(8,128)(2,1)S(1)}, u32[]{:S(2)}, u32[]{:S(2)}) collective-permute-start(bf16[16,1024]{1,0:T(8,128)(2,1)S(1)} %get-tuple-element.27), channel_id=1, source_target_pairs={{0,2},{1,3},{2,0},{3,1},{4,6},{5,7},{6,4},{7,5},{8,10},{9,11},{10,... | collective-permute-start | bytes 98312 | tf_op jit(solution)/shard_map/ppermute | solution.py:22

commit v14 on v13

--- a/solution.py
+++ b/solution.py
@@ -187,14 +187,12 @@
         fetch(space_links.at[t, 1])
     bases[1].wait()
     bases[2].wait()
-    found = []
     for a_x in range(2):
         copies[2 * a_x].wait()
         copies[2 * a_x + 1].wait()
         for c in range(2):
             x = 2 * a_x + c
-            image_item(links.at[x], vecs.at[1, x], vecs.at[2, x], c, left, right)
-        found.append(group_rows(left[...], right[...], MAT_DIMS, vectors))
+            image_item(links.at[x], vecs.at[1, x], vecs.at[2, x], c, left.at[a_x], right.at[a_x])
     bases[0].wait()
     bases[3].wait()
     for a_t in range(2):
@@ -202,8 +200,8 @@
         copies[5 + 2 * a_t].wait()
         for c in range(2):
             t = 2 * a_t + c
-            image_item(links.at[4 + t], vecs.at[t, 1], vecs.at[t, 2], c, left, right)
-        found.append(group_rows(left[...], right[...], MAT_DIMS, vectors))
+            image_item(links.at[4 + t], vecs.at[t, 1], vecs.at[t, 2], c, left.at[2 + a_t], right.at[2 + a_t])
+    found = [group_rows(left[group], right[group], MAT_DIMS, vectors) for group in range(4)]
     early[...] = jnp.concatenate(found, axis=0).astype(jnp.bfloat16)
     for x in range(4):
         copies[8 + x].wait()
@@ -258,10 +256,16 @@
 
 def unpack_kernel(place, *refs, turns):
     pair = place[0] // 2
-    result = refs[-1]
-    for turn, arrived in zip(turns, refs[:-1]):
+    result, rows, sems = refs[-3:]
+    copies = []
+    for slot, turn in enumerate(turns):
         source = jnp.bitwise_xor(pair, turn)
-        result[pl.ds(pl.multiple_of(source * 2 * MOST, 2 * MOST), 2 * MOST), :] = arrived[...].astype(jnp.float32)
+        rows[slot] = refs[slot][...].astype(jnp.float32)
+        target = result.at[pl.ds(pl.multiple_of(source * 2 * MOST, 2 * MOST), 2 * MOST)]
+        copies.append(pltpu.make_async_copy(rows.at[slot], target, sems.at[slot]))
+        copies[-1].start()
+    for copy in copies:
+        copy.wait()
 
 
 def on_device(nulls, time_links, space_links, owner_lists):
@@ -296,12 +300,9 @@
         )(nulls)
 
     half_space = space_count // 2
-    space_first, space_second, time_first, time_second = sliced(
-        "slices",
-        (0, half_time, 0, 1),
-        (half_time, half_time, 0, 1),
-        (0, 1, 0, half_space),
-        (0, 1, half_space, half_space),
+    (space_first,) = sliced("slice_first", (0, half_time, 0, 1))
+    space_second, time_first, time_second = sliced(
+        "slice_rest", (half_time, half_time, 0, 1), (0, 1, 0, half_space), (0, 1, half_space, half_space)
     )
     edge_first = shifted(space_first, "xyz", -1)
     edge_times = [shifted(time_first, "ta", -1), shifted(time_second, "ta", -1)]
@@ -317,8 +318,8 @@
         scratch_shapes=[
             pltpu.VMEM((16, sites, half, width), jnp.bfloat16),
             pltpu.VMEM(nulls.shape, nulls.dtype),
-            pltpu.VMEM((vectors * aggs, 8 * width), jnp.bfloat16),
-            pltpu.VMEM((8 * width, 2 * vectors * aggs), jnp.bfloat16),
+            pltpu.VMEM((4, vectors * aggs, 8 * width), jnp.bfloat16),
+            pltpu.VMEM((4, 8 * width, 2 * vectors * aggs), jnp.bfloat16),
             pltpu.SemaphoreType.DMA((20,)),
         ],
         compiler_params=roomy,
@@ -363,8 +364,12 @@
     arrived = pl.pallas_call(
         functools.partial(unpack_kernel, turns=turns + [0]),
         in_specs=[smem] + [vmem] * pairs,
-        out_specs=vmem,
+        out_specs=outside,
         out_shape=jax.ShapeDtypeStruct((shards * MOST, 2 * wide), jnp.float32),
+        scratch_shapes=[
+            pltpu.VMEM((pairs, 2 * MOST, 2 * wide), jnp.float32),
+            pltpu.SemaphoreType.DMA((pairs,)),
+        ],
         compiler_params=modest,
         cost_estimate=tiny,
         name="unpack",

time: 32 us -> 31.7 us (level)
    pallas_call x1, Pallas kernels: 7.19 us -> 6.12 us  [on_device(): pl.pallas_call(inner_kernel, in_specs=[outside] * 3, out_specs=[vmem] * 2...]
    pallas_call x1 -> x2, Pallas kernels: 1.34 us -> 2.18 us  [sliced(): pl.pallas_call(functools.partial(slice_kernel, sources=sources), in_specs...]
  transfers between devices with their start and end apart: 9 -> 9, of which waited for: 5 -> 5; matrix products, arithmetic and copies ran while one was open for 0% -> 0% of each run, Pallas kernels for 27% -> 28%
where the time goes in v14:
time: 31.7 us; the launch traced here: 31.5 us
  starting transfers between devices  13.9 us (44%)
  Pallas kernels  10.7 us (34%)
  waiting for transfers between devices  6.84 us (22%)
    ppermute x4, starting transfers between devices, shifted(): lax.ppermute(array, axis, [(i, (i + by) % count) for i in range(count)])  8.22 us
    ppermute x5, waiting for transfers between devices, crossed(): lax.ppermute(array, axis, [(i, i ^ bits) for i in range(lax.axis_size(axi...  6.83 us
    pallas_call x1, Pallas kernels, on_device(): pl.pallas_call(inner_kernel, in_specs=[outside] * 3, out_specs=[vmem] * 2...  6.12 us
    ppermute x5, starting transfers between devices, crossed(): lax.ppermute(array, axis, [(i, i ^ bits) for i in range(lax.axis_size(axi...  5.71 us
    pallas_call x2, Pallas kernels, sliced(): pl.pallas_call(functools.partial(slice_kernel, sources=sources), in_specs...  2.18 us
    pallas_call x1, Pallas kernels, on_device(): pl.pallas_call(middle_kernel, in_specs=[smem] + [vmem] * 5, out_specs=[vm...  0.91 us
    pallas_call x1, Pallas kernels, on_device(): pl.pallas_call(functools.partial(unpack_kernel, turns=turns + [0]), in_sp...  0.74 us
  transfers between devices with their start and end apart: 9, of which 5 were waited for; matrix products, arithmetic and copies ran while one was open for 0% of the time, Pallas kernels for 28%

profile of v14, /device:TPU:0, one launch (start us, length us, event | category | flops | bytes accessed | tf_op | source)
XLA Modules:
  0.0 31.5 jit_solution(14106309675463471913)
XLA Ops:
  0.0 1.0 %slice_first.1 = bf16[2,1,32,16,128]{4,3,2,1,0:T(8,128)(2,1)S(1)} custom-call(bf16[4,4,32,16,128]{4,3,2,1,0:T(8,128)(2,1)} %nulls.5), custom_call_target="tpu_custom_call" | custom-call | flops 1000 | bytes 1000 | tf_op jit(solution)/shard_map/slice_first/pallas_call | solution.py:291
  1.0 6.1 %collective-permute-start = (bf16[2,1,32,16,128]{4,3,2,1,0:T(8,128)(2,1)S(1)}, bf16[2,1,32,16,128]{4,3,2,1,0:T(8,128)(2,1)S(1)}, u32[]{:S(2)}, u32[]{:S(2)}) collective-permute-start(bf16[2,1,32,16,128]{4,3,2,1,0:T(8,128)(2,1)S(1)} %slice_first.1), channel_id=1, source_target_pairs={{0,7},{1,0},{2,1},{3,2},{4,3},{5,4},{6,5},{7,6},{8,15},{9,8},{10,9... | collective-permute-start | bytes 786440 | tf_op jit(solution)/shard_map/ppermute | solution.py:18
  7.0 1.2 %slice_rest.1 = (bf16[2,1,32,16,128]{4,3,2,1,0:T(8,128)(2,1)S(1)}, bf16[1,2,32,16,128]{4,3,2,1,0:T(8,128)(2,1)S(1)}, bf16[1,2,32,16,128]{4,3,2,1,0:T(8,128)(2,1)S(1)}) custom-call(bf16[4,4,32,16,128]{4,3,2,1,0:T(8,128)(2,1)} %nulls.5), custom_call_target="tpu_custom_call" | custom-call | flops 1000 | bytes 1000 | tf_op jit(solution)/shard_map/slice_rest/pallas_call | solution.py:291
  8.3 0.7 %collective-permute-start.1 = (bf16[1,2,32,16,128]{4,3,2,1,0:T(8,128)(2,1)S(1)}, bf16[1,2,32,16,128]{4,3,2,1,0:T(8,128)(2,1)S(1)}, u32[]{:S(2)}, u32[]{:S(2)}) collective-permute-start(bf16[1,2,32,16,128]{4,3,2,1,0:T(8,128)(2,1)S(1)} %get-tuple-element.16), channel_id=1, source_target_pairs={{0,24},{8,0},{16,8},{24,16},{1,25},{9,1},{17,9},{25,17},{2,26},{10... | collective-permute-start | bytes 786440 | tf_op jit(solution)/shard_map/ppermute | solution.py:18
  9.0 1.0 %collective-permute-start.2 = (bf16[1,2,32,16,128]{4,3,2,1,0:T(8,128)(2,1)S(1)}, bf16[1,2,32,16,128]{4,3,2,1,0:T(8,128)(2,1)S(1)}, u32[]{:S(2)}, u32[]{:S(2)}) collective-permute-start(bf16[1,2,32,16,128]{4,3,2,1,0:T(8,128)(2,1)S(1)} %get-tuple-element.17), channel_id=1, source_target_pairs={{0,24},{8,0},{16,8},{24,16},{1,25},{9,1},{17,9},{25,17},{2,26},{10... | collective-permute-start | bytes 786440 | tf_op jit(solution)/shard_map/ppermute | solution.py:18
  9.9 0.0 copy-start
  9.9 0.5 %collective-permute-start.4 = (bf16[2,1,32,16,128]{4,3,2,1,0:T(8,128)(2,1)S(1)}, bf16[2,1,32,16,128]{4,3,2,1,0:T(8,128)(2,1)S(1)}, u32[]{:S(2)}, u32[]{:S(2)}) collective-permute-start(bf16[2,1,32,16,128]{4,3,2,1,0:T(8,128)(2,1)S(1)} %get-tuple-element.21), channel_id=1, source_target_pairs={{0,7},{1,0},{2,1},{3,2},{4,3},{5,4},{6,5},{7,6},{8,15},{9,8},{10,9... | collective-permute-start | bytes 786440 | tf_op jit(solution)/shard_map/ppermute | solution.py:18
  10.4 6.1 %inner.1 = (bf16[32,512]{1,0:T(8,128)(2,1)S(1)}, bf16[4,128,1024]{2,1,0:T(8,128)(2,1)S(1)}) custom-call(bf16[4,4,32,16,128]{4,3,2,1,0:T(8,128)(2,1)} %nulls.5, bf16[2,4,32,64,128]{4,3,2,1,0:T(8,128)(2,1)} %time_links.1, bf16[4,2,32,64,128]{4,3,2,1,0:T(8,128)(2,1)} %space_links.1), custom_call_target="tpu_custom_call" | custom-call | flops 1000 | bytes 1000 | tf_op jit(solution)/shard_map/inner/pallas_call | solution.py:310
  16.5 1.6 %collective-permute-start.3 = (bf16[32,512]{1,0:T(8,128)(2,1)S(1)}, bf16[32,512]{1,0:T(8,128)(2,1)S(1)}, u32[]{:S(2)}, u32[]{:S(2)}) collective-permute-start(bf16[32,512]{1,0:T(8,128)(2,1)S(1)} %get-tuple-element.20.early), channel_id=1, source_target_pairs={{0,1},{1,0},{2,3},{3,2},{4,5},{5,4},{6,7},{7,6},{8,9},{9,8},{10,11... | collective-permute-start | bytes 98312 | tf_op jit(solution)/shard_map/ppermute | solution.py:22
  18.1 0.0 collective-permute-done.space_edge
  18.1 0.0 collective-permute-done.1.time_first
  18.1 0.0 collective-permute-done.2.time_second
  18.1 0.0 copy-done
  18.2 0.9 %middle.1 = (f32[24,512]{1,0:T(8,128)S(1)}, f32[2,64,64]{2,1,0:T(8,128)S(1)}) custom-call(s32[1]{0:T(128)} %bitcast.place, s32[8,64]{1,0:T(8,128)S(1)} %copy-done, bf16[2,1,32,16,128]{4,3,2,1,0:T(8,128)(2,1)S(1)} %collective-permute-done.space_edge, bf16[1,2,32,16,128]{4,3,2,1,0:T(8,128)(2,1)S(1)} %collective-permute-done.1.time_first, ...), custom_call_target="tpu_custom_call" | custom-call | flops 1000 | bytes 1000 | tf_op jit(solution)/shard_map/middle/pallas_call | solution.py:329
  19.1 0.0 collective-permute-done.4.space_edge
  19.1 0.6 %final.1.late = bf16[32,512]{1,0:T(8,128)(2,1)S(1)} custom-call(bf16[2,1,32,16,128]{4,3,2,1,0:T(8,128)(2,1)S(1)} %collective-permute-done.4.space_edge, bf16[4,128,1024]{2,1,0:T(8,128)(2,1)S(1)} %get-tuple-element.18.adjoint, f32[24,512]{1,0:T(8,128)S(1)} %get-tuple-element.22.found), custom_call_target="tpu_custom_call" | custom-call | flops 1000 | bytes 1000 | tf_op jit(solution)/shard_map/final/pallas_call | solution.py:341
  19.7 0.5 %collective-permute-start.5 = (bf16[32,512]{1,0:T(8,128)(2,1)S(1)}, bf16[32,512]{1,0:T(8,128)(2,1)S(1)}, u32[]{:S(2)}, u32[]{:S(2)}) collective-permute-start(bf16[32,512]{1,0:T(8,128)(2,1)S(1)} %final.1.late), channel_id=1, source_target_pairs={{0,1},{1,0},{2,3},{3,2},{4,5},{5,4},{6,7},{7,6},{8,9},{9,8},{10,11... | collective-permute-start | bytes 98312 | tf_op jit(solution)/shard_map/ppermute | solution.py:22
  20.2 0.4 %collective-permute-done.3.early_other = bf16[32,512]{1,0:T(8,128)(2,1)S(1)} collective-permute-done((bf16[32,512]{1,0:T(8,128)(2,1)S(1)}, bf16[32,512]{1,0:T(8,128)(2,1)S(1)}, u32[]{:S(2)}, u32[]{:S(2)}) %collective-permute-start.3) | collective-permute-done | bytes 32800 | tf_op jit(solution)/shard_map/ppermute | solution.py:22
  20.5 3.0 %collective-permute-done.5.late_other = bf16[32,512]{1,0:T(8,128)(2,1)S(1)} collective-permute-done((bf16[32,512]{1,0:T(8,128)(2,1)S(1)}, bf16[32,512]{1,0:T(8,128)(2,1)S(1)}, u32[]{:S(2)}, u32[]{:S(2)}) %collective-permute-start.5) | collective-permute-done | bytes 32800 | tf_op jit(solution)/shard_map/ppermute | solution.py:22
  23.6 0.2 pack.1
  23.7 0.2 collective-permute-start.6
  24.0 2.9 %collective-permute-start.7 = (bf16[16,1024]{1,0:T(8,128)(2,1)S(1)}, bf16[16,1024]{1,0:T(8,128)(2,1)S(1)}, u32[]{:S(2)}, u32[]{:S(2)}) collective-permute-start(bf16[16,1024]{1,0:T(8,128)(2,1)S(1)} %get-tuple-element.24), channel_id=1, source_target_pairs={{0,6},{1,7},{2,4},{3,5},{4,2},{5,3},{6,0},{7,1},{8,14},{9,15},{10,... | collective-permute-start | bytes 98312 | tf_op jit(solution)/shard_map/ppermute | solution.py:22
  26.9 0.5 %collective-permute-start.8 = (bf16[16,1024]{1,0:T(8,128)(2,1)S(1)}, bf16[16,1024]{1,0:T(8,128)(2,1)S(1)}, u32[]{:S(2)}, u32[]{:S(2)}) collective-permute-start(bf16[16,1024]{1,0:T(8,128)(2,1)S(1)} %get-tuple-element.25), channel_id=1, source_target_pairs={{0,2},{1,3},{2,0},{3,1},{4,6},{5,7},{6,4},{7,5},{8,10},{9,11},{10,... | collective-permute-start | bytes 98312 | tf_op jit(solution)/shard_map/ppermute | solution.py:22
  27.3 1.6 %collective-permute-done.6.refs_0_ = bf16[16,1024]{1,0:T(8,128)(2,1)S(1)} collective-permute-done((bf16[16,1024]{1,0:T(8,128)(2,1)S(1)}, bf16[16,1024]{1,0:T(8,128)(2,1)S(1)}, u32[]{:S(2)}, u32[]{:S(2)}) %collective-permute-start.6) | collective-permute-done | bytes 32800 | tf_op jit(solution)/shard_map/ppermute | solution.py:22
  28.9 0.8 %collective-permute-done.7.refs_1_ = bf16[16,1024]{1,0:T(8,128)(2,1)S(1)} collective-permute-done((bf16[16,1024]{1,0:T(8,128)(2,1)S(1)}, bf16[16,1024]{1,0:T(8,128)(2,1)S(1)}, u32[]{:S(2)}, u32[]{:S(2)}) %collective-permute-start.7) | collective-permute-done | bytes 32800 | tf_op jit(solution)/shard_map/ppermute | solution.py:22
  29.7 1.1 %collective-permute-done.8.refs_2_ = bf16[16,1024]{1,0:T(8,128)(2,1)S(1)} collective-permute-done((bf16[16,1024]{1,0:T(8,128)(2,1)S(1)}, bf16[16,1024]{1,0:T(8,128)(2,1)S(1)}, u32[]{:S(2)}, u32[]{:S(2)}) %collective-permute-start.8) | collective-permute-done | bytes 32800 | tf_op jit(solution)/shard_map/ppermute | solution.py:22
  30.8 0.7 %unpack.1 = f32[64,1024]{1,0:T(8,128)} custom-call(s32[1]{0:T(128)} %bitcast.place, bf16[16,1024]{1,0:T(8,128)(2,1)S(1)} %collective-permute-done.6.refs_0_, bf16[16,1024]{1,0:T(8,128)(2,1)S(1)} %collective-permute-done.7.refs_1_, bf16[16,1024]{1,0:T(8,128)(2,1)S(1)} %collective-permute-done.8.refs_2_, bf16[16,1024]{1,0:T(8,128)(2,1)S(1)} %get-tuple-element.26.refs_3_), custom_call_target="tpu_custom_call" | custom-call | flops 1000 | bytes 1000 | tf_op jit(solution)/shard_map/unpack/pallas_call | solution.py:364
Async XLA Ops:
  1.0 17.1 %collective-permute-start = (bf16[2,1,32,16,128]{4,3,2,1,0:T(8,128)(2,1)S(1)}, bf16[2,1,32,16,128]{4,3,2,1,0:T(8,128)(2,1)S(1)}, u32[]{:S(2)}, u32[]{:S(2)}) collective-permute-start(bf16[2,1,32,16,128]{4,3,2,1,0:T(8,128)(2,1)S(1)} %slice_first.1), channel_id=1, source_target_pairs={{0,7},{1,0},{2,1},{3,2},{4,3},{5,4},{6,5},{7,6},{8,15},{9,8},{10,9... | collective-permute-start | bytes 786440 | tf_op jit(solution)/shard_map/ppermute | solution.py:18
  8.3 9.9 %collective-permute-start.1 = (bf16[1,2,32,16,128]{4,3,2,1,0:T(8,128)(2,1)S(1)}, bf16[1,2,32,16,128]{4,3,2,1,0:T(8,128)(2,1)S(1)}, u32[]{:S(2)}, u32[]{:S(2)}) collective-permute-start(bf16[1,2,32,16,128]{4,3,2,1,0:T(8,128)(2,1)S(1)} %get-tuple-element.16), channel_id=1, source_target_pairs={{0,24},{8,0},{16,8},{24,16},{1,25},{9,1},{17,9},{25,17},{2,26},{10... | collective-permute-start | bytes 786440 | tf_op jit(solution)/shard_map/ppermute | solution.py:18
  9.0 9.2 %collective-permute-start.2 = (bf16[1,2,32,16,128]{4,3,2,1,0:T(8,128)(2,1)S(1)}, bf16[1,2,32,16,128]{4,3,2,1,0:T(8,128)(2,1)S(1)}, u32[]{:S(2)}, u32[]{:S(2)}) collective-permute-start(bf16[1,2,32,16,128]{4,3,2,1,0:T(8,128)(2,1)S(1)} %get-tuple-element.17), channel_id=1, source_target_pairs={{0,24},{8,0},{16,8},{24,16},{1,25},{9,1},{17,9},{25,17},{2,26},{10... | collective-permute-start | bytes 786440 | tf_op jit(solution)/shard_map/ppermute | solution.py:18
  9.9 8.2 %copy-start = (s32[8,64]{1,0:T(8,128)S(1)}, s32[8,64]{1,0:T(8,128)}, u32[]{:S(2)}) copy-start(s32[8,64]{1,0:T(8,128)} %lists.1) | copy-start | bytes 6148
  9.9 9.2 %collective-permute-start.4 = (bf16[2,1,32,16,128]{4,3,2,1,0:T(8,128)(2,1)S(1)}, bf16[2,1,32,16,128]{4,3,2,1,0:T(8,128)(2,1)S(1)}, u32[]{:S(2)}, u32[]{:S(2)}) collective-permute-start(bf16[2,1,32,16,128]{4,3,2,1,0:T(8,128)(2,1)S(1)} %get-tuple-element.21), channel_id=1, source_target_pairs={{0,7},{1,0},{2,1},{3,2},{4,3},{5,4},{6,5},{7,6},{8,15},{9,8},{10,9... | collective-permute-start | bytes 786440 | tf_op jit(solution)/shard_map/ppermute | solution.py:18
  16.5 4.0 %collective-permute-start.3 = (bf16[32,512]{1,0:T(8,128)(2,1)S(1)}, bf16[32,512]{1,0:T(8,128)(2,1)S(1)}, u32[]{:S(2)}, u32[]{:S(2)}) collective-permute-start(bf16[32,512]{1,0:T(8,128)(2,1)S(1)} %get-tuple-element.20.early), channel_id=1, source_target_pairs={{0,1},{1,0},{2,3},{3,2},{4,5},{5,4},{6,7},{7,6},{8,9},{9,8},{10,11... | collective-permute-start | bytes 98312 | tf_op jit(solution)/shard_map/ppermute | solution.py:22
  19.7 3.9 %collective-permute-start.5 = (bf16[32,512]{1,0:T(8,128)(2,1)S(1)}, bf16[32,512]{1,0:T(8,128)(2,1)S(1)}, u32[]{:S(2)}, u32[]{:S(2)}) collective-permute-start(bf16[32,512]{1,0:T(8,128)(2,1)S(1)} %final.1.late), channel_id=1, source_target_pairs={{0,1},{1,0},{2,3},{3,2},{4,5},{5,4},{6,7},{7,6},{8,9},{9,8},{10,11... | collective-permute-start | bytes 98312 | tf_op jit(solution)/shard_map/ppermute | solution.py:22
  23.7 5.2 %collective-permute-start.6 = (bf16[16,1024]{1,0:T(8,128)(2,1)S(1)}, bf16[16,1024]{1,0:T(8,128)(2,1)S(1)}, u32[]{:S(2)}, u32[]{:S(2)}) collective-permute-start(bf16[16,1024]{1,0:T(8,128)(2,1)S(1)} %get-tuple-element.23), channel_id=1, source_target_pairs={{0,4},{1,5},{2,6},{3,7},{4,0},{5,1},{6,2},{7,3},{8,12},{9,13},{10,... | collective-permute-start | bytes 98312 | tf_op jit(solution)/shard_map/ppermute | solution.py:22
  24.0 5.7 %collective-permute-start.7 = (bf16[16,1024]{1,0:T(8,128)(2,1)S(1)}, bf16[16,1024]{1,0:T(8,128)(2,1)S(1)}, u32[]{:S(2)}, u32[]{:S(2)}) collective-permute-start(bf16[16,1024]{1,0:T(8,128)(2,1)S(1)} %get-tuple-element.24), channel_id=1, source_target_pairs={{0,6},{1,7},{2,4},{3,5},{4,2},{5,3},{6,0},{7,1},{8,14},{9,15},{10,... | collective-permute-start | bytes 98312 | tf_op jit(solution)/shard_map/ppermute | solution.py:22
  26.9 3.9 %collective-permute-start.8 = (bf16[16,1024]{1,0:T(8,128)(2,1)S(1)}, bf16[16,1024]{1,0:T(8,128)(2,1)S(1)}, u32[]{:S(2)}, u32[]{:S(2)}) collective-permute-start(bf16[16,1024]{1,0:T(8,128)(2,1)S(1)} %get-tuple-element.25), channel_id=1, source_target_pairs={{0,2},{1,3},{2,0},{3,1},{4,6},{5,7},{6,4},{7,5},{8,10},{9,11},{10,... | collective-permute-start | bytes 98312 | tf_op jit(solution)/shard_map/ppermute | solution.py:22

commit v15 on v14

--- a/solution.py
+++ b/solution.py
@@ -125,9 +125,13 @@
     edges, sems = refs[:-1], refs[-1]
     copies = []
     for edge, (start, count, at, space) in zip(edges, sources):
+        quarter = edge.shape[2] // 4
         for row in range(count):
-            source = nulls.at[pl.ds(start + row, 1), pl.ds(at, space)]
-            copies.append(pltpu.make_async_copy(source, edge.at[pl.ds(row, 1)], sems.at[len(copies)]))
+            for part in range(4):
+                span = pl.ds(part * quarter, quarter)
+                source = nulls.at[pl.ds(start + row, 1), pl.ds(at, space), span]
+                target = edge.at[pl.ds(row, 1), :, span]
+                copies.append(pltpu.make_async_copy(source, target, sems.at[len(copies)]))
     for copy in copies:
         copy.start()
     for copy in copies:
@@ -202,7 +206,7 @@
             t = 2 * a_t + c
             image_item(links.at[4 + t], vecs.at[t, 1], vecs.at[t, 2], c, left.at[2 + a_t], right.at[2 + a_t])
     found = [group_rows(left[group], right[group], MAT_DIMS, vectors) for group in range(4)]
-    early[...] = jnp.concatenate(found, axis=0).astype(jnp.bfloat16)
+    early[...] = jnp.concatenate(found, axis=0)
     for x in range(4):
         copies[8 + x].wait()
     for x in range(4):
@@ -237,17 +241,17 @@
     found[...] = jnp.concatenate(rows, axis=0)
 
 
-def final_kernel(space_edge, adjoint, found, late):
+def final_kernel(space_edge, adjoint, early, found, late):
     vectors = space_edge.shape[3]
     rows = edge_rows([space_edge.at[c, 0] for c in range(2)], adjoint[3], vectors)
-    late[...] = jnp.concatenate([found[...], rows], axis=0).astype(jnp.bfloat16)
-
-
-def pack_kernel(picks, early, early_other, late, late_other, *packed):
-    half_count = late.shape[0] // 2
-    pieces = (early, late, early_other, late_other)
-    for half, width in enumerate((late.shape[1],) * 2):
-        rows = jnp.concatenate([piece[pl.ds(half * half_count, half_count), :] for piece in pieces], axis=0)
+    late[...] = jnp.concatenate([early[...], found[...], rows], axis=0).astype(jnp.bfloat16)
+
+
+def pack_kernel(picks, late, late_other, *packed):
+    quarter, width = late.shape[0] // 4, late.shape[1]
+    for half in range(2):
+        spans = [pl.ds((half + 2 * part) * quarter, quarter) for part in range(2)]
+        rows = jnp.concatenate([piece[span, :] for piece in (late, late_other) for span in spans], axis=0)
         sent = dot(picks[half].astype(jnp.bfloat16), rows, MAT_DIMS)
         for turn, out in enumerate(packed):
             mine = sent[turn * 2 * MOST : (turn + 1) * 2 * MOST]
@@ -293,7 +297,7 @@
             in_specs=[outside],
             out_specs=[vmem] * len(sources),
             out_shape=[jax.ShapeDtypeStruct(shape, nulls.dtype) for shape in shapes],
-            scratch_shapes=[pltpu.SemaphoreType.DMA((sum(source[1] for source in sources),))],
+            scratch_shapes=[pltpu.SemaphoreType.DMA((4 * sum(source[1] for source in sources),))],
             compiler_params=first,
             cost_estimate=tiny,
             name=name,
@@ -312,7 +316,7 @@
         in_specs=[outside] * 3,
         out_specs=[vmem] * 2,
         out_shape=[
-            jax.ShapeDtypeStruct((4 * aggs, wide), jnp.bfloat16),
+            jax.ShapeDtypeStruct((4 * aggs, wide), jnp.float32),
             jax.ShapeDtypeStruct((4, vectors * aggs, 8 * width), jnp.bfloat16),
         ],
         scratch_shapes=[
@@ -340,25 +344,24 @@
     )(place, owner_lists, edge_first, *edge_times, adjoint)
     late = pl.pallas_call(
         final_kernel,
-        in_specs=[vmem] * 3,
+        in_specs=[vmem] * 4,
         out_specs=vmem,
-        out_shape=jax.ShapeDtypeStruct((4 * aggs, wide), jnp.bfloat16),
+        out_shape=jax.ShapeDtypeStruct((8 * aggs, wide), jnp.bfloat16),
         compiler_params=modest,
         cost_estimate=tiny,
         name="final",
-    )(edge_second, adjoint, found)
-    early_other = crossed(early, "xyz", 1)
+    )(edge_second, adjoint, early, found)
     late_other = crossed(late, "xyz", 1)
     pairs = shards // 2
     packed = pl.pallas_call(
         pack_kernel,
-        in_specs=[vmem] * 5,
+        in_specs=[vmem] * 3,
         out_specs=[vmem] * pairs,
         out_shape=[jax.ShapeDtypeStruct((2 * MOST, 2 * wide), jnp.bfloat16)] * pairs,
         compiler_params=modest,
         cost_estimate=tiny,
         name="pack",
-    )(picks, early, early_other, late, late_other)
+    )(picks, late, late_other)
     turns = list(range(2, pairs)) + [1]
     arrived = [crossed(packed[turn], "xyz", 2 * turn) for turn in turns]
     arrived = pl.pallas_call(

time: 31.7 us -> 32 us (level)
  waiting for transfers between devices: 6.84 us -> 7.37 us
  starting transfers between devices: 13.9 us -> 13.5 us
    ppermute x4, waiting for transfers between devices: 0.01 us -> 0.6 us  [shifted(): lax.ppermute(array, axis, [(i, (i + by) % count) for i in range(count)])]
    ppermute x5 -> x4, starting transfers between devices: 5.71 us -> 5.3 us  [crossed(): lax.ppermute(array, axis, [(i, i ^ bits) for i in range(lax.axis_size(axi...]
    ppermute x5 -> x4, waiting for transfers between devices: 6.83 us -> 6.76 us  [crossed(): lax.ppermute(array, axis, [(i, i ^ bits) for i in range(lax.axis_size(axi...]
  transfers between devices with their start and end apart: 9 -> 8, of which waited for: 5 -> 5; matrix products, arithmetic and copies ran while one was open for 0% -> 0% of each run, Pallas kernels for 28% -> 26%
where the time goes in v15:
time: 32 us; the launch traced here: 31.7 us
  starting transfers between devices  13.5 us (42%)
  Pallas kernels  10.7 us (33%)
  waiting for transfers between devices  7.37 us (23%)
    ppermute x4, starting transfers between devices, shifted(): lax.ppermute(array, axis, [(i, (i + by) % count) for i in range(count)])  8.22 us
    ppermute x4, waiting for transfers between devices, crossed(): lax.ppermute(array, axis, [(i, i ^ bits) for i in range(lax.axis_size(axi...  6.76 us
    pallas_call x1, Pallas kernels, on_device(): pl.pallas_call(inner_kernel, in_specs=[outside] * 3, out_specs=[vmem] * 2...  6.12 us
    ppermute x4, starting transfers between devices, crossed(): lax.ppermute(array, axis, [(i, i ^ bits) for i in range(lax.axis_size(axi...  5.3 us
    pallas_call x2, Pallas kernels, sliced(): pl.pallas_call(functools.partial(slice_kernel, sources=sources), in_specs...  2.25 us
    pallas_call x1, Pallas kernels, on_device(): pl.pallas_call(middle_kernel, in_specs=[smem] + [vmem] * 5, out_specs=[vm...  0.92 us
    pallas_call x1, Pallas kernels, on_device(): pl.pallas_call(functools.partial(unpack_kernel, turns=turns + [0]), in_sp...  0.74 us
  transfers between devices with their start and end apart: 8, of which 5 were waited for; matrix products, arithmetic and copies ran while one was open for 0% of the time, Pallas kernels for 26%

profile of v15, /device:TPU:0, one launch (start us, length us, event | category | flops | bytes accessed | tf_op | source)
XLA Modules:
  0.0 31.7 jit_solution(12770182492010624112)
XLA Ops:
  0.0 0.9 %slice_first.1 = bf16[2,1,32,16,128]{4,3,2,1,0:T(8,128)(2,1)S(1)} custom-call(bf16[4,4,32,16,128]{4,3,2,1,0:T(8,128)(2,1)} %nulls.5), custom_call_target="tpu_custom_call" | custom-call | flops 1000 | bytes 1000 | tf_op jit(solution)/shard_map/slice_first/pallas_call | solution.py:295
  0.9 6.1 %collective-permute-start = (bf16[2,1,32,16,128]{4,3,2,1,0:T(8,128)(2,1)S(1)}, bf16[2,1,32,16,128]{4,3,2,1,0:T(8,128)(2,1)S(1)}, u32[]{:S(2)}, u32[]{:S(2)}) collective-permute-start(bf16[2,1,32,16,128]{4,3,2,1,0:T(8,128)(2,1)S(1)} %slice_first.1), channel_id=1, source_target_pairs={{0,7},{1,0},{2,1},{3,2},{4,3},{5,4},{6,5},{7,6},{8,15},{9,8},{10,9... | collective-permute-start | bytes 786440 | tf_op jit(solution)/shard_map/ppermute | solution.py:18
  7.0 1.3 %slice_rest.1 = (bf16[2,1,32,16,128]{4,3,2,1,0:T(8,128)(2,1)S(1)}, bf16[1,2,32,16,128]{4,3,2,1,0:T(8,128)(2,1)S(1)}, bf16[1,2,32,16,128]{4,3,2,1,0:T(8,128)(2,1)S(1)}) custom-call(bf16[4,4,32,16,128]{4,3,2,1,0:T(8,128)(2,1)} %nulls.5), custom_call_target="tpu_custom_call" | custom-call | flops 1000 | bytes 1000 | tf_op jit(solution)/shard_map/slice_rest/pallas_call | solution.py:295
  8.3 0.7 %collective-permute-start.1 = (bf16[1,2,32,16,128]{4,3,2,1,0:T(8,128)(2,1)S(1)}, bf16[1,2,32,16,128]{4,3,2,1,0:T(8,128)(2,1)S(1)}, u32[]{:S(2)}, u32[]{:S(2)}) collective-permute-start(bf16[1,2,32,16,128]{4,3,2,1,0:T(8,128)(2,1)S(1)} %get-tuple-element.16), channel_id=1, source_target_pairs={{0,24},{8,0},{16,8},{24,16},{1,25},{9,1},{17,9},{25,17},{2,26},{10... | collective-permute-start | bytes 786440 | tf_op jit(solution)/shard_map/ppermute | solution.py:18
  9.0 1.0 %collective-permute-start.2 = (bf16[1,2,32,16,128]{4,3,2,1,0:T(8,128)(2,1)S(1)}, bf16[1,2,32,16,128]{4,3,2,1,0:T(8,128)(2,1)S(1)}, u32[]{:S(2)}, u32[]{:S(2)}) collective-permute-start(bf16[1,2,32,16,128]{4,3,2,1,0:T(8,128)(2,1)S(1)} %get-tuple-element.17), channel_id=1, source_target_pairs={{0,24},{8,0},{16,8},{24,16},{1,25},{9,1},{17,9},{25,17},{2,26},{10... | collective-permute-start | bytes 786440 | tf_op jit(solution)/shard_map/ppermute | solution.py:18
  10.0 0.0 copy-start
  10.0 0.5 %collective-permute-start.3 = (bf16[2,1,32,16,128]{4,3,2,1,0:T(8,128)(2,1)S(1)}, bf16[2,1,32,16,128]{4,3,2,1,0:T(8,128)(2,1)S(1)}, u32[]{:S(2)}, u32[]{:S(2)}) collective-permute-start(bf16[2,1,32,16,128]{4,3,2,1,0:T(8,128)(2,1)S(1)} %get-tuple-element.20), channel_id=1, source_target_pairs={{0,7},{1,0},{2,1},{3,2},{4,3},{5,4},{6,5},{7,6},{8,15},{9,8},{10,9... | collective-permute-start | bytes 786440 | tf_op jit(solution)/shard_map/ppermute | solution.py:18
  10.5 6.1 %inner.1 = (f32[32,512]{1,0:T(8,128)S(1)}, bf16[4,128,1024]{2,1,0:T(8,128)(2,1)S(1)}) custom-call(bf16[4,4,32,16,128]{4,3,2,1,0:T(8,128)(2,1)} %nulls.5, bf16[2,4,32,64,128]{4,3,2,1,0:T(8,128)(2,1)} %time_links.1, bf16[4,2,32,64,128]{4,3,2,1,0:T(8,128)(2,1)} %space_links.1), custom_call_target="tpu_custom_call" | custom-call | flops 1000 | bytes 1000 | tf_op jit(solution)/shard_map/inner/pallas_call | solution.py:314
  16.6 0.0 collective-permute-done.space_edge
  16.6 0.0 collective-permute-done.1.time_first
  16.6 0.0 collective-permute-done.2.time_second
  16.7 0.0 copy-done
  16.7 0.9 %middle.1 = (f32[24,512]{1,0:T(8,128)S(1)}, f32[2,64,64]{2,1,0:T(8,128)S(1)}) custom-call(s32[1]{0:T(128)} %bitcast.place, s32[8,64]{1,0:T(8,128)S(1)} %copy-done, bf16[2,1,32,16,128]{4,3,2,1,0:T(8,128)(2,1)S(1)} %collective-permute-done.space_edge, bf16[1,2,32,16,128]{4,3,2,1,0:T(8,128)(2,1)S(1)} %collective-permute-done.1.time_first, ...), custom_call_target="tpu_custom_call" | custom-call | flops 1000 | bytes 1000 | tf_op jit(solution)/shard_map/middle/pallas_call | solution.py:333
  17.6 0.6 %collective-permute-done.3.space_edge = bf16[2,1,32,16,128]{4,3,2,1,0:T(8,128)(2,1)S(1)} collective-permute-done((bf16[2,1,32,16,128]{4,3,2,1,0:T(8,128)(2,1)S(1)}, bf16[2,1,32,16,128]{4,3,2,1,0:T(8,128)(2,1)S(1)}, u32[]{:S(2)}, u32[]{:S(2)}) %collective-permute-start.3) | collective-permute-done | bytes 262176 | tf_op jit(solution)/shard_map/ppermute | solution.py:18
  18.2 0.6 %final.1.late = bf16[64,512]{1,0:T(8,128)(2,1)S(1)} custom-call(bf16[2,1,32,16,128]{4,3,2,1,0:T(8,128)(2,1)S(1)} %collective-permute-done.3.space_edge, bf16[4,128,1024]{2,1,0:T(8,128)(2,1)S(1)} %get-tuple-element.18.adjoint, f32[32,512]{1,0:T(8,128)S(1)} %get-tuple-element.21.early, f32[24,512]{1,0:T(8,128)S(1)} %get-tuple-element.22.found), custom_call_target="tpu_custom_call" | custom-call | flops 1000 | bytes 1000 | tf_op jit(solution)/shard_map/final/pallas_call | solution.py:345
  18.7 0.9 %collective-permute-start.4 = (bf16[64,512]{1,0:T(8,128)(2,1)S(1)}, bf16[64,512]{1,0:T(8,128)(2,1)S(1)}, u32[]{:S(2)}, u32[]{:S(2)}) collective-permute-start(bf16[64,512]{1,0:T(8,128)(2,1)S(1)} %final.1.late), channel_id=1, source_target_pairs={{0,1},{1,0},{2,3},{3,2},{4,5},{5,4},{6,7},{7,6},{8,9},{9,8},{10,11... | collective-permute-start | bytes 196616 | tf_op jit(solution)/shard_map/ppermute | solution.py:22
  19.7 3.3 %collective-permute-done.4.late_other = bf16[64,512]{1,0:T(8,128)(2,1)S(1)} collective-permute-done((bf16[64,512]{1,0:T(8,128)(2,1)S(1)}, bf16[64,512]{1,0:T(8,128)(2,1)S(1)}, u32[]{:S(2)}, u32[]{:S(2)}) %collective-permute-start.4) | collective-permute-done | bytes 65568 | tf_op jit(solution)/shard_map/ppermute | solution.py:22
  23.0 0.2 pack.1
  23.2 1.0 %collective-permute-start.5 = (bf16[16,1024]{1,0:T(8,128)(2,1)S(1)}, bf16[16,1024]{1,0:T(8,128)(2,1)S(1)}, u32[]{:S(2)}, u32[]{:S(2)}) collective-permute-start(bf16[16,1024]{1,0:T(8,128)(2,1)S(1)} %get-tuple-element.23), channel_id=1, source_target_pairs={{0,4},{1,5},{2,6},{3,7},{4,0},{5,1},{6,2},{7,3},{8,12},{9,13},{10,... | collective-permute-start | bytes 98312 | tf_op jit(solution)/shard_map/ppermute | solution.py:22
  24.2 2.9 %collective-permute-start.6 = (bf16[16,1024]{1,0:T(8,128)(2,1)S(1)}, bf16[16,1024]{1,0:T(8,128)(2,1)S(1)}, u32[]{:S(2)}, u32[]{:S(2)}) collective-permute-start(bf16[16,1024]{1,0:T(8,128)(2,1)S(1)} %get-tuple-element.24), channel_id=1, source_target_pairs={{0,6},{1,7},{2,4},{3,5},{4,2},{5,3},{6,0},{7,1},{8,14},{9,15},{10,... | collective-permute-start | bytes 98312 | tf_op jit(solution)/shard_map/ppermute | solution.py:22
  27.1 0.5 %collective-permute-start.7 = (bf16[16,1024]{1,0:T(8,128)(2,1)S(1)}, bf16[16,1024]{1,0:T(8,128)(2,1)S(1)}, u32[]{:S(2)}, u32[]{:S(2)}) collective-permute-start(bf16[16,1024]{1,0:T(8,128)(2,1)S(1)} %get-tuple-element.25), channel_id=1, source_target_pairs={{0,2},{1,3},{2,0},{3,1},{4,6},{5,7},{6,4},{7,5},{8,10},{9,11},{10,... | collective-permute-start | bytes 98312 | tf_op jit(solution)/shard_map/ppermute | solution.py:22
  27.6 0.6 %collective-permute-done.5.refs_0_ = bf16[16,1024]{1,0:T(8,128)(2,1)S(1)} collective-permute-done((bf16[16,1024]{1,0:T(8,128)(2,1)S(1)}, bf16[16,1024]{1,0:T(8,128)(2,1)S(1)}, u32[]{:S(2)}, u32[]{:S(2)}) %collective-permute-start.5) | collective-permute-done | bytes 32800 | tf_op jit(solution)/shard_map/ppermute | solution.py:22
  28.2 1.7 %collective-permute-done.6.refs_1_ = bf16[16,1024]{1,0:T(8,128)(2,1)S(1)} collective-permute-done((bf16[16,1024]{1,0:T(8,128)(2,1)S(1)}, bf16[16,1024]{1,0:T(8,128)(2,1)S(1)}, u32[]{:S(2)}, u32[]{:S(2)}) %collective-permute-start.6) | collective-permute-done | bytes 32800 | tf_op jit(solution)/shard_map/ppermute | solution.py:22
  29.9 1.1 %collective-permute-done.7.refs_2_ = bf16[16,1024]{1,0:T(8,128)(2,1)S(1)} collective-permute-done((bf16[16,1024]{1,0:T(8,128)(2,1)S(1)}, bf16[16,1024]{1,0:T(8,128)(2,1)S(1)}, u32[]{:S(2)}, u32[]{:S(2)}) %collective-permute-start.7) | collective-permute-done | bytes 32800 | tf_op jit(solution)/shard_map/ppermute | solution.py:22
  31.0 0.7 %unpack.1 = f32[64,1024]{1,0:T(8,128)} custom-call(s32[1]{0:T(128)} %bitcast.place, bf16[16,1024]{1,0:T(8,128)(2,1)S(1)} %collective-permute-done.5.refs_0_, bf16[16,1024]{1,0:T(8,128)(2,1)S(1)} %collective-permute-done.6.refs_1_, bf16[16,1024]{1,0:T(8,128)(2,1)S(1)} %collective-permute-done.7.refs_2_, bf16[16,1024]{1,0:T(8,128)(2,1)S(1)} %get-tuple-element.26.refs_3_), custom_call_target="tpu_custom_call" | custom-call | flops 1000 | bytes 1000 | tf_op jit(solution)/shard_map/unpack/pallas_call | solution.py:367
Async XLA Ops:
  0.9 15.7 %collective-permute-start = (bf16[2,1,32,16,128]{4,3,2,1,0:T(8,128)(2,1)S(1)}, bf16[2,1,32,16,128]{4,3,2,1,0:T(8,128)(2,1)S(1)}, u32[]{:S(2)}, u32[]{:S(2)}) collective-permute-start(bf16[2,1,32,16,128]{4,3,2,1,0:T(8,128)(2,1)S(1)} %slice_first.1), channel_id=1, source_target_pairs={{0,7},{1,0},{2,1},{3,2},{4,3},{5,4},{6,5},{7,6},{8,15},{9,8},{10,9... | collective-permute-start | bytes 786440 | tf_op jit(solution)/shard_map/ppermute | solution.py:18
  8.3 8.3 %collective-permute-start.1 = (bf16[1,2,32,16,128]{4,3,2,1,0:T(8,128)(2,1)S(1)}, bf16[1,2,32,16,128]{4,3,2,1,0:T(8,128)(2,1)S(1)}, u32[]{:S(2)}, u32[]{:S(2)}) collective-permute-start(bf16[1,2,32,16,128]{4,3,2,1,0:T(8,128)(2,1)S(1)} %get-tuple-element.16), channel_id=1, source_target_pairs={{0,24},{8,0},{16,8},{24,16},{1,25},{9,1},{17,9},{25,17},{2,26},{10... | collective-permute-start | bytes 786440 | tf_op jit(solution)/shard_map/ppermute | solution.py:18
  9.0 7.6 %collective-permute-start.2 = (bf16[1,2,32,16,128]{4,3,2,1,0:T(8,128)(2,1)S(1)}, bf16[1,2,32,16,128]{4,3,2,1,0:T(8,128)(2,1)S(1)}, u32[]{:S(2)}, u32[]{:S(2)}) collective-permute-start(bf16[1,2,32,16,128]{4,3,2,1,0:T(8,128)(2,1)S(1)} %get-tuple-element.17), channel_id=1, source_target_pairs={{0,24},{8,0},{16,8},{24,16},{1,25},{9,1},{17,9},{25,17},{2,26},{10... | collective-permute-start | bytes 786440 | tf_op jit(solution)/shard_map/ppermute | solution.py:18
  10.0 6.7 %copy-start = (s32[8,64]{1,0:T(8,128)S(1)}, s32[8,64]{1,0:T(8,128)}, u32[]{:S(2)}) copy-start(s32[8,64]{1,0:T(8,128)} %lists.1) | copy-start | bytes 6148
  10.0 8.2 %collective-permute-start.3 = (bf16[2,1,32,16,128]{4,3,2,1,0:T(8,128)(2,1)S(1)}, bf16[2,1,32,16,128]{4,3,2,1,0:T(8,128)(2,1)S(1)}, u32[]{:S(2)}, u32[]{:S(2)}) collective-permute-start(bf16[2,1,32,16,128]{4,3,2,1,0:T(8,128)(2,1)S(1)} %get-tuple-element.20), channel_id=1, source_target_pairs={{0,7},{1,0},{2,1},{3,2},{4,3},{5,4},{6,5},{7,6},{8,15},{9,8},{10,9... | collective-permute-start | bytes 786440 | tf_op jit(solution)/shard_map/ppermute | solution.py:18
  18.7 4.3 %collective-permute-start.4 = (bf16[64,512]{1,0:T(8,128)(2,1)S(1)}, bf16[64,512]{1,0:T(8,128)(2,1)S(1)}, u32[]{:S(2)}, u32[]{:S(2)}) collective-permute-start(bf16[64,512]{1,0:T(8,128)(2,1)S(1)} %final.1.late), channel_id=1, source_target_pairs={{0,1},{1,0},{2,3},{3,2},{4,5},{5,4},{6,7},{7,6},{8,9},{9,8},{10,11... | collective-permute-start | bytes 196616 | tf_op jit(solution)/shard_map/ppermute | solution.py:22
  23.2 5.0 %collective-permute-start.5 = (bf16[16,1024]{1,0:T(8,128)(2,1)S(1)}, bf16[16,1024]{1,0:T(8,128)(2,1)S(1)}, u32[]{:S(2)}, u32[]{:S(2)}) collective-permute-start(bf16[16,1024]{1,0:T(8,128)(2,1)S(1)} %get-tuple-element.23), channel_id=1, source_target_pairs={{0,4},{1,5},{2,6},{3,7},{4,0},{5,1},{6,2},{7,3},{8,12},{9,13},{10,... | collective-permute-start | bytes 98312 | tf_op jit(solution)/shard_map/ppermute | solution.py:22
  24.2 5.7 %collective-permute-start.6 = (bf16[16,1024]{1,0:T(8,128)(2,1)S(1)}, bf16[16,1024]{1,0:T(8,128)(2,1)S(1)}, u32[]{:S(2)}, u32[]{:S(2)}) collective-permute-start(bf16[16,1024]{1,0:T(8,128)(2,1)S(1)} %get-tuple-element.24), channel_id=1, source_target_pairs={{0,6},{1,7},{2,4},{3,5},{4,2},{5,3},{6,0},{7,1},{8,14},{9,15},{10,... | collective-permute-start | bytes 98312 | tf_op jit(solution)/shard_map/ppermute | solution.py:22
  27.1 3.9 %collective-permute-start.7 = (bf16[16,1024]{1,0:T(8,128)(2,1)S(1)}, bf16[16,1024]{1,0:T(8,128)(2,1)S(1)}, u32[]{:S(2)}, u32[]{:S(2)}) collective-permute-start(bf16[16,1024]{1,0:T(8,128)(2,1)S(1)} %get-tuple-element.25), channel_id=1, source_target_pairs={{0,2},{1,3},{2,0},{3,1},{4,6},{5,7},{6,4},{7,5},{8,10},{9,11},{10,... | collective-permute-start | bytes 98312 | tf_op jit(solution)/shard_map/ppermute | solution.py:22

commit v16 on v14

--- a/solution.py
+++ b/solution.py
@@ -162,7 +162,7 @@
             picks[1, rows, :] = jnp.where(here & (turned == chosen), 1.0, 0.0)
 
 
-def inner_kernel(nulls, time_links, space_links, early, adjoint, links, vecs, left, right, sems):
+def inner_work(nulls, time_links, space_links, early, adjoint, links, vecs, left, right, sems):
     time_count, space_count, sites, vectors, width = nulls.shape
     copies = []
     bases = [pltpu.make_async_copy(nulls.at[t], vecs.at[t], sems.at[16 + t]) for t in range(4)]
@@ -213,6 +213,35 @@
         adjoint_item(links.at[12 + t], vecs.at[t, 3], t % 2, adjoint.at[2 + t // 2])
 
 
+def before_kernel(group, nulls, time_links, space_links, edge, *refs):
+    half = edge.shape[0]
+    sem = refs[-1]
+    copies = [
+        pltpu.make_async_copy(nulls.at[pl.ds(half + row, 1), pl.ds(0, 1)], edge.at[pl.ds(row, 1)], sem.at[row])
+        for row in range(half)
+    ]
+    for copy in copies:
+        copy.start()
+
+    @pl.when(lax.rem(group[0], 2) == 1)
+    def _():
+        inner_work(nulls, time_links, space_links, *refs[:-1])
+
+    for copy in copies:
+        copy.wait()
+
+
+def after_kernel(group, nulls, time_links, space_links, early_before, adjoint_before, early, adjoint, *refs):
+    @pl.when(lax.rem(group[0], 2) == 0)
+    def _():
+        inner_work(nulls, time_links, space_links, early, adjoint, *refs)
+
+    @pl.when(lax.rem(group[0], 2) == 1)
+    def _():
+        early[...] = early_before[...]
+        adjoint[...] = adjoint_before[...]
+
+
 def edge_rows(uppers, adjoint, vectors):
     width = uppers[0].shape[-1]
     sign = signs((vectors, width), jnp.bfloat16)
@@ -275,6 +304,7 @@
     local_count = (time_count // 2) * (space_count // 2) * aggs
     wide = 2 * vectors * vectors
     place = lax.axis_index("xyz").astype(jnp.int32).reshape(1)
+    group = lax.axis_index("ta").astype(jnp.int32).reshape(1)
     vmem = pl.BlockSpec(memory_space=pltpu.VMEM)
     smem = pl.BlockSpec(memory_space=pltpu.SMEM)
     anywhere = pl.BlockSpec(memory_space=pl.ANY)
@@ -300,32 +330,43 @@
         )(nulls)
 
     half_space = space_count // 2
-    (space_first,) = sliced("slice_first", (0, half_time, 0, 1))
-    space_second, time_first, time_second = sliced(
-        "slice_rest", (half_time, half_time, 0, 1), (0, 1, 0, half_space), (0, 1, half_space, half_space)
+    space_first, time_first, time_second = sliced(
+        "slices", (0, half_time, 0, 1), (0, 1, 0, half_space), (0, 1, half_space, half_space)
     )
     edge_first = shifted(space_first, "xyz", -1)
     edge_times = [shifted(time_first, "ta", -1), shifted(time_second, "ta", -1)]
+    inner_out = [
+        jax.ShapeDtypeStruct((4 * aggs, wide), jnp.bfloat16),
+        jax.ShapeDtypeStruct((4, vectors * aggs, 8 * width), jnp.bfloat16),
+    ]
+    inner_scratch = [
+        pltpu.VMEM((16, sites, half, width), jnp.bfloat16),
+        pltpu.VMEM(nulls.shape, nulls.dtype),
+        pltpu.VMEM((4, vectors * aggs, 8 * width), jnp.bfloat16),
+        pltpu.VMEM((4, 8 * width, 2 * vectors * aggs), jnp.bfloat16),
+        pltpu.SemaphoreType.DMA((20,)),
+    ]
+    space_second, early_one, adjoint_one = pl.pallas_call(
+        before_kernel,
+        in_specs=[smem] + [outside] * 3,
+        out_specs=[vmem] * 3,
+        out_shape=[jax.ShapeDtypeStruct(space_first.shape, nulls.dtype)] + inner_out,
+        scratch_shapes=inner_scratch + [pltpu.SemaphoreType.DMA((half_time,))],
+        compiler_params=roomy,
+        cost_estimate=tiny,
+        name="before",
+    )(group, nulls, time_links, space_links)
     edge_second = shifted(space_second, "xyz", -1)
     early, adjoint = pl.pallas_call(
-        inner_kernel,
-        in_specs=[outside] * 3,
+        after_kernel,
+        in_specs=[smem] + [outside] * 3 + [vmem] * 2,
         out_specs=[vmem] * 2,
-        out_shape=[
-            jax.ShapeDtypeStruct((4 * aggs, wide), jnp.bfloat16),
-            jax.ShapeDtypeStruct((4, vectors * aggs, 8 * width), jnp.bfloat16),
-        ],
-        scratch_shapes=[
-            pltpu.VMEM((16, sites, half, width), jnp.bfloat16),
-            pltpu.VMEM(nulls.shape, nulls.dtype),
-            pltpu.VMEM((4, vectors * aggs, 8 * width), jnp.bfloat16),
-            pltpu.VMEM((4, 8 * width, 2 * vectors * aggs), jnp.bfloat16),
-            pltpu.SemaphoreType.DMA((20,)),
-        ],
+        out_shape=inner_out,
+        scratch_shapes=inner_scratch,
         compiler_params=roomy,
         cost_estimate=tiny,
-        name="inner",
-    )(nulls, time_links, space_links)
+        name="after",
+    )(group, nulls, time_links, space_links, early_one, adjoint_one)
     found, picks = pl.pallas_call(
         middle_kernel,
         in_specs=[smem] + [vmem] * 5,

time: 31.7 us -> 31.3 us (0.987)
  waiting for transfers between devices: 6.84 us -> 6.3 us
    pallas_call x1 -> x2, Pallas kernels: 6.12 us -> 7.3 us  [the longest x1 6.14 us: on_device(): pl.pallas_call(after_kernel, in_specs=[smem] + [outside] * 3 + [vmem] * 2...]
    pallas_call x2 -> x1, Pallas kernels: 2.18 us -> 1.2 us  [sliced(): pl.pallas_call(functools.partial(slice_kernel, sources=sources), in_specs...]
    ppermute x5, waiting for transfers between devices: 6.83 us -> 6.29 us  [crossed(): lax.ppermute(array, axis, [(i, i ^ bits) for i in range(lax.axis_size(axi...]
where the time goes in v16:
time: 31.3 us; the launch traced here: 31.1 us
  starting transfers between devices  13.9 us (44%)
  Pallas kernels  10.9 us (35%)
  waiting for transfers between devices  6.3 us (20%)
    ppermute x4, starting transfers between devices, shifted(): lax.ppermute(array, axis, [(i, (i + by) % count) for i in range(count)])  8.22 us
    ppermute x5, waiting for transfers between devices, crossed(): lax.ppermute(array, axis, [(i, i ^ bits) for i in range(lax.axis_size(axi...  6.29 us
    pallas_call x1, Pallas kernels, on_device(): pl.pallas_call(after_kernel, in_specs=[smem] + [outside] * 3 + [vmem] * 2...  6.14 us
    ppermute x5, starting transfers between devices, crossed(): lax.ppermute(array, axis, [(i, i ^ bits) for i in range(lax.axis_size(axi...  5.65 us
    pallas_call x1, Pallas kernels, sliced(): pl.pallas_call(functools.partial(slice_kernel, sources=sources), in_specs...  1.2 us
    pallas_call x1, Pallas kernels, on_device(): pl.pallas_call(before_kernel, in_specs=[smem] + [outside] * 3, out_specs=...  1.16 us
    pallas_call x1, Pallas kernels, on_device(): pl.pallas_call(middle_kernel, in_specs=[smem] + [vmem] * 5, out_specs=[vm...  0.91 us
    pallas_call x1, Pallas kernels, on_device(): pl.pallas_call(functools.partial(unpack_kernel, turns=turns + [0]), in_sp...  0.74 us
  transfers between devices with their start and end apart: 9, of which 5 were waited for; matrix products, arithmetic and copies ran while one was open for 0% of the time, Pallas kernels for 28%

profile of v16, /device:TPU:0, one launch (start us, length us, event | category | flops | bytes accessed | tf_op | source)
XLA Modules:
  0.0 31.1 jit_solution(8991783270354501501)
XLA Ops:
  0.0 1.2 %slices.1 = (bf16[2,1,32,16,128]{4,3,2,1,0:T(8,128)(2,1)S(1)}, bf16[1,2,32,16,128]{4,3,2,1,0:T(8,128)(2,1)S(1)}, bf16[1,2,32,16,128]{4,3,2,1,0:T(8,128)(2,1)S(1)}) custom-call(bf16[4,4,32,16,128]{4,3,2,1,0:T(8,128)(2,1)} %nulls.5), custom_call_target="tpu_custom_call" | custom-call | flops 1000 | bytes 1000 | tf_op jit(solution)/shard_map/slices/pallas_call | solution.py:321
  1.2 6.1 %collective-permute-start = (bf16[2,1,32,16,128]{4,3,2,1,0:T(8,128)(2,1)S(1)}, bf16[2,1,32,16,128]{4,3,2,1,0:T(8,128)(2,1)S(1)}, u32[]{:S(2)}, u32[]{:S(2)}) collective-permute-start(bf16[2,1,32,16,128]{4,3,2,1,0:T(8,128)(2,1)S(1)} %get-tuple-element.19), channel_id=1, source_target_pairs={{0,7},{1,0},{2,1},{3,2},{4,3},{5,4},{6,5},{7,6},{8,15},{9,8},{10,9... | collective-permute-start | bytes 786440 | tf_op jit(solution)/shard_map/ppermute | solution.py:18
  7.3 0.7 %collective-permute-start.1 = (bf16[1,2,32,16,128]{4,3,2,1,0:T(8,128)(2,1)S(1)}, bf16[1,2,32,16,128]{4,3,2,1,0:T(8,128)(2,1)S(1)}, u32[]{:S(2)}, u32[]{:S(2)}) collective-permute-start(bf16[1,2,32,16,128]{4,3,2,1,0:T(8,128)(2,1)S(1)} %get-tuple-element.20), channel_id=1, source_target_pairs={{0,24},{8,0},{16,8},{24,16},{1,25},{9,1},{17,9},{25,17},{2,26},{10... | collective-permute-start | bytes 786440 | tf_op jit(solution)/shard_map/ppermute | solution.py:18
  7.9 1.0 %collective-permute-start.2 = (bf16[1,2,32,16,128]{4,3,2,1,0:T(8,128)(2,1)S(1)}, bf16[1,2,32,16,128]{4,3,2,1,0:T(8,128)(2,1)S(1)}, u32[]{:S(2)}, u32[]{:S(2)}) collective-permute-start(bf16[1,2,32,16,128]{4,3,2,1,0:T(8,128)(2,1)S(1)} %get-tuple-element.21), channel_id=1, source_target_pairs={{0,24},{8,0},{16,8},{24,16},{1,25},{9,1},{17,9},{25,17},{2,26},{10... | collective-permute-start | bytes 786440 | tf_op jit(solution)/shard_map/ppermute | solution.py:18
  8.9 1.2 %before.1 = (bf16[2,1,32,16,128]{4,3,2,1,0:T(8,128)(2,1)S(1)}, bf16[32,512]{1,0:T(8,128)(2,1)S(1)}, bf16[4,128,1024]{2,1,0:T(8,128)(2,1)S(1)}) custom-call(s32[1]{0:T(128)} %bitcast.1.group, bf16[4,4,32,16,128]{4,3,2,1,0:T(8,128)(2,1)} %nulls.5, bf16[2,4,32,64,128]{4,3,2,1,0:T(8,128)(2,1)} %time_links.3, bf16[4,2,32,64,128]{4,3,2,1,0:T(8,128)(2,1)} %space_links.3), custom_call_target="tpu_custom_call" | custom-call | flops 1000 | bytes 1000 | tf_op jit(solution)/shard_map/before/pallas_call | solution.py:349
  10.0 0.6 %collective-permute-start.4 = (bf16[2,1,32,16,128]{4,3,2,1,0:T(8,128)(2,1)S(1)}, bf16[2,1,32,16,128]{4,3,2,1,0:T(8,128)(2,1)S(1)}, u32[]{:S(2)}, u32[]{:S(2)}) collective-permute-start(bf16[2,1,32,16,128]{4,3,2,1,0:T(8,128)(2,1)S(1)} %get-tuple-element.27), channel_id=1, source_target_pairs={{0,7},{1,0},{2,1},{3,2},{4,3},{5,4},{6,5},{7,6},{8,15},{9,8},{10,9... | collective-permute-start | bytes 786440 | tf_op jit(solution)/shard_map/ppermute | solution.py:18
  10.6 0.0 copy-start
  10.6 6.1 %after.1 = (bf16[32,512]{1,0:T(8,128)(2,1)S(1)}, bf16[4,128,1024]{2,1,0:T(8,128)(2,1)S(1)}) custom-call(s32[1]{0:T(128)} %bitcast.1.group, bf16[4,4,32,16,128]{4,3,2,1,0:T(8,128)(2,1)} %nulls.5, bf16[2,4,32,64,128]{4,3,2,1,0:T(8,128)(2,1)} %time_links.3, bf16[4,2,32,64,128]{4,3,2,1,0:T(8,128)(2,1)} %space_links.3, ...), custom_call_target="tpu_custom_call" | custom-call | flops 1000 | bytes 1000 | tf_op jit(solution)/shard_map/after/pallas_call | solution.py:360
  16.7 1.6 %collective-permute-start.3 = (bf16[32,512]{1,0:T(8,128)(2,1)S(1)}, bf16[32,512]{1,0:T(8,128)(2,1)S(1)}, u32[]{:S(2)}, u32[]{:S(2)}) collective-permute-start(bf16[32,512]{1,0:T(8,128)(2,1)S(1)} %get-tuple-element.26.early), channel_id=1, source_target_pairs={{0,1},{1,0},{2,3},{3,2},{4,5},{5,4},{6,7},{7,6},{8,9},{9,8},{10,11... | collective-permute-start | bytes 98312 | tf_op jit(solution)/shard_map/ppermute | solution.py:22
  18.3 0.0 collective-permute-done.space_edge
  18.3 0.0 collective-permute-done.1.time_first
  18.3 0.0 collective-permute-done.2.time_second
  18.3 0.0 copy-done
  18.4 0.9 %middle.1 = (f32[24,512]{1,0:T(8,128)S(1)}, f32[2,64,64]{2,1,0:T(8,128)S(1)}) custom-call(s32[1]{0:T(128)} %bitcast.place, s32[8,64]{1,0:T(8,128)S(1)} %copy-done, bf16[2,1,32,16,128]{4,3,2,1,0:T(8,128)(2,1)S(1)} %collective-permute-done.space_edge, bf16[1,2,32,16,128]{4,3,2,1,0:T(8,128)(2,1)S(1)} %collective-permute-done.1.time_first, ...), custom_call_target="tpu_custom_call" | custom-call | flops 1000 | bytes 1000 | tf_op jit(solution)/shard_map/middle/pallas_call | solution.py:370
  19.3 0.0 collective-permute-done.4.space_edge
  19.3 0.6 %final.1.late = bf16[32,512]{1,0:T(8,128)(2,1)S(1)} custom-call(bf16[2,1,32,16,128]{4,3,2,1,0:T(8,128)(2,1)S(1)} %collective-permute-done.4.space_edge, bf16[4,128,1024]{2,1,0:T(8,128)(2,1)S(1)} %get-tuple-element.24.adjoint, f32[24,512]{1,0:T(8,128)S(1)} %get-tuple-element.28.found), custom_call_target="tpu_custom_call" | custom-call | flops 1000 | bytes 1000 | tf_op jit(solution)/shard_map/final/pallas_call | solution.py:382
  19.8 0.5 %collective-permute-start.5 = (bf16[32,512]{1,0:T(8,128)(2,1)S(1)}, bf16[32,512]{1,0:T(8,128)(2,1)S(1)}, u32[]{:S(2)}, u32[]{:S(2)}) collective-permute-start(bf16[32,512]{1,0:T(8,128)(2,1)S(1)} %final.1.late), channel_id=1, source_target_pairs={{0,1},{1,0},{2,3},{3,2},{4,5},{5,4},{6,7},{7,6},{8,9},{9,8},{10,11... | collective-permute-start | bytes 98312 | tf_op jit(solution)/shard_map/ppermute | solution.py:22
  20.4 0.8 %collective-permute-done.3.early_other = bf16[32,512]{1,0:T(8,128)(2,1)S(1)} collective-permute-done((bf16[32,512]{1,0:T(8,128)(2,1)S(1)}, bf16[32,512]{1,0:T(8,128)(2,1)S(1)}, u32[]{:S(2)}, u32[]{:S(2)}) %collective-permute-start.3) | collective-permute-done | bytes 32800 | tf_op jit(solution)/shard_map/ppermute | solution.py:22
  21.1 2.6 %collective-permute-done.5.late_other = bf16[32,512]{1,0:T(8,128)(2,1)S(1)} collective-permute-done((bf16[32,512]{1,0:T(8,128)(2,1)S(1)}, bf16[32,512]{1,0:T(8,128)(2,1)S(1)}, u32[]{:S(2)}, u32[]{:S(2)}) %collective-permute-start.5) | collective-permute-done | bytes 32800 | tf_op jit(solution)/shard_map/ppermute | solution.py:22
  23.8 0.2 pack.1
  23.9 0.1 collective-permute-start.6
  24.0 0.8 %collective-permute-start.7 = (bf16[16,1024]{1,0:T(8,128)(2,1)S(1)}, bf16[16,1024]{1,0:T(8,128)(2,1)S(1)}, u32[]{:S(2)}, u32[]{:S(2)}) collective-permute-start(bf16[16,1024]{1,0:T(8,128)(2,1)S(1)} %get-tuple-element.30), channel_id=1, source_target_pairs={{0,6},{1,7},{2,4},{3,5},{4,2},{5,3},{6,0},{7,1},{8,14},{9,15},{10,... | collective-permute-start | bytes 98312 | tf_op jit(solution)/shard_map/ppermute | solution.py:22
  24.8 2.7 %collective-permute-start.8 = (bf16[16,1024]{1,0:T(8,128)(2,1)S(1)}, bf16[16,1024]{1,0:T(8,128)(2,1)S(1)}, u32[]{:S(2)}, u32[]{:S(2)}) collective-permute-start(bf16[16,1024]{1,0:T(8,128)(2,1)S(1)} %get-tuple-element.31), channel_id=1, source_target_pairs={{0,2},{1,3},{2,0},{3,1},{4,6},{5,7},{6,4},{7,5},{8,10},{9,11},{10,... | collective-permute-start | bytes 98312 | tf_op jit(solution)/shard_map/ppermute | solution.py:22
  27.5 1.7 %collective-permute-done.6.refs_0_ = bf16[16,1024]{1,0:T(8,128)(2,1)S(1)} collective-permute-done((bf16[16,1024]{1,0:T(8,128)(2,1)S(1)}, bf16[16,1024]{1,0:T(8,128)(2,1)S(1)}, u32[]{:S(2)}, u32[]{:S(2)}) %collective-permute-start.6) | collective-permute-done | bytes 32800 | tf_op jit(solution)/shard_map/ppermute | solution.py:22
  29.2 1.0 %collective-permute-done.7.refs_1_ = bf16[16,1024]{1,0:T(8,128)(2,1)S(1)} collective-permute-done((bf16[16,1024]{1,0:T(8,128)(2,1)S(1)}, bf16[16,1024]{1,0:T(8,128)(2,1)S(1)}, u32[]{:S(2)}, u32[]{:S(2)}) %collective-permute-start.7) | collective-permute-done | bytes 32800 | tf_op jit(solution)/shard_map/ppermute | solution.py:22
  30.1 0.2 collective-permute-done.8.refs_2_
  30.4 0.7 %unpack.1 = f32[64,1024]{1,0:T(8,128)} custom-call(s32[1]{0:T(128)} %bitcast.place, bf16[16,1024]{1,0:T(8,128)(2,1)S(1)} %collective-permute-done.6.refs_0_, bf16[16,1024]{1,0:T(8,128)(2,1)S(1)} %collective-permute-done.7.refs_1_, bf16[16,1024]{1,0:T(8,128)(2,1)S(1)} %collective-permute-done.8.refs_2_, bf16[16,1024]{1,0:T(8,128)(2,1)S(1)} %get-tuple-element.32.refs_3_), custom_call_target="tpu_custom_call" | custom-call | flops 1000 | bytes 1000 | tf_op jit(solution)/shard_map/unpack/pallas_call | solution.py:405
Async XLA Ops:
  1.2 17.1 %collective-permute-start = (bf16[2,1,32,16,128]{4,3,2,1,0:T(8,128)(2,1)S(1)}, bf16[2,1,32,16,128]{4,3,2,1,0:T(8,128)(2,1)S(1)}, u32[]{:S(2)}, u32[]{:S(2)}) collective-permute-start(bf16[2,1,32,16,128]{4,3,2,1,0:T(8,128)(2,1)S(1)} %get-tuple-element.19), channel_id=1, source_target_pairs={{0,7},{1,0},{2,1},{3,2},{4,3},{5,4},{6,5},{7,6},{8,15},{9,8},{10,9... | collective-permute-start | bytes 786440 | tf_op jit(solution)/shard_map/ppermute | solution.py:18
  7.3 11.1 %collective-permute-start.1 = (bf16[1,2,32,16,128]{4,3,2,1,0:T(8,128)(2,1)S(1)}, bf16[1,2,32,16,128]{4,3,2,1,0:T(8,128)(2,1)S(1)}, u32[]{:S(2)}, u32[]{:S(2)}) collective-permute-start(bf16[1,2,32,16,128]{4,3,2,1,0:T(8,128)(2,1)S(1)} %get-tuple-element.20), channel_id=1, source_target_pairs={{0,24},{8,0},{16,8},{24,16},{1,25},{9,1},{17,9},{25,17},{2,26},{10... | collective-permute-start | bytes 786440 | tf_op jit(solution)/shard_map/ppermute | solution.py:18
  7.9 10.4 %collective-permute-start.2 = (bf16[1,2,32,16,128]{4,3,2,1,0:T(8,128)(2,1)S(1)}, bf16[1,2,32,16,128]{4,3,2,1,0:T(8,128)(2,1)S(1)}, u32[]{:S(2)}, u32[]{:S(2)}) collective-permute-start(bf16[1,2,32,16,128]{4,3,2,1,0:T(8,128)(2,1)S(1)} %get-tuple-element.21), channel_id=1, source_target_pairs={{0,24},{8,0},{16,8},{24,16},{1,25},{9,1},{17,9},{25,17},{2,26},{10... | collective-permute-start | bytes 786440 | tf_op jit(solution)/shard_map/ppermute | solution.py:18
  10.0 9.2 %collective-permute-start.4 = (bf16[2,1,32,16,128]{4,3,2,1,0:T(8,128)(2,1)S(1)}, bf16[2,1,32,16,128]{4,3,2,1,0:T(8,128)(2,1)S(1)}, u32[]{:S(2)}, u32[]{:S(2)}) collective-permute-start(bf16[2,1,32,16,128]{4,3,2,1,0:T(8,128)(2,1)S(1)} %get-tuple-element.27), channel_id=1, source_target_pairs={{0,7},{1,0},{2,1},{3,2},{4,3},{5,4},{6,5},{7,6},{8,15},{9,8},{10,9... | collective-permute-start | bytes 786440 | tf_op jit(solution)/shard_map/ppermute | solution.py:18
  10.6 7.7 %copy-start = (s32[8,64]{1,0:T(8,128)S(1)}, s32[8,64]{1,0:T(8,128)}, u32[]{:S(2)}) copy-start(s32[8,64]{1,0:T(8,128)} %lists.1) | copy-start | bytes 6148
  16.7 4.4 %collective-permute-start.3 = (bf16[32,512]{1,0:T(8,128)(2,1)S(1)}, bf16[32,512]{1,0:T(8,128)(2,1)S(1)}, u32[]{:S(2)}, u32[]{:S(2)}) collective-permute-start(bf16[32,512]{1,0:T(8,128)(2,1)S(1)} %get-tuple-element.26.early), channel_id=1, source_target_pairs={{0,1},{1,0},{2,3},{3,2},{4,5},{5,4},{6,7},{7,6},{8,9},{9,8},{10,11... | collective-permute-start | bytes 98312 | tf_op jit(solution)/shard_map/ppermute | solution.py:22
  19.8 3.9 %collective-permute-start.5 = (bf16[32,512]{1,0:T(8,128)(2,1)S(1)}, bf16[32,512]{1,0:T(8,128)(2,1)S(1)}, u32[]{:S(2)}, u32[]{:S(2)}) collective-permute-start(bf16[32,512]{1,0:T(8,128)(2,1)S(1)} %final.1.late), channel_id=1, source_target_pairs={{0,1},{1,0},{2,3},{3,2},{4,5},{5,4},{6,7},{7,6},{8,9},{9,8},{10,11... | collective-permute-start | bytes 98312 | tf_op jit(solution)/shard_map/ppermute | solution.py:22
  23.9 5.2 %collective-permute-start.6 = (bf16[16,1024]{1,0:T(8,128)(2,1)S(1)}, bf16[16,1024]{1,0:T(8,128)(2,1)S(1)}, u32[]{:S(2)}, u32[]{:S(2)}) collective-permute-start(bf16[16,1024]{1,0:T(8,128)(2,1)S(1)} %get-tuple-element.29), channel_id=1, source_target_pairs={{0,4},{1,5},{2,6},{3,7},{4,0},{5,1},{6,2},{7,3},{8,12},{9,13},{10,... | collective-permute-start | bytes 98312 | tf_op jit(solution)/shard_map/ppermute | solution.py:22
  24.0 6.1 %collective-permute-start.7 = (bf16[16,1024]{1,0:T(8,128)(2,1)S(1)}, bf16[16,1024]{1,0:T(8,128)(2,1)S(1)}, u32[]{:S(2)}, u32[]{:S(2)}) collective-permute-start(bf16[16,1024]{1,0:T(8,128)(2,1)S(1)} %get-tuple-element.30), channel_id=1, source_target_pairs={{0,6},{1,7},{2,4},{3,5},{4,2},{5,3},{6,0},{7,1},{8,14},{9,15},{10,... | collective-permute-start | bytes 98312 | tf_op jit(solution)/shard_map/ppermute | solution.py:22
  24.8 5.6 %collective-permute-start.8 = (bf16[16,1024]{1,0:T(8,128)(2,1)S(1)}, bf16[16,1024]{1,0:T(8,128)(2,1)S(1)}, u32[]{:S(2)}, u32[]{:S(2)}) collective-permute-start(bf16[16,1024]{1,0:T(8,128)(2,1)S(1)} %get-tuple-element.31), channel_id=1, source_target_pairs={{0,2},{1,3},{2,0},{3,1},{4,6},{5,7},{6,4},{7,5},{8,10},{9,11},{10,... | collective-permute-start | bytes 98312 | tf_op jit(solution)/shard_map/ppermute | solution.py:22

commit v17 on v16

--- a/solution.py
+++ b/solution.py
@@ -202,7 +202,7 @@
             t = 2 * a_t + c
             image_item(links.at[4 + t], vecs.at[t, 1], vecs.at[t, 2], c, left.at[2 + a_t], right.at[2 + a_t])
     found = [group_rows(left[group], right[group], MAT_DIMS, vectors) for group in range(4)]
-    early[...] = jnp.concatenate(found, axis=0).astype(jnp.bfloat16)
+    early[...] = jnp.concatenate(found, axis=0)
     for x in range(4):
         copies[8 + x].wait()
     for x in range(4):
@@ -213,22 +213,12 @@
         adjoint_item(links.at[12 + t], vecs.at[t, 3], t % 2, adjoint.at[2 + t // 2])
 
 
-def before_kernel(group, nulls, time_links, space_links, edge, *refs):
-    half = edge.shape[0]
-    sem = refs[-1]
-    copies = [
-        pltpu.make_async_copy(nulls.at[pl.ds(half + row, 1), pl.ds(0, 1)], edge.at[pl.ds(row, 1)], sem.at[row])
-        for row in range(half)
-    ]
-    for copy in copies:
-        copy.start()
+def before_kernel(group, nulls, time_links, space_links, sliced, edge, *refs):
+    edge[...] = sliced[...]
 
     @pl.when(lax.rem(group[0], 2) == 1)
     def _():
-        inner_work(nulls, time_links, space_links, *refs[:-1])
-
-    for copy in copies:
-        copy.wait()
+        inner_work(nulls, time_links, space_links, *refs)
 
 
 def after_kernel(group, nulls, time_links, space_links, early_before, adjoint_before, early, adjoint, *refs):
@@ -266,17 +256,17 @@
     found[...] = jnp.concatenate(rows, axis=0)
 
 
-def final_kernel(space_edge, adjoint, found, late):
+def final_kernel(space_edge, adjoint, early, found, late):
     vectors = space_edge.shape[3]
     rows = edge_rows([space_edge.at[c, 0] for c in range(2)], adjoint[3], vectors)
-    late[...] = jnp.concatenate([found[...], rows], axis=0).astype(jnp.bfloat16)
-
-
-def pack_kernel(picks, early, early_other, late, late_other, *packed):
-    half_count = late.shape[0] // 2
-    pieces = (early, late, early_other, late_other)
-    for half, width in enumerate((late.shape[1],) * 2):
-        rows = jnp.concatenate([piece[pl.ds(half * half_count, half_count), :] for piece in pieces], axis=0)
+    late[...] = jnp.concatenate([early[...], found[...], rows], axis=0).astype(jnp.bfloat16)
+
+
+def pack_kernel(picks, late, late_other, *packed):
+    quarter, width = late.shape[0] // 4, late.shape[1]
+    for half in range(2):
+        spans = [pl.ds((half + 2 * part) * quarter, quarter) for part in range(2)]
+        rows = jnp.concatenate([piece[span, :] for piece in (late, late_other) for span in spans], axis=0)
         sent = dot(picks[half].astype(jnp.bfloat16), rows, MAT_DIMS)
         for turn, out in enumerate(packed):
             mine = sent[turn * 2 * MOST : (turn + 1) * 2 * MOST]
@@ -330,13 +320,17 @@
         )(nulls)
 
     half_space = space_count // 2
-    space_first, time_first, time_second = sliced(
-        "slices", (0, half_time, 0, 1), (0, 1, 0, half_space), (0, 1, half_space, half_space)
+    space_first, space_later, time_first, time_second = sliced(
+        "slices",
+        (0, half_time, 0, 1),
+        (half_time, half_time, 0, 1),
+        (0, 1, 0, half_space),
+        (0, 1, half_space, half_space),
     )
     edge_first = shifted(space_first, "xyz", -1)
     edge_times = [shifted(time_first, "ta", -1), shifted(time_second, "ta", -1)]
     inner_out = [
-        jax.ShapeDtypeStruct((4 * aggs, wide), jnp.bfloat16),
+        jax.ShapeDtypeStruct((4 * aggs, wide), jnp.float32),
         jax.ShapeDtypeStruct((4, vectors * aggs, 8 * width), jnp.bfloat16),
     ]
     inner_scratch = [
@@ -348,14 +342,14 @@
     ]
     space_second, early_one, adjoint_one = pl.pallas_call(
         before_kernel,
-        in_specs=[smem] + [outside] * 3,
+        in_specs=[smem] + [outside] * 3 + [vmem],
         out_specs=[vmem] * 3,
         out_shape=[jax.ShapeDtypeStruct(space_first.shape, nulls.dtype)] + inner_out,
-        scratch_shapes=inner_scratch + [pltpu.SemaphoreType.DMA((half_time,))],
+        scratch_shapes=inner_scratch,
         compiler_params=roomy,
         cost_estimate=tiny,
         name="before",
-    )(group, nulls, time_links, space_links)
+    )(group, nulls, time_links, space_links, space_later)
     edge_second = shifted(space_second, "xyz", -1)
     early, adjoint = pl.pallas_call(
         after_kernel,
@@ -381,25 +375,24 @@
     )(place, owner_lists, edge_first, *edge_times, adjoint)
     late = pl.pallas_call(
         final_kernel,
-        in_specs=[vmem] * 3,
+        in_specs=[vmem] * 4,
         out_specs=vmem,
-        out_shape=jax.ShapeDtypeStruct((4 * aggs, wide), jnp.bfloat16),
+        out_shape=jax.ShapeDtypeStruct((8 * aggs, wide), jnp.bfloat16),
         compiler_params=modest,
         cost_estimate=tiny,
         name="final",
-    )(edge_second, adjoint, found)
-    early_other = crossed(early, "xyz", 1)
+    )(edge_second, adjoint, early, found)
     late_other = crossed(late, "xyz", 1)
     pairs = shards // 2
     packed = pl.pallas_call(
         pack_kernel,
-        in_specs=[vmem] * 5,
+        in_specs=[vmem] * 3,
         out_specs=[vmem] * pairs,
         out_shape=[jax.ShapeDtypeStruct((2 * MOST, 2 * wide), jnp.bfloat16)] * pairs,
         compiler_params=modest,
         cost_estimate=tiny,
         name="pack",
-    )(picks, early, early_other, late, late_other)
+    )(picks, late, late_other)
     turns = list(range(2, pairs)) + [1]
     arrived = [crossed(packed[turn], "xyz", 2 * turn) for turn in turns]
     arrived = pl.pallas_call(

time: 31.3 us -> 30.3 us (0.968)
  Pallas kernels: 10.9 us -> 10 us
  starting transfers between devices: 13.9 us -> 13.3 us
  waiting for transfers between devices: 6.3 us -> 6.72 us
    pallas_call x3, Pallas kernels: 1.88 us -> 0.92 us  [the longest x1 0.56 us: on_device(): pl.pallas_call(final_kernel, in_specs=[vmem] * 4, out_specs=vmem, out_sha...]
    ppermute x5 -> x4, starting transfers between devices: 5.65 us -> 5.08 us  [crossed(): lax.ppermute(array, axis, [(i, i ^ bits) for i in range(lax.axis_size(axi...]
    ppermute x5 -> x4, waiting for transfers between devices: 6.29 us -> 6.71 us  [crossed(): lax.ppermute(array, axis, [(i, i ^ bits) for i in range(lax.axis_size(axi...]
  transfers between devices with their start and end apart: 9 -> 8, of which waited for: 5 -> 4; matrix products, arithmetic and copies ran while one was open for 0% -> 0% of each run, Pallas kernels for 28% -> 24%
where the time goes in v17:
time: 30.3 us; the launch traced here: 30.2 us
  starting transfers between devices  13.3 us (44%)
  Pallas kernels  10 us (33%)
  waiting for transfers between devices  6.72 us (22%)
    ppermute x4, starting transfers between devices, shifted(): lax.ppermute(array, axis, [(i, (i + by) % count) for i in range(count)])  8.22 us
    ppermute x4, waiting for transfers between devices, crossed(): lax.ppermute(array, axis, [(i, i ^ bits) for i in range(lax.axis_size(axi...  6.71 us
    pallas_call x1, Pallas kernels, on_device(): pl.pallas_call(after_kernel, in_specs=[smem] + [outside] * 3 + [vmem] * 2...  6.14 us
    ppermute x4, starting transfers between devices, crossed(): lax.ppermute(array, axis, [(i, i ^ bits) for i in range(lax.axis_size(axi...  5.08 us
    pallas_call x1, Pallas kernels, sliced(): pl.pallas_call(functools.partial(slice_kernel, sources=sources), in_specs...  1.34 us
    pallas_call x1, Pallas kernels, on_device(): pl.pallas_call(middle_kernel, in_specs=[smem] + [vmem] * 5, out_specs=[vm...  0.92 us
    pallas_call x1, Pallas kernels, on_device(): pl.pallas_call(functools.partial(unpack_kernel, turns=turns + [0]), in_sp...  0.74 us
  transfers between devices with their start and end apart: 8, of which 4 were waited for; matrix products, arithmetic and copies ran while one was open for 0% of the time, Pallas kernels for 24%

profile of v17, /device:TPU:0, one launch (start us, length us, event | category | flops | bytes accessed | tf_op | source)
XLA Modules:
  0.0 30.2 jit_solution(9436985386735134577)
XLA Ops:
  0.0 1.3 %slices.1 = (bf16[2,1,32,16,128]{4,3,2,1,0:T(8,128)(2,1)S(1)}, bf16[2,1,32,16,128]{4,3,2,1,0:T(8,128)(2,1)S(1)}, bf16[1,2,32,16,128]{4,3,2,1,0:T(8,128)(2,1)S(1)}, bf16[1,2,32,16,128]{4,3,2,1,0:T(8,128)(2,1)S(1)}) custom-call(bf16[4,4,32,16,128]{4,3,2,1,0:T(8,128)(2,1)} %nulls.5), custom_call_target="tpu_custom_call" | custom-call | flops 1000 | bytes 1000 | tf_op jit(solution)/shard_map/slices/pallas_call | solution.py:311
  1.3 6.1 %collective-permute-start = (bf16[2,1,32,16,128]{4,3,2,1,0:T(8,128)(2,1)S(1)}, bf16[2,1,32,16,128]{4,3,2,1,0:T(8,128)(2,1)S(1)}, u32[]{:S(2)}, u32[]{:S(2)}) collective-permute-start(bf16[2,1,32,16,128]{4,3,2,1,0:T(8,128)(2,1)S(1)} %get-tuple-element.20), channel_id=1, source_target_pairs={{0,7},{1,0},{2,1},{3,2},{4,3},{5,4},{6,5},{7,6},{8,15},{9,8},{10,9... | collective-permute-start | bytes 786440 | tf_op jit(solution)/shard_map/ppermute | solution.py:18
  7.4 0.7 %collective-permute-start.1 = (bf16[1,2,32,16,128]{4,3,2,1,0:T(8,128)(2,1)S(1)}, bf16[1,2,32,16,128]{4,3,2,1,0:T(8,128)(2,1)S(1)}, u32[]{:S(2)}, u32[]{:S(2)}) collective-permute-start(bf16[1,2,32,16,128]{4,3,2,1,0:T(8,128)(2,1)S(1)} %get-tuple-element.21), channel_id=1, source_target_pairs={{0,24},{8,0},{16,8},{24,16},{1,25},{9,1},{17,9},{25,17},{2,26},{10... | collective-permute-start | bytes 786440 | tf_op jit(solution)/shard_map/ppermute | solution.py:18
  8.1 1.0 %collective-permute-start.2 = (bf16[1,2,32,16,128]{4,3,2,1,0:T(8,128)(2,1)S(1)}, bf16[1,2,32,16,128]{4,3,2,1,0:T(8,128)(2,1)S(1)}, u32[]{:S(2)}, u32[]{:S(2)}) collective-permute-start(bf16[1,2,32,16,128]{4,3,2,1,0:T(8,128)(2,1)S(1)} %get-tuple-element.22), channel_id=1, source_target_pairs={{0,24},{8,0},{16,8},{24,16},{1,25},{9,1},{17,9},{25,17},{2,26},{10... | collective-permute-start | bytes 786440 | tf_op jit(solution)/shard_map/ppermute | solution.py:18
  9.0 0.2 before.1
  9.2 0.6 %collective-permute-start.3 = (bf16[2,1,32,16,128]{4,3,2,1,0:T(8,128)(2,1)S(1)}, bf16[2,1,32,16,128]{4,3,2,1,0:T(8,128)(2,1)S(1)}, u32[]{:S(2)}, u32[]{:S(2)}) collective-permute-start(bf16[2,1,32,16,128]{4,3,2,1,0:T(8,128)(2,1)S(1)} %get-tuple-element.28), channel_id=1, source_target_pairs={{0,7},{1,0},{2,1},{3,2},{4,3},{5,4},{6,5},{7,6},{8,15},{9,8},{10,9... | collective-permute-start | bytes 786440 | tf_op jit(solution)/shard_map/ppermute | solution.py:18
  9.8 0.0 copy-start
  9.8 6.1 %after.1 = (f32[32,512]{1,0:T(8,128)S(1)}, bf16[4,128,1024]{2,1,0:T(8,128)(2,1)S(1)}) custom-call(s32[1]{0:T(128)} %bitcast.1.group, bf16[4,4,32,16,128]{4,3,2,1,0:T(8,128)(2,1)} %nulls.5, bf16[2,4,32,64,128]{4,3,2,1,0:T(8,128)(2,1)} %time_links.3, bf16[4,2,32,64,128]{4,3,2,1,0:T(8,128)(2,1)} %space_links.3, f32[32,512]{1,0:T(8,128)S(1)} %get-tuple-element.24.early_before, ...), custom_call_target="tpu_custom_call" | custom-call | flops 1000 | bytes 1000 | tf_op jit(solution)/shard_map/after/pallas_call | solution.py:354
  15.9 0.0 collective-permute-done.space_edge
  15.9 0.0 collective-permute-done.1.time_first
  15.9 0.0 collective-permute-done.2.time_second
  16.0 0.0 copy-done
  16.0 0.9 %middle.1 = (f32[24,512]{1,0:T(8,128)S(1)}, f32[2,64,64]{2,1,0:T(8,128)S(1)}) custom-call(s32[1]{0:T(128)} %bitcast.place, s32[8,64]{1,0:T(8,128)S(1)} %copy-done, bf16[2,1,32,16,128]{4,3,2,1,0:T(8,128)(2,1)S(1)} %collective-permute-done.space_edge, bf16[1,2,32,16,128]{4,3,2,1,0:T(8,128)(2,1)S(1)} %collective-permute-done.1.time_first, ...), custom_call_target="tpu_custom_call" | custom-call | flops 1000 | bytes 1000 | tf_op jit(solution)/shard_map/middle/pallas_call | solution.py:364
  16.9 0.0 collective-permute-done.3.space_edge
  16.9 0.6 %final.1.late = bf16[64,512]{1,0:T(8,128)(2,1)S(1)} custom-call(bf16[2,1,32,16,128]{4,3,2,1,0:T(8,128)(2,1)S(1)} %collective-permute-done.3.space_edge, bf16[4,128,1024]{2,1,0:T(8,128)(2,1)S(1)} %get-tuple-element.26.adjoint, f32[32,512]{1,0:T(8,128)S(1)} %get-tuple-element.29.early, f32[24,512]{1,0:T(8,128)S(1)} %get-tuple-element.30.found), custom_call_target="tpu_custom_call" | custom-call | flops 1000 | bytes 1000 | tf_op jit(solution)/shard_map/final/pallas_call | solution.py:376
  17.5 1.5 %collective-permute-start.4 = (bf16[64,512]{1,0:T(8,128)(2,1)S(1)}, bf16[64,512]{1,0:T(8,128)(2,1)S(1)}, u32[]{:S(2)}, u32[]{:S(2)}) collective-permute-start(bf16[64,512]{1,0:T(8,128)(2,1)S(1)} %final.1.late), channel_id=1, source_target_pairs={{0,1},{1,0},{2,3},{3,2},{4,5},{5,4},{6,7},{7,6},{8,9},{9,8},{10,11... | collective-permute-start | bytes 196616 | tf_op jit(solution)/shard_map/ppermute | solution.py:22
  19.0 2.8 %collective-permute-done.4.late_other = bf16[64,512]{1,0:T(8,128)(2,1)S(1)} collective-permute-done((bf16[64,512]{1,0:T(8,128)(2,1)S(1)}, bf16[64,512]{1,0:T(8,128)(2,1)S(1)}, u32[]{:S(2)}, u32[]{:S(2)}) %collective-permute-start.4) | collective-permute-done | bytes 65568 | tf_op jit(solution)/shard_map/ppermute | solution.py:22
  21.7 0.2 pack.1
  21.9 0.2 collective-permute-start.5
  22.1 2.9 %collective-permute-start.6 = (bf16[16,1024]{1,0:T(8,128)(2,1)S(1)}, bf16[16,1024]{1,0:T(8,128)(2,1)S(1)}, u32[]{:S(2)}, u32[]{:S(2)}) collective-permute-start(bf16[16,1024]{1,0:T(8,128)(2,1)S(1)} %get-tuple-element.32), channel_id=1, source_target_pairs={{0,6},{1,7},{2,4},{3,5},{4,2},{5,3},{6,0},{7,1},{8,14},{9,15},{10,... | collective-permute-start | bytes 98312 | tf_op jit(solution)/shard_map/ppermute | solution.py:22
  25.0 0.5 %collective-permute-start.7 = (bf16[16,1024]{1,0:T(8,128)(2,1)S(1)}, bf16[16,1024]{1,0:T(8,128)(2,1)S(1)}, u32[]{:S(2)}, u32[]{:S(2)}) collective-permute-start(bf16[16,1024]{1,0:T(8,128)(2,1)S(1)} %get-tuple-element.33), channel_id=1, source_target_pairs={{0,2},{1,3},{2,0},{3,1},{4,6},{5,7},{6,4},{7,5},{8,10},{9,11},{10,... | collective-permute-start | bytes 98312 | tf_op jit(solution)/shard_map/ppermute | solution.py:22
  25.5 1.7 %collective-permute-done.5.refs_0_ = bf16[16,1024]{1,0:T(8,128)(2,1)S(1)} collective-permute-done((bf16[16,1024]{1,0:T(8,128)(2,1)S(1)}, bf16[16,1024]{1,0:T(8,128)(2,1)S(1)}, u32[]{:S(2)}, u32[]{:S(2)}) %collective-permute-start.5) | collective-permute-done | bytes 32800 | tf_op jit(solution)/shard_map/ppermute | solution.py:22
  27.1 0.7 %collective-permute-done.6.refs_1_ = bf16[16,1024]{1,0:T(8,128)(2,1)S(1)} collective-permute-done((bf16[16,1024]{1,0:T(8,128)(2,1)S(1)}, bf16[16,1024]{1,0:T(8,128)(2,1)S(1)}, u32[]{:S(2)}, u32[]{:S(2)}) %collective-permute-start.6) | collective-permute-done | bytes 32800 | tf_op jit(solution)/shard_map/ppermute | solution.py:22
  27.9 1.5 %collective-permute-done.7.refs_2_ = bf16[16,1024]{1,0:T(8,128)(2,1)S(1)} collective-permute-done((bf16[16,1024]{1,0:T(8,128)(2,1)S(1)}, bf16[16,1024]{1,0:T(8,128)(2,1)S(1)}, u32[]{:S(2)}, u32[]{:S(2)}) %collective-permute-start.7) | collective-permute-done | bytes 32800 | tf_op jit(solution)/shard_map/ppermute | solution.py:22
  29.4 0.7 %unpack.1 = f32[64,1024]{1,0:T(8,128)} custom-call(s32[1]{0:T(128)} %bitcast.place, bf16[16,1024]{1,0:T(8,128)(2,1)S(1)} %collective-permute-done.5.refs_0_, bf16[16,1024]{1,0:T(8,128)(2,1)S(1)} %collective-permute-done.6.refs_1_, bf16[16,1024]{1,0:T(8,128)(2,1)S(1)} %collective-permute-done.7.refs_2_, bf16[16,1024]{1,0:T(8,128)(2,1)S(1)} %get-tuple-element.34.refs_3_), custom_call_target="tpu_custom_call" | custom-call | flops 1000 | bytes 1000 | tf_op jit(solution)/shard_map/unpack/pallas_call | solution.py:398
Async XLA Ops:
  1.3 14.6 %collective-permute-start = (bf16[2,1,32,16,128]{4,3,2,1,0:T(8,128)(2,1)S(1)}, bf16[2,1,32,16,128]{4,3,2,1,0:T(8,128)(2,1)S(1)}, u32[]{:S(2)}, u32[]{:S(2)}) collective-permute-start(bf16[2,1,32,16,128]{4,3,2,1,0:T(8,128)(2,1)S(1)} %get-tuple-element.20), channel_id=1, source_target_pairs={{0,7},{1,0},{2,1},{3,2},{4,3},{5,4},{6,5},{7,6},{8,15},{9,8},{10,9... | collective-permute-start | bytes 786440 | tf_op jit(solution)/shard_map/ppermute | solution.py:18
  7.4 8.5 %collective-permute-start.1 = (bf16[1,2,32,16,128]{4,3,2,1,0:T(8,128)(2,1)S(1)}, bf16[1,2,32,16,128]{4,3,2,1,0:T(8,128)(2,1)S(1)}, u32[]{:S(2)}, u32[]{:S(2)}) collective-permute-start(bf16[1,2,32,16,128]{4,3,2,1,0:T(8,128)(2,1)S(1)} %get-tuple-element.21), channel_id=1, source_target_pairs={{0,24},{8,0},{16,8},{24,16},{1,25},{9,1},{17,9},{25,17},{2,26},{10... | collective-permute-start | bytes 786440 | tf_op jit(solution)/shard_map/ppermute | solution.py:18
  8.1 7.9 %collective-permute-start.2 = (bf16[1,2,32,16,128]{4,3,2,1,0:T(8,128)(2,1)S(1)}, bf16[1,2,32,16,128]{4,3,2,1,0:T(8,128)(2,1)S(1)}, u32[]{:S(2)}, u32[]{:S(2)}) collective-permute-start(bf16[1,2,32,16,128]{4,3,2,1,0:T(8,128)(2,1)S(1)} %get-tuple-element.22), channel_id=1, source_target_pairs={{0,24},{8,0},{16,8},{24,16},{1,25},{9,1},{17,9},{25,17},{2,26},{10... | collective-permute-start | bytes 786440 | tf_op jit(solution)/shard_map/ppermute | solution.py:18
  9.2 7.7 %collective-permute-start.3 = (bf16[2,1,32,16,128]{4,3,2,1,0:T(8,128)(2,1)S(1)}, bf16[2,1,32,16,128]{4,3,2,1,0:T(8,128)(2,1)S(1)}, u32[]{:S(2)}, u32[]{:S(2)}) collective-permute-start(bf16[2,1,32,16,128]{4,3,2,1,0:T(8,128)(2,1)S(1)} %get-tuple-element.28), channel_id=1, source_target_pairs={{0,7},{1,0},{2,1},{3,2},{4,3},{5,4},{6,5},{7,6},{8,15},{9,8},{10,9... | collective-permute-start | bytes 786440 | tf_op jit(solution)/shard_map/ppermute | solution.py:18
  9.8 6.2 %copy-start = (s32[8,64]{1,0:T(8,128)S(1)}, s32[8,64]{1,0:T(8,128)}, u32[]{:S(2)}) copy-start(s32[8,64]{1,0:T(8,128)} %lists.1) | copy-start | bytes 6148
  17.5 4.3 %collective-permute-start.4 = (bf16[64,512]{1,0:T(8,128)(2,1)S(1)}, bf16[64,512]{1,0:T(8,128)(2,1)S(1)}, u32[]{:S(2)}, u32[]{:S(2)}) collective-permute-start(bf16[64,512]{1,0:T(8,128)(2,1)S(1)} %final.1.late), channel_id=1, source_target_pairs={{0,1},{1,0},{2,3},{3,2},{4,5},{5,4},{6,7},{7,6},{8,9},{9,8},{10,11... | collective-permute-start | bytes 196616 | tf_op jit(solution)/shard_map/ppermute | solution.py:22
  21.9 5.2 %collective-permute-start.5 = (bf16[16,1024]{1,0:T(8,128)(2,1)S(1)}, bf16[16,1024]{1,0:T(8,128)(2,1)S(1)}, u32[]{:S(2)}, u32[]{:S(2)}) collective-permute-start(bf16[16,1024]{1,0:T(8,128)(2,1)S(1)} %get-tuple-element.31), channel_id=1, source_target_pairs={{0,4},{1,5},{2,6},{3,7},{4,0},{5,1},{6,2},{7,3},{8,12},{9,13},{10,... | collective-permute-start | bytes 98312 | tf_op jit(solution)/shard_map/ppermute | solution.py:22
  22.1 5.8 %collective-permute-start.6 = (bf16[16,1024]{1,0:T(8,128)(2,1)S(1)}, bf16[16,1024]{1,0:T(8,128)(2,1)S(1)}, u32[]{:S(2)}, u32[]{:S(2)}) collective-permute-start(bf16[16,1024]{1,0:T(8,128)(2,1)S(1)} %get-tuple-element.32), channel_id=1, source_target_pairs={{0,6},{1,7},{2,4},{3,5},{4,2},{5,3},{6,0},{7,1},{8,14},{9,15},{10,... | collective-permute-start | bytes 98312 | tf_op jit(solution)/shard_map/ppermute | solution.py:22
  25.0 4.4 %collective-permute-start.7 = (bf16[16,1024]{1,0:T(8,128)(2,1)S(1)}, bf16[16,1024]{1,0:T(8,128)(2,1)S(1)}, u32[]{:S(2)}, u32[]{:S(2)}) collective-permute-start(bf16[16,1024]{1,0:T(8,128)(2,1)S(1)} %get-tuple-element.33), channel_id=1, source_target_pairs={{0,2},{1,3},{2,0},{3,1},{4,6},{5,7},{6,4},{7,5},{8,10},{9,11},{10,... | collective-permute-start | bytes 98312 | tf_op jit(solution)/shard_map/ppermute | solution.py:22

commit v18 on v17

--- a/solution.py
+++ b/solution.py
@@ -121,8 +121,8 @@
     return jnp.concatenate(pieces, axis=1)
 
 
-def slice_kernel(nulls, *refs, sources):
-    edges, sems = refs[:-1], refs[-1]
+def slice_kernel(nulls, *refs, sources, skip):
+    edges, sems = refs[skip:-1], refs[-1]
     copies = []
     for edge, (start, count, at, space) in zip(edges, sources):
         for row in range(count):
@@ -306,26 +306,23 @@
     tiny = pl.CostEstimate(flops=1000, bytes_accessed=1000, transcendentals=0)
     half_time = time_count // 2
 
-    def sliced(name, *sources):
+    def sliced(name, *sources, after=()):
         shapes = [(count, space, sites, vectors, width) for _, count, _, space in sources]
         return pl.pallas_call(
-            functools.partial(slice_kernel, sources=sources),
-            in_specs=[outside],
+            functools.partial(slice_kernel, sources=sources, skip=len(after)),
+            in_specs=[outside] + [anywhere] * len(after),
             out_specs=[vmem] * len(sources),
             out_shape=[jax.ShapeDtypeStruct(shape, nulls.dtype) for shape in shapes],
             scratch_shapes=[pltpu.SemaphoreType.DMA((sum(source[1] for source in sources),))],
             compiler_params=first,
             cost_estimate=tiny,
             name=name,
-        )(nulls)
+        )(nulls, *after)
 
     half_space = space_count // 2
-    space_first, space_later, time_first, time_second = sliced(
-        "slices",
-        (0, half_time, 0, 1),
-        (half_time, half_time, 0, 1),
-        (0, 1, 0, half_space),
-        (0, 1, half_space, half_space),
+    (space_first,) = sliced("slice_first", (0, half_time, 0, 1))
+    space_later, time_first, time_second = sliced(
+        "slice_rest", (half_time, half_time, 0, 1), (0, 1, 0, half_space), (0, 1, half_space, half_space), after=(space_first,)
     )
     edge_first = shifted(space_first, "xyz", -1)
     edge_times = [shifted(time_first, "ta", -1), shifted(time_second, "ta", -1)]

time: 30.3 us -> 30.2 us (level)
  the two profiles are of different devices: /device:TPU:0 before, /device:TPU:1 now
where the time goes in v18:
time: 30.2 us; the launch traced here: 30.1 us
  Pallas kernels  10.9 us (36%)
  starting transfers between devices  9.82 us (33%)
  waiting for transfers between devices  9.2 us (30%)
    ppermute x4, starting transfers between devices, shifted(): lax.ppermute(array, axis, [(i, (i + by) % count) for i in range(count)])  7.1 us
    pallas_call x1, Pallas kernels, on_device(): pl.pallas_call(before_kernel, in_specs=[smem] + [outside] * 3 + [vmem], o...  6.14 us
    ppermute x4, waiting for transfers between devices, crossed(): lax.ppermute(array, axis, [(i, i ^ bits) for i in range(lax.axis_size(axi...  5.41 us
    ppermute x4, waiting for transfers between devices, shifted(): lax.ppermute(array, axis, [(i, (i + by) % count) for i in range(count)])  3.8 us
    ppermute x4, starting transfers between devices, crossed(): lax.ppermute(array, axis, [(i, i ^ bits) for i in range(lax.axis_size(axi...  2.72 us
    pallas_call x2, Pallas kernels, sliced(): pl.pallas_call(functools.partial(slice_kernel, sources=sources, skip=len(...  2.18 us
    pallas_call x1, Pallas kernels, on_device(): pl.pallas_call(middle_kernel, in_specs=[smem] + [vmem] * 5, out_specs=[vm...  0.91 us
    pallas_call x1, Pallas kernels, on_device(): pl.pallas_call(functools.partial(unpack_kernel, turns=turns + [0]), in_sp...  0.74 us
  transfers between devices with their start and end apart: 8, of which 5 were waited for; matrix products, arithmetic and copies ran while one was open for 0% of the time, Pallas kernels for 28%

profile of v18, /device:TPU:1, one launch (start us, length us, event | category | flops | bytes accessed | tf_op | source)
XLA Modules:
  0.0 30.1 jit_solution(11795441729521726126)
XLA Ops:
  0.0 1.0 %slice_first.1.refs_0_ = bf16[2,1,32,16,128]{4,3,2,1,0:T(8,128)(2,1)S(1)} custom-call(bf16[4,4,32,16,128]{4,3,2,1,0:T(8,128)(2,1)} %nulls.7), custom_call_target="tpu_custom_call" | custom-call | flops 1000 | bytes 1000 | tf_op jit(solution)/shard_map/slice_first/pallas_call | solution.py:311
  1.0 5.2 %collective-permute-start = (bf16[2,1,32,16,128]{4,3,2,1,0:T(8,128)(2,1)S(1)}, bf16[2,1,32,16,128]{4,3,2,1,0:T(8,128)(2,1)S(1)}, u32[]{:S(2)}, u32[]{:S(2)}) collective-permute-start(bf16[2,1,32,16,128]{4,3,2,1,0:T(8,128)(2,1)S(1)} %slice_first.1.refs_0_), channel_id=1, source_target_pairs={{0,7},{1,0},{2,1},{3,2},{4,3},{5,4},{6,5},{7,6},{8,15},{9,8},{10,9... | collective-permute-start | bytes 786440 | tf_op jit(solution)/shard_map/ppermute | solution.py:18
  6.2 1.2 %slice_rest.1 = (bf16[2,1,32,16,128]{4,3,2,1,0:T(8,128)(2,1)S(1)}, bf16[1,2,32,16,128]{4,3,2,1,0:T(8,128)(2,1)S(1)}, bf16[1,2,32,16,128]{4,3,2,1,0:T(8,128)(2,1)S(1)}) custom-call(bf16[4,4,32,16,128]{4,3,2,1,0:T(8,128)(2,1)} %nulls.7, bf16[2,1,32,16,128]{4,3,2,1,0:T(8,128)(2,1)S(1)} %slice_first.1.refs_0_), custom_call_target="tpu_custom_call" | custom-call | flops 1000 | bytes 1000 | tf_op jit(solution)/shard_map/slice_rest/pallas_call | solution.py:311
  7.4 1.0 %collective-permute-start.1 = (bf16[1,2,32,16,128]{4,3,2,1,0:T(8,128)(2,1)S(1)}, bf16[1,2,32,16,128]{4,3,2,1,0:T(8,128)(2,1)S(1)}, u32[]{:S(2)}, u32[]{:S(2)}) collective-permute-start(bf16[1,2,32,16,128]{4,3,2,1,0:T(8,128)(2,1)S(1)} %get-tuple-element.19), channel_id=1, source_target_pairs={{0,24},{8,0},{16,8},{24,16},{1,25},{9,1},{17,9},{25,17},{2,26},{10... | collective-permute-start | bytes 786440 | tf_op jit(solution)/shard_map/ppermute | solution.py:18
  8.4 0.7 %collective-permute-start.2 = (bf16[1,2,32,16,128]{4,3,2,1,0:T(8,128)(2,1)S(1)}, bf16[1,2,32,16,128]{4,3,2,1,0:T(8,128)(2,1)S(1)}, u32[]{:S(2)}, u32[]{:S(2)}) collective-permute-start(bf16[1,2,32,16,128]{4,3,2,1,0:T(8,128)(2,1)S(1)} %get-tuple-element.20), channel_id=1, source_target_pairs={{0,24},{8,0},{16,8},{24,16},{1,25},{9,1},{17,9},{25,17},{2,26},{10... | collective-permute-start | bytes 786440 | tf_op jit(solution)/shard_map/ppermute | solution.py:18
  9.0 6.1 %before.1 = (bf16[2,1,32,16,128]{4,3,2,1,0:T(8,128)(2,1)S(1)}, f32[32,512]{1,0:T(8,128)S(1)}, bf16[4,128,1024]{2,1,0:T(8,128)(2,1)S(1)}) custom-call(s32[1]{0:T(128)} %bitcast.1.group, bf16[4,4,32,16,128]{4,3,2,1,0:T(8,128)(2,1)} %nulls.7, bf16[2,4,32,64,128]{4,3,2,1,0:T(8,128)(2,1)} %time_links.3, bf16[4,2,32,64,128]{4,3,2,1,0:T(8,128)(2,1)} %space_links.3, ...), custom_call_target="tpu_custom_call" | custom-call | flops 1000 | bytes 1000 | tf_op jit(solution)/shard_map/before/pallas_call | solution.py:340
  15.2 0.3 collective-permute-start.3
  15.4 0.0 copy-start
  15.4 0.3 after.1
  15.7 0.0 collective-permute-done.space_edge
  15.7 0.0 collective-permute-done.1.time_first
  15.7 0.6 %collective-permute-done.2.time_second = bf16[1,2,32,16,128]{4,3,2,1,0:T(8,128)(2,1)S(1)} collective-permute-done((bf16[1,2,32,16,128]{4,3,2,1,0:T(8,128)(2,1)S(1)}, bf16[1,2,32,16,128]{4,3,2,1,0:T(8,128)(2,1)S(1)}, u32[]{:S(2)}, u32[]{:S(2)}) %collective-permute-start.2) | collective-permute-done | bytes 262176 | tf_op jit(solution)/shard_map/ppermute | solution.py:18
  16.3 0.0 copy-done
  16.3 0.9 %middle.1 = (f32[24,512]{1,0:T(8,128)S(1)}, f32[2,64,64]{2,1,0:T(8,128)S(1)}) custom-call(s32[1]{0:T(128)} %bitcast.place, s32[8,64]{1,0:T(8,128)S(1)} %copy-done, bf16[2,1,32,16,128]{4,3,2,1,0:T(8,128)(2,1)S(1)} %collective-permute-done.space_edge, bf16[1,2,32,16,128]{4,3,2,1,0:T(8,128)(2,1)S(1)} %collective-permute-done.1.time_first, ...), custom_call_target="tpu_custom_call" | custom-call | flops 1000 | bytes 1000 | tf_op jit(solution)/shard_map/middle/pallas_call | solution.py:361
  17.2 3.2 %collective-permute-done.3.space_edge = bf16[2,1,32,16,128]{4,3,2,1,0:T(8,128)(2,1)S(1)} collective-permute-done((bf16[2,1,32,16,128]{4,3,2,1,0:T(8,128)(2,1)S(1)}, bf16[2,1,32,16,128]{4,3,2,1,0:T(8,128)(2,1)S(1)}, u32[]{:S(2)}, u32[]{:S(2)}) %collective-permute-start.3) | collective-permute-done | bytes 262176 | tf_op jit(solution)/shard_map/ppermute | solution.py:18
  20.4 0.6 %final.1.late = bf16[64,512]{1,0:T(8,128)(2,1)S(1)} custom-call(bf16[2,1,32,16,128]{4,3,2,1,0:T(8,128)(2,1)S(1)} %collective-permute-done.3.space_edge, bf16[4,128,1024]{2,1,0:T(8,128)(2,1)S(1)} %get-tuple-element.24.adjoint, f32[32,512]{1,0:T(8,128)S(1)} %get-tuple-element.27.early, f32[24,512]{1,0:T(8,128)S(1)} %get-tuple-element.28.found), custom_call_target="tpu_custom_call" | custom-call | flops 1000 | bytes 1000 | tf_op jit(solution)/shard_map/final/pallas_call | solution.py:373
  21.0 0.0 collective-permute-start.4
  21.0 3.1 %collective-permute-done.4.late_other = bf16[64,512]{1,0:T(8,128)(2,1)S(1)} collective-permute-done((bf16[64,512]{1,0:T(8,128)(2,1)S(1)}, bf16[64,512]{1,0:T(8,128)(2,1)S(1)}, u32[]{:S(2)}, u32[]{:S(2)}) %collective-permute-start.4) | collective-permute-done | bytes 65568 | tf_op jit(solution)/shard_map/ppermute | solution.py:22
  24.1 0.2 pack.1
  24.3 0.1 collective-permute-start.5
  24.4 1.8 %collective-permute-start.6 = (bf16[16,1024]{1,0:T(8,128)(2,1)S(1)}, bf16[16,1024]{1,0:T(8,128)(2,1)S(1)}, u32[]{:S(2)}, u32[]{:S(2)}) collective-permute-start(bf16[16,1024]{1,0:T(8,128)(2,1)S(1)} %get-tuple-element.30), channel_id=1, source_target_pairs={{0,6},{1,7},{2,4},{3,5},{4,2},{5,3},{6,0},{7,1},{8,14},{9,15},{10,... | collective-permute-start | bytes 98312 | tf_op jit(solution)/shard_map/ppermute | solution.py:22
  26.2 0.8 %collective-permute-start.7 = (bf16[16,1024]{1,0:T(8,128)(2,1)S(1)}, bf16[16,1024]{1,0:T(8,128)(2,1)S(1)}, u32[]{:S(2)}, u32[]{:S(2)}) collective-permute-start(bf16[16,1024]{1,0:T(8,128)(2,1)S(1)} %get-tuple-element.31), channel_id=1, source_target_pairs={{0,2},{1,3},{2,0},{3,1},{4,6},{5,7},{6,4},{7,5},{8,10},{9,11},{10,... | collective-permute-start | bytes 98312 | tf_op jit(solution)/shard_map/ppermute | solution.py:22
  27.0 1.5 %collective-permute-done.5.refs_0_ = bf16[16,1024]{1,0:T(8,128)(2,1)S(1)} collective-permute-done((bf16[16,1024]{1,0:T(8,128)(2,1)S(1)}, bf16[16,1024]{1,0:T(8,128)(2,1)S(1)}, u32[]{:S(2)}, u32[]{:S(2)}) %collective-permute-start.5) | collective-permute-done | bytes 32800 | tf_op jit(solution)/shard_map/ppermute | solution.py:22
  28.5 0.8 %collective-permute-done.6.refs_1_ = bf16[16,1024]{1,0:T(8,128)(2,1)S(1)} collective-permute-done((bf16[16,1024]{1,0:T(8,128)(2,1)S(1)}, bf16[16,1024]{1,0:T(8,128)(2,1)S(1)}, u32[]{:S(2)}, u32[]{:S(2)}) %collective-permute-start.6) | collective-permute-done | bytes 32800 | tf_op jit(solution)/shard_map/ppermute | solution.py:22
  29.3 0.0 collective-permute-done.7.refs_2_
  29.3 0.7 %unpack.1 = f32[64,1024]{1,0:T(8,128)} custom-call(s32[1]{0:T(128)} %bitcast.place, bf16[16,1024]{1,0:T(8,128)(2,1)S(1)} %collective-permute-done.5.refs_0_, bf16[16,1024]{1,0:T(8,128)(2,1)S(1)} %collective-permute-done.6.refs_1_, bf16[16,1024]{1,0:T(8,128)(2,1)S(1)} %collective-permute-done.7.refs_2_, bf16[16,1024]{1,0:T(8,128)(2,1)S(1)} %get-tuple-element.32.refs_3_), custom_call_target="tpu_custom_call" | custom-call | flops 1000 | bytes 1000 | tf_op jit(solution)/shard_map/unpack/pallas_call | solution.py:395
Async XLA Ops:
  1.0 14.7 %collective-permute-start = (bf16[2,1,32,16,128]{4,3,2,1,0:T(8,128)(2,1)S(1)}, bf16[2,1,32,16,128]{4,3,2,1,0:T(8,128)(2,1)S(1)}, u32[]{:S(2)}, u32[]{:S(2)}) collective-permute-start(bf16[2,1,32,16,128]{4,3,2,1,0:T(8,128)(2,1)S(1)} %slice_first.1.refs_0_), channel_id=1, source_target_pairs={{0,7},{1,0},{2,1},{3,2},{4,3},{5,4},{6,5},{7,6},{8,15},{9,8},{10,9... | collective-permute-start | bytes 786440 | tf_op jit(solution)/shard_map/ppermute | solution.py:18
  7.4 8.4 %collective-permute-start.1 = (bf16[1,2,32,16,128]{4,3,2,1,0:T(8,128)(2,1)S(1)}, bf16[1,2,32,16,128]{4,3,2,1,0:T(8,128)(2,1)S(1)}, u32[]{:S(2)}, u32[]{:S(2)}) collective-permute-start(bf16[1,2,32,16,128]{4,3,2,1,0:T(8,128)(2,1)S(1)} %get-tuple-element.19), channel_id=1, source_target_pairs={{0,24},{8,0},{16,8},{24,16},{1,25},{9,1},{17,9},{25,17},{2,26},{10... | collective-permute-start | bytes 786440 | tf_op jit(solution)/shard_map/ppermute | solution.py:18
  8.4 8.0 %collective-permute-start.2 = (bf16[1,2,32,16,128]{4,3,2,1,0:T(8,128)(2,1)S(1)}, bf16[1,2,32,16,128]{4,3,2,1,0:T(8,128)(2,1)S(1)}, u32[]{:S(2)}, u32[]{:S(2)}) collective-permute-start(bf16[1,2,32,16,128]{4,3,2,1,0:T(8,128)(2,1)S(1)} %get-tuple-element.20), channel_id=1, source_target_pairs={{0,24},{8,0},{16,8},{24,16},{1,25},{9,1},{17,9},{25,17},{2,26},{10... | collective-permute-start | bytes 786440 | tf_op jit(solution)/shard_map/ppermute | solution.py:18
  15.2 5.3 %collective-permute-start.3 = (bf16[2,1,32,16,128]{4,3,2,1,0:T(8,128)(2,1)S(1)}, bf16[2,1,32,16,128]{4,3,2,1,0:T(8,128)(2,1)S(1)}, u32[]{:S(2)}, u32[]{:S(2)}) collective-permute-start(bf16[2,1,32,16,128]{4,3,2,1,0:T(8,128)(2,1)S(1)} %get-tuple-element.26), channel_id=1, source_target_pairs={{0,7},{1,0},{2,1},{3,2},{4,3},{5,4},{6,5},{7,6},{8,15},{9,8},{10,9... | collective-permute-start | bytes 786440 | tf_op jit(solution)/shard_map/ppermute | solution.py:18
  15.4 0.9 %copy-start = (s32[8,64]{1,0:T(8,128)S(1)}, s32[8,64]{1,0:T(8,128)}, u32[]{:S(2)}) copy-start(s32[8,64]{1,0:T(8,128)} %lists.1) | copy-start | bytes 6148
  21.0 3.1 %collective-permute-start.4 = (bf16[64,512]{1,0:T(8,128)(2,1)S(1)}, bf16[64,512]{1,0:T(8,128)(2,1)S(1)}, u32[]{:S(2)}, u32[]{:S(2)}) collective-permute-start(bf16[64,512]{1,0:T(8,128)(2,1)S(1)} %final.1.late), channel_id=1, source_target_pairs={{0,1},{1,0},{2,3},{3,2},{4,5},{5,4},{6,7},{7,6},{8,9},{9,8},{10,11... | collective-permute-start | bytes 196616 | tf_op jit(solution)/shard_map/ppermute | solution.py:22
  24.3 4.2 %collective-permute-start.5 = (bf16[16,1024]{1,0:T(8,128)(2,1)S(1)}, bf16[16,1024]{1,0:T(8,128)(2,1)S(1)}, u32[]{:S(2)}, u32[]{:S(2)}) collective-permute-start(bf16[16,1024]{1,0:T(8,128)(2,1)S(1)} %get-tuple-element.29), channel_id=1, source_target_pairs={{0,4},{1,5},{2,6},{3,7},{4,0},{5,1},{6,2},{7,3},{8,12},{9,13},{10,... | collective-permute-start | bytes 98312 | tf_op jit(solution)/shard_map/ppermute | solution.py:22
  24.4 4.9 %collective-permute-start.6 = (bf16[16,1024]{1,0:T(8,128)(2,1)S(1)}, bf16[16,1024]{1,0:T(8,128)(2,1)S(1)}, u32[]{:S(2)}, u32[]{:S(2)}) collective-permute-start(bf16[16,1024]{1,0:T(8,128)(2,1)S(1)} %get-tuple-element.30), channel_id=1, source_target_pairs={{0,6},{1,7},{2,4},{3,5},{4,2},{5,3},{6,0},{7,1},{8,14},{9,15},{10,... | collective-permute-start | bytes 98312 | tf_op jit(solution)/shard_map/ppermute | solution.py:22
  26.2 3.1 %collective-permute-start.7 = (bf16[16,1024]{1,0:T(8,128)(2,1)S(1)}, bf16[16,1024]{1,0:T(8,128)(2,1)S(1)}, u32[]{:S(2)}, u32[]{:S(2)}) collective-permute-start(bf16[16,1024]{1,0:T(8,128)(2,1)S(1)} %get-tuple-element.31), channel_id=1, source_target_pairs={{0,2},{1,3},{2,0},{3,1},{4,6},{5,7},{6,4},{7,5},{8,10},{9,11},{10,... | collective-permute-start | bytes 98312 | tf_op jit(solution)/shard_map/ppermute | solution.py:22

commit v19 on v18

--- a/solution.py
+++ b/solution.py
@@ -162,55 +162,61 @@
             picks[1, rows, :] = jnp.where(here & (turned == chosen), 1.0, 0.0)
 
 
-def inner_work(nulls, time_links, space_links, early, adjoint, links, vecs, left, right, sems):
-    time_count, space_count, sites, vectors, width = nulls.shape
-    copies = []
-    bases = [pltpu.make_async_copy(nulls.at[t], vecs.at[t], sems.at[16 + t]) for t in range(4)]
-    bases[1].start()
-    bases[2].start()
-
-    def fetch(source):
-        slot = len(copies)
-        copy = pltpu.make_async_copy(source, links.at[slot], sems.at[slot])
-        copy.start()
-        copies.append(copy)
-
-    for x in range(4):
-        fetch(time_links.at[0, x])
-    bases[0].start()
-    bases[3].start()
-    for t in range(4):
-        fetch(space_links.at[t, 0])
-    for x in range(4):
-        fetch(time_links.at[1, x])
-    for t in range(4):
-        fetch(space_links.at[t, 1])
-    bases[1].wait()
-    bases[2].wait()
-    for a_x in range(2):
-        copies[2 * a_x].wait()
-        copies[2 * a_x + 1].wait()
+def inner_work(groups, images, nulls, time_links, space_links, early, adjoint, links, vecs, left, right, sems):
+    vectors = nulls.shape[3]
+    copies = {}
+    bases = {}
+    waited = set()
+
+    def fetch(source, slot):
+        copies[slot] = pltpu.make_async_copy(source, links.at[slot], sems.at[slot])
+        copies[slot].start()
+
+    def load(*rows):
+        for row in rows:
+            if row not in bases:
+                bases[row] = pltpu.make_async_copy(nulls.at[row], vecs.at[row], sems.at[16 + row])
+                bases[row].start()
+
+    def need(*rows):
+        for row in rows:
+            if row not in waited:
+                waited.add(row)
+                bases[row].wait()
+
+    if images:
+        load(1, 2)
+        for x in range(4):
+            fetch(time_links.at[0, x], x)
+        load(0, 3)
+        for t in range(4):
+            fetch(space_links.at[t, 0], 4 + t)
+    for group in groups:
         for c in range(2):
-            x = 2 * a_x + c
-            image_item(links.at[x], vecs.at[1, x], vecs.at[2, x], c, left.at[a_x], right.at[a_x])
-    bases[0].wait()
-    bases[3].wait()
-    for a_t in range(2):
-        copies[4 + 2 * a_t].wait()
-        copies[5 + 2 * a_t].wait()
+            at = 2 * group + c
+            source = time_links.at[1, at] if group < 2 else space_links.at[at - 4, 1]
+            load(3 if group < 2 else at - 4)
+            fetch(source, 8 + at)
+    if images:
+        for group in range(4):
+            need(*((1, 2) if group < 2 else (0, 3)))
+            copies[2 * group].wait()
+            copies[2 * group + 1].wait()
+            for c in range(2):
+                at = 2 * group + c
+                lower, upper = (vecs.at[1, at], vecs.at[2, at]) if group < 2 else (vecs.at[at - 4, 1], vecs.at[at - 4, 2])
+                image_item(links.at[at], lower, upper, c, left.at[group], right.at[group])
+        found = [group_rows(left[group], right[group], MAT_DIMS, vectors) for group in range(4)]
+        early[...] = jnp.concatenate(found, axis=0)
+    for group in groups:
         for c in range(2):
-            t = 2 * a_t + c
-            image_item(links.at[4 + t], vecs.at[t, 1], vecs.at[t, 2], c, left.at[2 + a_t], right.at[2 + a_t])
-    found = [group_rows(left[group], right[group], MAT_DIMS, vectors) for group in range(4)]
-    early[...] = jnp.concatenate(found, axis=0)
-    for x in range(4):
-        copies[8 + x].wait()
-    for x in range(4):
-        adjoint_item(links.at[8 + x], vecs.at[3, x], x % 2, adjoint.at[x // 2])
-    for t in range(4):
-        copies[12 + t].wait()
-    for t in range(4):
-        adjoint_item(links.at[12 + t], vecs.at[t, 3], t % 2, adjoint.at[2 + t // 2])
+            at = 2 * group + c
+            need(3 if group < 2 else at - 4)
+            copies[8 + at].wait()
+        for c in range(2):
+            at = 2 * group + c
+            lower = vecs.at[3, at] if group < 2 else vecs.at[at - 4, 3]
+            adjoint_item(links.at[8 + at], lower, c, adjoint.at[group])
 
 
 def before_kernel(group, nulls, time_links, space_links, sliced, edge, *refs):
@@ -218,18 +224,20 @@
 
     @pl.when(lax.rem(group[0], 2) == 1)
     def _():
-        inner_work(nulls, time_links, space_links, *refs)
+        inner_work(range(3), True, nulls, time_links, space_links, *refs)
 
 
 def after_kernel(group, nulls, time_links, space_links, early_before, adjoint_before, early, adjoint, *refs):
     @pl.when(lax.rem(group[0], 2) == 0)
     def _():
-        inner_work(nulls, time_links, space_links, early, adjoint, *refs)
+        inner_work(range(4), True, nulls, time_links, space_links, early, adjoint, *refs)
 
     @pl.when(lax.rem(group[0], 2) == 1)
     def _():
         early[...] = early_before[...]
-        adjoint[...] = adjoint_before[...]
+        for group in range(3):
+            adjoint[group] = adjoint_before[group]
+        inner_work([3], False, nulls, time_links, space_links, early, adjoint, *refs)
 
 
 def edge_rows(uppers, adjoint, vectors):

time: 30.2 us -> 30.7 us (1.017)
  the two profiles are of different devices: /device:TPU:1 before, /device:TPU:0 now
where the time goes in v19:
time: 30.7 us; the launch traced here: 30.5 us
  starting transfers between devices  13.4 us (44%)
  Pallas kernels  11.4 us (37%)
  waiting for transfers between devices  5.7 us (19%)
    ppermute x4, starting transfers between devices, shifted(): lax.ppermute(array, axis, [(i, (i + by) % count) for i in range(count)])  8.27 us
    pallas_call x1, Pallas kernels, on_device(): pl.pallas_call(after_kernel, in_specs=[smem] + [outside] * 3 + [vmem] * 2...  6.65 us
    ppermute x4, waiting for transfers between devices, crossed(): lax.ppermute(array, axis, [(i, i ^ bits) for i in range(lax.axis_size(axi...  5.69 us
    ppermute x4, starting transfers between devices, crossed(): lax.ppermute(array, axis, [(i, i ^ bits) for i in range(lax.axis_size(axi...  5.08 us
    pallas_call x2, Pallas kernels, sliced(): pl.pallas_call(functools.partial(slice_kernel, sources=sources, skip=len(...  2.18 us
    pallas_call x1, Pallas kernels, on_device(): pl.pallas_call(middle_kernel, in_specs=[smem] + [vmem] * 5, out_specs=[vm...  0.91 us
    pallas_call x1, Pallas kernels, on_device(): pl.pallas_call(functools.partial(unpack_kernel, turns=turns + [0]), in_sp...  0.74 us
  transfers between devices with their start and end apart: 8, of which 4 were waited for; matrix products, arithmetic and copies ran while one was open for 0% of the time, Pallas kernels for 29%

profile of v19, /device:TPU:0, one launch (start us, length us, event | category | flops | bytes accessed | tf_op | source)
XLA Modules:
  0.0 30.5 jit_solution(13592452089447790609)
XLA Ops:
  0.0 1.0 %slice_first.1.refs_0_ = bf16[2,1,32,16,128]{4,3,2,1,0:T(8,128)(2,1)S(1)} custom-call(bf16[4,4,32,16,128]{4,3,2,1,0:T(8,128)(2,1)} %nulls.7), custom_call_target="tpu_custom_call" | custom-call | flops 1000 | bytes 1000 | tf_op jit(solution)/shard_map/slice_first/pallas_call | solution.py:319
  1.0 6.1 %collective-permute-start = (bf16[2,1,32,16,128]{4,3,2,1,0:T(8,128)(2,1)S(1)}, bf16[2,1,32,16,128]{4,3,2,1,0:T(8,128)(2,1)S(1)}, u32[]{:S(2)}, u32[]{:S(2)}) collective-permute-start(bf16[2,1,32,16,128]{4,3,2,1,0:T(8,128)(2,1)S(1)} %slice_first.1.refs_0_), channel_id=1, source_target_pairs={{0,7},{1,0},{2,1},{3,2},{4,3},{5,4},{6,5},{7,6},{8,15},{9,8},{10,9... | collective-permute-start | bytes 786440 | tf_op jit(solution)/shard_map/ppermute | solution.py:18
  7.0 1.2 %slice_rest.1 = (bf16[2,1,32,16,128]{4,3,2,1,0:T(8,128)(2,1)S(1)}, bf16[1,2,32,16,128]{4,3,2,1,0:T(8,128)(2,1)S(1)}, bf16[1,2,32,16,128]{4,3,2,1,0:T(8,128)(2,1)S(1)}) custom-call(bf16[4,4,32,16,128]{4,3,2,1,0:T(8,128)(2,1)} %nulls.7, bf16[2,1,32,16,128]{4,3,2,1,0:T(8,128)(2,1)S(1)} %slice_first.1.refs_0_), custom_call_target="tpu_custom_call" | custom-call | flops 1000 | bytes 1000 | tf_op jit(solution)/shard_map/slice_rest/pallas_call | solution.py:319
  8.3 0.7 %collective-permute-start.1 = (bf16[1,2,32,16,128]{4,3,2,1,0:T(8,128)(2,1)S(1)}, bf16[1,2,32,16,128]{4,3,2,1,0:T(8,128)(2,1)S(1)}, u32[]{:S(2)}, u32[]{:S(2)}) collective-permute-start(bf16[1,2,32,16,128]{4,3,2,1,0:T(8,128)(2,1)S(1)} %get-tuple-element.19), channel_id=1, source_target_pairs={{0,24},{8,0},{16,8},{24,16},{1,25},{9,1},{17,9},{25,17},{2,26},{10... | collective-permute-start | bytes 786440 | tf_op jit(solution)/shard_map/ppermute | solution.py:18
  9.0 1.0 %collective-permute-start.2 = (bf16[1,2,32,16,128]{4,3,2,1,0:T(8,128)(2,1)S(1)}, bf16[1,2,32,16,128]{4,3,2,1,0:T(8,128)(2,1)S(1)}, u32[]{:S(2)}, u32[]{:S(2)}) collective-permute-start(bf16[1,2,32,16,128]{4,3,2,1,0:T(8,128)(2,1)S(1)} %get-tuple-element.20), channel_id=1, source_target_pairs={{0,24},{8,0},{16,8},{24,16},{1,25},{9,1},{17,9},{25,17},{2,26},{10... | collective-permute-start | bytes 786440 | tf_op jit(solution)/shard_map/ppermute | solution.py:18
  9.9 0.2 before.1
  10.1 0.6 %collective-permute-start.3 = (bf16[2,1,32,16,128]{4,3,2,1,0:T(8,128)(2,1)S(1)}, bf16[2,1,32,16,128]{4,3,2,1,0:T(8,128)(2,1)S(1)}, u32[]{:S(2)}, u32[]{:S(2)}) collective-permute-start(bf16[2,1,32,16,128]{4,3,2,1,0:T(8,128)(2,1)S(1)} %get-tuple-element.26), channel_id=1, source_target_pairs={{0,7},{1,0},{2,1},{3,2},{4,3},{5,4},{6,5},{7,6},{8,15},{9,8},{10,9... | collective-permute-start | bytes 786440 | tf_op jit(solution)/shard_map/ppermute | solution.py:18
  10.7 0.0 copy-start
  10.7 6.6 %after.1 = (f32[32,512]{1,0:T(8,128)S(1)}, bf16[4,128,1024]{2,1,0:T(8,128)(2,1)S(1)}) custom-call(s32[1]{0:T(128)} %bitcast.1.group, bf16[4,4,32,16,128]{4,3,2,1,0:T(8,128)(2,1)} %nulls.7, bf16[2,4,32,64,128]{4,3,2,1,0:T(8,128)(2,1)} %time_links.3, bf16[4,2,32,64,128]{4,3,2,1,0:T(8,128)(2,1)} %space_links.3, f32[32,512]{1,0:T(8,128)S(1)} %get-tuple-element.22.early_before, ...), custom_call_target="tpu_custom_call" | custom-call | flops 1000 | bytes 1000 | tf_op jit(solution)/shard_map/after/pallas_call | solution.py:359
  17.3 0.0 collective-permute-done.space_edge
  17.3 0.0 collective-permute-done.1.time_first
  17.4 0.0 collective-permute-done.2.time_second
  17.4 0.0 copy-done
  17.4 0.9 %middle.1 = (f32[24,512]{1,0:T(8,128)S(1)}, f32[2,64,64]{2,1,0:T(8,128)S(1)}) custom-call(s32[1]{0:T(128)} %bitcast.place, s32[8,64]{1,0:T(8,128)S(1)} %copy-done, bf16[2,1,32,16,128]{4,3,2,1,0:T(8,128)(2,1)S(1)} %collective-permute-done.space_edge, bf16[1,2,32,16,128]{4,3,2,1,0:T(8,128)(2,1)S(1)} %collective-permute-done.1.time_first, ...), custom_call_target="tpu_custom_call" | custom-call | flops 1000 | bytes 1000 | tf_op jit(solution)/shard_map/middle/pallas_call | solution.py:369
  18.3 0.0 collective-permute-done.3.space_edge
  18.3 0.6 %final.1.late = bf16[64,512]{1,0:T(8,128)(2,1)S(1)} custom-call(bf16[2,1,32,16,128]{4,3,2,1,0:T(8,128)(2,1)S(1)} %collective-permute-done.3.space_edge, bf16[4,128,1024]{2,1,0:T(8,128)(2,1)S(1)} %get-tuple-element.24.adjoint, f32[32,512]{1,0:T(8,128)S(1)} %get-tuple-element.27.early, f32[24,512]{1,0:T(8,128)S(1)} %get-tuple-element.28.found), custom_call_target="tpu_custom_call" | custom-call | flops 1000 | bytes 1000 | tf_op jit(solution)/shard_map/final/pallas_call | solution.py:381
  18.9 1.5 %collective-permute-start.4 = (bf16[64,512]{1,0:T(8,128)(2,1)S(1)}, bf16[64,512]{1,0:T(8,128)(2,1)S(1)}, u32[]{:S(2)}, u32[]{:S(2)}) collective-permute-start(bf16[64,512]{1,0:T(8,128)(2,1)S(1)} %final.1.late), channel_id=1, source_target_pairs={{0,1},{1,0},{2,3},{3,2},{4,5},{5,4},{6,7},{7,6},{8,9},{9,8},{10,11... | collective-permute-start | bytes 196616 | tf_op jit(solution)/shard_map/ppermute | solution.py:22
  20.4 2.7 %collective-permute-done.4.late_other = bf16[64,512]{1,0:T(8,128)(2,1)S(1)} collective-permute-done((bf16[64,512]{1,0:T(8,128)(2,1)S(1)}, bf16[64,512]{1,0:T(8,128)(2,1)S(1)}, u32[]{:S(2)}, u32[]{:S(2)}) %collective-permute-start.4) | collective-permute-done | bytes 65568 | tf_op jit(solution)/shard_map/ppermute | solution.py:22
  23.1 0.2 pack.1
  23.3 0.1 collective-permute-start.5
  23.4 0.9 %collective-permute-start.6 = (bf16[16,1024]{1,0:T(8,128)(2,1)S(1)}, bf16[16,1024]{1,0:T(8,128)(2,1)S(1)}, u32[]{:S(2)}, u32[]{:S(2)}) collective-permute-start(bf16[16,1024]{1,0:T(8,128)(2,1)S(1)} %get-tuple-element.30), channel_id=1, source_target_pairs={{0,6},{1,7},{2,4},{3,5},{4,2},{5,3},{6,0},{7,1},{8,14},{9,15},{10,... | collective-permute-start | bytes 98312 | tf_op jit(solution)/shard_map/ppermute | solution.py:22
  24.3 2.6 %collective-permute-start.7 = (bf16[16,1024]{1,0:T(8,128)(2,1)S(1)}, bf16[16,1024]{1,0:T(8,128)(2,1)S(1)}, u32[]{:S(2)}, u32[]{:S(2)}) collective-permute-start(bf16[16,1024]{1,0:T(8,128)(2,1)S(1)} %get-tuple-element.31), channel_id=1, source_target_pairs={{0,2},{1,3},{2,0},{3,1},{4,6},{5,7},{6,4},{7,5},{8,10},{9,11},{10,... | collective-permute-start | bytes 98312 | tf_op jit(solution)/shard_map/ppermute | solution.py:22
  26.9 1.6 %collective-permute-done.5.refs_0_ = bf16[16,1024]{1,0:T(8,128)(2,1)S(1)} collective-permute-done((bf16[16,1024]{1,0:T(8,128)(2,1)S(1)}, bf16[16,1024]{1,0:T(8,128)(2,1)S(1)}, u32[]{:S(2)}, u32[]{:S(2)}) %collective-permute-start.5) | collective-permute-done | bytes 32800 | tf_op jit(solution)/shard_map/ppermute | solution.py:22
  28.5 0.8 %collective-permute-done.6.refs_1_ = bf16[16,1024]{1,0:T(8,128)(2,1)S(1)} collective-permute-done((bf16[16,1024]{1,0:T(8,128)(2,1)S(1)}, bf16[16,1024]{1,0:T(8,128)(2,1)S(1)}, u32[]{:S(2)}, u32[]{:S(2)}) %collective-permute-start.6) | collective-permute-done | bytes 32800 | tf_op jit(solution)/shard_map/ppermute | solution.py:22
  29.3 0.5 %collective-permute-done.7.refs_2_ = bf16[16,1024]{1,0:T(8,128)(2,1)S(1)} collective-permute-done((bf16[16,1024]{1,0:T(8,128)(2,1)S(1)}, bf16[16,1024]{1,0:T(8,128)(2,1)S(1)}, u32[]{:S(2)}, u32[]{:S(2)}) %collective-permute-start.7) | collective-permute-done | bytes 32800 | tf_op jit(solution)/shard_map/ppermute | solution.py:22
  29.8 0.7 %unpack.1 = f32[64,1024]{1,0:T(8,128)} custom-call(s32[1]{0:T(128)} %bitcast.place, bf16[16,1024]{1,0:T(8,128)(2,1)S(1)} %collective-permute-done.5.refs_0_, bf16[16,1024]{1,0:T(8,128)(2,1)S(1)} %collective-permute-done.6.refs_1_, bf16[16,1024]{1,0:T(8,128)(2,1)S(1)} %collective-permute-done.7.refs_2_, bf16[16,1024]{1,0:T(8,128)(2,1)S(1)} %get-tuple-element.32.refs_3_), custom_call_target="tpu_custom_call" | custom-call | flops 1000 | bytes 1000 | tf_op jit(solution)/shard_map/unpack/pallas_call | solution.py:403
Async XLA Ops:
  1.0 16.3 %collective-permute-start = (bf16[2,1,32,16,128]{4,3,2,1,0:T(8,128)(2,1)S(1)}, bf16[2,1,32,16,128]{4,3,2,1,0:T(8,128)(2,1)S(1)}, u32[]{:S(2)}, u32[]{:S(2)}) collective-permute-start(bf16[2,1,32,16,128]{4,3,2,1,0:T(8,128)(2,1)S(1)} %slice_first.1.refs_0_), channel_id=1, source_target_pairs={{0,7},{1,0},{2,1},{3,2},{4,3},{5,4},{6,5},{7,6},{8,15},{9,8},{10,9... | collective-permute-start | bytes 786440 | tf_op jit(solution)/shard_map/ppermute | solution.py:18
  8.3 9.1 %collective-permute-start.1 = (bf16[1,2,32,16,128]{4,3,2,1,0:T(8,128)(2,1)S(1)}, bf16[1,2,32,16,128]{4,3,2,1,0:T(8,128)(2,1)S(1)}, u32[]{:S(2)}, u32[]{:S(2)}) collective-permute-start(bf16[1,2,32,16,128]{4,3,2,1,0:T(8,128)(2,1)S(1)} %get-tuple-element.19), channel_id=1, source_target_pairs={{0,24},{8,0},{16,8},{24,16},{1,25},{9,1},{17,9},{25,17},{2,26},{10... | collective-permute-start | bytes 786440 | tf_op jit(solution)/shard_map/ppermute | solution.py:18
  9.0 8.4 %collective-permute-start.2 = (bf16[1,2,32,16,128]{4,3,2,1,0:T(8,128)(2,1)S(1)}, bf16[1,2,32,16,128]{4,3,2,1,0:T(8,128)(2,1)S(1)}, u32[]{:S(2)}, u32[]{:S(2)}) collective-permute-start(bf16[1,2,32,16,128]{4,3,2,1,0:T(8,128)(2,1)S(1)} %get-tuple-element.20), channel_id=1, source_target_pairs={{0,24},{8,0},{16,8},{24,16},{1,25},{9,1},{17,9},{25,17},{2,26},{10... | collective-permute-start | bytes 786440 | tf_op jit(solution)/shard_map/ppermute | solution.py:18
  10.1 8.2 %collective-permute-start.3 = (bf16[2,1,32,16,128]{4,3,2,1,0:T(8,128)(2,1)S(1)}, bf16[2,1,32,16,128]{4,3,2,1,0:T(8,128)(2,1)S(1)}, u32[]{:S(2)}, u32[]{:S(2)}) collective-permute-start(bf16[2,1,32,16,128]{4,3,2,1,0:T(8,128)(2,1)S(1)} %get-tuple-element.26), channel_id=1, source_target_pairs={{0,7},{1,0},{2,1},{3,2},{4,3},{5,4},{6,5},{7,6},{8,15},{9,8},{10,9... | collective-permute-start | bytes 786440 | tf_op jit(solution)/shard_map/ppermute | solution.py:18
  10.7 6.7 %copy-start = (s32[8,64]{1,0:T(8,128)S(1)}, s32[8,64]{1,0:T(8,128)}, u32[]{:S(2)}) copy-start(s32[8,64]{1,0:T(8,128)} %lists.1) | copy-start | bytes 6148
  18.9 4.3 %collective-permute-start.4 = (bf16[64,512]{1,0:T(8,128)(2,1)S(1)}, bf16[64,512]{1,0:T(8,128)(2,1)S(1)}, u32[]{:S(2)}, u32[]{:S(2)}) collective-permute-start(bf16[64,512]{1,0:T(8,128)(2,1)S(1)} %final.1.late), channel_id=1, source_target_pairs={{0,1},{1,0},{2,3},{3,2},{4,5},{5,4},{6,7},{7,6},{8,9},{9,8},{10,11... | collective-permute-start | bytes 196616 | tf_op jit(solution)/shard_map/ppermute | solution.py:22
  23.3 5.1 %collective-permute-start.5 = (bf16[16,1024]{1,0:T(8,128)(2,1)S(1)}, bf16[16,1024]{1,0:T(8,128)(2,1)S(1)}, u32[]{:S(2)}, u32[]{:S(2)}) collective-permute-start(bf16[16,1024]{1,0:T(8,128)(2,1)S(1)} %get-tuple-element.29), channel_id=1, source_target_pairs={{0,4},{1,5},{2,6},{3,7},{4,0},{5,1},{6,2},{7,3},{8,12},{9,13},{10,... | collective-permute-start | bytes 98312 | tf_op jit(solution)/shard_map/ppermute | solution.py:22
  23.4 5.9 %collective-permute-start.6 = (bf16[16,1024]{1,0:T(8,128)(2,1)S(1)}, bf16[16,1024]{1,0:T(8,128)(2,1)S(1)}, u32[]{:S(2)}, u32[]{:S(2)}) collective-permute-start(bf16[16,1024]{1,0:T(8,128)(2,1)S(1)} %get-tuple-element.30), channel_id=1, source_target_pairs={{0,6},{1,7},{2,4},{3,5},{4,2},{5,3},{6,0},{7,1},{8,14},{9,15},{10,... | collective-permute-start | bytes 98312 | tf_op jit(solution)/shard_map/ppermute | solution.py:22
  24.3 5.5 %collective-permute-start.7 = (bf16[16,1024]{1,0:T(8,128)(2,1)S(1)}, bf16[16,1024]{1,0:T(8,128)(2,1)S(1)}, u32[]{:S(2)}, u32[]{:S(2)}) collective-permute-start(bf16[16,1024]{1,0:T(8,128)(2,1)S(1)} %get-tuple-element.31), channel_id=1, source_target_pairs={{0,2},{1,3},{2,0},{3,1},{4,6},{5,7},{6,4},{7,5},{8,10},{9,11},{10,... | collective-permute-start | bytes 98312 | tf_op jit(solution)/shard_map/ppermute | solution.py:22

commit v20 on v18

--- a/solution.py
+++ b/solution.py
@@ -390,7 +390,7 @@
         cost_estimate=tiny,
         name="pack",
     )(picks, late, late_other)
-    turns = list(range(2, pairs)) + [1]
+    turns = list(range(pairs - 1, 0, -1))
     arrived = [crossed(packed[turn], "xyz", 2 * turn) for turn in turns]
     arrived = pl.pallas_call(
         functools.partial(unpack_kernel, turns=turns + [0]),

time: 30.2 us -> 30.9 us (1.023)
  the two profiles are of different devices: /device:TPU:1 before, /device:TPU:0 now
where the time goes in v20:
time: 30.9 us; the launch traced here: 30.7 us
  starting transfers between devices  14.3 us (46%)
  Pallas kernels  10.9 us (35%)
  waiting for transfers between devices  5.5 us (18%)
    ppermute x4, starting transfers between devices, shifted(): lax.ppermute(array, axis, [(i, (i + by) % count) for i in range(count)])  8.27 us
    pallas_call x1, Pallas kernels, on_device(): pl.pallas_call(after_kernel, in_specs=[smem] + [outside] * 3 + [vmem] * 2...  6.13 us
    ppermute x4, starting transfers between devices, crossed(): lax.ppermute(array, axis, [(i, i ^ bits) for i in range(lax.axis_size(axi...  5.98 us
    ppermute x4, waiting for transfers between devices, crossed(): lax.ppermute(array, axis, [(i, i ^ bits) for i in range(lax.axis_size(axi...  5.48 us
    pallas_call x2, Pallas kernels, sliced(): pl.pallas_call(functools.partial(slice_kernel, sources=sources, skip=len(...  2.18 us
    pallas_call x1, Pallas kernels, on_device(): pl.pallas_call(middle_kernel, in_specs=[smem] + [vmem] * 5, out_specs=[vm...  0.91 us
    pallas_call x1, Pallas kernels, on_device(): pl.pallas_call(functools.partial(unpack_kernel, turns=turns + [0]), in_sp...  0.74 us
  transfers between devices with their start and end apart: 8, of which 3 were waited for; matrix products, arithmetic and copies ran while one was open for 0% of the time, Pallas kernels for 27%

profile of v20, /device:TPU:0, one launch (start us, length us, event | category | flops | bytes accessed | tf_op | source)
XLA Modules:
  0.0 30.7 jit_solution(7781601573769391310)
XLA Ops:
  0.0 1.0 %slice_first.1.refs_0_ = bf16[2,1,32,16,128]{4,3,2,1,0:T(8,128)(2,1)S(1)} custom-call(bf16[4,4,32,16,128]{4,3,2,1,0:T(8,128)(2,1)} %nulls.7), custom_call_target="tpu_custom_call" | custom-call | flops 1000 | bytes 1000 | tf_op jit(solution)/shard_map/slice_first/pallas_call | solution.py:311
  1.0 6.1 %collective-permute-start = (bf16[2,1,32,16,128]{4,3,2,1,0:T(8,128)(2,1)S(1)}, bf16[2,1,32,16,128]{4,3,2,1,0:T(8,128)(2,1)S(1)}, u32[]{:S(2)}, u32[]{:S(2)}) collective-permute-start(bf16[2,1,32,16,128]{4,3,2,1,0:T(8,128)(2,1)S(1)} %slice_first.1.refs_0_), channel_id=1, source_target_pairs={{0,7},{1,0},{2,1},{3,2},{4,3},{5,4},{6,5},{7,6},{8,15},{9,8},{10,9... | collective-permute-start | bytes 786440 | tf_op jit(solution)/shard_map/ppermute | solution.py:18
  7.0 1.2 %slice_rest.1 = (bf16[2,1,32,16,128]{4,3,2,1,0:T(8,128)(2,1)S(1)}, bf16[1,2,32,16,128]{4,3,2,1,0:T(8,128)(2,1)S(1)}, bf16[1,2,32,16,128]{4,3,2,1,0:T(8,128)(2,1)S(1)}) custom-call(bf16[4,4,32,16,128]{4,3,2,1,0:T(8,128)(2,1)} %nulls.7, bf16[2,1,32,16,128]{4,3,2,1,0:T(8,128)(2,1)S(1)} %slice_first.1.refs_0_), custom_call_target="tpu_custom_call" | custom-call | flops 1000 | bytes 1000 | tf_op jit(solution)/shard_map/slice_rest/pallas_call | solution.py:311
  8.3 0.7 %collective-permute-start.1 = (bf16[1,2,32,16,128]{4,3,2,1,0:T(8,128)(2,1)S(1)}, bf16[1,2,32,16,128]{4,3,2,1,0:T(8,128)(2,1)S(1)}, u32[]{:S(2)}, u32[]{:S(2)}) collective-permute-start(bf16[1,2,32,16,128]{4,3,2,1,0:T(8,128)(2,1)S(1)} %get-tuple-element.19), channel_id=1, source_target_pairs={{0,24},{8,0},{16,8},{24,16},{1,25},{9,1},{17,9},{25,17},{2,26},{10... | collective-permute-start | bytes 786440 | tf_op jit(solution)/shard_map/ppermute | solution.py:18
  9.0 1.0 %collective-permute-start.2 = (bf16[1,2,32,16,128]{4,3,2,1,0:T(8,128)(2,1)S(1)}, bf16[1,2,32,16,128]{4,3,2,1,0:T(8,128)(2,1)S(1)}, u32[]{:S(2)}, u32[]{:S(2)}) collective-permute-start(bf16[1,2,32,16,128]{4,3,2,1,0:T(8,128)(2,1)S(1)} %get-tuple-element.20), channel_id=1, source_target_pairs={{0,24},{8,0},{16,8},{24,16},{1,25},{9,1},{17,9},{25,17},{2,26},{10... | collective-permute-start | bytes 786440 | tf_op jit(solution)/shard_map/ppermute | solution.py:18
  9.9 0.2 before.1
  10.1 0.6 %collective-permute-start.3 = (bf16[2,1,32,16,128]{4,3,2,1,0:T(8,128)(2,1)S(1)}, bf16[2,1,32,16,128]{4,3,2,1,0:T(8,128)(2,1)S(1)}, u32[]{:S(2)}, u32[]{:S(2)}) collective-permute-start(bf16[2,1,32,16,128]{4,3,2,1,0:T(8,128)(2,1)S(1)} %get-tuple-element.26), channel_id=1, source_target_pairs={{0,7},{1,0},{2,1},{3,2},{4,3},{5,4},{6,5},{7,6},{8,15},{9,8},{10,9... | collective-permute-start | bytes 786440 | tf_op jit(solution)/shard_map/ppermute | solution.py:18
  10.7 0.0 copy-start
  10.7 6.1 %after.1 = (f32[32,512]{1,0:T(8,128)S(1)}, bf16[4,128,1024]{2,1,0:T(8,128)(2,1)S(1)}) custom-call(s32[1]{0:T(128)} %bitcast.1.group, bf16[4,4,32,16,128]{4,3,2,1,0:T(8,128)(2,1)} %nulls.7, bf16[2,4,32,64,128]{4,3,2,1,0:T(8,128)(2,1)} %time_links.3, bf16[4,2,32,64,128]{4,3,2,1,0:T(8,128)(2,1)} %space_links.3, f32[32,512]{1,0:T(8,128)S(1)} %get-tuple-element.22.early_before, ...), custom_call_target="tpu_custom_call" | custom-call | flops 1000 | bytes 1000 | tf_op jit(solution)/shard_map/after/pallas_call | solution.py:351
  16.8 0.0 collective-permute-done.space_edge
  16.8 0.0 collective-permute-done.1.time_first
  16.8 0.0 collective-permute-done.2.time_second
  16.9 0.0 copy-done
  16.9 0.9 %middle.1 = (f32[24,512]{1,0:T(8,128)S(1)}, f32[2,64,64]{2,1,0:T(8,128)S(1)}) custom-call(s32[1]{0:T(128)} %bitcast.place, s32[8,64]{1,0:T(8,128)S(1)} %copy-done, bf16[2,1,32,16,128]{4,3,2,1,0:T(8,128)(2,1)S(1)} %collective-permute-done.space_edge, bf16[1,2,32,16,128]{4,3,2,1,0:T(8,128)(2,1)S(1)} %collective-permute-done.1.time_first, ...), custom_call_target="tpu_custom_call" | custom-call | flops 1000 | bytes 1000 | tf_op jit(solution)/shard_map/middle/pallas_call | solution.py:361
  17.8 0.0 collective-permute-done.3.space_edge
  17.8 0.6 %final.1.late = bf16[64,512]{1,0:T(8,128)(2,1)S(1)} custom-call(bf16[2,1,32,16,128]{4,3,2,1,0:T(8,128)(2,1)S(1)} %collective-permute-done.3.space_edge, bf16[4,128,1024]{2,1,0:T(8,128)(2,1)S(1)} %get-tuple-element.24.adjoint, f32[32,512]{1,0:T(8,128)S(1)} %get-tuple-element.27.early, f32[24,512]{1,0:T(8,128)S(1)} %get-tuple-element.28.found), custom_call_target="tpu_custom_call" | custom-call | flops 1000 | bytes 1000 | tf_op jit(solution)/shard_map/final/pallas_call | solution.py:373
  18.4 1.5 %collective-permute-start.4 = (bf16[64,512]{1,0:T(8,128)(2,1)S(1)}, bf16[64,512]{1,0:T(8,128)(2,1)S(1)}, u32[]{:S(2)}, u32[]{:S(2)}) collective-permute-start(bf16[64,512]{1,0:T(8,128)(2,1)S(1)} %final.1.late), channel_id=1, source_target_pairs={{0,1},{1,0},{2,3},{3,2},{4,5},{5,4},{6,7},{7,6},{8,9},{9,8},{10,11... | collective-permute-start | bytes 196616 | tf_op jit(solution)/shard_map/ppermute | solution.py:22
  19.9 2.7 %collective-permute-done.4.late_other = bf16[64,512]{1,0:T(8,128)(2,1)S(1)} collective-permute-done((bf16[64,512]{1,0:T(8,128)(2,1)S(1)}, bf16[64,512]{1,0:T(8,128)(2,1)S(1)}, u32[]{:S(2)}, u32[]{:S(2)}) %collective-permute-start.4) | collective-permute-done | bytes 65568 | tf_op jit(solution)/shard_map/ppermute | solution.py:22
  22.6 0.2 pack.1
  22.8 1.4 %collective-permute-start.5 = (bf16[16,1024]{1,0:T(8,128)(2,1)S(1)}, bf16[16,1024]{1,0:T(8,128)(2,1)S(1)}, u32[]{:S(2)}, u32[]{:S(2)}) collective-permute-start(bf16[16,1024]{1,0:T(8,128)(2,1)S(1)} %get-tuple-element.29), channel_id=1, source_target_pairs={{0,6},{1,7},{2,4},{3,5},{4,2},{5,3},{6,0},{7,1},{8,14},{9,15},{10,... | collective-permute-start | bytes 98312 | tf_op jit(solution)/shard_map/ppermute | solution.py:22
  24.2 0.0 collective-permute-start.6
  24.2 3.0 %collective-permute-start.7 = (bf16[16,1024]{1,0:T(8,128)(2,1)S(1)}, bf16[16,1024]{1,0:T(8,128)(2,1)S(1)}, u32[]{:S(2)}, u32[]{:S(2)}) collective-permute-start(bf16[16,1024]{1,0:T(8,128)(2,1)S(1)} %get-tuple-element.31), channel_id=1, source_target_pairs={{0,2},{1,3},{2,0},{3,1},{4,6},{5,7},{6,4},{7,5},{8,10},{9,11},{10,... | collective-permute-start | bytes 98312 | tf_op jit(solution)/shard_map/ppermute | solution.py:22
  27.3 1.3 %collective-permute-done.5.refs_0_ = bf16[16,1024]{1,0:T(8,128)(2,1)S(1)} collective-permute-done((bf16[16,1024]{1,0:T(8,128)(2,1)S(1)}, bf16[16,1024]{1,0:T(8,128)(2,1)S(1)}, u32[]{:S(2)}, u32[]{:S(2)}) %collective-permute-start.5) | collective-permute-done | bytes 32800 | tf_op jit(solution)/shard_map/ppermute | solution.py:22
  28.6 1.4 %collective-permute-done.6.refs_1_ = bf16[16,1024]{1,0:T(8,128)(2,1)S(1)} collective-permute-done((bf16[16,1024]{1,0:T(8,128)(2,1)S(1)}, bf16[16,1024]{1,0:T(8,128)(2,1)S(1)}, u32[]{:S(2)}, u32[]{:S(2)}) %collective-permute-start.6) | collective-permute-done | bytes 32800 | tf_op jit(solution)/shard_map/ppermute | solution.py:22
  30.0 0.0 collective-permute-done.7.refs_2_
  30.0 0.7 %unpack.1 = f32[64,1024]{1,0:T(8,128)} custom-call(s32[1]{0:T(128)} %bitcast.place, bf16[16,1024]{1,0:T(8,128)(2,1)S(1)} %collective-permute-done.5.refs_0_, bf16[16,1024]{1,0:T(8,128)(2,1)S(1)} %collective-permute-done.6.refs_1_, bf16[16,1024]{1,0:T(8,128)(2,1)S(1)} %collective-permute-done.7.refs_2_, bf16[16,1024]{1,0:T(8,128)(2,1)S(1)} %get-tuple-element.32.refs_3_), custom_call_target="tpu_custom_call" | custom-call | flops 1000 | bytes 1000 | tf_op jit(solution)/shard_map/unpack/pallas_call | solution.py:395
Async XLA Ops:
  1.0 15.8 %collective-permute-start = (bf16[2,1,32,16,128]{4,3,2,1,0:T(8,128)(2,1)S(1)}, bf16[2,1,32,16,128]{4,3,2,1,0:T(8,128)(2,1)S(1)}, u32[]{:S(2)}, u32[]{:S(2)}) collective-permute-start(bf16[2,1,32,16,128]{4,3,2,1,0:T(8,128)(2,1)S(1)} %slice_first.1.refs_0_), channel_id=1, source_target_pairs={{0,7},{1,0},{2,1},{3,2},{4,3},{5,4},{6,5},{7,6},{8,15},{9,8},{10,9... | collective-permute-start | bytes 786440 | tf_op jit(solution)/shard_map/ppermute | solution.py:18
  8.3 8.6 %collective-permute-start.1 = (bf16[1,2,32,16,128]{4,3,2,1,0:T(8,128)(2,1)S(1)}, bf16[1,2,32,16,128]{4,3,2,1,0:T(8,128)(2,1)S(1)}, u32[]{:S(2)}, u32[]{:S(2)}) collective-permute-start(bf16[1,2,32,16,128]{4,3,2,1,0:T(8,128)(2,1)S(1)} %get-tuple-element.19), channel_id=1, source_target_pairs={{0,24},{8,0},{16,8},{24,16},{1,25},{9,1},{17,9},{25,17},{2,26},{10... | collective-permute-start | bytes 786440 | tf_op jit(solution)/shard_map/ppermute | solution.py:18
  9.0 7.9 %collective-permute-start.2 = (bf16[1,2,32,16,128]{4,3,2,1,0:T(8,128)(2,1)S(1)}, bf16[1,2,32,16,128]{4,3,2,1,0:T(8,128)(2,1)S(1)}, u32[]{:S(2)}, u32[]{:S(2)}) collective-permute-start(bf16[1,2,32,16,128]{4,3,2,1,0:T(8,128)(2,1)S(1)} %get-tuple-element.20), channel_id=1, source_target_pairs={{0,24},{8,0},{16,8},{24,16},{1,25},{9,1},{17,9},{25,17},{2,26},{10... | collective-permute-start | bytes 786440 | tf_op jit(solution)/shard_map/ppermute | solution.py:18
  10.1 7.7 %collective-permute-start.3 = (bf16[2,1,32,16,128]{4,3,2,1,0:T(8,128)(2,1)S(1)}, bf16[2,1,32,16,128]{4,3,2,1,0:T(8,128)(2,1)S(1)}, u32[]{:S(2)}, u32[]{:S(2)}) collective-permute-start(bf16[2,1,32,16,128]{4,3,2,1,0:T(8,128)(2,1)S(1)} %get-tuple-element.26), channel_id=1, source_target_pairs={{0,7},{1,0},{2,1},{3,2},{4,3},{5,4},{6,5},{7,6},{8,15},{9,8},{10,9... | collective-permute-start | bytes 786440 | tf_op jit(solution)/shard_map/ppermute | solution.py:18
  10.7 6.2 %copy-start = (s32[8,64]{1,0:T(8,128)S(1)}, s32[8,64]{1,0:T(8,128)}, u32[]{:S(2)}) copy-start(s32[8,64]{1,0:T(8,128)} %lists.1) | copy-start | bytes 6148
  18.4 4.3 %collective-permute-start.4 = (bf16[64,512]{1,0:T(8,128)(2,1)S(1)}, bf16[64,512]{1,0:T(8,128)(2,1)S(1)}, u32[]{:S(2)}, u32[]{:S(2)}) collective-permute-start(bf16[64,512]{1,0:T(8,128)(2,1)S(1)} %final.1.late), channel_id=1, source_target_pairs={{0,1},{1,0},{2,3},{3,2},{4,5},{5,4},{6,7},{7,6},{8,9},{9,8},{10,11... | collective-permute-start | bytes 196616 | tf_op jit(solution)/shard_map/ppermute | solution.py:22
  22.8 5.8 %collective-permute-start.5 = (bf16[16,1024]{1,0:T(8,128)(2,1)S(1)}, bf16[16,1024]{1,0:T(8,128)(2,1)S(1)}, u32[]{:S(2)}, u32[]{:S(2)}) collective-permute-start(bf16[16,1024]{1,0:T(8,128)(2,1)S(1)} %get-tuple-element.29), channel_id=1, source_target_pairs={{0,6},{1,7},{2,4},{3,5},{4,2},{5,3},{6,0},{7,1},{8,14},{9,15},{10,... | collective-permute-start | bytes 98312 | tf_op jit(solution)/shard_map/ppermute | solution.py:22
  24.2 5.8 %collective-permute-start.6 = (bf16[16,1024]{1,0:T(8,128)(2,1)S(1)}, bf16[16,1024]{1,0:T(8,128)(2,1)S(1)}, u32[]{:S(2)}, u32[]{:S(2)}) collective-permute-start(bf16[16,1024]{1,0:T(8,128)(2,1)S(1)} %get-tuple-element.30), channel_id=1, source_target_pairs={{0,4},{1,5},{2,6},{3,7},{4,0},{5,1},{6,2},{7,3},{8,12},{9,13},{10,... | collective-permute-start | bytes 98312 | tf_op jit(solution)/shard_map/ppermute | solution.py:22
  24.2 5.8 %collective-permute-start.7 = (bf16[16,1024]{1,0:T(8,128)(2,1)S(1)}, bf16[16,1024]{1,0:T(8,128)(2,1)S(1)}, u32[]{:S(2)}, u32[]{:S(2)}) collective-permute-start(bf16[16,1024]{1,0:T(8,128)(2,1)S(1)} %get-tuple-element.31), channel_id=1, source_target_pairs={{0,2},{1,3},{2,0},{3,1},{4,6},{5,7},{6,4},{7,5},{8,10},{9,11},{10,... | collective-permute-start | bytes 98312 | tf_op jit(solution)/shard_map/ppermute | solution.py:22
